TPU v7x, 32 devices: a whole 2x2x4 slice. The times are simulated.
32 devices in a mesh: rows: 8 (over z, y), batch: 4 (over x, core).
Axes of the slice: x: 2, y: 2, z: 4, core: 2. Of those that a mesh axis runs over, the one named last changes fastest.
Arguments:
- features: bfloat16 [3, 4, 208, 14, 1024], P(None, 'batch', 'rows'), may hold values from -29 to 29
- view_kind: int32 [3, 4, 24], P(None, 'batch'), may hold values from 0 to 1, as said below
- narrow_one: bfloat16 [1024, 256], P('rows'), may hold values from -0.1875 to 0.1875
- spatial_one: bfloat16 [2304, 256], P('rows'), may hold values from -0.125 to 0.125
- expand_one: bfloat16 [256, 1024], P('rows'), may hold values from -0.375 to 0.375
- gains_one: float32 [1536], replicated, may hold values from 0.1 to 1.9
- biases_one: float32 [1536], replicated, may hold values from -2.5 to 2.5
- narrow_two: bfloat16 [1024, 512], P('rows'), may hold values from -0.1875 to 0.1875
- spatial_two: bfloat16 [4608, 512], P('rows'), may hold values from -0.09375 to 0.09375
- expand_two: bfloat16 [512, 2048], P('rows'), may hold values from -0.25 to 0.25
- shortcut: bfloat16 [1024, 2048], P('rows'), may hold values from -0.1875 to 0.1875
- gains_two: float32 [5120], replicated, may hold values from 0.1 to 1.9
- biases_two: float32 [5120], replicated, may hold values from -2.5 to 2.5
- cotangent: bfloat16 [3, 4, 152, 7, 2048], P(None, 'batch', 'rows'), may hold values from -6 to 6
Outputs:
- outputs: bfloat16 [3, 4, 152, 7, 2048], P(None, 'batch', 'rows')
- grad_input: float32 [3, 4, 208, 14, 1024], P(None, 'batch', 'rows')
- grad_narrow_one: float32 [1024, 256], P('rows')
- grad_spatial_one: float32 [2304, 256], P('rows')
- grad_expand_one: float32 [256, 1024], P('rows')
- grad_gains_one: float32 [1536], replicated
- grad_biases_one: float32 [1536], replicated
- grad_narrow_two: float32 [1024, 512], P('rows')
- grad_spatial_two: float32 [4608, 512], P('rows')
- grad_expand_two: float32 [512, 2048], P('rows')
- grad_shortcut: float32 [1024, 2048], P('rows')
- grad_gains_two: float32 [5120], replicated
- grad_biases_two: float32 [5120], replicated
Inputs may be any that keep to these rules, and one draw needn't show every extreme that they name: `view_kind`: for each micro-batch and image group exactly 8 entries are 1 and 16 are 0, so the views fill the 208 stacked rows exactly.
All inputs are finite; a program needn't handle non-finite values.
Results may differ from a plain program's by a relative error of at most 0.02.
Values may be sent and summed in bfloat16 or wider, within the bound.
No kernel may reach another device: no remote copies, remote signals or barrier semaphores. Data moves between devices by JAX's collectives and lax.ppermute only.
A program may use at most 256 MiB of HBM per device.

v0:
```python
import jax
import jax.numpy as jnp
from jax import lax
from jax.sharding import PartitionSpec as P

SPILL = 12


EPS = 1e-05


def with_halo(cells, sides, width):
    for axis, dim in sides:
        count = lax.axis_size(axis)
        ends = count - 1
        head = lax.slice_in_dim(cells, 0, width, axis=dim)
        tail = lax.slice_in_dim(cells, cells.shape[dim] - width, cells.shape[dim], axis=dim)
        cells = jnp.concatenate(
            [
                lax.ppermute(tail, axis, [(i, (i + 1) % count) for i in range(ends)]),
                cells,
                lax.ppermute(head, axis, [((i + 1) % count, i) for i in range(ends)]),
            ],
            axis=dim,
        )
    return cells


def from_behind(x, axis, by):
    devices = lax.axis_size(axis)
    pairs = [(i, i + by) for i in range(devices) if 0 <= i + by < devices]
    return lax.ppermute(x, axis, pairs)


def layout(view_kinds, row_ids):
    heights = 6 + 8 * view_kinds
    row_ends = jnp.cumsum(heights, dtype=jnp.int32)
    starts = row_ends - heights
    inside = (
        (starts[None, :] <= row_ids[:, None]) & (row_ids[:, None] < row_ends[None, :])
    ).astype(jnp.int32)
    widths = jnp.sum(inside * heights[None, :], axis=1, dtype=jnp.int32)
    firsts = jnp.sum(inside * starts[None, :], axis=1, dtype=jnp.int32)
    return (widths, firsts)


def gelu_grad(location, upstream):
    return jax.vjp(jax.nn.gelu, location)[1](upstream)[0]


def patches_one(framed_in, upper_ok, lower_ok):
    across = framed_in.shape[1]
    above = framed_in[:-2] * upper_ok[:, None, None].astype(framed_in.dtype)
    below = framed_in[2:] * lower_ok[:, None, None].astype(framed_in.dtype)
    pieces = []
    for rowset in (above, framed_in[1:-1], below):
        framed = jnp.pad(rowset, ((0, 0), (1, 1), (0, 0)))
        for offset in range(3):
            pieces.append(framed[:, offset : offset + across])
    return jnp.concatenate(pieces, -1)


def patches_two(planes, not_first):
    row_count, across, middle = planes.shape
    paired = planes.reshape(row_count // 2, 2, across, middle)
    even_rows = paired[:, 0]
    odd_rows = paired[:, 1]
    prior_rows = jnp.concatenate([jnp.zeros_like(odd_rows[:1]), odd_rows[:-1]], 0) * not_first[
        :, None, None
    ].astype(planes.dtype)
    pieces = []
    for rowset in (prior_rows, even_rows, odd_rows):
        split_cols = rowset.reshape(row_count // 2, across // 2, 2, middle)
        even_cols = split_cols[:, :, 0]
        odd_cols = split_cols[:, :, 1]
        left_cols = jnp.concatenate([jnp.zeros_like(odd_cols[:, :1]), odd_cols[:, :-1]], 1)
        pieces.extend([left_cols, even_cols, odd_cols])
    return jnp.concatenate(pieces, -1)


def global_stats(values, cell_mask, population):
    masked = cell_mask[..., None]
    firsts = jnp.stack([jnp.sum(member * masked, axis=(0, 1)) for member in values])
    seconds = jnp.stack([jnp.sum(member * member * masked, axis=(0, 1)) for member in values])
    totals, squares = lax.psum((firsts, seconds), ("rows", "batch"))
    average = totals / population
    inv_std = lax.rsqrt(squares / population - average * average + EPS)
    return (average, inv_std)


def norm_back(slopes, normeds, cell_mask, gain_list, inv_std, population):
    masked = cell_mask[..., None]
    firsts = jnp.stack([jnp.sum(member * masked, axis=(0, 1)) for member in slopes])
    seconds = jnp.stack(
        [
            jnp.sum(member * partner * masked, axis=(0, 1))
            for member, partner in zip(slopes, normeds)
        ]
    )
    bias_sums, gain_sums = lax.psum((firsts, seconds), ("rows", "batch"))
    results = []
    for order_id in range(len(slopes)):
        scale_now = gain_list[order_id] * inv_std[order_id]
        centred = (
            slopes[order_id]
            - bias_sums[order_id] / population
            - normeds[order_id] * (gain_sums[order_id] / population)
        )
        results.append((scale_now * centred * masked).astype(jnp.bfloat16))
    return (results, bias_sums, gain_sums)


def reduce_grads(
    narrow_grad_a,
    spatial_grad_a,
    expand_grad_a,
    narrow_grad_b,
    spatial_grad_b,
    expand_grad_b,
    bypass_grad,
):
    shares = (
        lax.psum_scatter(narrow_grad_a, "rows", scatter_dimension=0, tiled=True),
        lax.psum_scatter(spatial_grad_a, "rows", scatter_dimension=0, tiled=True),
        lax.psum_scatter(expand_grad_a, "rows", scatter_dimension=0, tiled=True),
        lax.psum_scatter(narrow_grad_b, "rows", scatter_dimension=0, tiled=True),
        lax.psum_scatter(spatial_grad_b, "rows", scatter_dimension=0, tiled=True),
        lax.psum_scatter(expand_grad_b, "rows", scatter_dimension=0, tiled=True),
        lax.psum_scatter(bypass_grad, "rows", scatter_dimension=0, tiled=True),
    )
    return (
        lax.psum(shares[0].astype(jnp.bfloat16), "batch").astype(jnp.float32),
        lax.psum(shares[1].astype(jnp.bfloat16), "batch").astype(jnp.float32),
        lax.psum(shares[2].astype(jnp.bfloat16), "batch").astype(jnp.float32),
        lax.psum(shares[3].astype(jnp.bfloat16), "batch").astype(jnp.float32),
        lax.psum(shares[4].astype(jnp.bfloat16), "batch").astype(jnp.float32),
        lax.psum(shares[5].astype(jnp.bfloat16), "batch").astype(jnp.float32),
        lax.psum(shares[6].astype(jnp.bfloat16), "batch").astype(jnp.float32),
    )


def weight_term(left, right):
    return jnp.einsum("rwk,rwn->kn", left, right, preferred_element_type=jnp.float32)


def shards(
    features,
    view_kind,
    narrow_one,
    spatial_one,
    expand_one,
    gains_one,
    biases_one,
    narrow_two,
    spatial_two,
    expand_two,
    shortcut,
    gains_two,
    biases_two,
    cotangent,
):
    micro_count = features.shape[0]
    own_rows = features.shape[2]
    across = features.shape[3]
    middle_one = spatial_one.shape[1]
    middle_two = spatial_two.shape[1]
    outward = shortcut.shape[1]
    window_rows = own_rows + SPILL
    half_rows = window_rows // 2
    sources = lax.axis_size("rows") * own_rows // 52
    full_count = lax.axis_size("batch") * sources * 536
    half_count = lax.axis_size("batch") * sources * 134
    anchor = lax.axis_index("rows") * own_rows
    narrow_a, spatial_a, expand_a = (
        lax.all_gather(narrow_one, "rows", axis=0, tiled=True),
        lax.all_gather(spatial_one, "rows", axis=0, tiled=True),
        lax.all_gather(expand_one, "rows", axis=0, tiled=True),
    )
    narrow_b, spatial_b, expand_b, bypass = (
        lax.all_gather(narrow_two, "rows", axis=0, tiled=True),
        lax.all_gather(spatial_two, "rows", axis=0, tiled=True),
        lax.all_gather(expand_two, "rows", axis=0, tiled=True),
        lax.all_gather(shortcut, "rows", axis=0, tiled=True),
    )
    channels = narrow_a.shape[0]
    flipped = (
        spatial_a.reshape(9, middle_one, middle_one)[::-1]
        .transpose(0, 2, 1)
        .reshape(9 * middle_one, middle_one)
    )
    gain_parts = jnp.split(gains_one, [middle_one, 2 * middle_one])
    bias_parts = jnp.split(biases_one, [middle_one, 2 * middle_one])
    later_cuts = [middle_two, 2 * middle_two, 2 * middle_two + outward]
    gain_later = jnp.split(gains_two, later_cuts)
    bias_later = jnp.split(biases_two, later_cuts)
    columns = jnp.arange(across, dtype=jnp.int32)
    half_columns = jnp.arange(across // 2, dtype=jnp.int32)
    block_ids = anchor - 1 + jnp.arange(own_rows + 2, dtype=jnp.int32)
    window_ids = anchor + jnp.arange(window_rows, dtype=jnp.int32)
    shapes = [
        narrow_a.shape,
        spatial_a.shape,
        expand_a.shape,
        narrow_b.shape,
        spatial_b.shape,
        expand_b.shape,
        bypass.shape,
    ]
    local_grads = [jnp.zeros(shape_now, jnp.float32) for shape_now in shapes]
    gain_acc_one = jnp.zeros(gains_one.shape, jnp.float32)
    bias_acc_one = jnp.zeros(biases_one.shape, jnp.float32)
    gain_acc_two = jnp.zeros(gains_two.shape, jnp.float32)
    bias_acc_two = jnp.zeros(biases_two.shape, jnp.float32)
    outcomes = []
    grad_inputs = []
    for micro_id in range(micro_count):
        view_kinds = view_kind[micro_id, 0]
        widths_a, starts_a = layout(view_kinds, block_ids)
        cell_mask = (columns[None, :] < widths_a[1:-1, None]).astype(jnp.float32)
        masked_one = cell_mask[..., None]
        upper_ok = starts_a[:-2] == starts_a[1:-1]
        lower_ok = starts_a[2:] == starts_a[1:-1]
        widths_w, starts_w = layout(view_kinds, window_ids)
        owned_rows = (starts_w >= anchor) & (starts_w < anchor + own_rows) & (widths_w > 0)
        window_mask = (owned_rows[:, None] & (columns[None, :] < widths_w[:, None])).astype(
            jnp.float32
        )
        masked_win = window_mask[..., None]
        half_mask = (
            owned_rows[0::2, None] & (half_columns[None, :] < (widths_w[0::2] // 2)[:, None])
        ).astype(jnp.float32)
        masked_half = half_mask[..., None]
        not_first = starts_w[0::2] != window_ids[0::2]
        entry_rows = features[micro_id, 0] * masked_one.astype(jnp.bfloat16)
        pre_one = jnp.dot(entry_rows, narrow_a, preferred_element_type=jnp.float32)
        average, inv_one = global_stats([pre_one], cell_mask, full_count)
        normed_one = (pre_one - average[0]) * inv_one[0]
        shifted_one = gain_parts[0] * normed_one + bias_parts[0]
        act_one = (jax.nn.gelu(shifted_one) * masked_one).astype(jnp.bfloat16)
        framed_one = with_halo(act_one, (("rows", 0),), 1)
        patch_one = patches_one(framed_one, upper_ok, lower_ok)
        pre_two = jnp.dot(patch_one, spatial_a, preferred_element_type=jnp.float32)
        average, inv_two = global_stats([pre_two], cell_mask, full_count)
        normed_two = (pre_two - average[0]) * inv_two[0]
        shifted_two = gain_parts[1] * normed_two + bias_parts[1]
        act_two = (jax.nn.gelu(shifted_two) * masked_one).astype(jnp.bfloat16)
        pre_three = jnp.dot(act_two, expand_a, preferred_element_type=jnp.float32)
        average, inv_three = global_stats([pre_three], cell_mask, full_count)
        normed_three = (pre_three - average[0]) * inv_three[0]
        summed_one = gain_parts[2] * normed_three + bias_parts[2] + entry_rows.astype(jnp.float32)
        block_out = (jax.nn.gelu(summed_one) * masked_one).astype(jnp.bfloat16)
        borrowed = from_behind(block_out[:SPILL], "rows", -1)
        window = jnp.concatenate([block_out, borrowed], 0)
        pre_four = jnp.dot(window, narrow_b, preferred_element_type=jnp.float32)
        average, inv_four = global_stats([pre_four], window_mask, full_count)
        normed_four = (pre_four - average[0]) * inv_four[0]
        shifted_four = gain_later[0] * normed_four + bias_later[0]
        act_four = (jax.nn.gelu(shifted_four) * masked_win).astype(jnp.bfloat16)
        patch_two = patches_two(act_four, not_first)
        pre_five = jnp.dot(patch_two, spatial_b, preferred_element_type=jnp.float32)
        average, inv_five = global_stats([pre_five], half_mask, half_count)
        normed_five = (pre_five - average[0]) * inv_five[0]
        shifted_five = gain_later[1] * normed_five + bias_later[1]
        act_five = (jax.nn.gelu(shifted_five) * masked_half).astype(jnp.bfloat16)
        pre_six = jnp.dot(act_five, expand_b, preferred_element_type=jnp.float32)
        corner = window.reshape(half_rows, 2, across // 2, 2, channels)[:, 0, :, 0]
        pre_seven = jnp.dot(corner, bypass, preferred_element_type=jnp.float32)
        average, inv_last = global_stats([pre_six, pre_seven], half_mask, half_count)
        normed_six = (pre_six - average[0]) * inv_last[0]
        normed_seven = (pre_seven - average[1]) * inv_last[1]
        joined = (
            gain_later[2] * normed_six
            + bias_later[2]
            + gain_later[3] * normed_seven
            + bias_later[3]
        )
        outcomes.append((jax.nn.gelu(joined) * masked_half).astype(jnp.bfloat16))
        upstream = cotangent[micro_id, 0].astype(jnp.float32)
        d_joined = gelu_grad(joined, upstream * masked_half)
        pair_back, bias_last, gain_last = norm_back(
            [d_joined, d_joined],
            [normed_six, normed_seven],
            half_mask,
            [gain_later[2], gain_later[3]],
            inv_last,
            half_count,
        )
        d_pre_six, d_pre_seven = pair_back
        local_grads[5] = local_grads[5] + weight_term(act_five, d_pre_six)
        local_grads[6] = local_grads[6] + weight_term(corner, d_pre_seven)
        d_act_five = jnp.dot(d_pre_six, expand_b.T, preferred_element_type=jnp.float32)
        d_corner = jnp.dot(d_pre_seven, bypass.T, preferred_element_type=jnp.float32)
        d_five = gelu_grad(shifted_five, d_act_five * masked_half)
        five_back, bias_five, gain_five = norm_back(
            [d_five], [normed_five], half_mask, [gain_later[1]], inv_five, half_count
        )
        d_pre_five = five_back[0]
        local_grads[4] = local_grads[4] + weight_term(patch_two, d_pre_five)
        d_patch = jnp.dot(d_pre_five, spatial_b.T, preferred_element_type=jnp.float32)
        pull_patch = jax.vjp(
            lambda planes: patches_two(planes, not_first), act_four.astype(jnp.float32)
        )[1]
        d_act_four = pull_patch(d_patch)[0]
        d_four = gelu_grad(shifted_four, d_act_four * masked_win)
        four_back, bias_four, gain_four = norm_back(
            [d_four], [normed_four], window_mask, [gain_later[0]], inv_four, full_count
        )
        d_pre_four = four_back[0]
        local_grads[3] = local_grads[3] + weight_term(window, d_pre_four)
        placed = jnp.pad(
            d_corner[:, None, :, None, :], ((0, 0), (0, 1), (0, 0), (0, 1), (0, 0))
        ).reshape(window_rows, across, channels)
        d_window = (
            jnp.dot(d_pre_four, narrow_b.T, preferred_element_type=jnp.float32) + placed
        ).astype(jnp.bfloat16)
        returned = from_behind(d_window[own_rows:], "rows", 1)
        d_block = d_window[:own_rows].astype(jnp.float32) + jnp.pad(
            returned.astype(jnp.float32), ((0, own_rows - SPILL), (0, 0), (0, 0))
        )
        gain_acc_two = gain_acc_two + jnp.concatenate(
            [gain_four[0], gain_five[0], gain_last[0], gain_last[1]]
        )
        bias_acc_two = bias_acc_two + jnp.concatenate(
            [bias_four[0], bias_five[0], bias_last[0], bias_last[1]]
        )
        d_summed = gelu_grad(summed_one, d_block * masked_one)
        three_back, bias_three, gain_three = norm_back(
            [d_summed], [normed_three], cell_mask, [gain_parts[2]], inv_three, full_count
        )
        d_pre_three = three_back[0]
        local_grads[2] = local_grads[2] + weight_term(act_two, d_pre_three)
        d_act_two = jnp.dot(d_pre_three, expand_a.T, preferred_element_type=jnp.float32)
        d_two = gelu_grad(shifted_two, d_act_two * masked_one)
        two_back, bias_two, gain_two = norm_back(
            [d_two], [normed_two], cell_mask, [gain_parts[1]], inv_two, full_count
        )
        d_pre_two = two_back[0]
        local_grads[1] = local_grads[1] + weight_term(patch_one, d_pre_two)
        framed_grad = with_halo(d_pre_two, (("rows", 0),), 1)
        d_act_one = jnp.dot(
            patches_one(framed_grad, upper_ok, lower_ok),
            flipped,
            preferred_element_type=jnp.float32,
        )
        d_one = gelu_grad(shifted_one, d_act_one * masked_one)
        one_back, bias_first, gain_first = norm_back(
            [d_one], [normed_one], cell_mask, [gain_parts[0]], inv_one, full_count
        )
        d_pre_one = one_back[0]
        local_grads[0] = local_grads[0] + weight_term(entry_rows, d_pre_one)
        grad_inputs.append(
            (jnp.dot(d_pre_one, narrow_a.T, preferred_element_type=jnp.float32) + d_summed)
            * masked_one
        )
        gain_acc_one = gain_acc_one + jnp.concatenate([gain_first[0], gain_two[0], gain_three[0]])
        bias_acc_one = bias_acc_one + jnp.concatenate([bias_first[0], bias_two[0], bias_three[0]])
    final_grads = reduce_grads(
        local_grads[0],
        local_grads[1],
        local_grads[2],
        local_grads[3],
        local_grads[4],
        local_grads[5],
        local_grads[6],
    )
    outputs = jnp.stack(outcomes)[:, None]
    grad_input = jnp.stack(grad_inputs)[:, None]
    return (
        outputs,
        grad_input,
        final_grads[0],
        final_grads[1],
        final_grads[2],
        gain_acc_one,
        bias_acc_one,
        final_grads[3],
        final_grads[4],
        final_grads[5],
        final_grads[6],
        gain_acc_two,
        bias_acc_two,
    )


def solution(mesh):
    return jax.shard_map(
        shards,
        mesh=mesh,
        in_specs=(
            P(None, "batch", "rows", None, None),
            P(None, "batch", None),
            P("rows", None),
            P("rows", None),
            P("rows", None),
            P(),
            P(),
            P("rows", None),
            P("rows", None),
            P("rows", None),
            P("rows", None),
            P(),
            P(),
            P(None, "batch", "rows", None, None),
        ),
        out_specs=(
            P(None, "batch", "rows", None, None),
            P(None, "batch", "rows", None, None),
            P("rows", None),
            P("rows", None),
            P("rows", None),
            P(),
            P(),
            P("rows", None),
            P("rows", None),
            P("rows", None),
            P("rows", None),
            P(),
            P(),
        ),
        check_vma=False,
    )
```

profile of v0, /device:TPU:25, one launch (start us, length us, event | category | flops | bytes accessed | tf_op | source)
XLA Modules:
  0.0 1862.9 jit_solution(16543907573209324782)
XLA Ops:
  11.6 23.0 %all_gather.21 = bf16[1024,256]{1,0:T(8,128)(2,1)S(1)} all-gather(bf16[128,256]{1,0:T(8,128)(2,1)S(1)} %copy-done.209), channel_id=1, replica_groups=mesh['rows'=8,'batch'=4] {'rows'}, dimensions={0}, use_global_device_ids=true | all-gather | bytes 589824 | tf_op jit(solution)/shard_map/all_gather | solution.py:175
  40.5 47.0 %all-reduce.83 = (f32[1,256]{1,0:T(1,128)S(1)}, f32[1,256]{1,0:T(1,128)S(1)}, f32[1,256]{1,0:T(1,128)S(1)}, f32[1,256]{1,0:T(1,128)S(1)}, f32[1,256]{1,0:T(1,128)S(1)}, /*index=5*/f32[1,256]{1,0:T(1,128)S(1)}) all-reduce(f32[1,256]{1,0:T(1,128)S(1)} %bitcast.846, ...), channel_id=1, replica_groups=mesh['rows'=8,'batch'=4] {'rows','batch'}, use_global_device_ids=true, to_apply=%region_67.68 | all-reduce | flops 1536 | bytes 12288 | tf_op jit(solution)/shard_map/psum | solution.py:85
  89.6 4.7 collective-permute-start.7
  96.2 4.3 collective-permute-start.4
  102.5 4.3 collective-permute-start.1
  109.3 24.6 %all_gather.23 = bf16[256,1024]{1,0:T(8,128)(2,1)S(1)} all-gather(bf16[32,1024]{1,0:T(8,128)(2,1)S(1)} %copy-done.210), channel_id=1, replica_groups=mesh['rows'=8,'batch'=4] {'rows'}, dimensions={0}, use_global_device_ids=true | all-gather | bytes 589824 | tf_op jit(solution)/shard_map/all_gather | solution.py:177
  135.9 3.0 collective-permute-start
  156.2 47.0 %all-reduce.82 = (f32[1,256]{1,0:T(1,128)S(1)}, f32[1,256]{1,0:T(1,128)S(1)}, f32[1,256]{1,0:T(1,128)S(1)}, f32[1,256]{1,0:T(1,128)S(1)}, f32[1,256]{1,0:T(1,128)S(1)}, /*index=5*/f32[1,256]{1,0:T(1,128)S(1)}) all-reduce(f32[1,256]{1,0:T(1,128)S(1)} %bitcast.860, ...), channel_id=1, replica_groups=mesh['rows'=8,'batch'=4] {'rows','batch'}, use_global_device_ids=true, to_apply=%region_72.73 | all-reduce | flops 1536 | bytes 12288 | tf_op jit(solution)/shard_map/psum | solution.py:85
  208.7 45.3 %all-reduce.81 = (f32[1,1024]{1,0:T(1,128)S(1)}, f32[1,1024]{1,0:T(1,128)S(1)}, f32[1,1024]{1,0:T(1,128)S(1)}, f32[1,1024]{1,0:T(1,128)S(1)}, f32[1,1024]{1,0:T(1,128)S(1)}, /*index=5*/f32[1,1024]{1,0:T(1,128)S(1)}) all-reduce(f32[1,1024]{1,0:T(1,128)S(1)} %bitcast.850, ...), channel_id=1, replica_groups=mesh['rows'=8,'batch'=4] {'rows','batch'}, use_global_device_ids=true, to_apply=%region_76.77 | all-reduce | flops 6144 | bytes 49152 | tf_op jit(solution)/shard_map/psum | solution.py:85
  254.8 3.3 multiply_convert_fusion.4
  260.2 4.8 multiply_convert_fusion.5
  278.3 24.9 %collective-permute-done.2 = bf16[12,14,1024]{2,0,1:T(8,128)(2,1)} collective-permute-done((bf16[12,14,1024]{2,0,1:T(8,128)(2,1)}, bf16[12,14,1024]{2,0,1:T(8,128)(2,1)}, u32[]{:S(2)}, u32[]{:S(2)}) %collective-permute-start.2) | collective-permute-done | bytes 344096 | tf_op jit(solution)/shard_map/ppermute | solution.py:32
  318.3 51.1 %all-reduce.80 = (f32[1,512]{1,0:T(1,128)S(1)}, f32[1,512]{1,0:T(1,128)S(1)}, f32[1,512]{1,0:T(1,128)S(1)}, f32[1,512]{1,0:T(1,128)S(1)}, f32[1,512]{1,0:T(1,128)S(1)}, /*index=5*/f32[1,512]{1,0:T(1,128)S(1)}) all-reduce(f32[1,512]{1,0:T(1,128)S(1)} %bitcast.858, ...), channel_id=1, replica_groups=mesh['rows'=8,'batch'=4] {'rows','batch'}, use_global_device_ids=true, to_apply=%region_82.83 | all-reduce | flops 3072 | bytes 24576 | tf_op jit(solution)/shard_map/psum | solution.py:85
  369.6 12.2 multiply_convert_fusion.20
  415.7 5.0 fusion.20
  424.8 4.6 multiply_reduce_fusion.78
  431.8 3.7 multiply_reduce_fusion.80
  435.5 40.7 %all-reduce.79 = (f32[1,512]{1,0:T(1,128)S(1)}, f32[1,512]{1,0:T(1,128)S(1)}, f32[1,512]{1,0:T(1,128)S(1)}, f32[1,512]{1,0:T(1,128)S(1)}, f32[1,512]{1,0:T(1,128)S(1)}, /*index=5*/f32[1,512]{1,0:T(1,128)S(1)}) all-reduce(f32[1,512]{1,0:T(1,128)S(1)} %bitcast.826, ...), channel_id=1, replica_groups=mesh['rows'=8,'batch'=4] {'rows','batch'}, use_global_device_ids=true, to_apply=%region_86.87 | all-reduce | flops 3072 | bytes 24576 | tf_op jit(solution)/shard_map/psum | solution.py:85
  480.0 4.1 multiply_reduce_fusion.32
  494.4 123.6 %all-reduce.91.cloned.1.call-done = (f32[2,2048]{1,0:T(2,128)}, f32[2,2048]{1,0:T(2,128)}, f32[2,2048]{1,0:T(2,128)}, f32[2,2048]{1,0:T(2,128)}, f32[2,2048]{1,0:T(2,128)}, /*index=5*/f32[2,2048]{1,0:T(2,128)}) async-done(((f32[2,2048]{1,0:T(2,128)}, f32[2,2048]{1,0:T(2,128)}, f32[2,2048]{1,0:T(2,128)}, f32[2,2048]{1,0:T(2,128)}, f32[2,2048]{1,0:T(2,128)}, /*index=5*/f32[2,2048]{1,0:T(2,128)}), ...) | async-done | bytes 98320 | tf_op jit(solution)/shard_map/psum | solution.py:85
  621.7 5.1 multiply_reduce_fusion.14
  627.5 3.1 multiply_reduce_fusion.17
  631.2 3.1 multiply_reduce_fusion.20
  641.7 119.7 %all-reduce.89.cloned.1.call-done = (f32[2,2048]{1,0:T(2,128)}, f32[2,2048]{1,0:T(2,128)}, f32[2,2048]{1,0:T(2,128)}, f32[2,2048]{1,0:T(2,128)}, f32[2,2048]{1,0:T(2,128)}, /*index=5*/f32[2,2048]{1,0:T(2,128)}) async-done(((f32[2,2048]{1,0:T(2,128)}, f32[2,2048]{1,0:T(2,128)}, f32[2,2048]{1,0:T(2,128)}, f32[2,2048]{1,0:T(2,128)}, f32[2,2048]{1,0:T(2,128)}, /*index=5*/f32[2,2048]{1,0:T(2,128)}), ...) | async-done | bytes 98320 | tf_op jit(solution)/shard_map/psum | solution.py:100
  768.3 3.7 multiply_convert_fusion.7
  781.7 40.1 %all-reduce.76 = (f32[512]{0:T(512)S(1)}, f32[512]{0:T(512)S(1)}, f32[512]{0:T(512)S(1)}, f32[512]{0:T(512)S(1)}, f32[512]{0:T(512)S(1)}, /*index=5*/f32[512]{0:T(512)S(1)}) all-reduce(f32[512]{0:T(512)S(1)} %get-tuple-element.139, f32[512]{0:T(512)S(1)} %get-tuple-element.138, ...), channel_id=1, replica_groups=mesh['rows'=8,'batch'=4] {'rows','batch'}, use_global_device_ids=true, to_apply=%region_151.152 | all-reduce | flops 3072 | bytes 24576 | tf_op jit(solution)/shard_map/psum | solution.py:100
  822.5 4.1 fusion.65
  834.8 3.7 reshape.977
  840.7 3.7 reshape.982
  846.5 4.2 reshape.970
  850.8 4.3 fusion.4
  867.9 4.3 fusion
  885.2 4.3 fusion.2
  900.1 3.1 reshape.976
  903.3 6.5 multiply_reduce_fusion.38
  909.8 40.1 %all-reduce.75 = (f32[512]{0:T(512)S(1)}, f32[512]{0:T(512)S(1)}, f32[512]{0:T(512)S(1)}, f32[512]{0:T(512)S(1)}, f32[512]{0:T(512)S(1)}, /*index=5*/f32[512]{0:T(512)S(1)}) all-reduce(f32[512]{0:T(512)S(1)} %get-tuple-element.420, f32[512]{0:T(512)S(1)} %get-tuple-element.421, ...), channel_id=1, replica_groups=mesh['rows'=8,'batch'=4] {'rows','batch'}, use_global_device_ids=true, to_apply=%region_155.156 | all-reduce | flops 3072 | bytes 24576 | tf_op jit(solution)/shard_map/psum | solution.py:100
  958.1 3.0 collective-permute-start.15
  968.2 3.2 collective-permute-done.15
  971.5 5.1 multiply_reduce_fusion.1
  976.6 4.7 collective-permute-done.12
  981.3 9.8 collective-permute-done.9
  991.2 7.3 multiply_reduce_fusion.5
  998.4 41.5 %all-reduce.74 = (f32[1024]{0:T(1024)}, f32[1024]{0:T(1024)}, f32[1024]{0:T(1024)}, f32[1024]{0:T(1024)}, f32[1024]{0:T(1024)}, /*index=5*/f32[1024]{0:T(1024)}) all-reduce(f32[1024]{0:T(1024)} %get-tuple-element.70, f32[1024]{0:T(1024)} %get-tuple-element.69, ...), channel_id=1, replica_groups=mesh['rows'=8,'batch'=4] {'rows','batch'}, use_global_device_ids=true, to_apply=%region_159.160 | all-reduce | flops 6144 | bytes 49152 | tf_op jit(solution)/shard_map/psum | solution.py:100
  1054.2 4.0 multiply_reduce_fusion.56
  1058.2 40.6 %all-reduce.73 = (f32[256]{0:T(256)S(1)}, f32[256]{0:T(256)S(1)}, f32[256]{0:T(256)S(1)}, f32[256]{0:T(256)S(1)}, f32[256]{0:T(256)S(1)}, /*index=5*/f32[256]{0:T(256)S(1)}) all-reduce(f32[256]{0:T(256)S(1)} %get-tuple-element.438, f32[256]{0:T(256)S(1)} %get-tuple-element.439, ...), channel_id=1, replica_groups=mesh['rows'=8,'batch'=4] {'rows','batch'}, use_global_device_ids=true, to_apply=%region_163.164 | all-reduce | flops 1536 | bytes 12288 | tf_op jit(solution)/shard_map/psum | solution.py:100
  1100.8 2.9 collective-permute-start.16
  1103.9 3.3 collective-permute-start.17
  1112.5 3.5 collective-permute-start.11
  1128.8 42.3 %all-reduce.72 = (f32[256]{0:T(256)S(1)}, f32[256]{0:T(256)S(1)}, f32[256]{0:T(256)S(1)}, f32[256]{0:T(256)S(1)}, f32[256]{0:T(256)S(1)}, /*index=5*/f32[256]{0:T(256)S(1)}) all-reduce(f32[256]{0:T(256)S(1)} %copy-done.384, f32[256]{0:T(256)S(1)} %copy-done.383, ...), channel_id=1, replica_groups=mesh['rows'=8,'batch'=4] {'rows','batch'}, use_global_device_ids=true, to_apply=%region_167.168 | all-reduce | flops 1536 | bytes 12288 | tf_op jit(solution)/shard_map/psum | solution.py:100
  1187.8 4.0 fusion.25
  1194.9 3.3 bitcast_add_fusion.4
  1202.3 5.1 bitcast_add_fusion.2
  1210.3 3.0 fusion.59
  1213.3 5.6 bitcast_add_fusion
  1220.2 3.1 maximum_bitcast_fusion.1
  1228.0 13.6 reduce-scatter.8.cloned.1.call-done
  1243.1 68.4 %reduce-scatter.14.cloned.1.call-done = f32[128,512]{1,0:T(8,128)} async-done(((f32[1024,512]{1,0:T(8,128)}), f32[128,512]{1,0:T(8,128)}) %reduce-scatter.14.cloned.1.call-update) | async-done | bytes 262160 | tf_op jit(solution)/shard_map/reduce_scatter | solution.py:126
  1313.2 69.8 %reduce-scatter.10.cloned.1.call-done = f32[288,256]{1,0:T(8,128)} async-done(((f32[2304,256]{1,0:T(8,128)}), f32[288,256]{1,0:T(8,128)}) %reduce-scatter.10.cloned.1.call-update) | async-done | bytes 294928 | tf_op jit(solution)/shard_map/reduce_scatter | solution.py:124
  1384.7 91.5 %reduce-scatter.18.cloned.1.call-done = f32[64,2048]{1,0:T(8,128)} async-done(((f32[512,2048]{1,0:T(8,128)}), f32[64,2048]{1,0:T(8,128)}) %reduce-scatter.18.cloned.1.call-update) | async-done | bytes 524304 | tf_op jit(solution)/shard_map/reduce_scatter | solution.py:128
  1477.9 150.5 %reduce-scatter.20.cloned.1.call-done = f32[128,2048]{1,0:T(8,128)} async-done(((f32[1024,2048]{1,0:T(8,128)}), f32[128,2048]{1,0:T(8,128)}) %reduce-scatter.20.cloned.1.call-update) | async-done | bytes 1048592 | tf_op jit(solution)/shard_map/reduce_scatter | solution.py:129
  1630.6 163.6 %reduce-scatter.16.cloned.1.call-done = f32[576,512]{1,0:T(8,128)} async-done(((f32[4608,512]{1,0:T(8,128)}), f32[576,512]{1,0:T(8,128)}) %reduce-scatter.16.cloned.1.call-update) | async-done | bytes 1179664 | tf_op jit(solution)/shard_map/reduce_scatter | solution.py:127
  1800.0 3.2 maximum_bitcast_fusion
  1803.4 9.6 copy.371
  1814.3 32.1 %all-reduce.93.cloned.1.call-done = (bf16[128,256]{1,0:T(8,128)(2,1)}, bf16[288,256]{1,0:T(8,128)(2,1)}, bf16[32,1024]{1,0:T(8,128)(2,1)}, bf16[128,512]{1,0:T(8...) async-done(((bf16[128,256]{1,0:T(8,128)(2,1)}, bf16[288,256]{1,0:T(8,128)(2,1)}, bf16[32,1024]{1,0:T(8,128)(2,1)}, ...) | async-done | bytes 1785872 | tf_op jit(solution)/shard_map/psum | solution.py:132
  (1292 shorter events, 310.3 us)
Async XLA Ops:
  7.2 143.1 %all-gather.6.cloned.1.call-start = ((), (), s32[]{:S(2)}) async-start(), calls=%async_computation.7 | async-start | bytes 1327104 | tf_op jit(solution)/shard_map/all_gather | solution.py:176
  7.9 304.1 %all-gather.8.cloned.1.call-start = ((), (), s32[]{:S(2)}) async-start(), calls=%async_computation.8 | async-start | bytes 1179648 | tf_op jit(solution)/shard_map/all_gather | solution.py:180
  8.7 407.0 %all-gather.14.cloned.1.call-start = ((), (), s32[]{:S(2)}) async-start(), calls=%async_computation.11 | async-start | bytes 4718592 | tf_op jit(solution)/shard_map/all_gather | solution.py:183
  9.4 415.3 %all-gather.10.cloned.1.call-start = ((), (), s32[]{:S(2)}) async-start(), calls=%async_computation.9 | async-start | bytes 5308416 | tf_op jit(solution)/shard_map/all_gather | solution.py:181
  10.0 470.0 %all-gather.12.cloned.1.call-start = ((), (), s32[]{:S(2)}) async-start(), calls=%async_computation.10 | async-start | bytes 2359296 | tf_op jit(solution)/shard_map/all_gather | solution.py:182
  10.1 77.5 %copy-start.346 = (f32[256]{0:T(256)}, f32[256]{0:T(256)S(1)}, u32[]{:S(2)}) copy-start(f32[256]{0:T(256)S(1)} %split.146) | copy-start | bytes 3076
  11.2 248.8 %copy-start.143 = (f32[26,14]{0,1:T(8,128)}, f32[26,14]{0,1:T(8,128)S(1)}, u32[]{:S(2)}) copy-start(f32[26,14]{0,1:T(8,128)S(1)} %get-tuple-element.496) | copy-start | bytes 4372
  11.2 248.8 %copy-start.219 = (bf16[26,14]{0,1:T(8,128)(2,1)}, bf16[26,14]{0,1:T(8,128)(2,1)S(1)}, u32[]{:S(2)}) copy-start(bf16[26,14]{0,1:T(8,128)(2,1)S(1)} %get-tuple-element.497) | copy-start | bytes 2188
  11.3 192.6 %copy-start.118 = (f32[26,14]{1,0:T(8,128)}, f32[26,14]{1,0:T(8,128)S(1)}, u32[]{:S(2)}) copy-start(f32[26,14]{1,0:T(8,128)S(1)} %copy.273) | copy-start | bytes 4372
  11.4 243.4 %copy-start.146 = (f32[26,14]{0,1:T(8,128)}, f32[26,14]{0,1:T(8,128)S(1)}, u32[]{:S(2)}) copy-start(f32[26,14]{0,1:T(8,128)S(1)} %get-tuple-element.498) | copy-start | bytes 4372
  11.4 243.4 %copy-start.225 = (bf16[26,14]{0,1:T(8,128)(2,1)}, bf16[26,14]{0,1:T(8,128)(2,1)S(1)}, u32[]{:S(2)}) copy-start(bf16[26,14]{0,1:T(8,128)(2,1)S(1)} %get-tuple-element.499) | copy-start | bytes 2188
  11.5 192.5 %copy-start.120 = (f32[26,14]{1,0:T(8,128)}, f32[26,14]{1,0:T(8,128)S(1)}, u32[]{:S(2)}) copy-start(f32[26,14]{1,0:T(8,128)S(1)} %copy.291) | copy-start | bytes 4372
  11.5 248.6 %copy-start.140 = (f32[26,14]{0,1:T(8,128)}, f32[26,14]{0,1:T(8,128)S(1)}, u32[]{:S(2)}) copy-start(f32[26,14]{0,1:T(8,128)S(1)} %get-tuple-element.501) | copy-start | bytes 4372
  11.5 248.6 %copy-start.222 = (bf16[26,14]{0,1:T(8,128)(2,1)}, bf16[26,14]{0,1:T(8,128)(2,1)S(1)}, u32[]{:S(2)}) copy-start(bf16[26,14]{0,1:T(8,128)(2,1)S(1)} %get-tuple-element.500) | copy-start | bytes 2188
  11.6 192.4 %copy-start.122 = (f32[26,14]{1,0:T(8,128)}, f32[26,14]{1,0:T(8,128)S(1)}, u32[]{:S(2)}) copy-start(f32[26,14]{1,0:T(8,128)S(1)} %copy.309) | copy-start | bytes 4372
  36.8 223.3 %copy-start.26 = (bf16[1,1,26,14,1024]{4,3,2,1,0:T(8,128)(2,1)}, bf16[1,1,26,14,1024]{4,3,2,1,0:T(8,128)(2,1)S(1)}, u32[]{:S(2)}) copy-start(bf16[1,1,26,14,1024]{4,3,2,1,0:T(8,128)(2,1)S(1)} %get-tuple-element.293) | copy-start | bytes 2236420
  37.5 50.1 %copy-start.51 = (f32[26,14,256]{2,0,1:T(8,128)}, f32[26,14,256]{2,0,1:T(8,128)S(1)}, u32[]{:S(2)}) copy-start(f32[26,14,256]{2,0,1:T(8,128)S(1)} %fusion.187) | copy-start | bytes 1118212
  38.5 49.2 %copy-start.53 = (f32[26,14,256]{2,0,1:T(8,128)}, f32[26,14,256]{2,0,1:T(8,128)S(1)}, u32[]{:S(2)}) copy-start(f32[26,14,256]{2,0,1:T(8,128)S(1)} %fusion.185) | copy-start | bytes 1118212
  38.7 48.7 %copy-start.339 = (f32[1536]{0:T(1024)S(1)}, f32[1536]{0:T(1024)}, u32[]{:S(2)}) copy-start(f32[1536]{0:T(1024)} %param.20) | copy-start | bytes 18436
  40.5 68.8 %copy-start.210 = (bf16[32,1024]{1,0:T(8,128)(2,1)S(1)}, bf16[32,1024]{1,0:T(8,128)(2,1)}, u32[]{:S(2)}) copy-start(bf16[32,1024]{1,0:T(8,128)(2,1)} %param.18) | copy-start | bytes 196612
  87.5 115.8 %copy-start.269 = (f32[1,256]{1,0:T(1,128)}, f32[1,256]{1,0:T(1,128)S(1)}, u32[]{:S(2)}) copy-start(f32[1,256]{1,0:T(1,128)S(1)} %get-tuple-element.481) | copy-start | bytes 3076
  87.5 116.5 %copy-start.295 = (f32[256]{0:T(256)}, f32[256]{0:T(256)S(1)}, u32[]{:S(2)}) copy-start(f32[256]{0:T(256)S(1)} %get-tuple-element.415) | copy-start | bytes 3076
  87.6 115.7 %copy-start.271 = (f32[1,256]{1,0:T(1,128)}, f32[1,256]{1,0:T(1,128)S(1)}, u32[]{:S(2)}) copy-start(f32[1,256]{1,0:T(1,128)S(1)} %get-tuple-element.523) | copy-start | bytes 3076
  87.6 115.7 %copy-start.273 = (f32[1,256]{1,0:T(1,128)}, f32[1,256]{1,0:T(1,128)S(1)}, u32[]{:S(2)}) copy-start(f32[1,256]{1,0:T(1,128)S(1)} %get-tuple-element.485) | copy-start | bytes 3076
  89.6 49.7 %collective-permute-start.7 = (bf16[1,14,256]{2,1,0:T(8,128)(2,1)S(1)}, bf16[1,14,256]{2,1,0:T(8,128)(2,1)S(1)}, u32[]{:S(2)}, u32[]{:S(2)}) collective-permute-start(bf16[1,14,256]{2,1,0:T(8,128)(2,1)S(1)} %get-tuple-element.348), channel_id=1, source_target_pairs={{4,0},{8,4},{12,8},{16,12},{20,16},{24,20},{28,24},{5,1},{9,5},{13... | collective-permute-start | bytes 21512 | tf_op jit(solution)/shard_map/ppermute | solution.py:22
  94.3 41.6 %collective-permute-start.6 = (bf16[1,14,256]{2,1,0:T(8,128)(2,1)S(1)}, bf16[1,14,256]{2,1,0:T(8,128)(2,1)S(1)}, u32[]{:S(2)}, u32[]{:S(2)}) collective-permute-start(bf16[1,14,256]{2,1,0:T(8,128)(2,1)S(1)} %get-tuple-element.349), channel_id=1, source_target_pairs={{0,4},{4,8},{8,12},{12,16},{16,20},{20,24},{24,28},{1,5},{5,9},{9,... | collective-permute-start | bytes 21512 | tf_op jit(solution)/shard_map/ppermute | solution.py:20
  96.2 43.9 %collective-permute-start.4 = (bf16[1,14,256]{2,1,0:T(8,128)(2,1)S(1)}, bf16[1,14,256]{2,1,0:T(8,128)(2,1)S(1)}, u32[]{:S(2)}, u32[]{:S(2)}) collective-permute-start(bf16[1,14,256]{2,1,0:T(8,128)(2,1)S(1)} %get-tuple-element.344), channel_id=1, source_target_pairs={{4,0},{8,4},{12,8},{16,12},{20,16},{24,20},{28,24},{5,1},{9,5},{13... | collective-permute-start | bytes 21512 | tf_op jit(solution)/shard_map/ppermute | solution.py:22
  100.5 39.2 %collective-permute-start.3 = (bf16[1,14,256]{2,1,0:T(8,128)(2,1)S(1)}, bf16[1,14,256]{2,1,0:T(8,128)(2,1)S(1)}, u32[]{:S(2)}, u32[]{:S(2)}) collective-permute-start(bf16[1,14,256]{2,1,0:T(8,128)(2,1)S(1)} %get-tuple-element.345), channel_id=1, source_target_pairs={{0,4},{4,8},{8,12},{12,16},{16,20},{20,24},{24,28},{1,5},{5,9},{9,... | collective-permute-start | bytes 21512 | tf_op jit(solution)/shard_map/ppermute | solution.py:20
  102.5 44.6 %collective-permute-start.1 = (bf16[1,14,256]{2,1,0:T(8,128)(2,1)S(1)}, bf16[1,14,256]{2,1,0:T(8,128)(2,1)S(1)}, u32[]{:S(2)}, u32[]{:S(2)}) collective-permute-start(bf16[1,14,256]{2,1,0:T(8,128)(2,1)S(1)} %get-tuple-element.340), channel_id=1, source_target_pairs={{4,0},{8,4},{12,8},{16,12},{20,16},{24,20},{28,24},{5,1},{9,5},{13... | collective-permute-start | bytes 21512 | tf_op jit(solution)/shard_map/ppermute | solution.py:22
  106.7 511.2 %all-reduce.91.cloned.1.call-start = ((), (), s32[]{:S(2)}) async-start(), calls=%async_computation.20 | async-start | bytes 196608 | tf_op jit(solution)/shard_map/psum | solution.py:85
  107.2 204.8 %copy-start.161 = (f32[38,14]{0,1:T(8,128)}, f32[38,14]{0,1:T(8,128)S(1)}, u32[]{:S(2)}) copy-start(f32[38,14]{0,1:T(8,128)S(1)} %fusion.312) | copy-start | bytes 6388
  107.4 209.0 %copy-start.163 = (f32[38,14]{0,1:T(8,128)}, f32[38,14]{0,1:T(8,128)S(1)}, u32[]{:S(2)}) copy-start(f32[38,14]{0,1:T(8,128)S(1)} %fusion.315) | copy-start | bytes 6388
  107.7 206.9 %copy-start.165 = (f32[38,14]{0,1:T(8,128)}, f32[38,14]{0,1:T(8,128)S(1)}, u32[]{:S(2)}) copy-start(f32[38,14]{0,1:T(8,128)S(1)} %fusion.309) | copy-start | bytes 6388
  133.9 73.1 %copy-start.24 = (bf16[256,1024]{1,0:T(8,128)(2,1)}, bf16[256,1024]{1,0:T(8,128)(2,1)S(1)}, u32[]{:S(2)}) copy-start(bf16[256,1024]{1,0:T(8,128)(2,1)S(1)} %all_gather.23) | copy-start | bytes 1572868
  135.5 124.6 %copy-start.167 = (f32[1024]{0:T(1024)}, f32[1024]{0:T(1024)S(1)}, u32[]{:S(2)}) copy-start(f32[1024]{0:T(1024)S(1)} %split.149) | copy-start | bytes 12292
  135.9 7.2 collective-permute-start
  153.1 50.9 %copy-start.59 = (f32[26,14,256]{2,1,0:T(8,128)}, f32[26,14,256]{2,1,0:T(8,128)S(1)}, u32[]{:S(2)}) copy-start(f32[26,14,256]{2,1,0:T(8,128)S(1)} %get-tuple-element.502) | copy-start | bytes 1118212
  153.8 50.2 %copy-start.57 = (f32[26,14,256]{2,1,0:T(8,128)}, f32[26,14,256]{2,1,0:T(8,128)S(1)}, u32[]{:S(2)}) copy-start(f32[26,14,256]{2,1,0:T(8,128)S(1)} %get-tuple-element.503) | copy-start | bytes 1118212
  156.2 50.2 %copy-start.61 = (f32[26,14,256]{2,1,0:T(8,128)}, f32[26,14,256]{2,1,0:T(8,128)S(1)}, u32[]{:S(2)}) copy-start(f32[26,14,256]{2,1,0:T(8,128)S(1)} %get-tuple-element.504) | copy-start | bytes 1118212
  258.1 16.2 collective-permute-start.5
  266.8 41.3 %collective-permute-start.8 = (bf16[12,14,1024]{2,0,1:T(8,128)(2,1)}, bf16[12,14,1024]{2,0,1:T(8,128)(2,1)S(1)}, u32[]{:S(2)}, u32[]{:S(2)}) collective-permute-start(bf16[12,14,1024]{2,0,1:T(8,128)(2,1)} %slice.771), channel_id=1, source_target_pairs={{4,0},{8,4},{12,8},{16,12},{20,16},{24,20},{28,24},{5,1},{9,5},{13... | collective-permute-start | bytes 1032200 | tf_op jit(solution)/shard_map/ppermute | solution.py:32
  269.0 34.2 %collective-permute-start.2 = (bf16[12,14,1024]{2,0,1:T(8,128)(2,1)}, bf16[12,14,1024]{2,0,1:T(8,128)(2,1)}, u32[]{:S(2)}, u32[]{:S(2)}) collective-permute-start(bf16[12,14,1024]{2,0,1:T(8,128)(2,1)} %slice.731), channel_id=1, source_target_pairs={{4,0},{8,4},{12,8},{16,12},{20,16},{24,20},{28,24},{5,1},{9,5},{13... | collective-permute-start | bytes 1032200 | tf_op jit(solution)/shard_map/ppermute | solution.py:32
  314.6 54.9 %copy-start.15 = (f32[38,14,512]{2,0,1:T(8,128)}, f32[38,14,512]{2,0,1:T(8,128)S(1)}, u32[]{:S(2)}) copy-start(f32[38,14,512]{2,0,1:T(8,128)S(1)} %get-tuple-element.509) | copy-start | bytes 3268612
  492.4 269.0 %all-reduce.89.cloned.1.call-start = ((), (), s32[]{:S(2)}) async-start(), calls=%async_computation.19 | async-start | bytes 196608 | tf_op jit(solution)/shard_map/psum | solution.py:100
  636.8 589.7 %reduce-scatter.12.cloned.1.call-start = ((), (), s32[]{:S(2)}) async-start(), calls=%async_computation.14 | async-start | bytes 1179648 | tf_op jit(solution)/shard_map/reduce_scatter | solution.py:125
  903.3 47.3 %copy-start.307 = (f32[512]{0:T(512)S(1)}, f32[512]{0:T(512)}, u32[]{:S(2)}) copy-start(f32[512]{0:T(512)} %get-tuple-element.350) | copy-start | bytes 6148
  958.1 13.3 collective-permute-start.15
  963.9 17.3 collective-permute-start.12
  966.3 24.8 %collective-permute-start.9 = (bf16[12,14,1024]{2,0,1:T(8,128)(2,1)S(1)}, bf16[12,14,1024]{2,0,1:T(8,128)(2,1)S(1)}, u32[]{:S(2)}, u32[]{:S(2)}) collective-permute-start(bf16[12,14,1024]{2,0,1:T(8,128)(2,1)S(1)} %slice.795), channel_id=1, source_target_pairs={{0,4},{4,8},{8,12},{12,16},{16,20},{20,24},{24,28},{1,5},{5,9},{9,... | collective-permute-start | bytes 1032200 | tf_op jit(solution)/shard_map/ppermute | solution.py:32
  1054.0 187.5 %reduce-scatter.8.cloned.1.call-start = ((), (), s32[]{:S(2)}) async-start(), calls=%async_computation.12 | async-start | bytes 1179648 | tf_op jit(solution)/shard_map/reduce_scatter | solution.py:123
  1100.8 15.2 collective-permute-start.16
  1103.9 14.7 collective-permute-start.17
  1107.2 12.4 collective-permute-start.14
  1109.7 9.1 collective-permute-start.13
  1112.5 13.6 collective-permute-start.11
  1116.0 9.6 collective-permute-start.10
  1177.8 133.7 %reduce-scatter.14.cloned.1.call-start = ((), (), s32[]{:S(2)}) async-start(), calls=%async_computation.15 | async-start | bytes 2359296 | tf_op jit(solution)/shard_map/reduce_scatter | solution.py:126
  1184.1 198.9 %reduce-scatter.10.cloned.1.call-start = ((), (), s32[]{:S(2)}) async-start(), calls=%async_computation.13 | async-start | bytes 2654208 | tf_op jit(solution)/shard_map/reduce_scatter | solution.py:124
  1191.9 284.3 %reduce-scatter.18.cloned.1.call-start = ((), (), s32[]{:S(2)}) async-start(), calls=%async_computation.17 | async-start | bytes 4718592 | tf_op jit(solution)/shard_map/reduce_scatter | solution.py:128
  1198.2 430.3 %reduce-scatter.20.cloned.1.call-start = ((), (), s32[]{:S(2)}) async-start(), calls=%async_computation.18 | async-start | bytes 9437184 | tf_op jit(solution)/shard_map/reduce_scatter | solution.py:129
  1207.4 586.8 %reduce-scatter.16.cloned.1.call-start = ((), (), s32[]{:S(2)}) async-start(), calls=%async_computation.16 | async-start | bytes 10616832 | tf_op jit(solution)/shard_map/reduce_scatter | solution.py:127
  1218.9 627.5 %all-reduce.93.cloned.1.call-start = ((), (), s32[]{:S(2)}) async-start(), calls=%async_computation.21 | async-start | bytes 3571712 | tf_op jit(solution)/shard_map/psum | solution.py:132
  1630.6 165.8 %copy-start.113 = (bf16[26,14,256]{2,1,0:T(8,128)(2,1)S(1)}, bf16[26,14,256]{2,1,0:T(8,128)(2,1)}, u32[]{:S(2)}) copy-start(bf16[26,14,256]{2,1,0:T(8,128)(2,1)} %copy-done.112) | copy-start | bytes 559108
  1630.6 165.8 %copy-start.148 = (f32[26,14]{0,1:T(8,128)S(1)}, f32[26,14]{0,1:T(8,128)}, u32[]{:S(2)}) copy-start(f32[26,14]{0,1:T(8,128)} %copy-done.146) | copy-start | bytes 4372
  (364 other events, 2219.1 us)
Sparse Core Ops, SparseCore 0:
  10.2 41.1 all-gather.5
  53.6 39.4 all-gather.7
  95.2 76.8 all-gather.13
  174.1 80.6 all-gather.9
  256.8 58.5 all-gather.11
  492.6 125.3 all-reduce.90
  636.9 124.4 all-reduce.88
  1054.1 63.7 reduce-scatter.11
  1177.9 63.6 reduce-scatter.7
  1245.0 66.5 reduce-scatter.13
  1315.1 67.9 reduce-scatter.9
  1387.1 89.0 reduce-scatter.17
  1480.2 148.1 reduce-scatter.19
  1631.9 162.2 reduce-scatter.15
  1798.1 48.3 all-reduce.92
where the time goes:
time: 1880 us; the launch traced here: 1860 us
  waiting for transfers between devices  881 us (47%)
  blocking collectives  483 us (26%)
  other arithmetic  147 us (8%)
  local copies, waits for them, and re-layouts  145 us (8%)
  matrix products  134 us (7%)
  starting transfers between devices  52.2 us (3%)
  between operations  20.9 us (1%)
    psum x5, blocking collectives, global_stats(): totals, squares = lax.psum((firsts, seconds), ('rows', 'batch'))  231 us
    psum x5, blocking collectives, norm_back(): bias_sums, gain_sums = lax.psum((firsts, seconds), ('rows', 'batch'))  205 us
    reduce_scatter x1, waiting for transfers between devices, reduce_grads(): lax.psum_scatter(spatial_grad_b, 'rows', scatter_dimension=0, tiled=True)  164 us
    reduce_scatter x1, waiting for transfers between devices, reduce_grads(): lax.psum_scatter(bypass_grad, 'rows', scatter_dimension=0, tiled=True)  151 us
    psum x1, waiting for transfers between devices, global_stats(): totals, squares = lax.psum((firsts, seconds), ('rows', 'batch'))  124 us
    psum x1, waiting for transfers between devices, norm_back(): bias_sums, gain_sums = lax.psum((firsts, seconds), ('rows', 'batch'))  120 us
    reduce_scatter x1, waiting for transfers between devices, reduce_grads(): lax.psum_scatter(expand_grad_b, 'rows', scatter_dimension=0, tiled=True)  91.5 us
    reduce_scatter x1, waiting for transfers between devices, reduce_grads(): lax.psum_scatter(spatial_grad_a, 'rows', scatter_dimension=0, tiled=True)  69.8 us
  transfers between devices with their start and end apart: 33, of which 15 were waited for; matrix products, arithmetic and copies ran while one was open for 12% of the time, Pallas kernels for 0%

commit v1 on v0

v1 whole, which is shorter than its diff:
```python
import functools

import jax
import jax.numpy as jnp
from jax import lax
from jax.experimental import pallas as pl
from jax.experimental.pallas import tpu as pltpu
from jax.sharding import PartitionSpec as P

SPILL = 12
WIN = 40
COLS = 16
EPS = 1e-05
AXES = ("rows", "batch")
BF = jnp.bfloat16
F32 = jnp.float32
CHUNK = 32
TANH_SCALE = 0.7978845608028654
TANH_CUBE = 0.044715


def gelu(x):
    return 0.5 * x * (1.0 + jnp.tanh(TANH_SCALE * (x + TANH_CUBE * x * x * x)))


def gelu_slope(x):
    square = x * x
    t = jnp.tanh(TANH_SCALE * x * (1.0 + TANH_CUBE * square))
    return 0.5 * (1.0 + t) + 0.5 * TANH_SCALE * x * (1.0 - t * t) * (1.0 + 3.0 * TANH_CUBE * square)


def nn(a, b):
    return lax.dot_general(a, b, (((1,), (0,)), ((), ())), preferred_element_type=F32)


def nt(a, b):
    return lax.dot_general(a, b, (((1,), (1,)), ((), ())), preferred_element_type=F32)


def pick(ref, row, start=0, width=None):
    table = ref[:, start : start + (width or ref.shape[1])]
    rows = lax.broadcasted_iota(jnp.int32, table.shape, 0)
    return jnp.sum(jnp.where(rows == row, table, 0.0), axis=0, keepdims=True)


def moments(ref, m, population):
    average = pick(ref, 2 * m) * (1.0 / population)
    inv = lax.rsqrt(pick(ref, 2 * m + 1) * (1.0 / population) - average * average + EPS)
    return average, inv


def means(ref, m, population, start=0, width=None):
    share = 1.0 / population
    return pick(ref, 2 * m, start, width) * share, pick(ref, 2 * m + 1, start, width) * share


def put_sums(ref, m, first, second, start=0):
    c = first.shape[1]
    at = slice(start, start + c)

    @pl.when(m == 0)
    def _():
        ref[:, at] = jnp.zeros((ref.shape[0], c), F32)

    first = jnp.sum(first, axis=0, keepdims=True)
    second = jnp.sum(second, axis=0, keepdims=True)
    rows = lax.broadcasted_iota(jnp.int32, (ref.shape[0], c), 0)
    ref[:, at] = jnp.where(rows == 2 * m, first, jnp.where(rows == 2 * m + 1, second, ref[:, at]))


def fold(x):
    return jnp.sum(x.reshape(-1, 8, x.shape[-1]), axis=0)


def over(count, step, body, carry=None):
    def run(i, c):
        return body(pl.multiple_of(i * step, step), c)

    if carry is None:
        lax.fori_loop(0, count // step, lambda i, c: (run(i, None), 0)[1], 0)
        return None
    return lax.fori_loop(0, count // step, run, carry)


LANES = 128


def put_tall(ref, rows, value):
    for j in range(ref.shape[0]):
        ref[j, rows, :] = value[:, j * LANES : (j + 1) * LANES]


def get_tall(ref, rows):
    return jnp.concatenate([ref[j, rows, :] for j in range(ref.shape[0])], 1)


def zero_pair(c):
    return jnp.zeros((8, c), F32), jnp.zeros((8, c), F32)


def sum_pair(carry, a, b):
    return carry[0] + fold(a), carry[1] + fold(a * b)


OWN, MINE, UPPER, LOWER = 0, 1, 2, 3
HALF, INNER = 0, 1


def lane(ref, which, rows):
    return ref[0, rows, which : which + 1]


def k_masks(own, anchor, kinds, full, halved):
    first = anchor[0]
    height_of = lambda m, v: 6 + 8 * kinds[m, 0, v]
    for m in range(full.shape[0]):
        rows = full.shape[1] // COLS
        row = first + lax.broadcasted_iota(jnp.int32, (rows, LANES), 0)

        def view(v, c):
            at, width, start, last = c
            height = height_of(m, v)
            inside = (row >= at) & (row < at + height)
            return (
                at + height,
                jnp.where(inside, height, width),
                jnp.where(inside, at, start),
                jnp.where(inside, at + height - 1, last),
            )

        zero = jnp.zeros((rows, LANES), jnp.int32)
        _, width, start, last = lax.fori_loop(0, kinds.shape[2], view, (jnp.int32(0), zero, zero, zero))
        owned = (start >= first) & (start < first + own) & (width > 0)
        mine = jnp.where(owned, width, 0)
        above = (start != row).astype(F32)
        below = (last != row).astype(F32)
        cells = lambda v, n: jnp.broadcast_to(v[:, None, :], (v.shape[0], n, LANES))
        shape = (rows, COLS, LANES)
        column = lax.broadcasted_iota(jnp.int32, shape, 1)
        lanes = lax.broadcasted_iota(jnp.int32, shape, 2)
        value = jnp.where(lanes == OWN, (column < cells(width, COLS)).astype(F32), 0.0)
        value = jnp.where(lanes == MINE, (column < cells(mine, COLS)).astype(F32), value)
        value = jnp.where(lanes == UPPER, cells(above, COLS), value)
        value = jnp.where(lanes == LOWER, cells(below, COLS), value)
        full[m] = value.reshape(rows * COLS, LANES)
        shape = (rows, COLS // 2, LANES)
        column = lax.broadcasted_iota(jnp.int32, shape, 1)
        lanes = lax.broadcasted_iota(jnp.int32, shape, 2)
        value = jnp.where(lanes == HALF, (2 * column < cells(mine, COLS // 2)).astype(F32), 0.0)
        value = jnp.where(lanes == INNER, cells(above, COLS // 2), value)
        value = value.reshape(rows // 2, 2, COLS // 2, LANES)[:, 0]
        halved[m] = value.reshape(rows * COLS // 4, LANES)


def k_first(pieces, place, features, mask, *refs):
    parts, (pre, head, total, weight, rows) = refs[:pieces], refs[pieces:]
    m = pl.program_id(0)
    own, across = features.shape[2], features.shape[3]

    @pl.when(m == 0)
    def _():
        if pieces == 1:
            weight[...] = parts[0][...]
        else:
            size = parts[0].shape[0]
            half = size // 2
            weight[pl.ds(pl.multiple_of(place[0] * size, size), size), :] = parts[0][...]
            for k in range(1, pieces // 2 + 1):
                for side in range(2):
                    at = jnp.bitwise_xor(place[0], k) * size + jnp.bitwise_xor(place[1], side) * half
                    weight[pl.ds(pl.multiple_of(at, half), half), :] = parts[2 * k - 1 + side][...]
        rows[...] = jnp.zeros_like(rows)

    for r in range(own):
        rows[r * COLS : r * COLS + across, :] = features[0, 0, r]
    pre[0] = nn(rows[...] * lane(mask, OWN, slice(0, own * COLS)).astype(BF), weight[...])
    head[0] = pre[0, 0 : head.shape[1], :].astype(BF)

    def add(r, c):
        p = pre[0, pl.ds(r, CHUNK), :]
        return sum_pair(c, p, p)

    put_sums(total, m, *over(own * COLS, CHUNK, add, zero_pair(pre.shape[2])))


def k_entry(features, mask, *refs):
    spills, (entry, rows) = refs[:-2], refs[-2:]
    m = pl.program_id(0)
    own, across = features.shape[2], features.shape[3]

    @pl.when(m == 0)
    def _():
        rows[...] = jnp.zeros_like(rows)

    for r in range(own):
        rows[r * COLS : r * COLS + across, :] = features[0, 0, r]
    for k, spill in enumerate(spills):

        @pl.when(m == k)
        def _():
            for r in range(spill.shape[0]):
                at = (own + r) * COLS
                rows[at : at + across, :] = spill[r]

    entry[0] = rows[...] * lane(mask, MINE, slice(None)).astype(BF)


def load_pre_one(own, spill, r, size):
    edge = own.shape[1]
    if r < edge:
        return own[0, r : r + size, :]
    if r - edge < spill.shape[1]:
        return spill[0, r - edge : r - edge + size, :].astype(F32)
    return jnp.zeros((size, own.shape[2]), F32)


def spread_trio(source, trio, cells):
    c = source.shape[1]
    trio[0:COLS, :] = jnp.zeros((COLS, 3 * c), BF)
    trio[COLS + cells : 2 * COLS + cells, :] = jnp.zeros((COLS, 3 * c), BF)
    for r in range(0, cells, CHUNK):
        for tap in range(3):
            part = source[COLS + r + tap - 1 : COLS + r + tap - 1 + CHUNK, :]
            trio[COLS + r : COLS + r + CHUNK, tap * c : (tap + 1) * c] = part.astype(BF)


def conv_rows(trio, mask, weight, cells):
    width = trio.shape[1]
    upper = lane(mask, UPPER, slice(None)).astype(BF)
    lower = lane(mask, LOWER, slice(None)).astype(BF)
    above = trio[0:cells, :] * upper
    here = trio[COLS : COLS + cells, :]
    below = trio[2 * COLS : 2 * COLS + cells, :] * lower
    total = (
        nn(above, weight[0:width, :])
        + nn(here, weight[width : 2 * width, :])
        + nn(below, weight[2 * width : 3 * width, :])
    )
    return total, (above, here, below)


def k_second(count, own, spill, total, gain, bias, mask, weight, pre, patch, out_total, act, trio):
    m = pl.program_id(0)
    cells, c = mask.shape[1], own.shape[2]
    average, inv = moments(total, m, count)
    scale = inv * gain[...]
    act[0:COLS, :] = jnp.zeros((COLS, c), F32)
    act[COLS + cells : 2 * COLS + cells, :] = jnp.zeros((COLS, c), F32)
    for r in range(0, cells, CHUNK):
        x = (load_pre_one(own, spill, r, CHUNK) - average) * scale + bias[...]
        act[COLS + r : COLS + r + CHUNK, :] = gelu(x) * lane(mask, MINE, slice(r, r + CHUNK))
    spread_trio(act, trio, cells)
    result, parts = conv_rows(trio, mask, weight, cells)
    pre[0] = result
    for k, part in enumerate(parts):
        patch[0, :, k * 3 * c : (k + 1) * 3 * c] = part

    def add(r, carry):
        p = pre[0, pl.ds(r, CHUNK), :]
        return sum_pair(carry, p * lane(mask, MINE, pl.ds(r, CHUNK)), p)

    put_sums(out_total, m, *over(cells, CHUNK, add, zero_pair(c)))


def k_third(count, which, pre_in, total, gain, bias, mask, weight, act, pre, out_total):
    m = pl.program_id(0)
    cells = pre_in.shape[1]
    average, inv = moments(total, m, count)
    scale = inv * gain[...]

    def step(r, _):
        x = (pre_in[0, pl.ds(r, CHUNK), :] - average) * scale + bias[...]
        act[0, pl.ds(r, CHUNK), :] = (gelu(x) * lane(mask, which, pl.ds(r, CHUNK))).astype(BF)

    over(cells, CHUNK, step)
    pre[0] = nn(act[0], weight[...])

    def add(r, carry):
        p = pre[0, pl.ds(r, CHUNK), :]
        return sum_pair(carry, p, p)

    put_sums(out_total, m, *over(cells, CHUNK, add, zero_pair(pre.shape[2])))


def k_fourth(count, pre_in, entry, total, gain, bias, mask, weight, block, corner, pre, out_total, full):
    m = pl.program_id(0)
    cells, c = pre_in.shape[1], pre_in.shape[2]
    average, inv = moments(total, m, count)
    scale = inv * gain[...]

    def step(r, _):
        for k in range(4):
            at = pl.ds(r + k * COLS, COLS)
            x = (pre_in[0, at, :] - average) * scale + bias[...] + entry[0, at, :].astype(F32)
            y = gelu(x) * lane(mask, MINE, at)
            put_tall(full, slice(k * COLS, (k + 1) * COLS), y)
            block[0, at, :] = y.astype(BF)
        pair = [get_tall(full, pl.ds(k * COLS, COLS // 2, stride=2)) for k in (0, 2)]
        corner[0, pl.ds(pl.multiple_of(r // 4, COLS), COLS), :] = jnp.concatenate(pair, 0).astype(BF)

    over(cells, 4 * COLS, step)
    pre[0] = nn(block[0], weight[...])

    def add(r, carry):
        p = pre[0, pl.ds(r, CHUNK), :]
        return sum_pair(carry, p, p)

    put_sums(out_total, m, *over(cells, CHUNK, add, zero_pair(pre.shape[2])))


def k_seventh(corner, weight, pre, out_total):
    m = pl.program_id(1)
    pre[0] = nn(corner[0], weight[...])

    def add(r, carry):
        p = pre[0, pl.ds(r, CHUNK), :]
        return sum_pair(carry, p, p)

    put_sums(out_total, m, *over(pre.shape[1], CHUNK, add, zero_pair(pre.shape[2])))


def k_fifth(count, pre_in, total, gain, bias, mask, half_mask, weight, pre, patch, out_total, act, eo, oe, oo):
    m = pl.program_id(0)
    cells, c = pre_in.shape[1], pre_in.shape[2]
    half = cells // 4
    wide = COLS // 2
    average, inv = moments(total, m, count)
    scale = inv * gain[...]

    def step(r, _):
        x = (pre_in[0, pl.ds(r, CHUNK), :] - average) * scale + bias[...]
        put_tall(act, pl.ds(r, CHUNK), gelu(x) * lane(mask, MINE, pl.ds(r, CHUNK)))

    over(cells, CHUNK, step)
    pad = 2 * wide
    for buf in (eo, oe, oo):
        buf[0:pad, :] = jnp.zeros((pad, c), F32)
    for j in range(c // LANES):
        lanes = slice(j * LANES, (j + 1) * LANES)
        even = act[j, pl.ds(0, cells // 2, stride=2), :].reshape(half // wide, 2, wide, LANES)
        odd = act[j, pl.ds(1, cells // 2, stride=2), :].reshape(half // wide, 2, wide, LANES)
        patch[0, :, 4 * c + j * LANES : 4 * c + (j + 1) * LANES] = even[:, 0].reshape(half, LANES).astype(BF)
        oe[pad : pad + half, lanes] = even[:, 1].reshape(half, LANES)
        eo[pad : pad + half, lanes] = odd[:, 0].reshape(half, LANES)
        oo[pad : pad + half, lanes] = odd[:, 1].reshape(half, LANES)
    first = lane(half_mask, INNER, slice(None))
    take = lambda buf, back: buf[pad - back : pad - back + half, :]
    taps = (
        take(oo, wide + 1) * first, take(oe, wide) * first, take(oo, wide) * first,
        take(eo, 1), None, take(eo, 0),
        take(oo, 1), take(oe, 0), take(oo, 0),
    )
    for k, tap in enumerate(taps):
        if tap is not None:
            patch[0, :, k * c : (k + 1) * c] = tap.astype(BF)
    pre[0] = nn(patch[0], weight[...])

    def add(r, carry):
        p = pre[0, pl.ds(r, CHUNK), :]
        return sum_pair(carry, p * lane(half_mask, HALF, pl.ds(r, CHUNK)), p)

    put_sums(out_total, m, *over(half, CHUNK, add, zero_pair(pre.shape[2])))


def k_last(count, six, seven, tot6, tot7, g6, b6, g7, b7, half_mask, cot, out, slope, total, line):
    m = pl.program_id(0)
    half, c = six.shape[1], six.shape[2]
    wide = COLS // 2
    shown, across = out.shape[2], out.shape[3]
    avg6, inv6 = moments(tot6, m, count)
    avg7, inv7 = moments(tot7, m, count)
    line[...] = jnp.zeros_like(line)

    def step(p, carry):
        at = pl.ds(pl.multiple_of(p * wide, wide), wide)
        mask = lane(half_mask, HALF, at)
        n6 = (six[0, at, :] - avg6) * inv6
        n7 = (seven[0, at, :] - avg7) * inv7
        joined = g6[...] * n6 + b6[...] + g7[...] * n7 + b7[...]
        out[0, 0, p] = (gelu(joined) * mask)[:across].astype(BF)
        line[0:across, :] = cot[0, 0, p].astype(F32)
        d = gelu_slope(joined) * (line[...] * mask)
        slope[0, at, :] = d
        return carry[0] + d, carry[1] + d * n6, carry[2] + d * n7

    zero = jnp.zeros((wide, c), F32)
    first, second, third = lax.fori_loop(0, shown, step, (zero, zero, zero))
    slope[0, shown * wide :, :] = jnp.zeros((half - shown * wide, c), F32)
    put_sums(total, m, first, second)
    put_sums(total, m, first, third, c)


def k_back_six(
    count, slope, six, seven, tot6, tot7, back, g6, g7, five, tot5, g5, b5, half_mask, weight,
    d_six, d_seven, d_five, out_total,
):
    m = pl.program_id(0)
    half, c = six.shape[1], six.shape[2]
    avg6, inv6 = moments(tot6, m, count)
    avg7, inv7 = moments(tot7, m, count)
    bias6, gain6 = means(back, m, count, 0, c)
    bias7, gain7 = means(back, m, count, c, c)
    scale6, scale7 = g6[...] * inv6, g7[...] * inv7

    def step(r, _):
        at = pl.ds(r, COLS)
        d = slope[0, at, :]
        mask = lane(half_mask, HALF, at)
        n6 = (six[0, at, :] - avg6) * inv6
        d_six[0, at, :] = (scale6 * (d - bias6 - n6 * gain6) * mask).astype(BF)
        n7 = (seven[0, at, :] - avg7) * inv7
        d_seven[0, at, :] = (scale7 * (d - bias7 - n7 * gain7) * mask).astype(BF)

    over(half, COLS, step)
    d_five[0] = nt(d_six[0], weight[...])
    avg5, inv5 = moments(tot5, m, count)

    def add(r, carry):
        at = pl.ds(r, CHUNK)
        n = (five[0, at, :] - avg5) * inv5
        d = gelu_slope(g5[...] * n + b5[...]) * d_five[0, at, :] * lane(half_mask, HALF, at)
        d_five[0, at, :] = d
        return sum_pair(carry, d, n)

    put_sums(out_total, m, *over(half, CHUNK, add, zero_pair(d_five.shape[2])))


def k_corner(d_seven, weight, d_corner):
    d_corner[0] = nt(d_seven[0], weight[...])


def k_back_five(
    half_count, full_count, d_five, five, tot5, back5, g5, half_mask, weight, four, tot4, g4, b4, mask,
    d_pre, d_four, out_total, grid_scratch, shifted,
):
    m = pl.program_id(0)
    half, c = five.shape[1], five.shape[2]
    cells = 4 * half
    wide = COLS // 2
    avg5, inv5 = moments(tot5, m, half_count)
    bias5, gain5 = means(back5, m, half_count)
    n5 = (five[0] - avg5) * inv5
    d = (g5[...] * inv5 * (d_five[0] - bias5 - n5 * gain5) * lane(half_mask, HALF, slice(None))).astype(BF)
    d_pre[0] = d
    wide_d = d.astype(F32)
    tail = 2 * wide
    shifted[half : half + tail, :] = jnp.zeros((tail, c), F32)
    shifted[0:half, :] = wide_d
    right = shifted[1 : 1 + half, :].astype(BF)
    shifted[0:half, :] = wide_d * lane(half_mask, INNER, slice(None))
    down = shifted[wide : wide + half, :].astype(BF)
    down_right = shifted[wide + 1 : wide + 1 + half, :].astype(BF)
    w = lambda tap: weight[tap * c : (tap + 1) * c, :]
    ee = nt(d, w(4))
    eo = nt(d, w(5)) + nt(right, w(3))
    oe = nt(d, w(7)) + nt(down, w(1))
    oo = nt(d, w(8)) + nt(right, w(6)) + nt(down, w(2)) + nt(down_right, w(0))
    rows = half // wide
    even = jnp.stack([ee.reshape(rows, wide, c), oe.reshape(rows, wide, c)], 1).reshape(cells // 2, c)
    odd = jnp.stack([eo.reshape(rows, wide, c), oo.reshape(rows, wide, c)], 1).reshape(cells // 2, c)
    put_tall(grid_scratch, pl.ds(0, cells // 2, stride=2), even)
    put_tall(grid_scratch, pl.ds(1, cells // 2, stride=2), odd)
    avg4, inv4 = moments(tot4, m, full_count)

    def add(r, carry):
        at = pl.ds(r, CHUNK)
        n = (four[0, at, :] - avg4) * inv4
        d = gelu_slope(g4[...] * n + b4[...]) * get_tall(grid_scratch, at) * lane(mask, MINE, at)
        d_four[0, at, :] = d
        return sum_pair(carry, d, n)

    put_sums(out_total, m, *over(cells, CHUNK, add, zero_pair(c)))


def k_back_four(
    count, d_four, four, tot4, back4, g4, mask, weight, d_corner, three, entry, tot3, g3, b3,
    d_pre, d_summed, out_total, placed,
):
    m = pl.program_id(0)
    cells, c = three.shape[1], three.shape[2]
    avg4, inv4 = moments(tot4, m, count)
    bias4, gain4 = means(back4, m, count)
    scale4 = g4[...] * inv4

    def step(r, _):
        at = pl.ds(r, CHUNK)
        n = (four[0, at, :] - avg4) * inv4
        d = scale4 * (d_four[0, at, :] - bias4 - n * gain4) * lane(mask, MINE, at)
        d_pre[0, at, :] = d.astype(BF)

    over(cells, CHUNK, step)
    d_summed[0] = nt(d_pre[0], weight[...])
    avg3, inv3 = moments(tot3, m, count)
    wide = COLS // 2
    placed[...] = jnp.zeros_like(placed)

    def add(r, carry):
        at = pl.ds(r, CHUNK)
        corner_at = pl.ds(pl.multiple_of(r // 4, wide), wide)
        put_tall(placed, pl.ds(0, wide, stride=2), d_corner[0, corner_at, :])
        for k in range(2):
            at = pl.ds(r + k * COLS, COLS)
            got = d_summed[0, at, :]
            if k == 0:
                got = got + get_tall(placed, slice(0, COLS))
            n = (three[0, at, :] - avg3) * inv3
            x = g3[...] * n + b3[...] + entry[0, at, :].astype(F32)
            d = gelu_slope(x) * (got.astype(BF).astype(F32) * lane(mask, MINE, at))
            d_summed[0, at, :] = d
            carry = sum_pair(carry, d, n)
        return carry

    put_sums(out_total, m, *over(cells, CHUNK, add, zero_pair(c)))


def k_back_three(count, d_summed, three, tot3, back3, g3, mask, weight, two, tot2, g2, b2, d_pre, d_two, out_total):
    m = pl.program_id(0)
    cells = three.shape[1]
    avg3, inv3 = moments(tot3, m, count)
    bias3, gain3 = means(back3, m, count)
    scale3 = g3[...] * inv3

    def step(r, _):
        at = pl.ds(r, COLS)
        n = (three[0, at, :] - avg3) * inv3
        d = scale3 * (d_summed[0, at, :] - bias3 - n * gain3) * lane(mask, MINE, at)
        d_pre[0, at, :] = d.astype(BF)

    over(cells, COLS, step)
    d_two[0] = nt(d_pre[0], weight[...])
    avg2, inv2 = moments(tot2, m, count)

    def add(r, carry):
        at = pl.ds(r, CHUNK)
        n = (two[0, at, :] - avg2) * inv2
        d = gelu_slope(g2[...] * n + b2[...]) * d_two[0, at, :] * lane(mask, MINE, at)
        d_two[0, at, :] = d
        return sum_pair(carry, d, n)

    put_sums(out_total, m, *over(cells, CHUNK, add, zero_pair(d_two.shape[2])))


def k_back_two(
    count, d_two, two, tot2, back2, g2, mask, weight, own, spill, tot1, g1, b1,
    d_pre, d_one, out_total, source, trio,
):
    m = pl.program_id(0)
    cells, c = two.shape[1], two.shape[2]
    avg2, inv2 = moments(tot2, m, count)
    bias2, gain2 = means(back2, m, count)
    scale2 = g2[...] * inv2
    source[0:COLS, :] = jnp.zeros((COLS, c), F32)
    source[COLS + cells : 2 * COLS + cells, :] = jnp.zeros((COLS, c), F32)
    for r in range(0, cells, CHUNK):
        n = (two[0, r : r + CHUNK, :] - avg2) * inv2
        d = scale2 * (d_two[0, r : r + CHUNK, :] - bias2 - n * gain2) * lane(mask, MINE, slice(r, r + CHUNK))
        d_pre[0, r : r + CHUNK, :] = d.astype(BF)
        source[COLS + r : COLS + r + CHUNK, :] = d
    spread_trio(source, trio, cells)
    d_one[0] = conv_rows(trio, mask, weight, cells)[0]
    avg1, inv1 = moments(tot1, m, count)
    carry = zero_pair(c)
    for r in range(0, cells, CHUNK):
        n = (load_pre_one(own, spill, r, CHUNK) - avg1) * inv1
        d = gelu_slope(g1[...] * n + b1[...]) * d_one[0, r : r + CHUNK, :] * lane(mask, MINE, slice(r, r + CHUNK))
        d_one[0, r : r + CHUNK, :] = d
        carry = sum_pair(carry, d, n)
    put_sums(out_total, m, *carry)


def k_back_one(count, d_one, own, spill, tot1, back1, g1, mask, d_pre):
    m = pl.program_id(0)
    cells = d_one.shape[1]
    avg1, inv1 = moments(tot1, m, count)
    bias1, gain1 = means(back1, m, count)
    scale1 = g1[...] * inv1
    for r in range(0, cells, CHUNK):
        n = (load_pre_one(own, spill, r, CHUNK) - avg1) * inv1
        d = scale1 * (d_one[0, r : r + CHUNK, :] - bias1 - n * gain1) * lane(mask, MINE, slice(r, r + CHUNK))
        d_pre[0, r : r + CHUNK, :] = d.astype(BF)


def k_input(d_pre, more_pre, d_summed, weight, *refs):
    more_summed, (out, both, sums) = refs[:-3], refs[-3:]
    m = pl.program_id(0)
    own, across = out.shape[2], out.shape[3]
    spilled = more_pre.shape[1]
    cells = own * COLS
    both[...] = d_pre[0, 0:cells, :]
    both[0:spilled, :] = d_pre[0, 0:spilled, :] + more_pre[0]
    sums[...] = nt(both[...], weight[...])
    for r in range(own):
        at = r * COLS
        line = sums[at : at + COLS, :] + d_summed[0, at : at + COLS, :]
        if at < spilled:
            extra = more_summed[0][at : at + COLS, :].astype(F32)
            for k in range(1, len(more_summed)):
                extra = jnp.where(m == k, more_summed[k][at : at + COLS, :].astype(F32), extra)
            line = line + extra
        out[0, 0, r] = line[:across]


def exchange(x, mask):
    total = lax.axis_size("rows") * lax.axis_size("batch")
    return lax.ppermute(x, AXES, [(i, i ^ mask) for i in range(total)])


def from_behind(x, by):
    devices = lax.axis_size("rows")
    pairs = [(i, i + by) for i in range(devices) if 0 <= i + by < devices]
    return lax.ppermute(x, "rows", pairs)


class Chain:
    def __init__(self, steps):
        self.steps, self.flying, self.done, self.result = steps, None, False, None
        self.ready = next(steps)

    def launch(self, array):
        self.flying = self.ready[1](array)

    def land(self):
        try:
            self.ready = self.steps.send(self.flying)
        except StopIteration as end:
            self.done, self.result = True, end.value
        self.flying = None

    def value(self):
        while not self.done:
            if self.flying is None:
                self.launch(self.ready[0])
            self.land()
        return self.result


def hook(x, start=(), finish=(), need=()):
    if not (start or finish or need):
        return x
    landed = []
    for chain in finish:
        if not chain.done:
            landed.append(chain.flying)
            chain.land()
    live = [chain for chain in start if not chain.done]
    tied = lax.optimization_barrier((x, [c.ready[0] for c in live], landed, list(need)))
    for chain, array in zip(live, tied[1]):
        chain.launch(array)
    return tied[0]


def global_sum(x, b=None, c=None, d=None):
    bits = device_bits()
    x = hook(x + exchange(x, 1), **(b or {}))
    step = 1
    while step < bits:
        low = 1 << step
        if step + 1 < bits:
            p, q, r = exchange(x, low), exchange(x, 2 * low), exchange(x, 3 * low)
            x = (x + p) + (q + r)
        else:
            x = x + exchange(x, low)
        if step == 1:
            x = hook(x, **(c or {}))
        step += 2
    return hook(x, **(d or {}))


def device_bits():
    total = lax.axis_size("rows") * lax.axis_size("batch")
    return total.bit_length() - 1


def my_bit(bit):
    number = lax.axis_index("rows") * lax.axis_size("batch") + lax.axis_index("batch")
    return (number >> bit) & 1


def batch_bits():
    return lax.axis_size("batch").bit_length() - 1


def across(bit):
    return lambda x: exchange(x, 1 << bit)


def gather_pieces(w):
    devices = lax.axis_size("rows")
    if devices > 8:
        return [lax.all_gather(w, "rows", axis=0, tiled=True)]
    half = lax.dynamic_slice_in_dim(w, my_bit(0) * (w.shape[0] // 2), w.shape[0] // 2)
    mine = [lax.ppermute(half, "rows", [(i, i ^ k) for i in range(devices)]) for k in range(1, devices)]
    return [w] + [p for m in mine for p in (m, exchange(m, 1))]


def lanes_of(w, parts):
    x = w.reshape(parts, -1, w.shape[1] // 256, 256)
    return x.transpose(0, 2, 1, 3).reshape(parts, -1, 256)


def from_lanes(x, c):
    parts = x.shape[0]
    x = x.reshape(parts, c // 256, -1, 256)
    return x.transpose(0, 2, 1, 3).reshape(-1, c)


def ordered(mine, other, bit, axis):
    upper = my_bit(bit) == 1
    return jnp.stack([jnp.where(upper, other, mine), jnp.where(upper, mine, other)], axis)


def gather_steps(packed):
    bits, low = device_bits(), batch_bits()
    x = lax.dynamic_index_in_dim(packed, lax.axis_index("batch"), 0, keepdims=False)
    for bit in list(range(low + 1, bits)) + [low]:
        got = yield x, across(bit)
        x = ordered(x, got, bit, 0 if bit > low else bits - low - 1)
    for bit in reversed(range(low)):
        got = yield x, across(bit)
        x = ordered(x, got, bit, x.ndim - 2)
    return x.reshape((-1,) + x.shape[-2:])


def gather_offloaded(w):
    quarters = lax.axis_size("batch")
    part = w.reshape(quarters, -1, w.shape[1])
    part = lax.dynamic_index_in_dim(part, lax.axis_index("batch"), 0, keepdims=False)
    return lax.all_gather(part, AXES, axis=0, tiled=True)


def sharded(grad, c):
    total = lax.axis_size("rows") * lax.axis_size("batch")
    if grad.shape[1] == c:
        return grad.reshape(total, -1, c)
    return lanes_of(grad, total)


def spread_steps(x):
    for bit in reversed(range(batch_bits())):
        got = yield x, across(bit)
        x = ordered(x, got, bit, x.ndim - 2)
    return x.reshape((-1,) + x.shape[-2:])


def reduce_steps(parts, first_bits):
    bits = device_bits()
    x = jnp.concatenate(parts, 1) if len(parts) > 1 else parts[0]
    x = x.reshape((2,) * bits + x.shape[1:])
    left = list(reversed(range(bits)))
    got = None
    for bit in list(first_bits) + [b for b in left if b not in first_bits]:
        axis = left.index(bit)
        left.remove(bit)
        half = lambda v, b: lax.dynamic_index_in_dim(v, b, axis, keepdims=False)
        keep, send = my_bit(bit), 1 - my_bit(bit)
        if got is None:
            x, give = half(x, keep), half(x, send)
        else:
            x, give = half(x, keep) + half(got, keep), half(x, send) + half(got, send)
        got = yield give, across(bit)
    return (yield from spread_steps(x + got))


def one_step(x, send):
    return (yield x, send)


def unpack(shard, shapes):
    devices = lax.axis_size("rows")
    out, at = [], 0
    for k, c in shapes:
        n = k * c // devices // shard.shape[0] // shard.shape[2]
        part = shard[:, at : at + n]
        out.append((from_lanes(part, c) if shard.shape[2] != c else part.reshape(-1, c)).astype(F32))
        at += n
    return out


def per_micro(shape):
    zeros = (0,) * (len(shape) - 1)
    return pl.BlockSpec((1,) + tuple(shape[1:]), lambda m: (m,) + zeros)


def whole(shape):
    zeros = (0,) * len(shape)
    return pl.BlockSpec(tuple(shape), lambda m: zeros, pipeline_mode=pl.Buffered(1))


def table(shape):
    zeros = (0,) * len(shape)
    return pl.BlockSpec(tuple(shape), lambda m: zeros)


def call(kernel, micro, ins, outs, scratch=(), limit=40, after=()):
    kind = {"m": per_micro, "w": whole, "s": lambda shape: pl.BlockSpec(memory_space=pltpu.SMEM)}
    in_specs = [k if isinstance(k, pl.BlockSpec) else kind[k](a.shape) for a, k in ins]
    in_specs += [pl.BlockSpec(memory_space=pl.ANY)] * len(after)
    out_specs = [per_micro(sh) if k == "m" else table(sh) for sh, _, k in outs]

    def run(*refs):
        kernel(*refs[: len(ins)], *refs[len(ins) + len(after) :])

    return pl.pallas_call(
        run,
        grid=(micro,),
        in_specs=in_specs,
        out_specs=out_specs,
        out_shape=[jax.ShapeDtypeStruct(sh, t) for sh, t, _ in outs],
        scratch_shapes=[pltpu.VMEM(sh, t) for sh, t in scratch],
        compiler_params=pltpu.CompilerParams(
            dimension_semantics=("arbitrary",), vmem_limit_bytes=limit * 1024 * 1024
        ),
        name=getattr(kernel, "func", kernel).__name__,
    )(*[a for a, _ in ins], *after)


def weight_term(left, right):
    k, n = left.shape[-1], right.shape[-1]
    return lax.dot_general(
        left.reshape(-1, k), right.reshape(-1, n), (((0,), (0,)), ((), ())), preferred_element_type=F32
    ).astype(BF)


def shards(
    features, view_kind, narrow_one, spatial_one, expand_one, gains_one, biases_one,
    narrow_two, spatial_two, expand_two, shortcut, gains_two, biases_two, cotangent,
):
    micro, _, own, across, channels = features.shape
    m1 = spatial_one.shape[1]
    m2 = spatial_two.shape[1]
    outward = shortcut.shape[1]
    sources = lax.axis_size("rows") * own // 52
    full_count = float(lax.axis_size("batch") * sources * 536)
    half_count = float(lax.axis_size("batch") * sources * 134)
    anchor = lax.axis_index("rows") * own
    cells, half = WIN * COLS, WIN * COLS // 4
    mine, more = own * COLS, SPILL * COLS

    pieces = gather_pieces(narrow_one)
    pack_a = [lanes_of(w, 4) for w in (spatial_one, expand_one)]
    chain_a = Chain(gather_steps(jnp.concatenate(pack_a, 1)))
    chain_n2 = Chain(gather_steps(narrow_two.reshape(4, -1, m2)))
    chain_e2 = Chain(gather_steps(expand_two.reshape(4, -1, outward)))
    spatial_b = gather_offloaded(spatial_two)
    bypass = gather_offloaded(shortcut)
    chain_f = [
        Chain(one_step(features[k, 0, :SPILL], lambda x: from_behind(x, -1))) for k in range(micro)
    ]
    g1, g2, g3 = (v[None] for v in jnp.split(gains_one, [m1, 2 * m1]))
    b1, b2, b3 = (v[None] for v in jnp.split(biases_one, [m1, 2 * m1]))
    cuts = [m2, 2 * m2, 2 * m2 + outward]
    g4, g5, g6, g7 = (v[None] for v in jnp.split(gains_two, cuts))
    b4, b5, b6, b7 = (v[None] for v in jnp.split(biases_two, cuts))
    mask, half_mask = pl.pallas_call(
        functools.partial(k_masks, own),
        in_specs=[pl.BlockSpec(memory_space=pltpu.SMEM)] * 2,
        out_shape=[
            jax.ShapeDtypeStruct((micro, cells, LANES), F32),
            jax.ShapeDtypeStruct((micro, half, LANES), F32),
        ],
        name="k_masks",
    )(anchor[None].astype(jnp.int32), view_kind)
    place = jnp.stack([lax.axis_index("rows"), my_bit(0)]).astype(jnp.int32)

    full_table = lambda c: ((8, c), F32, "t")
    per = lambda c, t=F32, n=cells: ((micro, n, c), t, "m")

    pre_one, head, t1, narrow_a = call(
        functools.partial(k_first, len(pieces)), micro,
        [(place, "s"), (features, "m"), (mask, "m")] + [(p, "w") for p in pieces],
        [per(m1, F32, mine), per(m1, BF, more), full_table(m1), ((channels, m1), BF, "t")],
        [((mine, channels), BF)],
    )
    chain_h = Chain(one_step(head, lambda x: from_behind(x, -1)))
    for _ in range(3):
        chain_a.launch(chain_a.ready[0])
        chain_a.land()
    t1 = global_sum(
        t1,
        c=dict(start=[chain_h, chain_a]),
        d=dict(finish=[chain_h, chain_a], start=[chain_a, chain_n2, chain_f[0]]),
    )
    pre_spill = chain_h.value()
    total_a = chain_a.value()
    spatial_a = total_a[:, : pack_a[0].shape[1]].reshape(-1, m1)
    expand_a = from_lanes(total_a[:, pack_a[0].shape[1] :], channels)
    flipped = spatial_a.reshape(9, m1, m1)[::-1].transpose(0, 2, 1).reshape(9 * m1, m1)
    pre_two, patch_one, t2 = call(
        functools.partial(k_second, full_count), micro,
        [(pre_one, "m"), (pre_spill, "m"), (t1, "w"), (g1, "w"), (b1, "w"), (mask, "m"),
         (spatial_a, "w")],
        [per(m1), per(9 * m1, BF), full_table(m1)],
        [((cells + 2 * COLS, m1), F32), ((cells + 2 * COLS, 3 * m1), BF)],
    )
    t2 = global_sum(
        t2,
        b=dict(finish=[chain_n2, chain_f[0]], start=[chain_n2]),
        c=dict(finish=[chain_n2], start=[chain_n2]),
        d=dict(finish=[chain_n2], start=[chain_n2, chain_e2, chain_f[1]]),
    )
    act_two, pre_three, t3 = call(
        functools.partial(k_third, full_count, MINE), micro,
        [(pre_two, "m"), (t2, "w"), (g2, "w"), (b2, "w"), (mask, "m"), (expand_a, "w")],
        [per(m1, BF), per(channels), full_table(channels)],
    )
    t3 = global_sum(
        t3,
        b=dict(finish=[chain_n2, chain_e2, chain_f[1]], start=[chain_n2, chain_e2]),
        c=dict(finish=[chain_n2, chain_e2], start=[chain_e2]),
        d=dict(finish=[chain_e2], start=[chain_e2] + chain_f[2:]),
    )
    narrow_b = chain_n2.value().reshape(-1, m2)
    (entry,) = call(
        k_entry, micro,
        [(features, "m"), (mask, "m")] + [(f.value(), "w") for f in chain_f],
        [per(channels, BF)], [((cells, channels), BF)],
    )
    block_out, corner, pre_four, t4 = call(
        functools.partial(k_fourth, full_count), micro,
        [(pre_three, "m"), (entry, "m"), (t3, "w"), (g3, "w"), (b3, "w"), (mask, "m"), (narrow_b, "w")],
        [per(channels, BF), per(channels, BF, half), per(m2), full_table(m2)],
        [((channels // LANES, 4 * COLS, LANES), F32)],
    )
    t4 = global_sum(t4, b=dict(finish=[chain_e2], start=[chain_e2]), c=dict(finish=[chain_e2]))
    expand_b = chain_e2.value().reshape(-1, outward)
    pre_five, patch_two, t5 = call(
        functools.partial(k_fifth, full_count), micro,
        [(pre_four, "m"), (t4, "w"), (g4, "w"), (b4, "w"), (mask, "m"), (half_mask, "m"),
         (spatial_b, "w")],
        [per(m2, F32, half), per(9 * m2, BF, half), full_table(m2)],
        [((m2 // LANES, cells, LANES), F32)] + [((half + COLS, m2), F32)] * 3,
    )
    t5 = global_sum(t5)
    act_five, pre_six, t6 = call(
        functools.partial(k_third, half_count, HALF), micro,
        [(pre_five, "m"), (t5, "w"), (g5, "w"), (b5, "w"), (half_mask, "m"), (expand_b, "w")],
        [per(m2, BF, half), per(outward, F32, half), full_table(outward)],
    )
    tile = outward // 4
    pre_seven, t7 = pl.pallas_call(
        k_seventh,
        grid=(4, micro),
        in_specs=[
            pl.BlockSpec((1, half, channels), lambda n, m: (m, 0, 0)),
            pl.BlockSpec((channels, tile), lambda n, m: (0, n)),
        ],
        out_specs=[
            pl.BlockSpec((1, half, tile), lambda n, m: (m, 0, n)),
            pl.BlockSpec((8, tile), lambda n, m: (0, n)),
        ],
        out_shape=[
            jax.ShapeDtypeStruct((micro, half, outward), F32),
            jax.ShapeDtypeStruct((8, outward), F32),
        ],
        compiler_params=pltpu.CompilerParams(vmem_limit_bytes=40 * 1024 * 1024),
    )(corner, bypass)
    t67 = global_sum(jnp.concatenate([t6, t7], 1))
    t6, t7 = t67[:, :outward], t67[:, outward:]
    outputs, slope, u67 = call(
        functools.partial(k_last, half_count), micro,
        [(pre_six, "m"), (pre_seven, "m"), (t6, "w"), (t7, "w"), (g6, "w"), (b6, "w"), (g7, "w"), (b7, "w"),
         (half_mask, "m"), (cotangent, "m")],
        [(cotangent.shape, BF, "m"), per(outward, F32, half), full_table(2 * outward)],
        [((COLS // 2, outward), F32)],
    )
    u67 = global_sum(u67)
    d_six, d_seven, d_five, u5 = call(
        functools.partial(k_back_six, half_count), micro,
        [(slope, "m"), (pre_six, "m"), (pre_seven, "m"), (t6, "w"), (t7, "w"), (u67, "w"), (g6, "w"), (g7, "w"),
         (pre_five, "m"), (t5, "w"), (g5, "w"), (b5, "w"), (half_mask, "m"), (expand_b, "w")],
        [per(outward, BF, half), per(outward, BF, half), per(m2, F32, half), full_table(m2)],
    )
    (d_corner,) = call(
        k_corner, micro, [(d_seven, "m"), (bypass, "w")], [per(channels, F32, half)]
    )
    grad_e2 = weight_term(act_five, d_six)
    grad_sc = weight_term(corner, d_seven)
    chain_re2 = Chain(reduce_steps([sharded(grad_e2, outward)], (0, 1, 2)))
    u5 = global_sum(u5, c=dict(need=[grad_sc, chain_re2.ready[0]]), d=dict(start=[chain_re2]))
    part_sc = lax.psum_scatter(grad_sc, AXES, scatter_dimension=0, tiled=True)
    d_pre_five, d_four, u4 = call(
        functools.partial(k_back_five, half_count, full_count), micro,
        [(d_five, "m"), (pre_five, "m"), (t5, "w"), (u5, "w"), (g5, "w"), (half_mask, "m"),
         (spatial_b, "w"), (pre_four, "m"), (t4, "w"), (g4, "w"), (b4, "w"), (mask, "m")],
        [per(m2, BF, half), per(m2), full_table(m2)],
        [((m2 // LANES, cells, LANES), F32), ((half + COLS, m2), F32)],
    )
    grad_s2 = sharded(weight_term(patch_two, d_pre_five), m2)
    cut = grad_s2.shape[1] // 32 * 16 or grad_s2.shape[1] // 2
    chain_rs = [
        Chain(reduce_steps([grad_s2[:, :cut]], (0, 2, 1))),
        Chain(reduce_steps([grad_s2[:, cut:]], (0, 1, 2))),
    ]
    u4 = global_sum(
        u4,
        b=dict(finish=[chain_re2]),
        c=dict(start=[chain_re2], need=[r.ready[0] for r in chain_rs]),
        d=dict(start=chain_rs),
    )
    d_pre_four, d_summed, u3 = call(
        functools.partial(k_back_four, full_count), micro,
        [(d_four, "m"), (pre_four, "m"), (t4, "w"), (u4, "w"), (g4, "w"), (mask, "m"), (narrow_b, "w"),
         (d_corner, "m"), (pre_three, "m"), (entry, "m"), (t3, "w"), (g3, "w"), (b3, "w")],
        [per(m2, BF), per(channels), full_table(channels)],
        [((channels // LANES, COLS, LANES), F32)],
    )
    grad_n2 = weight_term(block_out, d_pre_four)
    spilled = [d_summed[k, mine : mine + more].astype(BF) for k in range(micro)]
    chain_ds = [Chain(one_step(v, lambda x: from_behind(x, 1))) for v in spilled]
    u3 = global_sum(
        u3,
        b=dict(finish=[chain_re2] + chain_rs),
        c=dict(start=[chain_re2] + chain_rs, need=[grad_n2]),
        d=dict(finish=[chain_re2], start=[chain_re2, chain_ds[0]]),
    )
    d_pre_three, d_two, u2 = call(
        functools.partial(k_back_three, full_count), micro,
        [(d_summed, "m"), (pre_three, "m"), (t3, "w"), (u3, "w"), (g3, "w"), (mask, "m"), (expand_a, "w"),
         (pre_two, "m"), (t2, "w"), (g2, "w"), (b2, "w")],
        [per(channels, BF), per(m1), full_table(m1)],
    )
    grad_e1 = weight_term(act_two, d_pre_three)
    chain_rq = Chain(reduce_steps([sharded(grad_n2, 256), sharded(grad_e1, 256)], (0, 1, 2)))
    u2 = global_sum(
        u2,
        b=dict(finish=chain_rs + chain_ds[:1], start=[chain_rq]),
        c=dict(finish=[chain_re2, chain_rq], start=chain_rs),
        d=dict(finish=chain_rs, start=chain_rs + [chain_re2, chain_rq] + chain_ds[1:2]),
    )
    d_pre_two, d_one, u1 = call(
        functools.partial(k_back_two, full_count), micro,
        [(d_two, "m"), (pre_two, "m"), (t2, "w"), (u2, "w"), (g2, "w"), (mask, "m"),
         (flipped, "w"), (pre_one, "m"), (pre_spill, "m"), (t1, "w"), (g1, "w"), (b1, "w")],
        [per(m1, BF), per(m1), full_table(m1)],
        [((cells + 2 * COLS, m1), F32), ((cells + 2 * COLS, 3 * m1), BF)],
    )
    grad_s1 = weight_term(patch_one, d_pre_two)
    chain_r1 = Chain(reduce_steps([sharded(grad_s1, 256)], (0, 2, 1)))
    u1 = global_sum(
        u1,
        b=dict(finish=[chain_re2, chain_rq] + chain_ds[1:2], start=[chain_r1]),
        c=dict(finish=chain_rs + [chain_r1], start=[chain_re2, chain_rq]),
        d=dict(finish=[chain_re2, chain_rq], start=chain_rs + [chain_re2, chain_rq, chain_r1] + chain_ds[2:]),
    )
    (d_pre_one,) = call(
        functools.partial(k_back_one, full_count), micro,
        [(d_one, "m"), (pre_one, "m"), (pre_spill, "m"), (t1, "w"), (u1, "w"), (g1, "w"), (mask, "m")],
        [per(m1, BF)],
    )
    chain_dp = Chain(one_step(d_pre_one[:, mine : mine + more], lambda x: from_behind(x, 1)))
    grad_n1 = weight_term(entry, d_pre_one)
    chain_rn = Chain(reduce_steps([sharded(grad_n1, 256)], (0, 1, 2)))
    chain_rc = Chain(spread_steps(part_sc))
    out_n2, out_e1 = unpack(chain_rq.value(), [(channels, m2), (m1, channels)])
    (out_e2,) = unpack(chain_re2.value(), [(m2, outward)])
    (out_s2,) = unpack(jnp.concatenate([r.value() for r in chain_rs], 1), [(9 * m2, m2)])
    (out_s1,) = unpack(chain_r1.value(), [(9 * m1, m1)])
    (out_n1,) = unpack(chain_rn.value(), [(channels, m1)])
    (out_sc,) = unpack(chain_rc.value(), [(channels, outward)])
    (grad_input,) = call(
        k_input, micro,
        [(d_pre_one, "m"), (chain_dp.value(), "m"), (d_summed, "m"), (narrow_a, "w")]
        + [(c.value(), "w") for c in chain_ds],
        [(features.shape, F32, "m")],
        [((mine, m1), BF), ((mine, channels), F32)],
    )
    added = lambda k, us: jnp.concatenate([u[k] + u[k + 2] + u[k + 4] for u in us])
    first = (u1, u2, u3)
    later = (u4, u5, u67)
    return (
        outputs, grad_input, out_n1, out_s1, out_e1,
        added(1, first), added(0, first),
        out_n2, out_s2, out_e2, out_sc,
        added(1, later), added(0, later),
    )


def solution(mesh):
    wide = P(None, "batch", "rows", None, None)
    shard = P("rows", None)
    return jax.shard_map(
        shards,
        mesh=mesh,
        in_specs=(
            wide, P(None, "batch", None), shard, shard, shard, P(), P(),
            shard, shard, shard, shard, P(), P(), wide,
        ),
        out_specs=(
            wide, wide, shard, shard, shard, P(), P(),
            shard, shard, shard, shard, P(), P(),
        ),
        check_vma=False,
    )
```

time: 1880 us -> 677 us (0.36)
  waiting for transfers between devices: 881 us -> 152 us
  blocking collectives: 483 us -> 0 us
  starting transfers between devices: 52.2 us -> 231 us
  Pallas kernels: 0 us -> 139 us
  other arithmetic: 147 us -> 21.9 us
  matrix products: 134 us -> 22.5 us
  local copies, waits for them, and re-layouts: 145 us -> 82.6 us
    reduce_scatter x7 -> x1, waiting for transfers between devices: 558 us -> 0.01 us  [shards(): part_sc = lax.psum_scatter(grad_sc, AXES, scatter_dimension=0, tiled=True)]
    psum x10 -> x0, blocking collectives: 436 us -> none  [the longest x5 231 us: global_stats(): totals, squares = lax.psum((firsts, seconds), ('rows', 'batch'))]
    psum x3 -> x0, waiting for transfers between devices: 275 us -> none  [the longest x1 124 us: global_stats(): totals, squares = lax.psum((firsts, seconds), ('rows', 'batch'))]
    ppermute x18 -> x165, starting transfers between devices: 51.1 us -> 231 us  [the longest x150 198 us: exchange(): return lax.ppermute(x, AXES, [(i, i ^ mask) for i in range(total)])]
    pallas_call x0 -> x18, Pallas kernels: none -> 139 us  [the longest x16 130 us: call(): pl.pallas_call(run, grid=(micro,), in_specs=in_specs, out_specs=out_specs...]
    dot_general x63 -> x7, matrix products: 134 us -> 22.5 us  [weight_term(): lax.dot_general(left.reshape(-1, k), right.reshape(-1, n), (((0,), (0,)),...]
    ppermute x18 -> x165, waiting for transfers between devices: 45.3 us -> 152 us  [the longest x150 120 us: exchange(): return lax.ppermute(x, AXES, [(i, i ^ mask) for i in range(total)])]
    convert_element_type x50 -> x7, other arithmetic: 67.8 us -> 2.04 us  [unpack(): (from_lanes(part, c) if shard.shape[2] != c else part.reshape(-1, c)).ast...]
  transfers between devices with their start and end apart: 33 -> 168, of which waited for: 15 -> 72; matrix products, arithmetic and copies ran while one was open for 12% -> 10% of each run, Pallas kernels for 0% -> 17%
where the time goes in v1:
time: 677 us; the launch traced here: 665 us
  starting transfers between devices  231 us (34%)
  waiting for transfers between devices  152 us (22%)
  Pallas kernels  139 us (21%)
  local copies, waits for them, and re-layouts  82.6 us (12%)
  matrix products  22.5 us (3%)
  other arithmetic  21.9 us (3%)
  between operations  16.6 us (2%)
    ppermute x150, starting transfers between devices, exchange(): return lax.ppermute(x, AXES, [(i, i ^ mask) for i in range(total)])  198 us
    pallas_call x16, Pallas kernels, call(): pl.pallas_call(run, grid=(micro,), in_specs=in_specs, out_specs=out_specs...  130 us
    ppermute x150, waiting for transfers between devices, exchange(): return lax.ppermute(x, AXES, [(i, i ^ mask) for i in range(total)])  120 us
    unnamed x243, local copies, waits for them, and re-layouts  59.4 us
    ppermute x8, waiting for transfers between devices, from_behind(): return lax.ppermute(x, 'rows', pairs)  32 us
    ppermute x8, starting transfers between devices, from_behind(): return lax.ppermute(x, 'rows', pairs)  23.9 us
    dot_general x7, matrix products, weight_term(): lax.dot_general(left.reshape(-1, k), right.reshape(-1, n), (((0,), (0,)),...  22.5 us
  transfers between devices with their start and end apart: 168, of which 72 were waited for; matrix products, arithmetic and copies ran while one was open for 10% of the time, Pallas kernels for 17%

profile of v1, /device:TPU:25, one launch (start us, length us, event | category | flops | bytes accessed | tf_op | source)
XLA Modules:
  0.0 665.2 jit_solution(4056528554263052869)
XLA Ops:
  13.4 3.3 collective-permute-start.8
  27.7 3.1 k_masks.1
  45.6 3.0 collective-permute-done.20
  56.8 3.4 collective-permute-start.21
  61.3 11.4 %collective-permute-done.21.refs_1_.refs_8_.refs_2_ = bf16[3,192,256]{2,1,0:T(8,128)(2,1)S(1)} collective-permute-done((bf16[3,192,256]{2,1,0:T(8,128)(2,1)S(1)}, bf16[3,192,256]{2,1,0:T(8,128)(2,1)S(1)}, u32[]{:S(2)}, u32[]{:S(2)}) %collective-permute-start.21) | collective-permute-done | bytes 294944 | tf_op jit(solution)/shard_map/ppermute | solution.py:611
  72.8 3.4 collective-permute-start.26
  83.9 8.8 %k_second.1 = (f32[3,640,256]{2,1,0:T(8,128)S(1)}, bf16[3,640,2304]{2,1,0:T(8,128)(2,1)S(1)}, f32[8,256]{1,0:T(8,128)S(1)}) custom-call(f32[3,416,256]{2,1,0:T(8,128)S(1)} %copy-done.20, bf16[3,192,256]{2,1,0:T(8,128)(2,1)S(1)} %collective-permute-done.21.refs_1_.refs_8_.refs_2_, f32[8,256]{1,0:T(8,128)S(1)} %add_add_fusion.22.refs_2_.refs_9_.refs_3_, ...), custom_call_target="tpu_custom_call" | custom-call | tf_op jit(solution)/shard_map/k_second/pallas_call | solution.py:803
  92.7 3.4 copy-done.90
  102.8 3.8 collective-permute-done.33
  111.1 3.3 collective-permute-done.37
  116.6 7.3 %k_third.2 = (bf16[3,640,256]{2,1,0:T(8,128)(2,1)S(1)}, f32[3,640,1024]{2,1,0:T(8,128)S(1)}, f32[8,1024]{1,0:T(8,128)S(1)}) custom-call(f32[3,640,256]{2,1,0:T(8,128)S(1)} %get-tuple-element.131.refs_0_.refs_7_.refs_1_, f32[8,256]{1,0:T(8,128)S(1)} %add_add_fusion.20.refs_1_.refs_8_.refs_2_, f32[1,256]{1,0:T(1,128)S(1)} %bitcast.539, ...), custom_call_target="tpu_custom_call" | custom-call | tf_op jit(solution)/shard_map/k_third/pallas_call | solution.py:803
  123.9 3.1 copy-done.4
  127.0 3.6 collective-permute-start.39
  130.6 3.2 collective-permute-start.38
  135.4 6.1 collective-permute-done.40
  141.6 3.2 collective-permute-done.38.refs_3_
  151.2 8.2 %collective-permute-done.45 = bf16[2,16,2048]{2,1,0:T(8,128)(2,1)S(1)} collective-permute-done((bf16[2,16,2048]{2,1,0:T(8,128)(2,1)S(1)}, bf16[2,16,2048]{2,1,0:T(8,128)(2,1)S(1)}, u32[]{:S(2)}, u32[]{:S(2)}) %collective-permute-start.45) | collective-permute-done | bytes 131104 | tf_op jit(solution)/shard_map/ppermute | solution.py:605
  159.5 4.2 collective-permute-start.50
  171.3 3.2 collective-permute-start.51
  174.7 6.9 %collective-permute-done.51.refs_4_ = bf16[12,14,1024]{2,1,0:T(8,128)(2,1)S(1)} collective-permute-done((bf16[12,14,1024]{2,1,0:T(8,128)(2,1)S(1)}, bf16[12,14,1024]{2,1,0:T(8,128)(2,1)S(1)}, u32[]{:S(2)}, u32[]{:S(2)}) %collective-permute-start.51) | collective-permute-done | bytes 344096 | tf_op jit(solution)/shard_map/ppermute | solution.py:611
  184.3 10.2 %k_fourth.1 = (bf16[3,640,1024]{2,1,0:T(8,128)(2,1)S(1)}, bf16[3,160,1024]{2,1,0:T(8,128)(2,1)S(1)}, f32[3,640,512]{2,1,0:T(8,128)S(1)}, f32[8,512]{1,0:T(8,128)S(1)}) custom-call(f32[3,640,1024]{2,1,0:T(8,128)} %copy-done.4, bf16[3,640,1024]{2,1,0:T(8,128)(2,1)} %copy-done.5, f32[8,1024]{1,0:T(8,128)S(1)} %add_add_fusion.6.refs_2_.refs_10_, ...), custom_call_target="tpu_custom_call" | custom-call | tf_op jit(solution)/shard_map/k_fourth/pallas_call | solution.py:803
  197.4 3.5 collective-permute-start.52
  215.8 11.3 %k_fifth.1 = (f32[3,160,512]{2,1,0:T(8,128)S(1)}, bf16[3,160,4608]{2,1,0:T(8,128)(2,1)S(1)}, f32[8,512]{1,0:T(8,128)S(1)}) custom-call(f32[3,640,512]{2,1,0:T(8,128)S(1)} %copy-done.8, f32[8,512]{1,0:T(8,128)S(1)} %add_add_fusion.14.refs_1_.refs_8_.refs_2_, f32[1,512]{1,0:T(1,128)S(1)} %bitcast.524, f32[1,512]{1,0:T(1,128)S(1)} %bitcast.532, ...), custom_call_target="tpu_custom_call" | custom-call | tf_op jit(solution)/shard_map/k_fifth/pallas_call | solution.py:803
  243.7 5.8 shard_map.237
  249.7 3.5 k_third.3
  254.0 3.0 collective-permute-start.68
  260.7 3.4 collective-permute-done.70
  270.1 7.8 %collective-permute-done.73 = f32[8,4096]{1,0:T(8,128)S(1)} collective-permute-done((f32[8,4096]{1,0:T(8,128)S(1)}, f32[8,4096]{1,0:T(8,128)S(1)}, u32[]{:S(2)}, u32[]{:S(2)}) %collective-permute-start.73) | collective-permute-done | bytes 131104 | tf_op jit(solution)/shard_map/ppermute | solution.py:605
  278.0 8.8 %k_last.1 = (bf16[3,1,19,7,2048]{4,3,2,1,0:T(8,128)(2,1)}, f32[3,160,2048]{2,1,0:T(8,128)S(1)}, f32[8,4096]{1,0:T(8,128)S(1)}) custom-call(f32[3,160,2048]{2,1,0:T(8,128)S(1)} %get-tuple-element.161.refs_0_.refs_1_, f32[3,160,2048]{2,1,0:T(8,128)S(1)} %get-tuple-element.163.refs_1_.refs_2_, f32[8,2048]{1,0:T(8,128)S(1)} %get-tuple-element.357.refs_2_.refs_3_, ...), custom_call_target="tpu_custom_call" | custom-call | tf_op jit(solution)/shard_map/k_last/pallas_call | solution.py:803
  288.7 3.0 collective-permute-start.75
  321.7 9.8 %k_back_six.1 = (bf16[3,160,2048]{2,1,0:T(8,128)(2,1)S(1)}, bf16[3,160,2048]{2,1,0:T(8,128)(2,1)S(1)}, f32[3,160,512]{2,1,0:T(8,128)S(1)}, f32[8,512]{1,0:T(8,128)S(1)}) custom-call(f32[3,160,2048]{2,1,0:T(8,128)S(1)} %copy-done.34, f32[3,160,2048]{2,1,0:T(8,128)} %copy-done.16, f32[3,160,2048]{2,1,0:T(8,128)} %copy-done.15, f32[8,2048]{1,0:T(8,128)S(1)} %copy-done.48, ...), custom_call_target="tpu_custom_call" | custom-call | tf_op jit(solution)/shard_map/k_back_six/pallas_call | solution.py:803
  334.3 4.3 bitcast_convert_fusion.1
  343.6 4.8 k_corner.1.refs_7_
  348.4 4.9 collective-permute-start.82
  353.4 3.1 bitcast_convert_fusion.2
  370.9 12.8 %k_back_five.1 = (bf16[3,160,512]{2,1,0:T(8,128)(2,1)S(1)}, f32[3,640,512]{2,1,0:T(8,128)S(1)}, f32[8,512]{1,0:T(8,128)S(1)}) custom-call(f32[3,160,512]{2,1,0:T(8,128)S(1)} %copy-done.46, f32[3,160,512]{2,1,0:T(8,128)S(1)} %copy-done.28, f32[8,512]{1,0:T(8,128)S(1)} %copy-done.55, f32[8,512]{1,0:T(8,128)S(1)} %add_add_fusion.10.refs_3_, ...), custom_call_target="tpu_custom_call" | custom-call | tf_op jit(solution)/shard_map/k_back_five/pallas_call | solution.py:803
  383.7 2.9 bitcast_convert_fusion
  398.3 20.7 %k_back_four.1 = (bf16[3,640,512]{2,1,0:T(8,128)(2,1)S(1)}, f32[3,640,1024]{2,1,0:T(8,128)}, f32[8,1024]{1,0:T(8,128)S(1)}) custom-call(f32[3,640,512]{2,1,0:T(8,128)S(1)} %get-tuple-element.176.refs_0_, f32[3,640,512]{2,1,0:T(8,128)S(1)} %copy-done.9, f32[8,512]{1,0:T(8,128)S(1)} %copy-done.57, f32[8,512]{1,0:T(8,128)S(1)} %add_add_fusion.8.refs_3_, ...), custom_call_target="tpu_custom_call" | custom-call | tf_op jit(solution)/shard_map/k_back_four/pallas_call | solution.py:803
  419.0 3.3 collective-permute-start.97
  422.8 3.3 bitcast_convert_fusion.3
  437.1 2.9 collective-permute-start.106
  448.2 18.5 %k_back_three.1 = (bf16[3,640,1024]{2,1,0:T(8,128)(2,1)S(1)}, f32[3,640,256]{2,1,0:T(8,128)S(1)}, f32[8,256]{1,0:T(8,128)S(1)}) custom-call(f32[3,640,1024]{2,1,0:T(8,128)} %get-tuple-element.184.refs_0_.refs_2_, f32[3,640,1024]{2,1,0:T(8,128)} %copy-done.4, f32[8,1024]{1,0:T(8,128)S(1)} %add_add_fusion.6.refs_2_.refs_10_, ...), custom_call_target="tpu_custom_call" | custom-call | tf_op jit(solution)/shard_map/k_back_three/pallas_call | solution.py:803
  466.7 4.0 collective-permute-start.108
  470.7 3.9 collective-permute-start.111
  476.3 9.0 %collective-permute-done.111.refs_4_ = bf16[192,1024]{1,0:T(8,128)(2,1)S(1)} collective-permute-done((bf16[192,1024]{1,0:T(8,128)(2,1)S(1)}, bf16[192,1024]{1,0:T(8,128)(2,1)S(1)}, u32[]{:S(2)}, u32[]{:S(2)}) %collective-permute-start.111) | collective-permute-done | bytes 393248 | tf_op jit(solution)/shard_map/ppermute | solution.py:611
  486.1 6.5 collective-permute-start.113
  501.1 2.9 collective-permute-done.120
  505.7 4.8 k_back_two.1
  510.4 4.1 collective-permute-start.122
  518.4 6.2 fusion
  530.0 6.3 collective-permute-done.129
  536.3 3.5 collective-permute-done.130
  554.8 3.2 collective-permute-start.137
  561.5 5.8 collective-permute-start.139
  567.3 2.9 collective-permute-start.156
  576.7 4.7 collective-permute-done.152
  584.5 3.0 collective-permute-start.162
  597.8 3.7 collective-permute-start.158
  608.0 6.2 collective-permute-start.141
  617.2 4.4 k_input.1
  624.0 9.3 %copy.114 = f32[3,1,26,14,1024]{4,1,3,2,0:T(1,128)} copy(f32[3,1,26,14,1024]{4,3,2,1,0:T(8,128)} %copy-done.10) | data formatting | bytes 8945664
  639.5 4.6 collective-permute-start.145
  647.3 4.6 collective-permute-start.151
  652.9 2.9 collective-permute-start.164
  (724 shorter events, 294.3 us)
Async XLA Ops:
  7.2 206.5 %all-gather.5.cloned.1.call-start = ((), (), s32[]{:S(2)}) async-start(), calls=%async_computation.2 | async-start | bytes 4866048 | tf_op jit(solution)/shard_map/all_gather | solution.py:728
  8.9 231.4 %all-gather.7.cloned.1.call-start = ((), (), s32[]{:S(2)}) async-start(), calls=%async_computation.3 | async-start | bytes 4325376 | tf_op jit(solution)/shard_map/all_gather | solution.py:728
  13.2 6.7 %collective-permute-start.4 = (bf16[64,256]{1,0:T(8,128)(2,1)S(1)}, bf16[64,256]{1,0:T(8,128)(2,1)S(1)}, u32[]{:S(2)}, u32[]{:S(2)}) collective-permute-start(bf16[64,256]{1,0:T(8,128)(2,1)S(1)} %constant_dynamic-slice_fusion.6), channel_id=1, source_target_pairs={{0,12},{4,8},{8,4},{12,0},{16,28},{20,24},{24,20},{28,16},{1,13},{... | collective-permute-start | bytes 98312 | tf_op jit(solution)/shard_map/ppermute | solution.py:692
  13.3 9.5 %collective-permute-start.6 = (bf16[64,256]{1,0:T(8,128)(2,1)S(1)}, bf16[64,256]{1,0:T(8,128)(2,1)S(1)}, u32[]{:S(2)}, u32[]{:S(2)}) collective-permute-start(bf16[64,256]{1,0:T(8,128)(2,1)S(1)} %constant_dynamic-slice_fusion.6), channel_id=1, source_target_pairs={{0,16},{4,20},{8,24},{12,28},{16,0},{20,4},{24,8},{28,12},{1,17},{... | collective-permute-start | bytes 98312 | tf_op jit(solution)/shard_map/ppermute | solution.py:692
  13.4 9.6 %collective-permute-start.8 = (bf16[64,256]{1,0:T(8,128)(2,1)S(1)}, bf16[64,256]{1,0:T(8,128)(2,1)S(1)}, u32[]{:S(2)}, u32[]{:S(2)}) collective-permute-start(bf16[64,256]{1,0:T(8,128)(2,1)S(1)} %constant_dynamic-slice_fusion.6), channel_id=1, source_target_pairs={{0,20},{4,16},{8,28},{12,24},{16,4},{20,0},{24,12},{28,8},{1,21},{... | collective-permute-start | bytes 98312 | tf_op jit(solution)/shard_map/ppermute | solution.py:692
  17.8 7.1 %collective-permute-start.12 = (bf16[64,256]{1,0:T(8,128)(2,1)S(1)}, bf16[64,256]{1,0:T(8,128)(2,1)S(1)}, u32[]{:S(2)}, u32[]{:S(2)}) collective-permute-start(bf16[64,256]{1,0:T(8,128)(2,1)S(1)} %constant_dynamic-slice_fusion.6), channel_id=1, source_target_pairs={{0,28},{4,24},{8,20},{12,16},{16,12},{20,8},{24,4},{28,0},{1,29},{... | collective-permute-start | bytes 98312 | tf_op jit(solution)/shard_map/ppermute | solution.py:692
  20.0 7.1 %collective-permute-start.1 = (bf16[64,256]{1,0:T(8,128)(2,1)S(1)}, bf16[64,256]{1,0:T(8,128)(2,1)S(1)}, u32[]{:S(2)}, u32[]{:S(2)}) collective-permute-start(bf16[64,256]{1,0:T(8,128)(2,1)S(1)} %collective-permute-done.refs_4_), channel_id=1, source_target_pairs={{0,1},{1,0},{2,3},{3,2},{4,5},{5,4},{6,7},{7,6},{8,9},{9,8},{10,11... | collective-permute-start | bytes 98312 | tf_op jit(solution)/shard_map/ppermute | solution.py:605
  23.4 7.4 %collective-permute-start.7 = (bf16[64,256]{1,0:T(8,128)(2,1)S(1)}, bf16[64,256]{1,0:T(8,128)(2,1)S(1)}, u32[]{:S(2)}, u32[]{:S(2)}) collective-permute-start(bf16[64,256]{1,0:T(8,128)(2,1)S(1)} %collective-permute-done.6.refs_10_), channel_id=1, source_target_pairs={{0,1},{1,0},{2,3},{3,2},{4,5},{5,4},{6,7},{7,6},{8,9},{9,8},{10,11... | collective-permute-start | bytes 98312 | tf_op jit(solution)/shard_map/ppermute | solution.py:605
  27.6 15.1 %collective-permute-start.19 = (bf16[2,104,256]{2,1,0:T(8,128)(2,1)S(1)}, bf16[2,104,256]{2,1,0:T(8,128)(2,1)S(1)}, u32[]{:S(2)}, u32[]{:S(2)}) collective-permute-start(bf16[2,104,256]{2,1,0:T(8,128)(2,1)S(1)} %pad_maximum_fusion.21), channel_id=1, source_target_pairs={{0,16},{1,17},{2,18},{3,19},{4,20},{5,21},{6,22},{7,23},{8,24},{9,... | collective-permute-start | bytes 319496 | tf_op jit(solution)/shard_map/ppermute | solution.py:605
  48.7 11.6 %collective-permute-start.25 = (bf16[2,2,2,104,256]{4,3,2,1,0:T(8,128)(2,1)S(1)}, bf16[2,2,2,104,256]{4,3,2,1,0:T(8,128)(2,1)S(1)}, u32[]{:S(2)}, u32[]{:S(2)}) collective-permute-start(bf16[2,2,2,104,256]{4,3,2,1,0:T(8,128)(2,1)S(1)} %pad_maximum_fusion.8), channel_id=1, source_target_pairs={{0,2},{1,3},{2,0},{3,1},{4,6},{5,7},{6,4},{7,5},{8,10},{9,11},{10,... | collective-permute-start | bytes 1277960 | tf_op jit(solution)/shard_map/ppermute | solution.py:605
  52.2 8.0 %collective-permute-start.23 = (f32[8,256]{1,0:T(8,128)S(1)}, f32[8,256]{1,0:T(8,128)S(1)}, u32[]{:S(2)}, u32[]{:S(2)}) collective-permute-start(f32[8,256]{1,0:T(8,128)S(1)} %add_add_fusion.23), channel_id=1, source_target_pairs={{0,16},{1,17},{2,18},{3,19},{4,20},{5,21},{6,22},{7,23},{8,24},{9,... | collective-permute-start | bytes 24584 | tf_op jit(solution)/shard_map/ppermute | solution.py:605
  56.8 16.0 %collective-permute-start.21 = (bf16[3,192,256]{2,1,0:T(8,128)(2,1)S(1)}, bf16[3,192,256]{2,1,0:T(8,128)(2,1)S(1)}, u32[]{:S(2)}, u32[]{:S(2)}) collective-permute-start(bf16[3,192,256]{2,1,0:T(8,128)(2,1)S(1)} %get-tuple-element.126), channel_id=1, source_target_pairs={{4,0},{8,4},{12,8},{16,12},{20,16},{24,20},{28,24},{5,1},{9,5},{13... | collective-permute-start | bytes 884744 | tf_op jit(solution)/shard_map/ppermute | solution.py:611
  72.8 8.3 %collective-permute-start.26 = (bf16[2,2,2,2,104,256]{5,4,3,2,1,0:T(8,128)(2,1)}, bf16[2,2,2,2,104,256]{5,4,3,2,1,0:T(8,128)(2,1)S(1)}, u32[]{:S(2)}, u32[]{:S(2)}) collective-permute-start(bf16[2,2,2,2,104,256]{5,4,3,2,1,0:T(8,128)(2,1)} %pad_maximum_fusion.4), channel_id=1, source_target_pairs={{0,1},{1,0},{2,3},{3,2},{4,5},{5,4},{6,7},{7,6},{8,9},{9,8},{10,11... | collective-permute-start | bytes 2555912 | tf_op jit(solution)/shard_map/ppermute | solution.py:605
  76.5 21.0 %collective-permute-start.29 = (bf16[12,14,1024]{2,1,0:T(8,128)(2,1)}, bf16[12,14,1024]{2,1,0:T(8,128)(2,1)S(1)}, u32[]{:S(2)}, u32[]{:S(2)}) collective-permute-start(bf16[12,14,1024]{2,1,0:T(8,128)(2,1)} %get-tuple-element.134), channel_id=1, source_target_pairs={{4,0},{8,4},{12,8},{16,12},{20,16},{24,20},{28,24},{5,1},{9,5},{13... | collective-permute-start | bytes 1032200 | tf_op jit(solution)/shard_map/ppermute | solution.py:611
  102.5 543.2 %reduce-scatter.2.cloned.1.call-start = ((), (), s32[]{:S(2)}) async-start(), calls=%async_computation.1 | async-start | bytes 4325376 | tf_op jit(solution)/shard_map/reduce_scatter | solution.py:980
  114.5 20.0 %collective-permute-start.41 = (bf16[16,2048]{1,0:T(8,128)(2,1)S(1)}, bf16[16,2048]{1,0:T(8,128)(2,1)S(1)}, u32[]{:S(2)}, u32[]{:S(2)}) collective-permute-start(bf16[16,2048]{1,0:T(8,128)(2,1)S(1)} %dynamic-slice_bitcast_fusion.5), channel_id=1, source_target_pairs={{0,8},{1,9},{2,10},{3,11},{4,12},{5,13},{6,14},{7,15},{8,0},{9,1},... | collective-permute-start | bytes 196616 | tf_op jit(solution)/shard_map/ppermute | solution.py:605
  127.0 7.5 %collective-permute-start.39 = (f32[8,1024]{1,0:T(8,128)S(1)}, f32[8,1024]{1,0:T(8,128)S(1)}, u32[]{:S(2)}, u32[]{:S(2)}) collective-permute-start(f32[8,1024]{1,0:T(8,128)S(1)} %get-tuple-element.142), channel_id=1, source_target_pairs={{0,1},{1,0},{2,3},{3,2},{4,5},{5,4},{6,7},{7,6},{8,9},{9,8},{10,11... | collective-permute-start | bytes 98312 | tf_op jit(solution)/shard_map/ppermute | solution.py:605
  130.6 14.2 %collective-permute-start.38 = (bf16[12,14,1024]{2,1,0:T(8,128)(2,1)S(1)}, bf16[12,14,1024]{2,1,0:T(8,128)(2,1)S(1)}, u32[]{:S(2)}, u32[]{:S(2)}) collective-permute-start(bf16[12,14,1024]{2,1,0:T(8,128)(2,1)S(1)} %copy-done.110), channel_id=1, source_target_pairs={{4,0},{8,4},{12,8},{16,12},{20,16},{24,20},{28,24},{5,1},{9,5},{13... | collective-permute-start | bytes 1032200 | tf_op jit(solution)/shard_map/ppermute | solution.py:611
  133.8 7.7 %collective-permute-start.40 = (bf16[2,2,2,32,512]{4,3,2,1,0:T(8,128)(2,1)S(1)}, bf16[2,2,2,32,512]{4,3,2,1,0:T(8,128)(2,1)S(1)}, u32[]{:S(2)}, u32[]{:S(2)}) collective-permute-start(bf16[2,2,2,32,512]{4,3,2,1,0:T(8,128)(2,1)S(1)} %pad_maximum_fusion.10), channel_id=1, source_target_pairs={{0,2},{1,3},{2,0},{3,1},{4,6},{5,7},{6,4},{7,5},{8,10},{9,11},{10,... | collective-permute-start | bytes 786440 | tf_op jit(solution)/shard_map/ppermute | solution.py:605
  147.5 11.9 %collective-permute-start.45 = (bf16[2,16,2048]{2,1,0:T(8,128)(2,1)S(1)}, bf16[2,16,2048]{2,1,0:T(8,128)(2,1)S(1)}, u32[]{:S(2)}, u32[]{:S(2)}) collective-permute-start(bf16[2,16,2048]{2,1,0:T(8,128)(2,1)S(1)} %pad_maximum_fusion.18), channel_id=1, source_target_pairs={{0,16},{1,17},{2,18},{3,19},{4,20},{5,21},{6,22},{7,23},{8,24},{9,... | collective-permute-start | bytes 393224 | tf_op jit(solution)/shard_map/ppermute | solution.py:605
  149.9 9.6 %collective-permute-start.46 = (bf16[2,2,2,2,32,512]{5,4,3,2,1,0:T(8,128)(2,1)S(1)}, bf16[2,2,2,2,32,512]{5,4,3,2,1,0:T(8,128)(2,1)S(1)}, u32[]{:S(2)}, u32[]{:S(2)}) collective-permute-start(bf16[2,2,2,2,32,512]{5,4,3,2,1,0:T(8,128)(2,1)S(1)} %pad_maximum_fusion.6), channel_id=1, source_target_pairs={{0,1},{1,0},{2,3},{3,2},{4,5},{5,4},{6,7},{7,6},{8,9},{9,8},{10,11... | collective-permute-start | bytes 1572872 | tf_op jit(solution)/shard_map/ppermute | solution.py:605
  159.5 10.0 %collective-permute-start.50 = (bf16[2,2,16,2048]{3,2,1,0:T(8,128)(2,1)S(1)}, bf16[2,2,16,2048]{3,2,1,0:T(8,128)(2,1)S(1)}, u32[]{:S(2)}, u32[]{:S(2)}) collective-permute-start(bf16[2,2,16,2048]{3,2,1,0:T(8,128)(2,1)S(1)} %pad_maximum_fusion.11), channel_id=1, source_target_pairs={{0,4},{1,5},{2,6},{3,7},{4,0},{5,1},{6,2},{7,3},{8,12},{9,13},{10,... | collective-permute-start | bytes 786440 | tf_op jit(solution)/shard_map/ppermute | solution.py:605
  169.6 32.1 %collective-permute-start.53 = (bf16[2,2,2,16,2048]{4,3,2,1,0:T(8,128)(2,1)S(1)}, bf16[2,2,2,16,2048]{4,3,2,1,0:T(8,128)(2,1)S(1)}, u32[]{:S(2)}, u32[]{:S(2)}) collective-permute-start(bf16[2,2,2,16,2048]{4,3,2,1,0:T(8,128)(2,1)S(1)} %pad_maximum_fusion.7), channel_id=1, source_target_pairs={{0,2},{1,3},{2,0},{3,1},{4,6},{5,7},{6,4},{7,5},{8,10},{9,11},{10,... | collective-permute-start | bytes 1572872 | tf_op jit(solution)/shard_map/ppermute | solution.py:605
  171.3 10.2 %collective-permute-start.51 = (bf16[12,14,1024]{2,1,0:T(8,128)(2,1)S(1)}, bf16[12,14,1024]{2,1,0:T(8,128)(2,1)S(1)}, u32[]{:S(2)}, u32[]{:S(2)}) collective-permute-start(bf16[12,14,1024]{2,1,0:T(8,128)(2,1)S(1)} %copy-done.108), channel_id=1, source_target_pairs={{4,0},{8,4},{12,8},{16,12},{20,16},{24,20},{28,24},{5,1},{9,5},{13... | collective-permute-start | bytes 1032200 | tf_op jit(solution)/shard_map/ppermute | solution.py:611
  237.4 12.2 %collective-permute-start.66 = (f32[8,512]{1,0:T(8,128)S(1)}, f32[8,512]{1,0:T(8,128)S(1)}, u32[]{:S(2)}, u32[]{:S(2)}) collective-permute-start(f32[8,512]{1,0:T(8,128)S(1)} %add_add_fusion.13), channel_id=1, source_target_pairs={{0,16},{1,17},{2,18},{3,19},{4,20},{5,21},{6,22},{7,23},{8,24},{9,... | collective-permute-start | bytes 49160 | tf_op jit(solution)/shard_map/ppermute | solution.py:605
  239.1 10.5 %collective-permute-start.67 = (f32[8,512]{1,0:T(8,128)S(1)}, f32[8,512]{1,0:T(8,128)S(1)}, u32[]{:S(2)}, u32[]{:S(2)}) collective-permute-start(f32[8,512]{1,0:T(8,128)S(1)} %add_add_fusion.13), channel_id=1, source_target_pairs={{0,24},{1,25},{2,26},{3,27},{4,28},{5,29},{6,30},{7,31},{8,16},{9,... | collective-permute-start | bytes 49160 | tf_op jit(solution)/shard_map/ppermute | solution.py:605
  239.7 9.9 %collective-permute-start.65 = (f32[8,512]{1,0:T(8,128)S(1)}, f32[8,512]{1,0:T(8,128)S(1)}, u32[]{:S(2)}, u32[]{:S(2)}) collective-permute-start(f32[8,512]{1,0:T(8,128)S(1)} %add_add_fusion.13), channel_id=1, source_target_pairs={{0,8},{1,9},{2,10},{3,11},{4,12},{5,13},{6,14},{7,15},{8,0},{9,1},... | collective-permute-start | bytes 49160 | tf_op jit(solution)/shard_map/ppermute | solution.py:605
  266.6 11.4 %collective-permute-start.73 = (f32[8,4096]{1,0:T(8,128)S(1)}, f32[8,4096]{1,0:T(8,128)S(1)}, u32[]{:S(2)}, u32[]{:S(2)}) collective-permute-start(f32[8,4096]{1,0:T(8,128)S(1)} %add_add_fusion.3), channel_id=1, source_target_pairs={{0,16},{1,17},{2,18},{3,19},{4,20},{5,21},{6,22},{7,23},{8,24},{9,... | collective-permute-start | bytes 393224 | tf_op jit(solution)/shard_map/ppermute | solution.py:605
  269.4 8.5 %collective-permute-start.74 = (f32[8,4096]{1,0:T(8,128)S(1)}, f32[8,4096]{1,0:T(8,128)S(1)}, u32[]{:S(2)}, u32[]{:S(2)}) collective-permute-start(f32[8,4096]{1,0:T(8,128)S(1)} %add_add_fusion.3), channel_id=1, source_target_pairs={{0,24},{1,25},{2,26},{3,27},{4,28},{5,29},{6,30},{7,31},{8,16},{9,... | collective-permute-start | bytes 393224 | tf_op jit(solution)/shard_map/ppermute | solution.py:605
  270.1 7.8 %collective-permute-start.72 = (f32[8,4096]{1,0:T(8,128)S(1)}, f32[8,4096]{1,0:T(8,128)S(1)}, u32[]{:S(2)}, u32[]{:S(2)}) collective-permute-start(f32[8,4096]{1,0:T(8,128)S(1)} %add_add_fusion.3), channel_id=1, source_target_pairs={{0,8},{1,9},{2,10},{3,11},{4,12},{5,13},{6,14},{7,15},{8,0},{9,1},... | collective-permute-start | bytes 393224 | tf_op jit(solution)/shard_map/ppermute | solution.py:605
  294.5 6.9 %collective-permute-start.76 = (f32[8,4096]{1,0:T(8,128)S(1)}, f32[8,4096]{1,0:T(8,128)}, u32[]{:S(2)}, u32[]{:S(2)}) collective-permute-start(f32[8,4096]{1,0:T(8,128)S(1)} %add.1020), channel_id=1, source_target_pairs={{0,2},{1,3},{2,0},{3,1},{4,6},{5,7},{6,4},{7,5},{8,10},{9,11},{10,... | collective-permute-start | bytes 393224 | tf_op jit(solution)/shard_map/ppermute | solution.py:605
  303.1 8.5 %collective-permute-start.80 = (f32[8,4096]{1,0:T(8,128)}, f32[8,4096]{1,0:T(8,128)S(1)}, u32[]{:S(2)}, u32[]{:S(2)}) collective-permute-start(f32[8,4096]{1,0:T(8,128)} %add_add_fusion.1), channel_id=1, source_target_pairs={{0,16},{1,17},{2,18},{3,19},{4,20},{5,21},{6,22},{7,23},{8,24},{9,... | collective-permute-start | bytes 393224 | tf_op jit(solution)/shard_map/ppermute | solution.py:605
  305.3 7.2 %collective-permute-start.81 = (f32[8,4096]{1,0:T(8,128)}, f32[8,4096]{1,0:T(8,128)}, u32[]{:S(2)}, u32[]{:S(2)}) collective-permute-start(f32[8,4096]{1,0:T(8,128)} %add_add_fusion.1), channel_id=1, source_target_pairs={{0,24},{1,25},{2,26},{3,27},{4,28},{5,29},{6,30},{7,31},{8,16},{9,... | collective-permute-start | bytes 393224 | tf_op jit(solution)/shard_map/ppermute | solution.py:605
  348.4 8.2 %collective-permute-start.82 = (f32[8,512]{1,0:T(8,128)S(1)}, f32[8,512]{1,0:T(8,128)S(1)}, u32[]{:S(2)}, u32[]{:S(2)}) collective-permute-start(f32[8,512]{1,0:T(8,128)S(1)} %copy-done.81), channel_id=1, source_target_pairs={{0,1},{1,0},{2,3},{3,2},{4,5},{5,4},{6,7},{7,6},{8,9},{9,8},{10,11... | collective-permute-start | bytes 49160 | tf_op jit(solution)/shard_map/ppermute | solution.py:605
  368.9 19.4 %collective-permute-start.90 = (bf16[2,2,2,2,16,2048]{5,4,3,2,1,0:T(8,128)(2,1)}, bf16[2,2,2,2,16,2048]{5,4,3,2,1,0:T(8,128)(2,1)}, u32[]{:S(2)}, u32[]{:S(2)}) collective-permute-start(bf16[2,2,2,2,16,2048]{5,4,3,2,1,0:T(8,128)(2,1)} %dynamic-slice_bitcast_fusion.2), channel_id=1, source_target_pairs={{0,1},{1,0},{2,3},{3,2},{4,5},{5,4},{6,7},{7,6},{8,9},{9,8},{10,11... | collective-permute-start | bytes 3145736 | tf_op jit(solution)/shard_map/ppermute | solution.py:605
  396.0 31.9 %collective-permute-start.98 = (bf16[2,2,2,16,2048]{4,3,2,1,0:T(8,128)(2,1)}, bf16[2,2,2,16,2048]{4,3,2,1,0:T(8,128)(2,1)}, u32[]{:S(2)}, u32[]{:S(2)}) collective-permute-start(bf16[2,2,2,16,2048]{4,3,2,1,0:T(8,128)(2,1)} %get-tuple-element.186), channel_id=1, source_target_pairs={{0,2},{1,3},{2,0},{3,1},{4,6},{5,7},{6,4},{7,5},{8,10},{9,11},{10,... | collective-permute-start | bytes 1572872 | tf_op jit(solution)/shard_map/ppermute | solution.py:605
  419.0 8.8 %collective-permute-start.97 = (f32[8,1024]{1,0:T(8,128)S(1)}, f32[8,1024]{1,0:T(8,128)S(1)}, u32[]{:S(2)}, u32[]{:S(2)}) collective-permute-start(f32[8,1024]{1,0:T(8,128)S(1)} %get-tuple-element.185), channel_id=1, source_target_pairs={{0,1},{1,0},{2,3},{3,2},{4,5},{5,4},{6,7},{7,6},{8,9},{9,8},{10,11... | collective-permute-start | bytes 98312 | tf_op jit(solution)/shard_map/ppermute | solution.py:605
  422.3 7.5 %collective-permute-start.99 = (bf16[2,2,2,2,64,512]{5,4,3,2,1,0:T(8,128)(2,1)}, bf16[2,2,2,2,64,512]{5,4,3,2,1,0:T(8,128)(2,1)S(1)}, u32[]{:S(2)}, u32[]{:S(2)}) collective-permute-start(bf16[2,2,2,2,64,512]{5,4,3,2,1,0:T(8,128)(2,1)} %dynamic-slice_bitcast_fusion.1), channel_id=1, source_target_pairs={{0,1},{1,0},{2,3},{3,2},{4,5},{5,4},{6,7},{7,6},{8,9},{9,8},{10,11... | collective-permute-start | bytes 3145736 | tf_op jit(solution)/shard_map/ppermute | solution.py:605
  422.3 8.6 %collective-permute-start.100 = (bf16[2,2,2,2,80,512]{5,4,3,2,1,0:T(8,128)(2,1)S(1)}, bf16[2,2,2,2,80,512]{5,4,3,2,1,0:T(8,128)(2,1)S(1)}, u32[]{:S(2)}, u32[]{:S(2)}) collective-permute-start(bf16[2,2,2,2,80,512]{5,4,3,2,1,0:T(8,128)(2,1)S(1)} %dynamic-slice_bitcast_fusion), channel_id=1, source_target_pairs={{0,1},{1,0},{2,3},{3,2},{4,5},{5,4},{6,7},{7,6},{8,9},{9,8},{10,11... | collective-permute-start | bytes 3932168 | tf_op jit(solution)/shard_map/ppermute | solution.py:605
  436.1 10.0 %collective-permute-start.105 = (f32[8,1024]{1,0:T(8,128)S(1)}, f32[8,1024]{1,0:T(8,128)}, u32[]{:S(2)}, u32[]{:S(2)}) collective-permute-start(f32[8,1024]{1,0:T(8,128)S(1)} %add_add_fusion.5), channel_id=1, source_target_pairs={{0,16},{1,17},{2,18},{3,19},{4,20},{5,21},{6,22},{7,23},{8,24},{9,... | collective-permute-start | bytes 98312 | tf_op jit(solution)/shard_map/ppermute | solution.py:605
  437.1 9.2 %collective-permute-start.106 = (f32[8,1024]{1,0:T(8,128)S(1)}, f32[8,1024]{1,0:T(8,128)}, u32[]{:S(2)}, u32[]{:S(2)}) collective-permute-start(f32[8,1024]{1,0:T(8,128)S(1)} %add_add_fusion.5), channel_id=1, source_target_pairs={{0,24},{1,25},{2,26},{3,27},{4,28},{5,29},{6,30},{7,31},{8,16},{9,... | collective-permute-start | bytes 98312 | tf_op jit(solution)/shard_map/ppermute | solution.py:605
  440.1 7.1 %collective-permute-start.107 = (bf16[2,2,16,2048]{3,2,1,0:T(8,128)(2,1)}, bf16[2,2,16,2048]{3,2,1,0:T(8,128)(2,1)}, u32[]{:S(2)}, u32[]{:S(2)}) collective-permute-start(bf16[2,2,16,2048]{3,2,1,0:T(8,128)(2,1)} %get-tuple-element.193), channel_id=1, source_target_pairs={{0,4},{1,5},{2,6},{3,7},{4,0},{5,1},{6,2},{7,3},{8,12},{9,13},{10,... | collective-permute-start | bytes 786440 | tf_op jit(solution)/shard_map/ppermute | solution.py:605
  445.6 30.7 %collective-permute-start.109 = (bf16[2,2,2,64,512]{4,3,2,1,0:T(8,128)(2,1)S(1)}, bf16[2,2,2,64,512]{4,3,2,1,0:T(8,128)(2,1)S(1)}, u32[]{:S(2)}, u32[]{:S(2)}) collective-permute-start(bf16[2,2,2,64,512]{4,3,2,1,0:T(8,128)(2,1)S(1)} %copy-done.106), channel_id=1, source_target_pairs={{0,4},{1,5},{2,6},{3,7},{4,0},{5,1},{6,2},{7,3},{8,12},{9,13},{10,... | collective-permute-start | bytes 1572872 | tf_op jit(solution)/shard_map/ppermute | solution.py:605
  446.1 30.2 %collective-permute-start.110 = (bf16[2,2,2,80,512]{4,3,2,1,0:T(8,128)(2,1)S(1)}, bf16[2,2,2,80,512]{4,3,2,1,0:T(8,128)(2,1)S(1)}, u32[]{:S(2)}, u32[]{:S(2)}) collective-permute-start(bf16[2,2,2,80,512]{4,3,2,1,0:T(8,128)(2,1)S(1)} %copy-done.105), channel_id=1, source_target_pairs={{0,2},{1,3},{2,0},{3,1},{4,6},{5,7},{6,4},{7,5},{8,10},{9,11},{10,... | collective-permute-start | bytes 1966088 | tf_op jit(solution)/shard_map/ppermute | solution.py:605
  466.7 9.6 %collective-permute-start.108 = (f32[8,256]{1,0:T(8,128)S(1)}, f32[8,256]{1,0:T(8,128)S(1)}, u32[]{:S(2)}, u32[]{:S(2)}) collective-permute-start(f32[8,256]{1,0:T(8,128)S(1)} %get-tuple-element.196), channel_id=1, source_target_pairs={{0,1},{1,0},{2,3},{3,2},{4,5},{5,4},{6,7},{7,6},{8,9},{9,8},{10,11... | collective-permute-start | bytes 24584 | tf_op jit(solution)/shard_map/ppermute | solution.py:605
  470.7 14.6 %collective-permute-start.111 = (bf16[192,1024]{1,0:T(8,128)(2,1)S(1)}, bf16[192,1024]{1,0:T(8,128)(2,1)S(1)}, u32[]{:S(2)}, u32[]{:S(2)}) collective-permute-start(bf16[192,1024]{1,0:T(8,128)(2,1)S(1)} %copy-done.111), channel_id=1, source_target_pairs={{0,4},{4,8},{8,12},{12,16},{16,20},{20,24},{24,28},{1,5},{5,9},{9,... | collective-permute-start | bytes 1179656 | tf_op jit(solution)/shard_map/ppermute | solution.py:611
  474.6 11.4 %collective-permute-start.115 = (bf16[2,16,2048]{2,1,0:T(8,128)(2,1)S(1)}, bf16[2,16,2048]{2,1,0:T(8,128)(2,1)S(1)}, u32[]{:S(2)}, u32[]{:S(2)}) collective-permute-start(bf16[2,16,2048]{2,1,0:T(8,128)(2,1)S(1)} %get-tuple-element.203), channel_id=1, source_target_pairs={{0,16},{1,17},{2,18},{3,19},{4,20},{5,21},{6,22},{7,23},{8,24},{9,... | collective-permute-start | bytes 393224 | tf_op jit(solution)/shard_map/ppermute | solution.py:605
  485.3 10.7 %collective-permute-start.116 = (bf16[2,2,2,2,96,256]{5,4,3,2,1,0:T(8,128)(2,1)S(1)}, bf16[2,2,2,2,96,256]{5,4,3,2,1,0:T(8,128)(2,1)S(1)}, u32[]{:S(2)}, u32[]{:S(2)}) collective-permute-start(bf16[2,2,2,2,96,256]{5,4,3,2,1,0:T(8,128)(2,1)S(1)} %fusion.4), channel_id=1, source_target_pairs={{0,1},{1,0},{2,3},{3,2},{4,5},{5,4},{6,7},{7,6},{8,9},{9,8},{10,11... | collective-permute-start | bytes 2359304 | tf_op jit(solution)/shard_map/ppermute | solution.py:605
  486.1 7.8 %collective-permute-start.113 = (f32[8,256]{1,0:T(8,128)S(1)}, f32[8,256]{1,0:T(8,128)S(1)}, u32[]{:S(2)}, u32[]{:S(2)}) collective-permute-start(f32[8,256]{1,0:T(8,128)S(1)} %add.1064), channel_id=1, source_target_pairs={{0,4},{1,5},{2,6},{3,7},{4,0},{5,1},{6,2},{7,3},{8,12},{9,13},{10,... | collective-permute-start | bytes 24584 | tf_op jit(solution)/shard_map/ppermute | solution.py:605
  510.4 15.3 %collective-permute-start.122 = (f32[8,256]{1,0:T(8,128)S(1)}, f32[8,256]{1,0:T(8,128)S(1)}, u32[]{:S(2)}, u32[]{:S(2)}) collective-permute-start(f32[8,256]{1,0:T(8,128)S(1)} %get-tuple-element.210), channel_id=1, source_target_pairs={{0,1},{1,0},{2,3},{3,2},{4,5},{5,4},{6,7},{7,6},{8,9},{9,8},{10,11... | collective-permute-start | bytes 24584 | tf_op jit(solution)/shard_map/ppermute | solution.py:605
  514.5 12.6 %collective-permute-start.123 = (bf16[16,2048]{1,0:T(8,128)(2,1)S(1)}, bf16[16,2048]{1,0:T(8,128)(2,1)S(1)}, u32[]{:S(2)}, u32[]{:S(2)}) collective-permute-start(bf16[16,2048]{1,0:T(8,128)(2,1)S(1)} %fusion.19), channel_id=1, source_target_pairs={{0,8},{1,9},{2,10},{3,11},{4,12},{5,13},{6,14},{7,15},{8,0},{9,1},... | collective-permute-start | bytes 196616 | tf_op jit(solution)/shard_map/ppermute | solution.py:605
  515.0 12.2 %collective-permute-start.124 = (bf16[2,2,2,96,256]{4,3,2,1,0:T(8,128)(2,1)S(1)}, bf16[2,2,2,96,256]{4,3,2,1,0:T(8,128)(2,1)S(1)}, u32[]{:S(2)}, u32[]{:S(2)}) collective-permute-start(bf16[2,2,2,96,256]{4,3,2,1,0:T(8,128)(2,1)S(1)} %get-tuple-element.214), channel_id=1, source_target_pairs={{0,2},{1,3},{2,0},{3,1},{4,6},{5,7},{6,4},{7,5},{8,10},{9,11},{10,... | collective-permute-start | bytes 1179656 | tf_op jit(solution)/shard_map/ppermute | solution.py:605
  515.6 13.0 %collective-permute-start.125 = (bf16[192,1024]{1,0:T(8,128)(2,1)S(1)}, bf16[192,1024]{1,0:T(8,128)(2,1)S(1)}, u32[]{:S(2)}, u32[]{:S(2)}) collective-permute-start(bf16[192,1024]{1,0:T(8,128)(2,1)S(1)} %copy-done.109), channel_id=1, source_target_pairs={{0,4},{4,8},{8,12},{12,16},{16,20},{20,24},{24,28},{1,5},{5,9},{9,... | collective-permute-start | bytes 1179656 | tf_op jit(solution)/shard_map/ppermute | solution.py:611
  524.7 11.6 %collective-permute-start.129 = (bf16[2,64,512]{2,1,0:T(8,128)(2,1)S(1)}, bf16[2,64,512]{2,1,0:T(8,128)(2,1)S(1)}, u32[]{:S(2)}, u32[]{:S(2)}) collective-permute-start(bf16[2,64,512]{2,1,0:T(8,128)(2,1)S(1)} %get-tuple-element.217), channel_id=1, source_target_pairs={{0,16},{1,17},{2,18},{3,19},{4,20},{5,21},{6,22},{7,23},{8,24},{9,... | collective-permute-start | bytes 393224 | tf_op jit(solution)/shard_map/ppermute | solution.py:605
  525.7 14.1 %collective-permute-start.130 = (bf16[2,80,512]{2,1,0:T(8,128)(2,1)S(1)}, bf16[2,80,512]{2,1,0:T(8,128)(2,1)S(1)}, u32[]{:S(2)}, u32[]{:S(2)}) collective-permute-start(bf16[2,80,512]{2,1,0:T(8,128)(2,1)S(1)} %get-tuple-element.218), channel_id=1, source_target_pairs={{0,16},{1,17},{2,18},{3,19},{4,20},{5,21},{6,22},{7,23},{8,24},{9,... | collective-permute-start | bytes 491528 | tf_op jit(solution)/shard_map/ppermute | solution.py:605
  528.7 17.4 %collective-permute-start.131 = (bf16[2,2,2,2,72,256]{5,4,3,2,1,0:T(8,128)(2,1)S(1)}, bf16[2,2,2,2,72,256]{5,4,3,2,1,0:T(8,128)(2,1)S(1)}, u32[]{:S(2)}, u32[]{:S(2)}) collective-permute-start(bf16[2,2,2,2,72,256]{5,4,3,2,1,0:T(8,128)(2,1)S(1)} %dynamic-slice_bitcast_fusion.3), channel_id=1, source_target_pairs={{0,1},{1,0},{2,3},{3,2},{4,5},{5,4},{6,7},{7,6},{8,9},{9,8},{10,11... | collective-permute-start | bytes 1769480 | tf_op jit(solution)/shard_map/ppermute | solution.py:605
  554.8 62.4 %collective-permute-start.137 = (bf16[3,192,256]{2,1,0:T(8,128)(2,1)S(1)}, bf16[3,192,256]{2,1,0:T(8,128)(2,1)S(1)}, u32[]{:S(2)}, u32[]{:S(2)}) collective-permute-start(bf16[3,192,256]{2,1,0:T(8,128)(2,1)S(1)} %slice.216), channel_id=1, source_target_pairs={{0,4},{4,8},{8,12},{12,16},{16,20},{20,24},{24,28},{1,5},{5,9},{9,... | collective-permute-start | bytes 884744 | tf_op jit(solution)/shard_map/ppermute | solution.py:611
  558.0 59.2 %collective-permute-start.138 = (bf16[192,1024]{1,0:T(8,128)(2,1)S(1)}, bf16[192,1024]{1,0:T(8,128)(2,1)S(1)}, u32[]{:S(2)}, u32[]{:S(2)}) collective-permute-start(bf16[192,1024]{1,0:T(8,128)(2,1)S(1)} %copy-done.107), channel_id=1, source_target_pairs={{0,4},{4,8},{8,12},{12,16},{16,20},{20,24},{24,28},{1,5},{5,9},{9,... | collective-permute-start | bytes 1179656 | tf_op jit(solution)/shard_map/ppermute | solution.py:611
  561.5 41.4 %collective-permute-start.139 = (bf16[2,2,2,2,32,256]{5,4,3,2,1,0:T(8,128)(2,1)S(1)}, bf16[2,2,2,2,32,256]{5,4,3,2,1,0:T(8,128)(2,1)S(1)}, u32[]{:S(2)}, u32[]{:S(2)}) collective-permute-start(bf16[2,2,2,2,32,256]{5,4,3,2,1,0:T(8,128)(2,1)S(1)} %dynamic-slice_bitcast_fusion.4), channel_id=1, source_target_pairs={{0,1},{1,0},{2,3},{3,2},{4,5},{5,4},{6,7},{7,6},{8,9},{9,8},{10,11... | collective-permute-start | bytes 786440 | tf_op jit(solution)/shard_map/ppermute | solution.py:605
  567.3 35.9 %collective-permute-start.146 = (bf16[2,2,2,72,256]{4,3,2,1,0:T(8,128)(2,1)S(1)}, bf16[2,2,2,72,256]{4,3,2,1,0:T(8,128)(2,1)S(1)}, u32[]{:S(2)}, u32[]{:S(2)}) collective-permute-start(bf16[2,2,2,72,256]{4,3,2,1,0:T(8,128)(2,1)S(1)} %get-tuple-element.226), channel_id=1, source_target_pairs={{0,4},{1,5},{2,6},{3,7},{4,0},{5,1},{6,2},{7,3},{8,12},{9,13},{10,... | collective-permute-start | bytes 884744 | tf_op jit(solution)/shard_map/ppermute | solution.py:605
  604.3 30.2 %collective-permute-start.147 = (bf16[2,2,72,256]{3,2,1,0:T(8,128)(2,1)S(1)}, bf16[2,2,72,256]{3,2,1,0:T(8,128)(2,1)S(1)}, u32[]{:S(2)}, u32[]{:S(2)}) collective-permute-start(bf16[2,2,72,256]{3,2,1,0:T(8,128)(2,1)S(1)} %get-tuple-element.309), channel_id=1, source_target_pairs={{0,2},{1,3},{2,0},{3,1},{4,6},{5,7},{6,4},{7,5},{8,10},{9,11},{10,... | collective-permute-start | bytes 442376 | tf_op jit(solution)/shard_map/ppermute | solution.py:605
  608.0 7.9 %collective-permute-start.141 = (bf16[2,2,32,256]{3,2,1,0:T(8,128)(2,1)S(1)}, bf16[2,2,32,256]{3,2,1,0:T(8,128)(2,1)S(1)}, u32[]{:S(2)}, u32[]{:S(2)}) collective-permute-start(bf16[2,2,32,256]{3,2,1,0:T(8,128)(2,1)S(1)} %get-tuple-element.335), channel_id=1, source_target_pairs={{0,4},{1,5},{2,6},{3,7},{4,0},{5,1},{6,2},{7,3},{8,12},{9,13},{10,... | collective-permute-start | bytes 196616 | tf_op jit(solution)/shard_map/ppermute | solution.py:605
  615.9 17.4 %collective-permute-start.142 = (bf16[2,32,256]{2,1,0:T(8,128)(2,1)S(1)}, bf16[2,32,256]{2,1,0:T(8,128)(2,1)S(1)}, u32[]{:S(2)}, u32[]{:S(2)}) collective-permute-start(bf16[2,32,256]{2,1,0:T(8,128)(2,1)S(1)} %get-tuple-element.353), channel_id=1, source_target_pairs={{0,16},{1,17},{2,18},{3,19},{4,20},{5,21},{6,22},{7,23},{8,24},{9,... | collective-permute-start | bytes 98312 | tf_op jit(solution)/shard_map/ppermute | solution.py:605
  647.3 8.5 %collective-permute-start.151 = (bf16[2,72,256]{2,1,0:T(8,128)(2,1)S(1)}, bf16[2,72,256]{2,1,0:T(8,128)(2,1)S(1)}, u32[]{:S(2)}, u32[]{:S(2)}) collective-permute-start(bf16[2,72,256]{2,1,0:T(8,128)(2,1)S(1)} %pad_maximum_fusion.23), channel_id=1, source_target_pairs={{0,1},{1,0},{2,3},{3,2},{4,5},{5,4},{6,7},{7,6},{8,9},{9,8},{10,11... | collective-permute-start | bytes 221192 | tf_op jit(solution)/shard_map/ppermute | solution.py:605
  (224 other events, 1710.1 us)
Sparse Core Ops, SparseCore 0:
  10.9 72.5 all-gather.4
  102.6 63.6 all-gather.6
  353.5 125.5 reduce-scatter.1

commit v2 on v1

v2 whole, which is shorter than its diff:
```python
import functools

import jax
import jax.numpy as jnp
from jax import lax
from jax.experimental import pallas as pl
from jax.experimental.pallas import tpu as pltpu
from jax.sharding import PartitionSpec as P

SPILL = 12
WIN = 40
COLS = 16
EPS = 1e-05
AXES = ("rows", "batch")
BF = jnp.bfloat16
F32 = jnp.float32
CHUNK = 32
TANH_SCALE = 0.7978845608028654
TANH_CUBE = 0.044715


def gelu(x):
    t = jnp.tanh(x * (TANH_SCALE + TANH_SCALE * TANH_CUBE * (x * x)))
    return x * (0.5 + 0.5 * t)


def gelu_slope(x):
    square = x * x
    t = jnp.tanh(x * (TANH_SCALE + TANH_SCALE * TANH_CUBE * square))
    inner = x * (TANH_SCALE + 3.0 * TANH_SCALE * TANH_CUBE * square)
    return (0.5 + 0.5 * t) * (1.0 + inner * (1.0 - t))


def nn(a, b):
    return lax.dot_general(a, b, (((1,), (0,)), ((), ())), preferred_element_type=F32)


def nt(a, b):
    return lax.dot_general(a, b, (((1,), (1,)), ((), ())), preferred_element_type=F32)


def wide_of(ref):
    return ref[...].reshape(-1, ref.shape[-1])


def pick(ref, row, start=0, width=None):
    table = ref[:, start : start + (width or ref.shape[1])]
    rows = lax.broadcasted_iota(jnp.int32, table.shape, 0)
    return jnp.sum(jnp.where(rows == row, table, 0.0), axis=0, keepdims=True)


def moments(ref, m, population, start=0, width=None):
    share = 1.0 / population
    average = pick(ref, 2 * m, start, width) * share
    return average, lax.rsqrt(pick(ref, 2 * m + 1, start, width) * share - average * average + EPS)


def line(ref, m, population, gain, bias):
    average, inv = moments(ref, m, population)
    scale = inv * gain[...]
    return scale, bias[...] - average * scale


def back_line(ref, back, m, population, gain, start=0):
    average, inv = moments(ref, m, population)
    share = 1.0 / population
    width = ref.shape[1]
    mean_d = pick(back, 2 * m, start, width) * share
    mean_dn = pick(back, 2 * m + 1, start, width) * share
    by_d = gain[...] * inv
    by_p = -by_d * inv * mean_dn
    return by_d, by_p, -by_d * mean_d - by_p * average


def centred(ref, m, population, first, second):
    average, inv = moments(ref, m, population)
    first = jnp.sum(first, axis=0, keepdims=True)
    second = jnp.sum(second, axis=0, keepdims=True)
    return first, inv * (second - average * first)


def put_sums(ref, m, first, second, start=0):
    c = first.shape[1]
    at = slice(start, start + c)

    @pl.when(m == 0)
    def _():
        ref[:, at] = jnp.zeros((ref.shape[0], c), F32)

    first = jnp.sum(first, axis=0, keepdims=True)
    second = jnp.sum(second, axis=0, keepdims=True)
    rows = lax.broadcasted_iota(jnp.int32, (ref.shape[0], c), 0)
    ref[:, at] = jnp.where(rows == 2 * m, first, jnp.where(rows == 2 * m + 1, second, ref[:, at]))


def sweep(rows, c, vectors, body, sums=0, chunk=CHUNK, width=256):
    out = [[] for _ in range(sums)]
    for j in range(c // width):
        lanes = slice(j * width, (j + 1) * width)
        spread = [jnp.broadcast_to(v[:, lanes], (8, width))[None] for v in vectors]

        def step(i, carry):
            at = pl.ds(pl.multiple_of(i * chunk, chunk), chunk)
            return tuple(t + jnp.sum(v, axis=0) for t, v in zip(carry, body(at, lanes, spread) or ()))

        total = lax.fori_loop(0, rows // chunk, step, (jnp.zeros((8, width), F32),) * sums)
        for k in range(sums):
            out[k].append(total[k])
    return [jnp.concatenate(v, 1) for v in out]


def eight(x):
    return x.reshape(-1, 8, x.shape[-1])


def flat(x):
    return x.reshape(-1, x.shape[-1])


def get(ref, at, lanes):
    return eight(ref[0, at, lanes].astype(F32))


def get_mask(ref, at, lanes):
    m = eight(ref[0, at, :])
    times = (lanes.stop - lanes.start) // LANES
    return jnp.concatenate([m] * times, 2) if times > 1 else m


def put(ref, at, lanes, value):
    ref[0, at, lanes] = flat(value).astype(ref.dtype)


def count_up(ref, out_total, m, mask=None):
    def add(at, lanes, _):
        p = get(ref, at, lanes)
        q = p if mask is None else p * get_mask(mask, at, lanes)
        return q, q * p

    put_sums(out_total, m, *sweep(ref.shape[1], ref.shape[2], (), add, 2))


LANES = 128


def put_tall(ref, rows, value, first=0):
    for j in range(value.shape[1] // LANES):
        ref[first // LANES + j, rows, :] = value[:, j * LANES : (j + 1) * LANES]


def get_tall(ref, rows, lanes):
    return jnp.concatenate([ref[j, rows, :] for j in range(lanes.start // LANES, lanes.stop // LANES)], 1)


OWN, UPPER, LOWER, INNER = 0, 1, 2, 3


def lane(ref, which, rows):
    return ref[0, rows, which : which + 1]


def k_masks(own, anchor, kinds, mine_out, half_out, flags, inner):
    first = anchor[0]
    height_of = lambda m, v: 6 + 8 * kinds[m, 0, v]
    for m in range(flags.shape[0]):
        rows = flags.shape[1] // COLS
        row = first + lax.broadcasted_iota(jnp.int32, (rows, LANES), 0)

        def view(v, c):
            at, width, start, last = c
            height = height_of(m, v)
            inside = (row >= at) & (row < at + height)
            return (
                at + height,
                jnp.where(inside, height, width),
                jnp.where(inside, at, start),
                jnp.where(inside, at + height - 1, last),
            )

        zero = jnp.zeros((rows, LANES), jnp.int32)
        _, width, start, last = lax.fori_loop(0, kinds.shape[2], view, (jnp.int32(0), zero, zero, zero))
        owned = (start >= first) & (start < first + own) & (width > 0)
        mine = jnp.where(owned, width, 0)
        above = (start != row).astype(F32)
        below = (last != row).astype(F32)
        cells = lambda v, n: jnp.broadcast_to(v[:, None, :], (v.shape[0], n, LANES))
        shape = (rows, COLS, LANES)
        column = lax.broadcasted_iota(jnp.int32, shape, 1)
        lanes = lax.broadcasted_iota(jnp.int32, shape, 2)
        value = jnp.where(lanes == OWN, (column < cells(width, COLS)).astype(F32), 0.0)
        value = jnp.where(lanes == UPPER, cells(above, COLS), value)
        value = jnp.where(lanes == LOWER, cells(below, COLS), value)
        flags[m] = value.reshape(rows * COLS, LANES)
        mine_out[m] = (column < cells(mine, COLS)).astype(F32).reshape(rows * COLS, LANES)
        shape = (rows, COLS // 2, LANES)
        column = lax.broadcasted_iota(jnp.int32, shape, 1)
        even = lambda v: v.reshape(rows // 2, 2, COLS // 2, LANES)[:, 0].reshape(rows * COLS // 4, LANES)
        half_out[m] = even((2 * column < cells(mine, COLS // 2)).astype(F32))
        inner[m] = even(cells(above, COLS // 2))


def k_first(features, mask, weight, pre, head, total, rows):
    m = pl.program_id(0)
    own, across = features.shape[2], features.shape[3]

    @pl.when(m == 0)
    def _():
        rows[...] = jnp.zeros_like(rows)

    for r in range(own):
        rows[r * COLS : r * COLS + across, :] = features[0, 0, r]
    pre[0] = nn(rows[...] * lane(mask, OWN, slice(0, own * COLS)).astype(BF), weight[...])
    head[0] = pre[0, 0 : head.shape[1], :].astype(BF)

    count_up(pre, total, m)


def k_entry(features, mask, *refs):
    spills, (entry, rows) = refs[:-2], refs[-2:]
    m = pl.program_id(0)
    own, across = features.shape[2], features.shape[3]

    @pl.when(m == 0)
    def _():
        rows[...] = jnp.zeros_like(rows)

    for r in range(own):
        rows[r * COLS : r * COLS + across, :] = features[0, 0, r]
    for k, spill in enumerate(spills):

        @pl.when(m == k)
        def _():
            for r in range(spill.shape[0]):
                at = (own + r) * COLS
                rows[at : at + across, :] = spill[r]

    entry[0] = rows[...] * lane(mask, 0, slice(None)).astype(BF)


def join_pre_one(own, spill, pre, c):
    edge, more = own.shape[1], spill.shape[1]
    pre[0, 0:edge, :] = own[0]
    pre[0, edge : edge + more, :] = spill[0].astype(F32)
    pre[0, edge + more :, :] = jnp.zeros((pre.shape[1] - edge - more, c), F32)


def spread_trio(source, trio, cells):
    c = source.shape[1]
    trio[0:COLS, :] = jnp.zeros((COLS, 3 * c), BF)
    trio[COLS + cells : 2 * COLS + cells, :] = jnp.zeros((COLS, 3 * c), BF)
    for r in range(0, cells, CHUNK):
        for tap in range(3):
            part = source[COLS + r + tap - 1 : COLS + r + tap - 1 + CHUNK, :]
            trio[COLS + r : COLS + r + CHUNK, tap * c : (tap + 1) * c] = part.astype(BF)


def conv_rows(trio, flags, weight, cells):
    width = trio.shape[1]
    upper = lane(flags, UPPER, slice(None)).astype(BF)
    lower = lane(flags, LOWER, slice(None)).astype(BF)
    above = trio[0:cells, :] * upper
    here = trio[COLS : COLS + cells, :]
    below = trio[2 * COLS : 2 * COLS + cells, :] * lower
    total = (
        nn(above, weight[0:width, :])
        + nn(here, weight[width : 2 * width, :])
        + nn(below, weight[2 * width : 3 * width, :])
    )
    return total, (above, here, below)


def clear_ends(source, cells):
    c = source.shape[1]
    source[0:COLS, :] = jnp.zeros((COLS, c), F32)
    source[COLS + cells : 2 * COLS + cells, :] = jnp.zeros((COLS, c), F32)


def later(at, by):
    return pl.ds(pl.multiple_of(at.start + by, 8), at.size)


def k_second(count, own, spill, total, gain, bias, mask, flags, weight, pre, patch, out_total, act, trio, joined):
    m = pl.program_id(0)
    cells, c = mask.shape[1], own.shape[2]
    join_pre_one(own, spill, joined, c)
    clear_ends(act, cells)

    def step(at, lanes, v):
        x = get(joined, at, lanes) * v[0] + v[1]
        act[later(at, COLS), lanes] = flat(gelu(x) * get_mask(mask, at, lanes))

    sweep(cells, c, line(total, m, count, gain, bias), step)
    spread_trio(act, trio, cells)
    result, parts = conv_rows(trio, flags, weight, cells)
    pre[0] = result
    for k, part in enumerate(parts):
        patch[0, :, k * 3 * c : (k + 1) * 3 * c] = part
    count_up(pre, out_total, m, mask)


def k_third(count, pre_in, total, gain, bias, mask, weight, act, pre, out_total):
    m = pl.program_id(0)

    def step(at, lanes, v):
        x = get(pre_in, at, lanes) * v[0] + v[1]
        put(act, at, lanes, gelu(x) * get_mask(mask, at, lanes))

    sweep(pre_in.shape[1], pre_in.shape[2], line(total, m, count, gain, bias), step)
    pre[0] = nn(act[0], wide_of(weight)).astype(pre.dtype)
    count_up(pre, out_total, m)


def k_fourth(count, pre_in, entry, total, gain, bias, mask, weight, block, corner, pre, out_total, full):
    m = pl.program_id(0)
    wide = COLS // 2
    chunk = 4 * COLS

    def step(at, lanes, v):
        x = get(pre_in, at, lanes) * v[0] + v[1] + get(entry, at, lanes)
        y = gelu(x) * get_mask(mask, at, lanes)
        put(block, at, lanes, y)
        put_tall(full, slice(0, chunk), flat(y), lanes.start)
        pair = [get_tall(full, pl.ds(k * COLS, wide, stride=2), lanes) for k in (0, 2)]
        corner[0, pl.ds(pl.multiple_of(at.start // 4, COLS), COLS), lanes] = jnp.concatenate(pair, 0).astype(BF)

    sweep(pre_in.shape[1], pre_in.shape[2], line(total, m, count, gain, bias), step, chunk=chunk)
    pre[0] = nn(block[0], wide_of(weight)).astype(pre.dtype)
    count_up(pre, out_total, m)


def k_seventh(corner, weight, pre, out_total):
    pre[0] = nn(corner[0], wide_of(weight)).astype(pre.dtype)
    count_up(pre, out_total, pl.program_id(1))


def k_fifth(count, pre_in, total, gain, bias, mask, half_mask, inner, weight, pre, patch, out_total, act, eo, oe, oo):
    m = pl.program_id(0)
    cells, c = pre_in.shape[1], pre_in.shape[2]
    half = cells // 4
    wide = COLS // 2

    def step(at, lanes, v):
        x = get(pre_in, at, lanes) * v[0] + v[1]
        put_tall(act, at, flat(gelu(x) * get_mask(mask, at, lanes)), lanes.start)

    sweep(cells, c, line(total, m, count, gain, bias), step)
    pad = 2 * wide
    for buf in (eo, oe, oo):
        buf[0:pad, :] = jnp.zeros((pad, c), F32)
    for j in range(c // LANES):
        lanes = slice(j * LANES, (j + 1) * LANES)
        even = act[j, pl.ds(0, cells // 2, stride=2), :].reshape(half // wide, 2, wide, LANES)
        odd = act[j, pl.ds(1, cells // 2, stride=2), :].reshape(half // wide, 2, wide, LANES)
        patch[0, :, 4 * c + j * LANES : 4 * c + (j + 1) * LANES] = even[:, 0].reshape(half, LANES).astype(BF)
        oe[pad : pad + half, lanes] = even[:, 1].reshape(half, LANES)
        eo[pad : pad + half, lanes] = odd[:, 0].reshape(half, LANES)
        oo[pad : pad + half, lanes] = odd[:, 1].reshape(half, LANES)
    first = jnp.concatenate([inner[0]] * (c // LANES), 1)
    take = lambda buf, back: buf[pad - back : pad - back + half, :]
    taps = (
        take(oo, wide + 1) * first, take(oe, wide) * first, take(oo, wide) * first,
        take(eo, 1), None, take(eo, 0),
        take(oo, 1), take(oe, 0), take(oo, 0),
    )
    for k, tap in enumerate(taps):
        if tap is not None:
            patch[0, :, k * c : (k + 1) * c] = tap.astype(BF)
    pre[0] = nn(patch[0], wide_of(weight))
    count_up(pre, out_total, m, half_mask)


def k_last(count, six, seven, tot6, tot7, g6, b6, g7, b7, half_mask, cot, out, slope, total, row):
    m = pl.program_id(0)
    half, c = six.shape[1], six.shape[2]
    wide = COLS // 2
    shown, across = out.shape[2], out.shape[3]
    scale6, shift6 = line(tot6, m, count, g6, b6)
    scale7, shift7 = line(tot7, m, count, g7, b7)
    row[...] = jnp.zeros_like(row)

    def step(at, lanes, v):
        p = 2 * (at.start // (2 * wide))
        mask = get_mask(half_mask, at, lanes)
        s6, s7 = get(six, at, lanes), get(seven, at, lanes)
        joined = s6 * v[0] + s7 * v[1] + v[2]
        square = joined * joined
        t = jnp.tanh(joined * (TANH_SCALE + TANH_SCALE * TANH_CUBE * square))
        inside = joined * (TANH_SCALE + 3.0 * TANH_SCALE * TANH_CUBE * square)
        part = (0.5 + 0.5 * t) * mask
        result = flat(joined * part)
        for k in range(2):
            q = jnp.minimum(p + k, shown - 1)
            if shown % 2 == 0 or k == 0:
                out[0, 0, q, :, lanes] = result[k * wide : k * wide + across].astype(BF)
            else:

                @pl.when(p + k < shown)
                def _():
                    out[0, 0, q, :, lanes] = result[k * wide : k * wide + across].astype(BF)

            row[k * wide : k * wide + across, lanes] = cot[0, 0, q, :, lanes].astype(F32)
        d = part * (1.0 + inside * (1.0 - t)) * eight(row[:, lanes])
        put(slope, at, lanes, d)
        return d, d * s6, d * s7

    sums = sweep(half, c, (scale6, scale7, shift6 + shift7), step, 3, chunk=2 * wide, width=512)
    put_sums(total, m, *centred(tot6, m, count, sums[0], sums[1]))
    put_sums(total, m, *centred(tot7, m, count, sums[0], sums[2]), c)


def slope_sums(d_out, pre, tot, m, population, gain, bias, mask, out_total, more=None):
    def add(at, lanes, v):
        p = get(pre, at, lanes)
        d = gelu_slope(p * v[0] + v[1]) * get(d_out, at, lanes) * get_mask(mask, at, lanes)
        put(d_out, at, lanes, d)
        return d, d * p

    sums = sweep(pre.shape[1], pre.shape[2], line(tot, m, population, gain, bias), add, 2)
    put_sums(out_total, m, *centred(tot, m, population, *sums))


def norm_back(d_pre, d, pre, tot, back, m, population, gain, mask):
    def step(at, lanes, v):
        value = get(d, at, lanes) * v[0] + get(pre, at, lanes) * v[1] + v[2]
        put(d_pre, at, lanes, value * get_mask(mask, at, lanes))

    sweep(pre.shape[1], pre.shape[2], back_line(tot, back, m, population, gain), step)


def k_back_six(
    count, slope, six, seven, tot6, tot7, back, g6, g7, five, tot5, g5, b5, half_mask, weight,
    d_six, d_seven, d_five, out_total,
):
    m = pl.program_id(0)
    half, c = six.shape[1], six.shape[2]

    def step(at, lanes, v):
        d = get(slope, at, lanes)
        mask = get_mask(half_mask, at, lanes)
        put(d_six, at, lanes, (d * v[0] + get(six, at, lanes) * v[1] + v[2]) * mask)
        put(d_seven, at, lanes, (d * v[3] + get(seven, at, lanes) * v[4] + v[5]) * mask)

    vectors = back_line(tot6, back, m, count, g6) + back_line(tot7, back, m, count, g7, c)
    sweep(half, c, vectors, step)
    d_five[0] = nt(d_six[0], wide_of(weight))
    slope_sums(d_five, five, tot5, m, count, g5, b5, half_mask, out_total)


def k_corner(d_seven, weight, d_corner):
    d_corner[0] = nt(d_seven[0], wide_of(weight)).astype(d_corner.dtype)


def k_back_five(
    half_count, full_count, d_five, five, tot5, back5, g5, half_mask, inner, weight, four, tot4, g4, b4, mask,
    d_pre, d_four, out_total, grid_scratch, shifted,
):
    m = pl.program_id(0)
    half, c = five.shape[1], five.shape[2]
    cells = 4 * half
    wide = COLS // 2
    norm_back(d_pre, d_five, five, tot5, back5, m, half_count, g5, half_mask)
    d = d_pre[0]
    wide_d = d.astype(F32)
    tail = 2 * wide
    shifted[half : half + tail, :] = jnp.zeros((tail, c), F32)
    shifted[0:half, :] = wide_d
    right = shifted[1 : 1 + half, :].astype(BF)
    shifted[0:half, :] = wide_d * jnp.concatenate([inner[0]] * (c // LANES), 1)
    down = shifted[wide : wide + half, :].astype(BF)
    down_right = shifted[wide + 1 : wide + 1 + half, :].astype(BF)
    taps = wide_of(weight)
    w = lambda tap: taps[tap * c : (tap + 1) * c]
    ee = nt(d, w(4))
    eo = nt(d, w(5)) + nt(right, w(3))
    oe = nt(d, w(7)) + nt(down, w(1))
    oo = nt(d, w(8)) + nt(right, w(6)) + nt(down, w(2)) + nt(down_right, w(0))
    rows = half // wide
    even = jnp.stack([ee.reshape(rows, wide, c), oe.reshape(rows, wide, c)], 1).reshape(cells // 2, c)
    odd = jnp.stack([eo.reshape(rows, wide, c), oo.reshape(rows, wide, c)], 1).reshape(cells // 2, c)
    put_tall(grid_scratch, pl.ds(0, cells // 2, stride=2), even)
    put_tall(grid_scratch, pl.ds(1, cells // 2, stride=2), odd)

    def add(at, lanes, v):
        p = get(four, at, lanes)
        got = eight(get_tall(grid_scratch, at, lanes))
        d = gelu_slope(p * v[0] + v[1]) * got * get_mask(mask, at, lanes)
        put(d_four, at, lanes, d)
        return d, d * p

    sums = sweep(cells, c, line(tot4, m, full_count, g4, b4), add, 2)
    put_sums(out_total, m, *centred(tot4, m, full_count, *sums))


def k_back_four(
    count, d_four, four, tot4, back4, g4, mask, weight, d_corner, three, entry, tot3, g3, b3,
    d_pre, d_summed, out_total, placed, d_block,
):
    m = pl.program_id(0)
    cells, c = three.shape[1], three.shape[2]
    norm_back(d_pre, d_four, four, tot4, back4, m, count, g4, mask)
    d_block[0] = nt(d_pre[0], wide_of(weight))
    wide = COLS // 2
    placed[...] = jnp.zeros_like(placed)

    def add(at, lanes, v):
        corner_at = pl.ds(pl.multiple_of(at.start // 4, COLS), COLS)
        value = d_corner[0, corner_at, lanes].astype(F32)
        for k in range(2):
            rows = pl.ds(2 * k * COLS, wide, stride=2)
            put_tall(placed, rows, value[k * wide : (k + 1) * wide], lanes.start)
        got = get(d_block, at, lanes) + eight(get_tall(placed, slice(0, 4 * COLS), lanes))
        p = get(three, at, lanes)
        x = p * v[0] + v[1] + get(entry, at, lanes)
        d = gelu_slope(x) * got * get_mask(mask, at, lanes)
        put(d_summed, at, lanes, d)
        return d, d * p

    sums = sweep(cells, c, line(tot3, m, count, g3, b3), add, 2, chunk=4 * COLS)
    put_sums(out_total, m, *centred(tot3, m, count, *sums))


def k_back_three(count, d_summed, three, tot3, back3, g3, mask, weight, two, tot2, g2, b2, d_pre, d_two, out_total):
    m = pl.program_id(0)
    norm_back(d_pre, d_summed, three, tot3, back3, m, count, g3, mask)
    d_two[0] = nt(d_pre[0], wide_of(weight))
    slope_sums(d_two, two, tot2, m, count, g2, b2, mask, out_total)


def k_back_two(
    count, d_two, two, tot2, back2, g2, mask, flags, weight, own, spill, tot1, g1, b1,
    d_pre, d_one, out_total, source, trio, joined,
):
    m = pl.program_id(0)
    cells, c = two.shape[1], two.shape[2]
    clear_ends(source, cells)

    def step(at, lanes, v):
        value = get(d_two, at, lanes) * v[0] + get(two, at, lanes) * v[1] + v[2]
        value = value * get_mask(mask, at, lanes)
        put(d_pre, at, lanes, value)
        source[later(at, COLS), lanes] = flat(value)

    sweep(cells, c, back_line(tot2, back2, m, count, g2), step)
    spread_trio(source, trio, cells)
    upper = lane(flags, UPPER, slice(None)).astype(BF)
    lower = lane(flags, LOWER, slice(None)).astype(BF)
    shifted = (
        trio[0:cells, :] * upper,
        trio[COLS : COLS + cells, :],
        trio[2 * COLS : 2 * COLS + cells, :] * lower,
    )
    tap = lambda k: nt(shifted[k // 3][:, k % 3 * c : (k % 3 + 1) * c], weight[(8 - k) * c : (9 - k) * c, :])
    d_one[0] = sum((tap(k) for k in range(1, 9)), tap(0))
    join_pre_one(own, spill, joined, c)
    slope_sums(d_one, joined, tot1, m, count, g1, b1, mask, out_total)


def k_back_one(count, d_one, own, spill, tot1, back1, g1, mask, d_pre, joined):
    m = pl.program_id(0)
    join_pre_one(own, spill, joined, d_one.shape[2])
    norm_back(d_pre, d_one, joined, tot1, back1, m, count, g1, mask)


def k_input(d_pre, more_pre, d_summed, weight, *refs):
    more_summed, (out, both, sums) = refs[:-3], refs[-3:]
    m = pl.program_id(0)
    spilled, cells = more_pre.shape[1], both.shape[0]
    blocks = sums.shape[1] // LANES
    own = cells // COLS
    across = out.shape[1] // blocks // own
    both[...] = d_pre[0, 0:cells, :]
    both[0:spilled, :] = d_pre[0, 0:spilled, :] + more_pre[0]
    sums[...] = nt(both[...], weight[...])
    for r in range(own):
        at = r * COLS
        value = sums[at : at + COLS, :] + d_summed[0, at : at + COLS, :].astype(F32)
        if at < spilled:
            extra = more_summed[0][at : at + COLS, :].astype(F32)
            for k in range(1, len(more_summed)):
                extra = jnp.where(m == k, more_summed[k][at : at + COLS, :].astype(F32), extra)
            value = value + extra
        for j in range(blocks):
            rows = pl.ds(r * across * blocks + j, across, stride=blocks)
            out[0, rows, :] = value[:across, j * LANES : (j + 1) * LANES]


def exchange(x, mask):
    total = lax.axis_size("rows") * lax.axis_size("batch")
    return lax.ppermute(x, AXES, [(i, i ^ mask) for i in range(total)])


def from_behind(x, by):
    devices = lax.axis_size("rows")
    pairs = [(i, i + by) for i in range(devices) if 0 <= i + by < devices]
    return lax.ppermute(x, "rows", pairs)


class Chain:
    def __init__(self, steps):
        self.steps, self.flying, self.done, self.result = steps, None, False, None
        self.ready = next(steps)

    def launch(self, array):
        self.flying = self.ready[1](array)

    def land(self):
        try:
            self.ready = self.steps.send(self.flying)
        except StopIteration as end:
            self.done, self.result = True, end.value
        self.flying = None

    def value(self):
        while not self.done:
            if self.flying is None:
                self.launch(self.ready[0])
            self.land()
        return self.result


def hook(x, start=(), finish=(), need=()):
    if not (start or finish or need):
        return x
    landed = []
    for chain in finish:
        if not chain.done:
            landed.append(chain.flying)
            chain.land()
    live = [chain for chain in start if not chain.done]
    tied = lax.optimization_barrier((x, [c.ready[0] for c in live], landed, list(need)))
    for chain, array in zip(live, tied[1]):
        chain.launch(array)
    return tied[0]


def global_sum(x, b=None, c=None, d=None):
    bits = device_bits()
    split = x.shape[1] >= 2048
    if split:
        half = x.shape[1] // 2
        part = lambda bit: lax.dynamic_slice_in_dim(x, bit * half, half, 1)
        x = part(my_bit(0)) + exchange(part(1 - my_bit(0)), 1)
    else:
        x = x + exchange(x, 1)
    x = hook(x, **(b or {}))
    step = 1
    while step < bits:
        low = 1 << step
        if step + 1 < bits:
            p, q, r = exchange(x, low), exchange(x, 2 * low), exchange(x, 3 * low)
            x = (x + p) + (q + r)
        else:
            x = x + exchange(x, low)
        if step == 1:
            x = hook(x, **(c or {}))
        step += 2
    if split:
        other = exchange(x, 1)
        upper = my_bit(0) == 1
        x = jnp.concatenate([jnp.where(upper, other, x), jnp.where(upper, x, other)], 1)
    return hook(x, **(d or {}))


def device_bits():
    total = lax.axis_size("rows") * lax.axis_size("batch")
    return total.bit_length() - 1


def my_bit(bit):
    number = lax.axis_index("rows") * lax.axis_size("batch") + lax.axis_index("batch")
    return (number >> bit) & 1


def batch_bits():
    return lax.axis_size("batch").bit_length() - 1


def across(bit):
    return lambda x: exchange(x, 1 << bit)


def lanes_of(w, parts):
    x = w.reshape(parts, -1, w.shape[1] // 256, 256)
    return x.transpose(0, 2, 1, 3).reshape(parts, -1, 256)


def from_lanes(x, c):
    parts = x.shape[0]
    x = x.reshape(parts, c // 256, -1, 256)
    return x.transpose(0, 2, 1, 3).reshape(-1, c)


def ordered(mine, other, bit, axis):
    upper = my_bit(bit) == 1
    return jnp.stack([jnp.where(upper, other, mine), jnp.where(upper, mine, other)], axis)


def gather_steps(packed, parts):
    bits, low = device_bits(), batch_bits()
    number = my_bit(0) if parts == 1 else lax.axis_index("batch")
    x = lax.dynamic_index_in_dim(packed, number, 0, keepdims=False)
    for bit in list(reversed(range(low, bits))) + list(reversed(range(parts))):
        got = yield x, across(bit)
        x = ordered(x, got, bit, x.ndim - 2)
    return x.reshape((-1,) + x.shape[-2:])


def gather_offloaded(ws):
    quarters, wide = lax.axis_size("batch"), ws[0].shape[1]
    packed = jnp.concatenate([w.reshape(quarters, -1, wide) for w in ws], 1)
    part = lax.dynamic_index_in_dim(packed, lax.axis_index("batch"), 0, keepdims=False)
    whole = lax.all_gather(part, AXES, axis=0)
    out, at = [], 0
    for w in ws:
        n = w.shape[0] // quarters
        if n % 16 == 0 and at % n == 0:
            block = at // n
            spec = pl.BlockSpec(
                (whole.shape[0], n, wide), lambda m, k=block: (0, k, 0), pipeline_mode=pl.Buffered(1)
            )
            out.append((whole, spec))
        else:
            part = whole[:, at : at + n].reshape(-1, wide)
            out.append((part, pl.BlockSpec(part.shape, lambda m: (0, 0), pipeline_mode=pl.Buffered(1))))
        at += n
    return out


def sharded(grad, c):
    total = lax.axis_size("rows") * lax.axis_size("batch")
    if grad.shape[1] == c:
        return grad.reshape(total, -1, c)
    return lanes_of(grad, total)


def spread_steps(x):
    for bit in reversed(range(batch_bits())):
        got = yield x, across(bit)
        x = ordered(x, got, bit, x.ndim - 2)
    return x.reshape((-1,) + x.shape[-2:])


def reduce_steps(parts):
    bits = device_bits()
    x = jnp.concatenate(parts, 1) if len(parts) > 1 else parts[0]
    x = x.reshape((2,) * bits + x.shape[1:])
    left = list(reversed(range(bits)))
    got = None
    for bit in range(bits):
        axis = left.index(bit)
        left.remove(bit)
        half = lambda v, b: lax.dynamic_index_in_dim(v, b, axis, keepdims=False)
        keep, send = my_bit(bit), 1 - my_bit(bit)
        if got is None:
            x, give = half(x, keep), half(x, send)
        else:
            x, give = half(x, keep) + half(got, keep), half(x, send) + half(got, send)
        got = yield give, across(bit)
    return (yield from spread_steps(x + got))


def reduce_first(part):
    bits, low = device_bits(), batch_bits()
    x = part.reshape((2,) * bits + part.shape[1:])
    left = list(reversed(range(bits)))
    got = None
    for bit in [0] + list(range(low, bits - 1)):
        axis = left.index(bit)
        left.remove(bit)
        half = lambda v, b: lax.dynamic_index_in_dim(v, b, axis, keepdims=False)
        keep, send = my_bit(bit), 1 - my_bit(bit)
        if got is None:
            x, give = half(x, keep), half(x, send)
        else:
            x, give = half(x, keep) + half(got, keep), half(x, send) + half(got, send)
        got = yield give, across(bit)
    return x + got


def reduce_last(x):
    low, last = batch_bits(), device_bits() - 1
    bit = my_bit(last)
    half = lambda b: lax.dynamic_index_in_dim(x, b, 0, keepdims=False)
    got = yield half(1 - bit), across(last)
    x = half(bit) + got
    for b in range(1, low):
        got = yield x, across(b)
        x = x + got
    got = yield x, across(0)
    x = ordered(x, got, 0, x.ndim - 2)
    return x.reshape((-1,) + x.shape[-2:])


def one_step(x, send):
    return (yield x, send)


def unpack(shard, shapes):
    devices = lax.axis_size("rows")
    out, at = [], 0
    for k, c in shapes:
        n = k * c // devices // shard.shape[0] // shard.shape[2]
        part = shard[:, at : at + n]
        out.append((from_lanes(part, c) if shard.shape[2] != c else part.reshape(-1, c)).astype(F32))
        at += n
    return out


LIMIT = 26


def per_micro(shape):
    zeros = (0,) * (len(shape) - 1)
    return pl.BlockSpec((1,) + tuple(shape[1:]), lambda m: (m,) + zeros)


def whole(shape):
    zeros = (0,) * len(shape)
    return pl.BlockSpec(tuple(shape), lambda m: zeros, pipeline_mode=pl.Buffered(1))


def table(shape):
    zeros = (0,) * len(shape)
    return pl.BlockSpec(tuple(shape), lambda m: zeros)


def call(kernel, micro, ins, outs, scratch=(), limit=LIMIT, after=()):
    kind = {"m": per_micro, "w": whole, "s": lambda shape: pl.BlockSpec(memory_space=pltpu.SMEM)}
    in_specs = [k if isinstance(k, pl.BlockSpec) else kind[k](a.shape) for a, k in ins]
    in_specs += [pl.BlockSpec(memory_space=pl.ANY)] * len(after)
    out_specs = [per_micro(sh) if k == "m" else table(sh) for sh, _, k in outs]

    def run(*refs):
        kernel(*refs[: len(ins)], *refs[len(ins) + len(after) :])

    return pl.pallas_call(
        run,
        grid=(micro,),
        in_specs=in_specs,
        out_specs=out_specs,
        out_shape=[jax.ShapeDtypeStruct(sh, t) for sh, t, _ in outs],
        scratch_shapes=[pltpu.VMEM(sh, t) for sh, t in scratch],
        compiler_params=pltpu.CompilerParams(
            dimension_semantics=("arbitrary",), vmem_limit_bytes=limit * 1024 * 1024
        ),
        name=getattr(kernel, "func", kernel).__name__,
    )(*[a for a, _ in ins], *after)


def weight_term(left, right):
    k, n = left.shape[-1], right.shape[-1]
    return lax.dot_general(
        left.reshape(-1, k), right.reshape(-1, n), (((0,), (0,)), ((), ())), preferred_element_type=F32
    ).astype(BF)


def shards(
    features, view_kind, narrow_one, spatial_one, expand_one, gains_one, biases_one,
    narrow_two, spatial_two, expand_two, shortcut, gains_two, biases_two, cotangent,
):
    micro, _, own, across, channels = features.shape
    m1 = spatial_one.shape[1]
    m2 = spatial_two.shape[1]
    outward = shortcut.shape[1]
    sources = lax.axis_size("rows") * own // 52
    full_count = float(lax.axis_size("batch") * sources * 536)
    half_count = float(lax.axis_size("batch") * sources * 134)
    anchor = lax.axis_index("rows") * own
    cells, half = WIN * COLS, WIN * COLS // 4
    mine, more = own * COLS, SPILL * COLS

    chain_n1 = Chain(gather_steps(narrow_one.reshape(2, -1, m1), 1))
    pack_a = [lanes_of(w, 4) for w in (spatial_one, expand_one)]
    chain_a = Chain(gather_steps(jnp.concatenate(pack_a, 1), 2))
    spatial_b, narrow_b = gather_offloaded([spatial_two, narrow_two])
    bypass, expand_b = gather_offloaded([shortcut, expand_two])
    chain_f = [
        Chain(one_step(features[k, 0, :SPILL], lambda x: from_behind(x, -1))) for k in range(micro)
    ]
    g1, g2, g3 = (v[None] for v in jnp.split(gains_one, [m1, 2 * m1]))
    b1, b2, b3 = (v[None] for v in jnp.split(biases_one, [m1, 2 * m1]))
    cuts = [m2, 2 * m2, 2 * m2 + outward]
    g4, g5, g6, g7 = (v[None] for v in jnp.split(gains_two, cuts))
    b4, b5, b6, b7 = (v[None] for v in jnp.split(biases_two, cuts))
    mask, half_mask, flags, inner = pl.pallas_call(
        functools.partial(k_masks, own),
        in_specs=[pl.BlockSpec(memory_space=pltpu.SMEM)] * 2,
        out_shape=[
            jax.ShapeDtypeStruct((micro, cells, LANES), F32),
            jax.ShapeDtypeStruct((micro, half, LANES), F32),
        ]
        * 2,
        name="k_masks",
    )(anchor[None].astype(jnp.int32), view_kind)

    full_table = lambda c: ((8, c), F32, "t")
    per = lambda c, t=F32, n=cells: ((micro, n, c), t, "m")

    for chain in (chain_n1, chain_a):
        chain.launch(chain.ready[0])
    chain_n1.land()
    before = [mask]
    while not chain_n1.done:
        chain_n1.launch(lax.optimization_barrier((chain_n1.ready[0], before))[0])
        landed = chain_n1.flying
        chain_n1.land()
        if chain_a.flying is not None and len(before) < 3 and not chain_n1.done:
            chain_a.land()
            chain_a.launch(lax.optimization_barrier((chain_a.ready[0], landed))[0])
            before = before + [landed]
            if len(before) == 3:
                hook(landed, start=chain_f[2:])
    narrow_a = chain_n1.value().reshape(-1, m1)
    pre_one, head, t1 = call(
        k_first, micro, [(features, "m"), (flags, "m"), (narrow_a, "w")],
        [per(m1, F32, mine), per(m1, BF, more), full_table(m1)], [((mine, channels), BF)],
    )
    chain_h = Chain(one_step(head, lambda x: from_behind(x, -1)))
    t1 = global_sum(
        t1,
        b=dict(finish=[chain_a]),
        c=dict(start=[chain_a, chain_h]),
        d=dict(finish=[chain_a, chain_h], start=[chain_a] + chain_f[:1]),
    )
    pre_spill = chain_h.value()
    total_a = chain_a.value()
    spatial_a = total_a[:, : pack_a[0].shape[1]].reshape(-1, m1)
    expand_a = from_lanes(total_a[:, pack_a[0].shape[1] :], channels)
    pre_two, patch_one, t2 = call(
        functools.partial(k_second, full_count), micro,
        [(pre_one, "m"), (pre_spill, "m"), (t1, "w"), (g1, "w"), (b1, "w"), (mask, "m"),
         (flags, "m"), (spatial_a, "w")],
        [per(m1), per(9 * m1, BF), full_table(m1)],
        [((cells + 2 * COLS, m1), F32), ((cells + 2 * COLS, 3 * m1), BF), ((1, cells, m1), F32)],
    )
    t2 = global_sum(t2, b=dict(finish=chain_f[:1]), d=dict(start=chain_f[1:2]))
    act_two, pre_three, t3 = call(
        functools.partial(k_third, full_count), micro,
        [(pre_two, "m"), (t2, "w"), (g2, "w"), (b2, "w"), (mask, "m"), (expand_a, "w")],
        [per(m1, BF), per(channels, BF), full_table(channels)],
    )
    t3 = global_sum(t3, b=dict(finish=chain_f[1:]))
    (entry,) = call(
        k_entry, micro,
        [(features, "m"), (mask, "m")] + [(f.value(), "w") for f in chain_f],
        [per(channels, BF)], [((cells, channels), BF)],
    )
    block_out, corner, pre_four, t4 = call(
        functools.partial(k_fourth, full_count), micro,
        [(pre_three, "m"), (entry, "m"), (t3, "w"), (g3, "w"), (b3, "w"), (mask, "m"), narrow_b],
        [per(channels, BF), per(channels, BF, half), per(m2, BF), full_table(m2)],
        [((channels // LANES, 4 * COLS, LANES), F32)],
    )
    t4 = global_sum(t4)
    pre_five, patch_two, t5 = call(
        functools.partial(k_fifth, full_count), micro,
        [(pre_four, "m"), (t4, "w"), (g4, "w"), (b4, "w"), (mask, "m"), (half_mask, "m"), (inner, "m"),
         spatial_b],
        [per(m2, F32, half), per(9 * m2, BF, half), full_table(m2)],
        [((m2 // LANES, cells, LANES), F32)] + [((half + COLS, m2), F32)] * 3,
    )
    t5 = global_sum(t5)
    act_five, pre_six, t6 = call(
        functools.partial(k_third, half_count), micro,
        [(pre_five, "m"), (t5, "w"), (g5, "w"), (b5, "w"), (half_mask, "m"), expand_b],
        [per(m2, BF, half), per(outward, BF, half), full_table(outward)],
    )
    tile = outward // 4
    by_tile = bypass[1].block_shape[:-1] + (tile,)
    pre_seven, t7 = pl.pallas_call(
        k_seventh,
        grid=(4, micro),
        in_specs=[
            pl.BlockSpec((1, half, channels), lambda n, m: (m, 0, 0)),
            pl.BlockSpec(by_tile, lambda n, m: (0,) * (len(by_tile) - 1) + (n,)),
        ],
        out_specs=[
            pl.BlockSpec((1, half, tile), lambda n, m: (m, 0, n)),
            pl.BlockSpec((8, tile), lambda n, m: (0, n)),
        ],
        out_shape=[
            jax.ShapeDtypeStruct((micro, half, outward), BF),
            jax.ShapeDtypeStruct((8, outward), F32),
        ],
        compiler_params=pltpu.CompilerParams(vmem_limit_bytes=LIMIT * 1024 * 1024),
    )(corner, bypass[0])
    t67 = global_sum(jnp.concatenate([t6, t7], 1))
    t6, t7 = t67[:, :outward], t67[:, outward:]
    outputs, slope, u67 = call(
        functools.partial(k_last, half_count), micro,
        [(pre_six, "m"), (pre_seven, "m"), (t6, "w"), (t7, "w"), (g6, "w"), (b6, "w"), (g7, "w"), (b7, "w"),
         (half_mask, "m"), (cotangent, "m")],
        [(cotangent.shape, BF, "m"), per(outward, BF, half), full_table(2 * outward)],
        [((COLS, outward), F32)],
    )
    u67 = global_sum(u67)
    d_six, d_seven, d_five, u5 = call(
        functools.partial(k_back_six, half_count), micro,
        [(slope, "m"), (pre_six, "m"), (pre_seven, "m"), (t6, "w"), (t7, "w"), (u67, "w"), (g6, "w"), (g7, "w"),
         (pre_five, "m"), (t5, "w"), (g5, "w"), (b5, "w"), (half_mask, "m"), expand_b],
        [per(outward, BF, half), per(outward, BF, half), per(m2, F32, half), full_table(m2)],
    )
    (d_corner,) = call(
        k_corner, micro, [(d_seven, "m"), bypass], [per(channels, BF, half)]
    )
    grad_e2 = weight_term(act_five, d_six)
    grad_sc = weight_term(corner, d_seven)
    pack_b = jnp.concatenate([sharded(grad_sc, outward), sharded(grad_e2, outward)], 1).reshape(-1, outward)
    u5 = global_sum(u5, c=dict(need=[pack_b]))
    part_b = lax.psum_scatter(pack_b, AXES, scatter_dimension=0, tiled=True)
    d_pre_five, d_four, u4 = call(
        functools.partial(k_back_five, half_count, full_count), micro,
        [(d_five, "m"), (pre_five, "m"), (t5, "w"), (u5, "w"), (g5, "w"), (half_mask, "m"), (inner, "m"),
         spatial_b, (pre_four, "m"), (t4, "w"), (g4, "w"), (b4, "w"), (mask, "m")],
        [per(m2, BF, half), per(m2), full_table(m2)],
        [((m2 // LANES, cells, LANES), F32), ((half + COLS, m2), F32)],
    )
    chain_rs = Chain(reduce_steps([sharded(weight_term(patch_two, d_pre_five), m2)]))
    u4 = global_sum(u4, b=dict(start=[chain_rs]), c=dict(finish=[chain_rs], start=[chain_rs]))
    d_pre_four, d_summed, u3 = call(
        functools.partial(k_back_four, full_count), micro,
        [(d_four, "m"), (pre_four, "m"), (t4, "w"), (u4, "w"), (g4, "w"), (mask, "m"), narrow_b,
         (d_corner, "m"), (pre_three, "m"), (entry, "m"), (t3, "w"), (g3, "w"), (b3, "w")],
        [per(m2, BF), per(channels, BF), full_table(channels)],
        [((channels // LANES, 4 * COLS, LANES), F32), ((1, cells, channels), F32)],
    )
    grad_n2 = [
        sharded(weight_term(block_out, d_pre_four[..., k : k + 256]), 256) for k in range(0, m2, 256)
    ]
    spilled = d_summed[:, mine : mine + more]
    chain_ds = [Chain(one_step(spilled[k], lambda x: from_behind(x, 1))) for k in range(micro)]
    chain_r2 = Chain(reduce_first(jnp.concatenate(grad_n2, 1)))
    u3 = global_sum(
        u3,
        b=dict(finish=[chain_rs], start=[chain_r2]),
        c=dict(finish=[chain_r2], start=[chain_rs, chain_r2]),
        d=dict(finish=[chain_r2], start=[chain_r2, chain_ds[0]]),
    )
    d_pre_three, d_two, u2 = call(
        functools.partial(k_back_three, full_count), micro,
        [(d_summed, "m"), (pre_three, "m"), (t3, "w"), (u3, "w"), (g3, "w"), (mask, "m"), (expand_a, "w"),
         (pre_two, "m"), (t2, "w"), (g2, "w"), (b2, "w")],
        [per(channels, BF), per(m1), full_table(m1)],
    )
    grad_e1 = weight_term(act_two, d_pre_three)
    chain_r3 = Chain(reduce_first(sharded(grad_e1, 256)))
    u2 = global_sum(
        u2,
        b=dict(finish=[chain_rs, chain_r2, chain_ds[0]], start=[chain_r3]),
        c=dict(finish=[chain_r3], start=[chain_r3]),
        d=dict(finish=[chain_r3], start=[chain_rs, chain_r3] + chain_ds[1:2]),
    )
    d_pre_two, d_one, u1 = call(
        functools.partial(k_back_two, full_count), micro,
        [(d_two, "m"), (pre_two, "m"), (t2, "w"), (u2, "w"), (g2, "w"), (mask, "m"), (flags, "m"),
         (spatial_a, "w"), (pre_one, "m"), (pre_spill, "m"), (t1, "w"), (g1, "w"), (b1, "w")],
        [per(m1, BF), per(m1), full_table(m1)],
        [((cells + 2 * COLS, m1), F32), ((cells + 2 * COLS, 3 * m1), BF), ((1, cells, m1), F32)],
    )
    grad_s1 = weight_term(patch_one, d_pre_two)
    chain_r1 = Chain(reduce_first(sharded(grad_s1, 256)))
    u1 = global_sum(
        u1,
        b=dict(finish=[chain_r3] + chain_ds[1:2], start=[chain_r1]),
        c=dict(finish=[chain_r1, chain_rs], start=[chain_r1]),
        d=dict(finish=[chain_r1], start=[chain_r1, chain_rs]),
    )
    (d_pre_one,) = call(
        functools.partial(k_back_one, full_count), micro,
        [(d_one, "m"), (pre_one, "m"), (pre_spill, "m"), (t1, "w"), (u1, "w"), (g1, "w"), (mask, "m")],
        [per(m1, BF)], [((1, cells, m1), F32)],
    )
    chain_rn = Chain(reduce_first(sharded(weight_term(entry, d_pre_one), 256)))
    firsts = [c.value() for c in (chain_rn, chain_r1, chain_r2, chain_r3)]
    chain_last = Chain(reduce_last(jnp.concatenate(firsts, -2)))
    d_more = lax.optimization_barrier((d_pre_one[:, mine : mine + more], firsts[0]))[0]
    chain_dp = Chain(one_step(d_more, lambda x: from_behind(x, 1)))
    out_n1, out_s1, out_n2, out_e1 = unpack(
        chain_last.value(), [(channels, m1), (9 * m1, m1), (channels, m2), (m1, channels)]
    )
    (out_s2,) = unpack(chain_rs.value(), [(9 * m2, m2)])
    out_sc, out_e2 = unpack(Chain(spread_steps(part_b)).value(), [(channels, outward), (m2, outward)])
    (grad_input,) = call(
        k_input, micro,
        [(d_pre_one, "m"), (chain_dp.value(), "m"), (d_summed, "m"), (narrow_a, "w")]
        + [(c.value(), "w") for c in chain_ds],
        [((micro, own * across * channels // LANES, LANES), F32, "m")],
        [((mine, m1), BF), ((mine, channels), F32)],
    )
    grad_input = grad_input.reshape(features.shape)
    added = lambda k, us: jnp.concatenate([u[k] + u[k + 2] + u[k + 4] for u in us])
    first = (u1, u2, u3)
    later = (u4, u5, u67)
    return (
        outputs, grad_input, out_n1, out_s1, out_e1,
        added(1, first), added(0, first),
        out_n2, out_s2, out_e2, out_sc,
        added(1, later), added(0, later),
    )


def solution(mesh):
    wide = P(None, "batch", "rows", None, None)
    shard = P("rows", None)
    return jax.shard_map(
        shards,
        mesh=mesh,
        in_specs=(
            wide, P(None, "batch", None), shard, shard, shard, P(), P(),
            shard, shard, shard, shard, P(), P(), wide,
        ),
        out_specs=(
            wide, wide, shard, shard, shard, P(), P(),
            shard, shard, shard, shard, P(), P(),
        ),
        check_vma=False,
    )
```

time: 677 us -> 545 us (0.81)
  waiting for transfers between devices: 152 us -> 116 us
  Pallas kernels: 139 us -> 106 us
  local copies, waits for them, and re-layouts: 82.6 us -> 54 us
  starting transfers between devices: 231 us -> 208 us
    pallas_call x16, Pallas kernels: 130 us -> 95.9 us  [call(): pl.pallas_call(run, grid=(micro,), in_specs=in_specs, out_specs=out_specs...]
    ppermute x150 -> x119, waiting for transfers between devices: 120 us -> 96.1 us  [exchange(): return lax.ppermute(x, AXES, [(i, i ^ mask) for i in range(total)])]
    unnamed x243 -> x188, local copies, waits for them, and re-layouts: 59.4 us -> 41.5 us
    ppermute x8, waiting for transfers between devices: 32 us -> 19.4 us  [from_behind(): return lax.ppermute(x, 'rows', pairs)]
    ppermute x150 -> x119, starting transfers between devices: 198 us -> 186 us  [exchange(): return lax.ppermute(x, AXES, [(i, i ^ mask) for i in range(total)])]
    ppermute x7 -> x0, starting transfers between devices: 9.24 us -> none  [gather_pieces(): lax.ppermute(half, 'rows', [(i, i ^ k) for i in range(devices)])]
    dot_general x7 -> x8, matrix products: 22.5 us -> 16.9 us  [weight_term(): lax.dot_general(left.reshape(-1, k), right.reshape(-1, n), (((0,), (0,)),...]
  transfers between devices with their start and end apart: 168 -> 130, of which waited for: 72 -> 67; matrix products, arithmetic and copies ran while one was open for 10% -> 9% of each run, Pallas kernels for 17% -> 13%
where the time goes in v2:
time: 545 us; the launch traced here: 539 us
  starting transfers between devices  208 us (38%)
  waiting for transfers between devices  116 us (21%)
  Pallas kernels  106 us (19%)
  local copies, waits for them, and re-layouts  54 us (10%)
  other arithmetic  22.6 us (4%)
  matrix products  16.9 us (3%)
  between operations  16 us (3%)
    ppermute x119, starting transfers between devices, exchange(): return lax.ppermute(x, AXES, [(i, i ^ mask) for i in range(total)])  186 us
    ppermute x119, waiting for transfers between devices, exchange(): return lax.ppermute(x, AXES, [(i, i ^ mask) for i in range(total)])  96.1 us
    pallas_call x16, Pallas kernels, call(): pl.pallas_call(run, grid=(micro,), in_specs=in_specs, out_specs=out_specs...  95.9 us
    unnamed x188, local copies, waits for them, and re-layouts  41.5 us
    ppermute x8, starting transfers between devices, from_behind(): return lax.ppermute(x, 'rows', pairs)  21.2 us
    ppermute x8, waiting for transfers between devices, from_behind(): return lax.ppermute(x, 'rows', pairs)  19.4 us
    dot_general x8, matrix products, weight_term(): lax.dot_general(left.reshape(-1, k), right.reshape(-1, n), (((0,), (0,)),...  16.9 us
  transfers between devices with their start and end apart: 130, of which 67 were waited for; matrix products, arithmetic and copies ran while one was open for 9% of the time, Pallas kernels for 13%

profile of v2, /device:TPU:25, one launch (start us, length us, event | category | flops | bytes accessed | tf_op | source)
XLA Modules:
  0.0 538.5 jit_solution(9260597065565482761)
XLA Ops:
  11.5 3.4 k_masks.1
  23.2 3.6 collective-permute-start.3
  31.2 5.3 collective-permute-start.4
  49.7 5.5 %collective-permute-done.15 = bf16[2,2,2,104,256]{4,3,2,1,0:T(8,128)(2,1)} collective-permute-done((bf16[2,2,2,104,256]{4,3,2,1,0:T(8,128)(2,1)}, bf16[2,2,2,104,256]{4,3,2,1,0:T(8,128)(2,1)}, u32[]{:S(2)}, u32[]{:S(2)}) %collective-permute-start.15) | collective-permute-done | bytes 426016 | tf_op jit(solution)/shard_map/ppermute | solution.py:589
  56.4 3.8 collective-permute-start.16
  61.7 2.7 collective-permute-start.18
  67.0 5.6 %k_second.1 = (f32[3,640,256]{2,1,0:T(8,128)S(1)}, bf16[3,640,2304]{2,1,0:T(8,128)(2,1)S(1)}, f32[8,256]{1,0:T(8,128)S(1)}) custom-call(f32[3,416,256]{2,1,0:T(8,128)S(1)} %copy-done.18, bf16[3,192,256]{2,1,0:T(8,128)(2,1)S(1)} %collective-permute-done.11.refs_1_.refs_9_.refs_2_, f32[8,256]{1,0:T(8,128)S(1)} %add_add_fusion.22.refs_2_.refs_10_.refs_3_, ...), custom_call_target="tpu_custom_call" | custom-call | tf_op jit(solution)/shard_map/k_second/pallas_call | solution.py:836
  72.6 3.5 copy-done.67
  78.7 2.3 collective-permute-start.20
  83.6 8.5 %collective-permute-start.24 = (f32[8,256]{1,0:T(8,128)S(1)}, f32[8,256]{1,0:T(8,128)S(1)}, u32[]{:S(2)}, u32[]{:S(2)}) collective-permute-start(f32[8,256]{1,0:T(8,128)S(1)} %add_add_fusion.21), channel_id=1, source_target_pairs={{0,24},{1,25},{2,26},{3,27},{4,28},{5,29},{6,30},{7,31},{8,16},{9,... | collective-permute-start | bytes 24584 | tf_op jit(solution)/shard_map/ppermute | solution.py:589
  92.5 4.4 collective-permute-start.26
  99.3 6.0 %k_third.2 = (bf16[3,640,256]{2,1,0:T(8,128)(2,1)S(1)}, bf16[3,640,1024]{2,1,0:T(8,128)(2,1)S(1)}, f32[8,1024]{1,0:T(8,128)S(1)}) custom-call(f32[3,640,256]{2,1,0:T(8,128)S(1)} %get-tuple-element.119.refs_0_.refs_7_.refs_1_, f32[8,256]{1,0:T(8,128)S(1)} %add_add_fusion.20.refs_1_.refs_8_.refs_2_, f32[1,256]{1,0:T(1,128)S(1)} %bitcast.403, ...), custom_call_target="tpu_custom_call" | custom-call | tf_op jit(solution)/shard_map/k_third/pallas_call | solution.py:836
  108.2 3.3 collective-permute-start.27
  112.4 5.4 %collective-permute-done.25.refs_3_ = bf16[12,14,1024]{2,1,0:T(8,128)(2,1)S(1)} collective-permute-done((bf16[12,14,1024]{2,1,0:T(8,128)(2,1)S(1)}, bf16[12,14,1024]{2,1,0:T(8,128)(2,1)S(1)}, u32[]{:S(2)}, u32[]{:S(2)}) %collective-permute-start.25) | collective-permute-done | bytes 344096 | tf_op jit(solution)/shard_map/ppermute | solution.py:595
  123.2 2.9 collective-permute-start.33
  132.2 2.5 copy-done.5
  134.7 3.0 copy-done.8
  139.0 9.4 %k_fourth.1 = (bf16[3,640,1024]{2,1,0:T(8,128)(2,1)S(1)}, bf16[3,160,1024]{2,1,0:T(8,128)(2,1)S(1)}, bf16[3,640,512]{2,1,0:T(8,128)(2,1)S(1)}, f32[8,512]{1,0:T(8,128)S(1)}) custom-call(bf16[3,640,1024]{2,1,0:T(8,128)(2,1)S(1)} %copy-done.8, bf16[3,640,1024]{2,1,0:T(8,128)(2,1)S(1)} %copy-done.5, f32[8,1024]{1,0:T(8,128)S(1)} %add_add_fusion.6.refs_2_.refs_10_, ...), custom_call_target="tpu_custom_call" | custom-call | tf_op jit(solution)/shard_map/k_fourth/pallas_call | solution.py:836
  149.4 9.0 %collective-permute-start.34 = (f32[8,512]{1,0:T(8,128)S(1)}, f32[8,512]{1,0:T(8,128)S(1)}, u32[]{:S(2)}, u32[]{:S(2)}) collective-permute-start(f32[8,512]{1,0:T(8,128)S(1)} %get-tuple-element.130), channel_id=1, source_target_pairs={{0,1},{1,0},{2,3},{3,2},{4,5},{5,4},{6,7},{7,6},{8,9},{9,8},{10,11... | collective-permute-start | bytes 49160 | tf_op jit(solution)/shard_map/ppermute | solution.py:589
  169.2 6.5 %k_fifth.1 = (f32[3,160,512]{2,1,0:T(8,128)S(1)}, bf16[3,160,4608]{2,1,0:T(8,128)(2,1)S(1)}, f32[8,512]{1,0:T(8,128)S(1)}) custom-call(bf16[3,640,512]{2,1,0:T(8,128)(2,1)S(1)} %get-tuple-element.129.refs_0_.refs_8_.refs_1_, f32[8,512]{1,0:T(8,128)S(1)} %add_add_fusion.14.refs_1_.refs_9_.refs_2_, f32[1,512]{1,0:T(1,128)S(1)} %bitcast.393, ...), custom_call_target="tpu_custom_call" | custom-call | tf_op jit(solution)/shard_map/k_fifth/pallas_call | solution.py:836
  175.7 3.2 collective-permute-start.41
  179.8 2.4 collective-permute-start.44
  190.2 2.8 copy-done
  193.0 4.1 k_third.3
  197.9 6.4 %shard_map.237 = (bf16[3,160,2048]{2,1,0:T(8,128)(2,1)S(1)}, f32[8,2048]{1,0:T(8,128)S(1)}) custom-call(bf16[3,160,1024]{2,1,0:T(8,128)(2,1)S(1)} %copy-done.47, bf16[32,48,2048]{2,1,0:T(8,128)(2,1)S(1)} %copy-done.1), custom_call_target="tpu_custom_call" | custom-call | tf_op jit(solution)/shard_map/pallas_call | solution.py:970
  206.3 3.9 collective-permute-start.48
  223.4 3.8 collective-permute-done.53
  233.8 8.2 %k_last.1 = (bf16[3,1,19,7,2048]{4,3,2,1,0:T(8,128)(2,1)}, bf16[3,160,2048]{2,1,0:T(8,128)(2,1)S(1)}, f32[8,4096]{1,0:T(8,128)S(1)}) custom-call(bf16[3,160,2048]{2,1,0:T(8,128)(2,1)S(1)} %copy-done.31, bf16[3,160,2048]{2,1,0:T(8,128)(2,1)S(1)} %copy-done.33, f32[8,2048]{1,0:T(8,128)S(1)} %get-tuple-element.303.refs_2_.refs_3_, ...), custom_call_target="tpu_custom_call" | custom-call | tf_op jit(solution)/shard_map/k_last/pallas_call | solution.py:836
  254.7 3.4 collective-permute-done.61
  259.9 7.4 %k_back_six.1 = (bf16[3,160,2048]{2,1,0:T(8,128)(2,1)S(1)}, bf16[3,160,2048]{2,1,0:T(8,128)(2,1)S(1)}, f32[3,160,512]{2,1,0:T(8,128)S(1)}, f32[8,512]{1,0:T(8,128)S(1)}) custom-call(bf16[3,160,2048]{2,1,0:T(8,128)(2,1)S(1)} %get-tuple-element.141.refs_0_, bf16[3,160,2048]{2,1,0:T(8,128)(2,1)S(1)} %copy-done.31, bf16[3,160,2048]{2,1,0:T(8,128)(2,1)S(1)} %copy-done.33, ...), custom_call_target="tpu_custom_call" | custom-call | tf_op jit(solution)/shard_map/k_back_six/pallas_call | solution.py:836
  267.8 2.4 bitcast_convert_fusion.1
  274.3 3.5 pad_maximum_fusion
  282.8 2.6 copy-done.11
  288.8 10.1 %k_back_five.1 = (bf16[3,160,512]{2,1,0:T(8,128)(2,1)S(1)}, f32[3,640,512]{2,1,0:T(8,128)S(1)}, f32[8,512]{1,0:T(8,128)S(1)}) custom-call(f32[3,160,512]{2,1,0:T(8,128)S(1)} %copy-done.52, f32[3,160,512]{2,1,0:T(8,128)S(1)} %copy-done.26, f32[8,512]{1,0:T(8,128)S(1)} %add_add_fusion.12.refs_1_.refs_9_.refs_2_, f32[8,512]{1,0:T(8,128)S(1)} %add_add_fusion.10.refs_3_, ...), custom_call_target="tpu_custom_call" | custom-call | tf_op jit(solution)/shard_map/k_back_five/pallas_call | solution.py:836
  298.9 2.5 collective-permute-start.71
  301.4 5.3 bitcast_convert_fusion
  313.7 2.8 copy-done.2
  318.0 4.9 k_corner.1.refs_7_
  323.0 2.9 bitcast_add_fusion
  331.8 13.2 %k_back_four.1 = (bf16[3,640,512]{2,1,0:T(8,128)(2,1)S(1)}, bf16[3,640,1024]{2,1,0:T(8,128)(2,1)S(1)}, f32[8,1024]{1,0:T(8,128)S(1)}) custom-call(f32[3,640,512]{2,1,0:T(8,128)S(1)} %copy-done.40, bf16[3,640,512]{2,1,0:T(8,128)(2,1)S(1)} %copy-done.15, f32[8,512]{1,0:T(8,128)S(1)} %add_add_fusion.14.refs_1_.refs_9_.refs_2_, ...), custom_call_target="tpu_custom_call" | custom-call | tf_op jit(solution)/shard_map/k_back_four/pallas_call | solution.py:836
  349.9 5.4 %collective-permute-done.80 = bf16[2,2,2,144,512]{4,3,2,1,0:T(8,128)(2,1)S(1)} collective-permute-done((bf16[2,2,2,144,512]{4,3,2,1,0:T(8,128)(2,1)S(1)}, bf16[2,2,2,144,512]{4,3,2,1,0:T(8,128)(2,1)S(1)}, u32[]{:S(2)}, u32[]{:S(2)}) %collective-permute-start.80) | collective-permute-done | bytes 1179680 | tf_op jit(solution)/shard_map/ppermute | solution.py:589
  355.4 2.6 collective-permute-start.84
  358.0 3.2 collective-permute-start.117
  366.0 11.3 %collective-permute-done.82 = f32[8,1024]{1,0:T(8,128)S(1)} collective-permute-done((f32[8,1024]{1,0:T(8,128)S(1)}, f32[8,1024]{1,0:T(8,128)S(1)}, u32[]{:S(2)}, u32[]{:S(2)}) %collective-permute-start.82) | collective-permute-done | bytes 32800 | tf_op jit(solution)/shard_map/ppermute | solution.py:589
  381.0 2.3 collective-permute-start.88
  391.3 7.7 %k_back_three.1 = (bf16[3,640,1024]{2,1,0:T(8,128)(2,1)S(1)}, f32[3,640,256]{2,1,0:T(8,128)S(1)}, f32[8,256]{1,0:T(8,128)S(1)}) custom-call(bf16[3,640,1024]{2,1,0:T(8,128)(2,1)S(1)} %get-tuple-element.156.refs_0_.refs_2_, bf16[3,640,1024]{2,1,0:T(8,128)(2,1)S(1)} %copy-done.9, f32[8,1024]{1,0:T(8,128)S(1)} %add_add_fusion.6.refs_2_.refs_10_, ...), custom_call_target="tpu_custom_call" | custom-call | tf_op jit(solution)/shard_map/k_back_three/pallas_call | solution.py:836
  399.0 6.2 %collective-permute-start.89 = (f32[8,256]{1,0:T(8,128)S(1)}, f32[8,256]{1,0:T(8,128)S(1)}, u32[]{:S(2)}, u32[]{:S(2)}) collective-permute-start(f32[8,256]{1,0:T(8,128)S(1)} %get-tuple-element.167), channel_id=1, source_target_pairs={{0,1},{1,0},{2,3},{3,2},{4,5},{5,4},{6,7},{7,6},{8,9},{9,8},{10,11... | collective-permute-start | bytes 24584 | tf_op jit(solution)/shard_map/ppermute | solution.py:589
  406.7 4.7 collective-permute-done.90
  416.2 4.7 collective-permute-start.96
  429.6 5.8 %k_back_two.1 = (bf16[3,640,256]{2,1,0:T(8,128)(2,1)S(1)}, f32[3,640,256]{2,1,0:T(8,128)S(1)}, f32[8,256]{1,0:T(8,128)S(1)}) custom-call(f32[3,640,256]{2,1,0:T(8,128)S(1)} %get-tuple-element.166.refs_0_, f32[3,640,256]{2,1,0:T(8,128)S(1)} %copy-done.13, f32[8,256]{1,0:T(8,128)S(1)} %add_add_fusion.20.refs_1_.refs_8_.refs_2_, ...), custom_call_target="tpu_custom_call" | custom-call | tf_op jit(solution)/shard_map/k_back_two/pallas_call | solution.py:836
  435.3 5.0 collective-permute-start.101
  441.8 2.4 collective-permute-start.103
  444.3 2.8 fusion
  447.1 11.9 %collective-permute-done.103.refs_5_ = bf16[192,1024]{1,0:T(8,128)(2,1)S(1)} collective-permute-done((bf16[192,1024]{1,0:T(8,128)(2,1)S(1)}, bf16[192,1024]{1,0:T(8,128)(2,1)S(1)}, u32[]{:S(2)}, u32[]{:S(2)}) %collective-permute-start.103) | collective-permute-done | bytes 393248 | tf_op jit(solution)/shard_map/ppermute | solution.py:595
  459.9 2.7 collective-permute-start.105
  465.6 3.2 collective-permute-start.109
  469.8 4.9 collective-permute-done.112
  477.5 3.5 collective-permute-start.113
  482.4 4.1 collective-permute-done.114
  492.3 4.0 collective-permute-start.124
  502.9 7.8 %collective-permute-start.121 = (bf16[2,200,256]{2,1,0:T(8,128)(2,1)S(1)}, bf16[2,200,256]{2,1,0:T(8,128)(2,1)S(1)}, u32[]{:S(2)}, u32[]{:S(2)}) collective-permute-start(bf16[2,200,256]{2,1,0:T(8,128)(2,1)S(1)} %add.888), channel_id=1, source_target_pairs={{0,1},{1,0},{2,3},{3,2},{4,5},{5,4},{6,7},{7,6},{8,9},{9,8},{10,11... | collective-permute-start | bytes 614408 | tf_op jit(solution)/shard_map/ppermute | solution.py:589
  511.9 3.4 k_input.1
  518.5 2.6 collective-permute-done.125
  522.2 5.9 %collective-permute-start.126 = (bf16[2,48,2048]{2,1,0:T(8,128)(2,1)S(1)}, bf16[2,48,2048]{2,1,0:T(8,128)(2,1)S(1)}, u32[]{:S(2)}, u32[]{:S(2)}) collective-permute-start(bf16[2,48,2048]{2,1,0:T(8,128)(2,1)S(1)} %pad_maximum_fusion.8), channel_id=1, source_target_pairs={{0,1},{1,0},{2,3},{3,2},{4,5},{5,4},{6,7},{7,6},{8,9},{9,8},{10,11... | collective-permute-start | bytes 1179656 | tf_op jit(solution)/shard_map/ppermute | solution.py:589
  (557 shorter events, 212.0 us)
Async XLA Ops:
  7.2 123.6 %all-gather.3.cloned.1.call-start = ((), (), s32[]{:S(2)}) async-start(), calls=%async_computation.1 | async-start | bytes 5947392 | tf_op jit(solution)/shard_map/all_gather | solution.py:712
  8.9 181.3 %all-gather.5.cloned.1.call-start = ((), (), s32[]{:S(2)}) async-start(), calls=%async_computation.2 | async-start | bytes 6488064 | tf_op jit(solution)/shard_map/all_gather | solution.py:712
  10.6 505.8 %reduce-scatter.2.cloned.1.call-start = ((), (), s32[]{:S(2)}) async-start(), calls=%async_computation.3 | async-start | bytes 6488064 | tf_op jit(solution)/shard_map/reduce_scatter | solution.py:1010
  21.2 5.6 %collective-permute-start.6 = (bf16[2,104,256]{2,1,0:T(8,128)(2,1)S(1)}, bf16[2,104,256]{2,1,0:T(8,128)(2,1)S(1)}, u32[]{:S(2)}, u32[]{:S(2)}) collective-permute-start(bf16[2,104,256]{2,1,0:T(8,128)(2,1)S(1)} %pad_maximum_fusion.14), channel_id=1, source_target_pairs={{0,8},{1,9},{2,10},{3,11},{4,12},{5,13},{6,14},{7,15},{8,0},{9,1},... | collective-permute-start | bytes 319496 | tf_op jit(solution)/shard_map/ppermute | solution.py:589
  23.2 5.0 collective-permute-start.3
  26.9 9.6 %collective-permute-start.7 = (bf16[2,2,104,256]{3,2,1,0:T(8,128)(2,1)S(1)}, bf16[2,2,104,256]{3,2,1,0:T(8,128)(2,1)S(1)}, u32[]{:S(2)}, u32[]{:S(2)}) collective-permute-start(bf16[2,2,104,256]{3,2,1,0:T(8,128)(2,1)S(1)} %pad_maximum_fusion.12), channel_id=1, source_target_pairs={{0,4},{1,5},{2,6},{3,7},{4,0},{5,1},{6,2},{7,3},{8,12},{9,13},{10,... | collective-permute-start | bytes 638984 | tf_op jit(solution)/shard_map/ppermute | solution.py:589
  31.2 6.1 %collective-permute-start.4 = (f32[8,256]{1,0:T(8,128)S(1)}, f32[8,256]{1,0:T(8,128)S(1)}, u32[]{:S(2)}, u32[]{:S(2)}) collective-permute-start(f32[8,256]{1,0:T(8,128)S(1)} %get-tuple-element.109), channel_id=1, source_target_pairs={{0,1},{1,0},{2,3},{3,2},{4,5},{5,4},{6,7},{7,6},{8,9},{9,8},{10,11... | collective-permute-start | bytes 24584 | tf_op jit(solution)/shard_map/ppermute | solution.py:589
  42.8 6.8 %collective-permute-start.14 = (f32[8,256]{1,0:T(8,128)S(1)}, f32[8,256]{1,0:T(8,128)S(1)}, u32[]{:S(2)}, u32[]{:S(2)}) collective-permute-start(f32[8,256]{1,0:T(8,128)S(1)} %add_add_fusion.23), channel_id=1, source_target_pairs={{0,24},{1,25},{2,26},{3,27},{4,28},{5,29},{6,30},{7,31},{8,16},{9,... | collective-permute-start | bytes 24584 | tf_op jit(solution)/shard_map/ppermute | solution.py:589
  44.8 4.9 collective-permute-start.12
  46.3 8.9 %collective-permute-start.15 = (bf16[2,2,2,104,256]{4,3,2,1,0:T(8,128)(2,1)}, bf16[2,2,2,104,256]{4,3,2,1,0:T(8,128)(2,1)}, u32[]{:S(2)}, u32[]{:S(2)}) collective-permute-start(bf16[2,2,2,104,256]{4,3,2,1,0:T(8,128)(2,1)} %pad_maximum_fusion.5), channel_id=1, source_target_pairs={{0,2},{1,3},{2,0},{3,1},{4,6},{5,7},{6,4},{7,5},{8,10},{9,11},{10,... | collective-permute-start | bytes 1277960 | tf_op jit(solution)/shard_map/ppermute | solution.py:589
  47.6 8.8 %collective-permute-start.11 = (bf16[3,192,256]{2,1,0:T(8,128)(2,1)S(1)}, bf16[3,192,256]{2,1,0:T(8,128)(2,1)S(1)}, u32[]{:S(2)}, u32[]{:S(2)}) collective-permute-start(bf16[3,192,256]{2,1,0:T(8,128)(2,1)S(1)} %copy-done.74), channel_id=1, source_target_pairs={{4,0},{8,4},{12,8},{16,12},{20,16},{24,20},{28,24},{5,1},{9,5},{13... | collective-permute-start | bytes 884744 | tf_op jit(solution)/shard_map/ppermute | solution.py:595
  56.4 8.0 %collective-permute-start.16 = (bf16[2,2,2,2,104,256]{5,4,3,2,1,0:T(8,128)(2,1)S(1)}, bf16[2,2,2,2,104,256]{5,4,3,2,1,0:T(8,128)(2,1)S(1)}, u32[]{:S(2)}, u32[]{:S(2)}) collective-permute-start(bf16[2,2,2,2,104,256]{5,4,3,2,1,0:T(8,128)(2,1)S(1)} %pad_maximum_fusion.2), channel_id=1, source_target_pairs={{0,1},{1,0},{2,3},{3,2},{4,5},{5,4},{6,7},{7,6},{8,9},{9,8},{10,11... | collective-permute-start | bytes 2555912 | tf_op jit(solution)/shard_map/ppermute | solution.py:589
  61.7 16.9 %collective-permute-start.18 = (bf16[12,14,1024]{2,1,0:T(8,128)(2,1)S(1)}, bf16[12,14,1024]{2,1,0:T(8,128)(2,1)S(1)}, u32[]{:S(2)}, u32[]{:S(2)}) collective-permute-start(bf16[12,14,1024]{2,1,0:T(8,128)(2,1)S(1)} %copy-done.81), channel_id=1, source_target_pairs={{4,0},{8,4},{12,8},{16,12},{20,16},{24,20},{28,24},{5,1},{9,5},{13... | collective-permute-start | bytes 1032200 | tf_op jit(solution)/shard_map/ppermute | solution.py:595
  83.6 13.3 %collective-permute-start.24 = (f32[8,256]{1,0:T(8,128)S(1)}, f32[8,256]{1,0:T(8,128)S(1)}, u32[]{:S(2)}, u32[]{:S(2)}) collective-permute-start(f32[8,256]{1,0:T(8,128)S(1)} %add_add_fusion.21), channel_id=1, source_target_pairs={{0,24},{1,25},{2,26},{3,27},{4,28},{5,29},{6,30},{7,31},{8,16},{9,... | collective-permute-start | bytes 24584 | tf_op jit(solution)/shard_map/ppermute | solution.py:589
  92.5 19.9 %collective-permute-start.26 = (bf16[12,14,1024]{2,1,0:T(8,128)(2,1)S(1)}, bf16[12,14,1024]{2,1,0:T(8,128)(2,1)S(1)}, u32[]{:S(2)}, u32[]{:S(2)}) collective-permute-start(bf16[12,14,1024]{2,1,0:T(8,128)(2,1)S(1)} %copy-done.80), channel_id=1, source_target_pairs={{4,0},{8,4},{12,8},{16,12},{20,16},{24,20},{28,24},{5,1},{9,5},{13... | collective-permute-start | bytes 1032200 | tf_op jit(solution)/shard_map/ppermute | solution.py:595
  97.0 20.8 %collective-permute-start.25 = (bf16[12,14,1024]{2,1,0:T(8,128)(2,1)S(1)}, bf16[12,14,1024]{2,1,0:T(8,128)(2,1)S(1)}, u32[]{:S(2)}, u32[]{:S(2)}) collective-permute-start(bf16[12,14,1024]{2,1,0:T(8,128)(2,1)S(1)} %copy-done.79), channel_id=1, source_target_pairs={{4,0},{8,4},{12,8},{16,12},{20,16},{24,20},{28,24},{5,1},{9,5},{13... | collective-permute-start | bytes 1032200 | tf_op jit(solution)/shard_map/ppermute | solution.py:595
  123.2 7.6 %collective-permute-start.33 = (f32[8,1024]{1,0:T(8,128)S(1)}, f32[8,1024]{1,0:T(8,128)S(1)}, u32[]{:S(2)}, u32[]{:S(2)}) collective-permute-start(f32[8,1024]{1,0:T(8,128)S(1)} %add_add_fusion.7), channel_id=1, source_target_pairs={{0,24},{1,25},{2,26},{3,27},{4,28},{5,29},{6,30},{7,31},{8,16},{9,... | collective-permute-start | bytes 98312 | tf_op jit(solution)/shard_map/ppermute | solution.py:589
  149.4 9.9 %collective-permute-start.34 = (f32[8,512]{1,0:T(8,128)S(1)}, f32[8,512]{1,0:T(8,128)S(1)}, u32[]{:S(2)}, u32[]{:S(2)}) collective-permute-start(f32[8,512]{1,0:T(8,128)S(1)} %get-tuple-element.130), channel_id=1, source_target_pairs={{0,1},{1,0},{2,3},{3,2},{4,5},{5,4},{6,7},{7,6},{8,9},{9,8},{10,11... | collective-permute-start | bytes 49160 | tf_op jit(solution)/shard_map/ppermute | solution.py:589
  218.3 5.0 collective-permute-start.54
  220.0 7.1 %collective-permute-start.53 = (f32[8,2048]{1,0:T(8,128)S(1)}, f32[8,2048]{1,0:T(8,128)S(1)}, u32[]{:S(2)}, u32[]{:S(2)}) collective-permute-start(f32[8,2048]{1,0:T(8,128)S(1)} %add_add_fusion.3), channel_id=1, source_target_pairs={{0,16},{1,17},{2,18},{3,19},{4,20},{5,21},{6,22},{7,23},{8,24},{9,... | collective-permute-start | bytes 196616 | tf_op jit(solution)/shard_map/ppermute | solution.py:589
  220.7 6.5 %collective-permute-start.52 = (f32[8,2048]{1,0:T(8,128)S(1)}, f32[8,2048]{1,0:T(8,128)S(1)}, u32[]{:S(2)}, u32[]{:S(2)}) collective-permute-start(f32[8,2048]{1,0:T(8,128)S(1)} %add_add_fusion.3), channel_id=1, source_target_pairs={{0,8},{1,9},{2,10},{3,11},{4,12},{5,13},{6,14},{7,15},{8,0},{9,1},... | collective-permute-start | bytes 196616 | tf_op jit(solution)/shard_map/ppermute | solution.py:589
  244.7 4.9 collective-permute-start.58
  249.7 5.0 collective-permute-start.62
  251.2 7.0 %collective-permute-start.61 = (f32[8,2048]{1,0:T(8,128)S(1)}, f32[8,2048]{1,0:T(8,128)S(1)}, u32[]{:S(2)}, u32[]{:S(2)}) collective-permute-start(f32[8,2048]{1,0:T(8,128)S(1)} %add_add_fusion.1), channel_id=1, source_target_pairs={{0,16},{1,17},{2,18},{3,19},{4,20},{5,21},{6,22},{7,23},{8,24},{9,... | collective-permute-start | bytes 196616 | tf_op jit(solution)/shard_map/ppermute | solution.py:589
  251.2 7.0 %collective-permute-start.60 = (f32[8,2048]{1,0:T(8,128)S(1)}, f32[8,2048]{1,0:T(8,128)S(1)}, u32[]{:S(2)}, u32[]{:S(2)}) collective-permute-start(f32[8,2048]{1,0:T(8,128)S(1)} %add_add_fusion.1), channel_id=1, source_target_pairs={{0,8},{1,9},{2,10},{3,11},{4,12},{5,13},{6,14},{7,15},{8,0},{9,1},... | collective-permute-start | bytes 196616 | tf_op jit(solution)/shard_map/ppermute | solution.py:589
  271.5 6.2 %collective-permute-start.67 = (f32[8,512]{1,0:T(8,128)S(1)}, f32[8,512]{1,0:T(8,128)S(1)}, u32[]{:S(2)}, u32[]{:S(2)}) collective-permute-start(f32[8,512]{1,0:T(8,128)S(1)} %add.805), channel_id=1, source_target_pairs={{0,6},{1,7},{2,4},{3,5},{4,2},{5,3},{6,0},{7,1},{8,14},{9,15},{10,... | collective-permute-start | bytes 49160 | tf_op jit(solution)/shard_map/ppermute | solution.py:589
  298.9 9.6 %collective-permute-start.71 = (f32[8,512]{1,0:T(8,128)S(1)}, f32[8,512]{1,0:T(8,128)S(1)}, u32[]{:S(2)}, u32[]{:S(2)}) collective-permute-start(f32[8,512]{1,0:T(8,128)S(1)} %get-tuple-element.150), channel_id=1, source_target_pairs={{0,1},{1,0},{2,3},{3,2},{4,5},{5,4},{6,7},{7,6},{8,9},{9,8},{10,11... | collective-permute-start | bytes 49160 | tf_op jit(solution)/shard_map/ppermute | solution.py:589
  309.6 13.4 %collective-permute-start.75 = (bf16[2,2,2,2,144,512]{5,4,3,2,1,0:T(8,128)(2,1)}, bf16[2,2,2,2,144,512]{5,4,3,2,1,0:T(8,128)(2,1)}, u32[]{:S(2)}, u32[]{:S(2)}) collective-permute-start(bf16[2,2,2,2,144,512]{5,4,3,2,1,0:T(8,128)(2,1)} %dynamic-slice_bitcast_fusion), channel_id=1, source_target_pairs={{0,1},{1,0},{2,3},{3,2},{4,5},{5,4},{6,7},{7,6},{8,9},{9,8},{10,11... | collective-permute-start | bytes 7077896 | tf_op jit(solution)/shard_map/ppermute | solution.py:589
  311.0 11.9 %collective-permute-start.74 = (f32[8,512]{1,0:T(8,128)S(1)}, f32[8,512]{1,0:T(8,128)S(1)}, u32[]{:S(2)}, u32[]{:S(2)}) collective-permute-start(f32[8,512]{1,0:T(8,128)S(1)} %add.812), channel_id=1, source_target_pairs={{0,6},{1,7},{2,4},{3,5},{4,2},{5,3},{6,0},{7,1},{8,14},{9,15},{10,... | collective-permute-start | bytes 49160 | tf_op jit(solution)/shard_map/ppermute | solution.py:589
  312.5 10.4 %collective-permute-start.73 = (f32[8,512]{1,0:T(8,128)S(1)}, f32[8,512]{1,0:T(8,128)S(1)}, u32[]{:S(2)}, u32[]{:S(2)}) collective-permute-start(f32[8,512]{1,0:T(8,128)S(1)} %add.812), channel_id=1, source_target_pairs={{0,4},{1,5},{2,6},{3,7},{4,0},{5,1},{6,2},{7,3},{8,12},{9,13},{10,... | collective-permute-start | bytes 49160 | tf_op jit(solution)/shard_map/ppermute | solution.py:589
  313.1 9.9 %collective-permute-start.72 = (f32[8,512]{1,0:T(8,128)S(1)}, f32[8,512]{1,0:T(8,128)S(1)}, u32[]{:S(2)}, u32[]{:S(2)}) collective-permute-start(f32[8,512]{1,0:T(8,128)S(1)} %add.812), channel_id=1, source_target_pairs={{0,2},{1,3},{2,0},{3,1},{4,6},{5,7},{6,4},{7,5},{8,10},{9,11},{10,... | collective-permute-start | bytes 49160 | tf_op jit(solution)/shard_map/ppermute | solution.py:589
  329.5 25.8 %collective-permute-start.80 = (bf16[2,2,2,144,512]{4,3,2,1,0:T(8,128)(2,1)S(1)}, bf16[2,2,2,144,512]{4,3,2,1,0:T(8,128)(2,1)S(1)}, u32[]{:S(2)}, u32[]{:S(2)}) collective-permute-start(bf16[2,2,2,144,512]{4,3,2,1,0:T(8,128)(2,1)S(1)} %get-tuple-element.160), channel_id=1, source_target_pairs={{0,2},{1,3},{2,0},{3,1},{4,6},{5,7},{6,4},{7,5},{8,10},{9,11},{10,... | collective-permute-start | bytes 3538952 | tf_op jit(solution)/shard_map/ppermute | solution.py:589
  345.0 4.9 collective-permute-start.79
  355.4 22.0 %collective-permute-start.84 = (bf16[2,2,2,2,64,256]{5,4,3,2,1,0:T(8,128)(2,1)S(1)}, bf16[2,2,2,2,64,256]{5,4,3,2,1,0:T(8,128)(2,1)S(1)}, u32[]{:S(2)}, u32[]{:S(2)}) collective-permute-start(bf16[2,2,2,2,64,256]{5,4,3,2,1,0:T(8,128)(2,1)S(1)} %fusion.8), channel_id=1, source_target_pairs={{0,1},{1,0},{2,3},{3,2},{4,5},{5,4},{6,7},{7,6},{8,9},{9,8},{10,11... | collective-permute-start | bytes 1572872 | tf_op jit(solution)/shard_map/ppermute | solution.py:589
  358.0 153.9 %collective-permute-start.117 = (bf16[192,1024]{1,0:T(8,128)(2,1)S(1)}, bf16[192,1024]{1,0:T(8,128)(2,1)S(1)}, u32[]{:S(2)}, u32[]{:S(2)}) collective-permute-start(bf16[192,1024]{1,0:T(8,128)(2,1)S(1)} %get-tuple-element.260), channel_id=1, source_target_pairs={{0,4},{4,8},{8,12},{12,16},{16,20},{20,24},{24,28},{1,5},{5,9},{9,... | collective-permute-start | bytes 1179656 | tf_op jit(solution)/shard_map/ppermute | solution.py:595
  361.9 15.4 %collective-permute-start.82 = (f32[8,1024]{1,0:T(8,128)S(1)}, f32[8,1024]{1,0:T(8,128)S(1)}, u32[]{:S(2)}, u32[]{:S(2)}) collective-permute-start(f32[8,1024]{1,0:T(8,128)S(1)} %add.822), channel_id=1, source_target_pairs={{0,4},{1,5},{2,6},{3,7},{4,0},{5,1},{6,2},{7,3},{8,12},{9,13},{10,... | collective-permute-start | bytes 98312 | tf_op jit(solution)/shard_map/ppermute | solution.py:589
  363.6 13.8 %collective-permute-start.81 = (f32[8,1024]{1,0:T(8,128)S(1)}, f32[8,1024]{1,0:T(8,128)S(1)}, u32[]{:S(2)}, u32[]{:S(2)}) collective-permute-start(f32[8,1024]{1,0:T(8,128)S(1)} %add.822), channel_id=1, source_target_pairs={{0,2},{1,3},{2,0},{3,1},{4,6},{5,7},{6,4},{7,5},{8,10},{9,11},{10,... | collective-permute-start | bytes 98312 | tf_op jit(solution)/shard_map/ppermute | solution.py:589
  377.4 6.0 %collective-permute-start.87 = (f32[8,1024]{1,0:T(8,128)S(1)}, f32[8,1024]{1,0:T(8,128)S(1)}, u32[]{:S(2)}, u32[]{:S(2)}) collective-permute-start(f32[8,1024]{1,0:T(8,128)S(1)} %add_add_fusion.5), channel_id=1, source_target_pairs={{0,24},{1,25},{2,26},{3,27},{4,28},{5,29},{6,30},{7,31},{8,16},{9,... | collective-permute-start | bytes 98312 | tf_op jit(solution)/shard_map/ppermute | solution.py:589
  379.7 6.6 %collective-permute-start.86 = (f32[8,1024]{1,0:T(8,128)S(1)}, f32[8,1024]{1,0:T(8,128)S(1)}, u32[]{:S(2)}, u32[]{:S(2)}) collective-permute-start(f32[8,1024]{1,0:T(8,128)S(1)} %add_add_fusion.5), channel_id=1, source_target_pairs={{0,16},{1,17},{2,18},{3,19},{4,20},{5,21},{6,22},{7,23},{8,24},{9,... | collective-permute-start | bytes 98312 | tf_op jit(solution)/shard_map/ppermute | solution.py:589
  379.7 6.6 %collective-permute-start.85 = (f32[8,1024]{1,0:T(8,128)S(1)}, f32[8,1024]{1,0:T(8,128)S(1)}, u32[]{:S(2)}, u32[]{:S(2)}) collective-permute-start(f32[8,1024]{1,0:T(8,128)S(1)} %add_add_fusion.5), channel_id=1, source_target_pairs={{0,8},{1,9},{2,10},{3,11},{4,12},{5,13},{6,14},{7,15},{8,0},{9,1},... | collective-permute-start | bytes 98312 | tf_op jit(solution)/shard_map/ppermute | solution.py:589
  381.0 6.6 %collective-permute-start.88 = (bf16[2,2,2,64,256]{4,3,2,1,0:T(8,128)(2,1)S(1)}, bf16[2,2,2,64,256]{4,3,2,1,0:T(8,128)(2,1)S(1)}, u32[]{:S(2)}, u32[]{:S(2)}) collective-permute-start(bf16[2,2,2,64,256]{4,3,2,1,0:T(8,128)(2,1)S(1)} %fusion.14), channel_id=1, source_target_pairs={{0,4},{1,5},{2,6},{3,7},{4,0},{5,1},{6,2},{7,3},{8,12},{9,13},{10,... | collective-permute-start | bytes 786440 | tf_op jit(solution)/shard_map/ppermute | solution.py:589
  383.4 28.0 %collective-permute-start.90 = (bf16[2,2,144,512]{3,2,1,0:T(8,128)(2,1)S(1)}, bf16[2,2,144,512]{3,2,1,0:T(8,128)(2,1)S(1)}, u32[]{:S(2)}, u32[]{:S(2)}) collective-permute-start(bf16[2,2,144,512]{3,2,1,0:T(8,128)(2,1)S(1)} %get-tuple-element.170), channel_id=1, source_target_pairs={{0,4},{1,5},{2,6},{3,7},{4,0},{5,1},{6,2},{7,3},{8,12},{9,13},{10,... | collective-permute-start | bytes 1769480 | tf_op jit(solution)/shard_map/ppermute | solution.py:589
  387.7 19.0 %collective-permute-start.91 = (bf16[2,2,64,256]{3,2,1,0:T(8,128)(2,1)S(1)}, bf16[2,2,64,256]{3,2,1,0:T(8,128)(2,1)S(1)}, u32[]{:S(2)}, u32[]{:S(2)}) collective-permute-start(bf16[2,2,64,256]{3,2,1,0:T(8,128)(2,1)S(1)} %fusion.19), channel_id=1, source_target_pairs={{0,8},{1,9},{2,10},{3,11},{4,12},{5,13},{6,14},{7,15},{8,0},{9,1},... | collective-permute-start | bytes 393224 | tf_op jit(solution)/shard_map/ppermute | solution.py:589
  389.0 23.1 %collective-permute-start.92 = (bf16[192,1024]{1,0:T(8,128)(2,1)S(1)}, bf16[192,1024]{1,0:T(8,128)(2,1)S(1)}, u32[]{:S(2)}, u32[]{:S(2)}) collective-permute-start(bf16[192,1024]{1,0:T(8,128)(2,1)S(1)} %get-tuple-element.172), channel_id=1, source_target_pairs={{0,4},{4,8},{8,12},{12,16},{16,20},{20,24},{24,28},{1,5},{5,9},{9,... | collective-permute-start | bytes 1179656 | tf_op jit(solution)/shard_map/ppermute | solution.py:595
  399.0 7.6 %collective-permute-start.89 = (f32[8,256]{1,0:T(8,128)S(1)}, f32[8,256]{1,0:T(8,128)S(1)}, u32[]{:S(2)}, u32[]{:S(2)}) collective-permute-start(f32[8,256]{1,0:T(8,128)S(1)} %get-tuple-element.167), channel_id=1, source_target_pairs={{0,1},{1,0},{2,3},{3,2},{4,5},{5,4},{6,7},{7,6},{8,9},{9,8},{10,11... | collective-permute-start | bytes 24584 | tf_op jit(solution)/shard_map/ppermute | solution.py:589
  412.1 8.8 %collective-permute-start.95 = (f32[8,256]{1,0:T(8,128)S(1)}, f32[8,256]{1,0:T(8,128)S(1)}, u32[]{:S(2)}, u32[]{:S(2)}) collective-permute-start(f32[8,256]{1,0:T(8,128)S(1)} %add.840), channel_id=1, source_target_pairs={{0,6},{1,7},{2,4},{3,5},{4,2},{5,3},{6,0},{7,1},{8,14},{9,15},{10,... | collective-permute-start | bytes 24584 | tf_op jit(solution)/shard_map/ppermute | solution.py:589
  413.9 7.1 %collective-permute-start.94 = (f32[8,256]{1,0:T(8,128)S(1)}, f32[8,256]{1,0:T(8,128)S(1)}, u32[]{:S(2)}, u32[]{:S(2)}) collective-permute-start(f32[8,256]{1,0:T(8,128)S(1)} %add.840), channel_id=1, source_target_pairs={{0,4},{1,5},{2,6},{3,7},{4,0},{5,1},{6,2},{7,3},{8,12},{9,13},{10,... | collective-permute-start | bytes 24584 | tf_op jit(solution)/shard_map/ppermute | solution.py:589
  416.2 5.8 %collective-permute-start.96 = (bf16[2,2,2,2,32,256]{5,4,3,2,1,0:T(8,128)(2,1)S(1)}, bf16[2,2,2,2,32,256]{5,4,3,2,1,0:T(8,128)(2,1)S(1)}, u32[]{:S(2)}, u32[]{:S(2)}) collective-permute-start(bf16[2,2,2,2,32,256]{5,4,3,2,1,0:T(8,128)(2,1)S(1)} %dynamic-slice_bitcast_fusion.5), channel_id=1, source_target_pairs={{0,1},{1,0},{2,3},{3,2},{4,5},{5,4},{6,7},{7,6},{8,9},{9,8},{10,11... | collective-permute-start | bytes 786440 | tf_op jit(solution)/shard_map/ppermute | solution.py:589
  422.0 5.1 collective-permute-start.99
  435.3 11.8 %collective-permute-start.101 = (f32[8,256]{1,0:T(8,128)S(1)}, f32[8,256]{1,0:T(8,128)S(1)}, u32[]{:S(2)}, u32[]{:S(2)}) collective-permute-start(f32[8,256]{1,0:T(8,128)S(1)} %get-tuple-element.179), channel_id=1, source_target_pairs={{0,1},{1,0},{2,3},{3,2},{4,5},{5,4},{6,7},{7,6},{8,9},{9,8},{10,11... | collective-permute-start | bytes 24584 | tf_op jit(solution)/shard_map/ppermute | solution.py:589
  440.4 6.8 %collective-permute-start.102 = (bf16[2,2,32,256]{3,2,1,0:T(8,128)(2,1)S(1)}, bf16[2,2,32,256]{3,2,1,0:T(8,128)(2,1)S(1)}, u32[]{:S(2)}, u32[]{:S(2)}) collective-permute-start(bf16[2,2,32,256]{3,2,1,0:T(8,128)(2,1)S(1)} %fusion.21), channel_id=1, source_target_pairs={{0,8},{1,9},{2,10},{3,11},{4,12},{5,13},{6,14},{7,15},{8,0},{9,1},... | collective-permute-start | bytes 196616 | tf_op jit(solution)/shard_map/ppermute | solution.py:589
  440.4 22.2 %collective-permute-start.108 = (bf16[2,144,512]{2,1,0:T(8,128)(2,1)S(1)}, bf16[2,144,512]{2,1,0:T(8,128)(2,1)S(1)}, u32[]{:S(2)}, u32[]{:S(2)}) collective-permute-start(bf16[2,144,512]{2,1,0:T(8,128)(2,1)S(1)} %get-tuple-element.186), channel_id=1, source_target_pairs={{0,8},{1,9},{2,10},{3,11},{4,12},{5,13},{6,14},{7,15},{8,0},{9,1},... | collective-permute-start | bytes 884744 | tf_op jit(solution)/shard_map/ppermute | solution.py:589
  441.8 17.1 %collective-permute-start.103 = (bf16[192,1024]{1,0:T(8,128)(2,1)S(1)}, bf16[192,1024]{1,0:T(8,128)(2,1)S(1)}, u32[]{:S(2)}, u32[]{:S(2)}) collective-permute-start(bf16[192,1024]{1,0:T(8,128)(2,1)S(1)} %get-tuple-element.183), channel_id=1, source_target_pairs={{0,4},{4,8},{8,12},{12,16},{16,20},{20,24},{24,28},{1,5},{5,9},{9,... | collective-permute-start | bytes 1179656 | tf_op jit(solution)/shard_map/ppermute | solution.py:595
  459.0 6.1 %collective-permute-start.107 = (bf16[2,2,2,2,72,256]{5,4,3,2,1,0:T(8,128)(2,1)S(1)}, bf16[2,2,2,2,72,256]{5,4,3,2,1,0:T(8,128)(2,1)S(1)}, u32[]{:S(2)}, u32[]{:S(2)}) collective-permute-start(bf16[2,2,2,2,72,256]{5,4,3,2,1,0:T(8,128)(2,1)S(1)} %dynamic-slice_bitcast_fusion.1), channel_id=1, source_target_pairs={{0,1},{1,0},{2,3},{3,2},{4,5},{5,4},{6,7},{7,6},{8,9},{9,8},{10,11... | collective-permute-start | bytes 1769480 | tf_op jit(solution)/shard_map/ppermute | solution.py:589
  468.8 5.9 %collective-permute-start.112 = (bf16[2,2,2,72,256]{4,3,2,1,0:T(8,128)(2,1)S(1)}, bf16[2,2,2,72,256]{4,3,2,1,0:T(8,128)(2,1)S(1)}, u32[]{:S(2)}, u32[]{:S(2)}) collective-permute-start(bf16[2,2,2,72,256]{4,3,2,1,0:T(8,128)(2,1)S(1)} %bitcast_add_fusion.2), channel_id=1, source_target_pairs={{0,4},{1,5},{2,6},{3,7},{4,0},{5,1},{6,2},{7,3},{8,12},{9,13},{10,... | collective-permute-start | bytes 884744 | tf_op jit(solution)/shard_map/ppermute | solution.py:589
  474.8 6.8 %collective-permute-start.122 = (bf16[144,512]{1,0:T(8,128)(2,1)S(1)}, bf16[144,512]{1,0:T(8,128)(2,1)S(1)}, u32[]{:S(2)}, u32[]{:S(2)}) collective-permute-start(bf16[144,512]{1,0:T(8,128)(2,1)S(1)} %fusion.18), channel_id=1, source_target_pairs={{0,16},{1,17},{2,18},{3,19},{4,20},{5,21},{6,22},{7,23},{8,24},{9,... | collective-permute-start | bytes 442376 | tf_op jit(solution)/shard_map/ppermute | solution.py:589
  481.1 7.3 %collective-permute-start.118 = (bf16[2,2,72,256]{3,2,1,0:T(8,128)(2,1)S(1)}, bf16[2,2,72,256]{3,2,1,0:T(8,128)(2,1)S(1)}, u32[]{:S(2)}, u32[]{:S(2)}) collective-permute-start(bf16[2,2,72,256]{3,2,1,0:T(8,128)(2,1)S(1)} %fusion.17), channel_id=1, source_target_pairs={{0,8},{1,9},{2,10},{3,11},{4,12},{5,13},{6,14},{7,15},{8,0},{9,1},... | collective-permute-start | bytes 442376 | tf_op jit(solution)/shard_map/ppermute | solution.py:589
  481.6 10.6 %collective-permute-start.123 = (bf16[144,512]{1,0:T(8,128)(2,1)S(1)}, bf16[144,512]{1,0:T(8,128)(2,1)S(1)}, u32[]{:S(2)}, u32[]{:S(2)}) collective-permute-start(bf16[144,512]{1,0:T(8,128)(2,1)S(1)} %bitcast_add_fusion.7), channel_id=1, source_target_pairs={{0,2},{1,3},{2,0},{3,1},{4,6},{5,7},{6,4},{7,5},{8,10},{9,11},{10,... | collective-permute-start | bytes 442376 | tf_op jit(solution)/shard_map/ppermute | solution.py:589
  490.0 7.8 %collective-permute-start.119 = (bf16[2,200,256]{2,1,0:T(8,128)(2,1)S(1)}, bf16[2,200,256]{2,1,0:T(8,128)(2,1)S(1)}, u32[]{:S(2)}, u32[]{:S(2)}) collective-permute-start(bf16[2,200,256]{2,1,0:T(8,128)(2,1)S(1)} %dynamic-slice_bitcast_fusion.7), channel_id=1, source_target_pairs={{0,16},{1,17},{2,18},{3,19},{4,20},{5,21},{6,22},{7,23},{8,24},{9,... | collective-permute-start | bytes 614408 | tf_op jit(solution)/shard_map/ppermute | solution.py:589
  492.3 18.4 %collective-permute-start.124 = (bf16[2,144,512]{2,1,0:T(8,128)(2,1)S(1)}, bf16[2,144,512]{2,1,0:T(8,128)(2,1)S(1)}, u32[]{:S(2)}, u32[]{:S(2)}) collective-permute-start(bf16[2,144,512]{2,1,0:T(8,128)(2,1)S(1)} %pad_maximum_fusion.9), channel_id=1, source_target_pairs={{0,1},{1,0},{2,3},{3,2},{4,5},{5,4},{6,7},{7,6},{8,9},{9,8},{10,11... | collective-permute-start | bytes 884744 | tf_op jit(solution)/shard_map/ppermute | solution.py:589
  497.8 5.0 collective-permute-start.120
  499.4 12.5 %collective-permute-start.116 = (bf16[3,192,256]{2,1,0:T(8,128)(2,1)S(1)}, bf16[3,192,256]{2,1,0:T(8,128)(2,1)S(1)}, u32[]{:S(2)}, u32[]{:S(2)}) collective-permute-start(bf16[3,192,256]{2,1,0:T(8,128)(2,1)S(1)} %slice.223), channel_id=1, source_target_pairs={{0,4},{4,8},{8,12},{12,16},{16,20},{20,24},{24,28},{1,5},{5,9},{9,... | collective-permute-start | bytes 884744 | tf_op jit(solution)/shard_map/ppermute | solution.py:595
  502.9 12.5 %collective-permute-start.121 = (bf16[2,200,256]{2,1,0:T(8,128)(2,1)S(1)}, bf16[2,200,256]{2,1,0:T(8,128)(2,1)S(1)}, u32[]{:S(2)}, u32[]{:S(2)}) collective-permute-start(bf16[2,200,256]{2,1,0:T(8,128)(2,1)S(1)} %add.888), channel_id=1, source_target_pairs={{0,1},{1,0},{2,3},{3,2},{4,5},{5,4},{6,7},{7,6},{8,9},{9,8},{10,11... | collective-permute-start | bytes 614408 | tf_op jit(solution)/shard_map/ppermute | solution.py:589
  522.2 7.4 %collective-permute-start.126 = (bf16[2,48,2048]{2,1,0:T(8,128)(2,1)S(1)}, bf16[2,48,2048]{2,1,0:T(8,128)(2,1)S(1)}, u32[]{:S(2)}, u32[]{:S(2)}) collective-permute-start(bf16[2,48,2048]{2,1,0:T(8,128)(2,1)S(1)} %pad_maximum_fusion.8), channel_id=1, source_target_pairs={{0,1},{1,0},{2,3},{3,2},{4,5},{5,4},{6,7},{7,6},{8,9},{9,8},{10,11... | collective-permute-start | bytes 1179656 | tf_op jit(solution)/shard_map/ppermute | solution.py:589
  (159 other events, 1510.1 us)
Sparse Core Ops, SparseCore 0:
  10.9 70.9 all-gather.2
  84.7 73.2 all-gather.4
  313.8 126.3 reduce-scatter.1

commit v3 on v2

--- a/solution.py
+++ b/solution.py
@@ -310,15 +310,20 @@
     count_up(pre, out_total, m)
 
 
-def k_fourth(count, pre_in, entry, total, gain, bias, mask, weight, block, corner, pre, out_total, full):
+def k_fourth(count, pre_in, entry, total, gain, bias, mask, weight, block, corner, slope, pre, out_total, full):
     m = pl.program_id(0)
     wide = COLS // 2
     chunk = 4 * COLS
 
     def step(at, lanes, v):
         x = get(pre_in, at, lanes) * v[0] + v[1] + get(entry, at, lanes)
-        y = gelu(x) * get_mask(mask, at, lanes)
+        square = x * x
+        t = jnp.tanh(x * (TANH_SCALE + TANH_SCALE * TANH_CUBE * square))
+        inside = x * (TANH_SCALE + 3.0 * TANH_SCALE * TANH_CUBE * square)
+        part = (0.5 + 0.5 * t) * get_mask(mask, at, lanes)
+        y = x * part
         put(block, at, lanes, y)
+        put(slope, at, lanes, part + part * inside * (1.0 - t))
         put_tall(full, slice(0, chunk), flat(y), lanes.start)
         pair = [get_tall(full, pl.ds(k * COLS, wide, stride=2), lanes) for k in (0, 2)]
         corner[0, pl.ds(pl.multiple_of(at.start // 4, COLS), COLS), lanes] = jnp.concatenate(pair, 0).astype(BF)
@@ -329,8 +334,15 @@
 
 
 def k_seventh(corner, weight, pre, out_total):
-    pre[0] = nn(corner[0], wide_of(weight)).astype(pre.dtype)
-    count_up(pre, out_total, pl.program_id(1))
+    micro, half, tile = pre.shape
+    value = nn(corner[...].reshape(micro * half, -1), wide_of(weight))
+    pre[...] = value.reshape(pre.shape).astype(pre.dtype)
+    for m in range(micro):
+        part = eight(value[m * half : (m + 1) * half])
+        sums = [jnp.sum(v, axis=(0, 1))[None] for v in (part, part * part)]
+        rows = lax.broadcasted_iota(jnp.int32, out_total.shape, 0)
+        table = jnp.zeros_like(sums[0]) if m == 0 else out_total[...]
+        out_total[...] = jnp.where(rows == 2 * m, sums[0], jnp.where(rows == 2 * m + 1, sums[1], table))
 
 
 def k_fifth(count, pre_in, total, gain, bias, mask, half_mask, inner, weight, pre, patch, out_total, act, eo, oe, oo):
@@ -492,7 +504,7 @@
 
 
 def k_back_four(
-    count, d_four, four, tot4, back4, g4, mask, weight, d_corner, three, entry, tot3, g3, b3,
+    count, d_four, four, tot4, back4, g4, mask, weight, d_corner, three, slope, tot3,
     d_pre, d_summed, out_total, placed, d_block,
 ):
     m = pl.program_id(0)
@@ -509,13 +521,11 @@
             rows = pl.ds(2 * k * COLS, wide, stride=2)
             put_tall(placed, rows, value[k * wide : (k + 1) * wide], lanes.start)
         got = get(d_block, at, lanes) + eight(get_tall(placed, slice(0, 4 * COLS), lanes))
-        p = get(three, at, lanes)
-        x = p * v[0] + v[1] + get(entry, at, lanes)
-        d = gelu_slope(x) * got * get_mask(mask, at, lanes)
+        d = get(slope, at, lanes) * got
         put(d_summed, at, lanes, d)
-        return d, d * p
-
-    sums = sweep(cells, c, line(tot3, m, count, g3, b3), add, 2, chunk=4 * COLS)
+        return d, d * get(three, at, lanes)
+
+    sums = sweep(cells, c, (), add, 2, chunk=4 * COLS)
     put_sums(out_total, m, *centred(tot3, m, count, *sums))
 
 
@@ -679,14 +689,14 @@
     return lambda x: exchange(x, 1 << bit)
 
 
-def lanes_of(w, parts):
-    x = w.reshape(parts, -1, w.shape[1] // 256, 256)
-    return x.transpose(0, 2, 1, 3).reshape(parts, -1, 256)
+def lanes_of(w, parts, wide=256):
+    x = w.reshape(parts, -1, w.shape[1] // wide, wide)
+    return x.transpose(0, 2, 1, 3).reshape(parts, -1, wide)
 
 
 def from_lanes(x, c):
-    parts = x.shape[0]
-    x = x.reshape(parts, c // 256, -1, 256)
+    parts, wide = x.shape[0], x.shape[2]
+    x = x.reshape(parts, c // wide, -1, wide)
     return x.transpose(0, 2, 1, 3).reshape(-1, c)
 
 
@@ -740,13 +750,12 @@
     return x.reshape((-1,) + x.shape[-2:])
 
 
-def reduce_steps(parts):
+def reduce_scattered(part, order):
     bits = device_bits()
-    x = jnp.concatenate(parts, 1) if len(parts) > 1 else parts[0]
-    x = x.reshape((2,) * bits + x.shape[1:])
+    x = part.reshape((2,) * bits + part.shape[1:])
     left = list(reversed(range(bits)))
     got = None
-    for bit in range(bits):
+    for bit in order:
         axis = left.index(bit)
         left.remove(bit)
         half = lambda v, b: lax.dynamic_index_in_dim(v, b, axis, keepdims=False)
@@ -756,7 +765,15 @@
         else:
             x, give = half(x, keep) + half(got, keep), half(x, send) + half(got, send)
         got = yield give, across(bit)
-    return (yield from spread_steps(x + got))
+    return x + got
+
+
+def lanes_back(filter_and_spec, c):
+    whole, spec = filter_and_spec
+    if whole.ndim == 3:
+        n, k = spec.block_shape[1], spec.index_map(0)[1]
+        return from_lanes(whole[:, k * n : (k + 1) * n], c)
+    return from_lanes(whole.reshape(lax.axis_size("rows") * lax.axis_size("batch"), -1, whole.shape[1]), c)
 
 
 def reduce_first(part):
@@ -806,7 +823,7 @@
     return out
 
 
-LIMIT = 26
+LIMIT = 16
 
 
 def per_micro(shape):
@@ -870,9 +887,10 @@
     mine, more = own * COLS, SPILL * COLS
 
     chain_n1 = Chain(gather_steps(narrow_one.reshape(2, -1, m1), 1))
-    pack_a = [lanes_of(w, 4) for w in (spatial_one, expand_one)]
-    chain_a = Chain(gather_steps(jnp.concatenate(pack_a, 1), 2))
-    spatial_b, narrow_b = gather_offloaded([spatial_two, narrow_two])
+    chain_a = Chain(gather_steps(spatial_one.reshape(4, -1, m1), 2))
+    thin = [lanes_of(expand_one, 4, m2).reshape(-1, m2)]
+    spatial_b, narrow_b, thin_a = gather_offloaded([spatial_two, narrow_two] + thin)
+    expand_a = lanes_back(thin_a, channels)
     bypass, expand_b = gather_offloaded([shortcut, expand_two])
     chain_f = [
         Chain(one_step(features[k, 0, :SPILL], lambda x: from_behind(x, -1))) for k in range(micro)
@@ -909,7 +927,7 @@
             chain_a.launch(lax.optimization_barrier((chain_a.ready[0], landed))[0])
             before = before + [landed]
             if len(before) == 3:
-                hook(landed, start=chain_f[2:])
+                hook(landed, start=chain_f)
     narrow_a = chain_n1.value().reshape(-1, m1)
     pre_one, head, t1 = call(
         k_first, micro, [(features, "m"), (flags, "m"), (narrow_a, "w")],
@@ -920,35 +938,34 @@
         t1,
         b=dict(finish=[chain_a]),
         c=dict(start=[chain_a, chain_h]),
-        d=dict(finish=[chain_a, chain_h], start=[chain_a] + chain_f[:1]),
+        d=dict(finish=[chain_a, chain_h], start=[chain_a]),
     )
     pre_spill = chain_h.value()
-    total_a = chain_a.value()
-    spatial_a = total_a[:, : pack_a[0].shape[1]].reshape(-1, m1)
-    expand_a = from_lanes(total_a[:, pack_a[0].shape[1] :], channels)
+    spatial_a = chain_a.value().reshape(-1, m1)
     pre_two, patch_one, t2 = call(
         functools.partial(k_second, full_count), micro,
         [(pre_one, "m"), (pre_spill, "m"), (t1, "w"), (g1, "w"), (b1, "w"), (mask, "m"),
          (flags, "m"), (spatial_a, "w")],
         [per(m1), per(9 * m1, BF), full_table(m1)],
         [((cells + 2 * COLS, m1), F32), ((cells + 2 * COLS, 3 * m1), BF), ((1, cells, m1), F32)],
-    )
-    t2 = global_sum(t2, b=dict(finish=chain_f[:1]), d=dict(start=chain_f[1:2]))
+        limit=20,
+    )
+    (entry,) = call(
+        k_entry, micro,
+        [(features, "m"), (mask, "m")] + [(f.value(), "w") for f in chain_f],
+        [per(channels, BF)], [((cells, channels), BF)],
+    )
+    t2 = global_sum(t2, c=dict(need=[entry]))
     act_two, pre_three, t3 = call(
         functools.partial(k_third, full_count), micro,
         [(pre_two, "m"), (t2, "w"), (g2, "w"), (b2, "w"), (mask, "m"), (expand_a, "w")],
         [per(m1, BF), per(channels, BF), full_table(channels)],
     )
-    t3 = global_sum(t3, b=dict(finish=chain_f[1:]))
-    (entry,) = call(
-        k_entry, micro,
-        [(features, "m"), (mask, "m")] + [(f.value(), "w") for f in chain_f],
-        [per(channels, BF)], [((cells, channels), BF)],
-    )
-    block_out, corner, pre_four, t4 = call(
+    t3 = global_sum(t3)
+    block_out, corner, slope_three, pre_four, t4 = call(
         functools.partial(k_fourth, full_count), micro,
         [(pre_three, "m"), (entry, "m"), (t3, "w"), (g3, "w"), (b3, "w"), (mask, "m"), narrow_b],
-        [per(channels, BF), per(channels, BF, half), per(m2, BF), full_table(m2)],
+        [per(channels, BF), per(channels, BF, half), per(channels, BF), per(m2, BF), full_table(m2)],
         [((channels // LANES, 4 * COLS, LANES), F32)],
     )
     t4 = global_sum(t4)
@@ -958,6 +975,7 @@
          spatial_b],
         [per(m2, F32, half), per(9 * m2, BF, half), full_table(m2)],
         [((m2 // LANES, cells, LANES), F32)] + [((half + COLS, m2), F32)] * 3,
+        limit=20,
     )
     t5 = global_sum(t5)
     act_five, pre_six, t6 = call(
@@ -969,20 +987,21 @@
     by_tile = bypass[1].block_shape[:-1] + (tile,)
     pre_seven, t7 = pl.pallas_call(
         k_seventh,
-        grid=(4, micro),
+        grid=(4,),
         in_specs=[
-            pl.BlockSpec((1, half, channels), lambda n, m: (m, 0, 0)),
-            pl.BlockSpec(by_tile, lambda n, m: (0,) * (len(by_tile) - 1) + (n,)),
+            pl.BlockSpec(corner.shape, lambda n: (0, 0, 0)),
+            pl.BlockSpec(by_tile, lambda n: (0,) * (len(by_tile) - 1) + (n,)),
         ],
         out_specs=[
-            pl.BlockSpec((1, half, tile), lambda n, m: (m, 0, n)),
-            pl.BlockSpec((8, tile), lambda n, m: (0, n)),
+            pl.BlockSpec((micro, half, tile), lambda n: (0, 0, n)),
+            pl.BlockSpec((8, tile), lambda n: (0, n)),
         ],
         out_shape=[
             jax.ShapeDtypeStruct((micro, half, outward), BF),
             jax.ShapeDtypeStruct((8, outward), F32),
         ],
         compiler_params=pltpu.CompilerParams(vmem_limit_bytes=LIMIT * 1024 * 1024),
+        name="k_seventh",
     )(corner, bypass[0])
     t67 = global_sum(jnp.concatenate([t6, t7], 1))
     t6, t7 = t67[:, :outward], t67[:, outward:]
@@ -1014,15 +1033,23 @@
          spatial_b, (pre_four, "m"), (t4, "w"), (g4, "w"), (b4, "w"), (mask, "m")],
         [per(m2, BF, half), per(m2), full_table(m2)],
         [((m2 // LANES, cells, LANES), F32), ((half + COLS, m2), F32)],
-    )
-    chain_rs = Chain(reduce_steps([sharded(weight_term(patch_two, d_pre_five), m2)]))
-    u4 = global_sum(u4, b=dict(start=[chain_rs]), c=dict(finish=[chain_rs], start=[chain_rs]))
+        limit=22,
+    )
+    grad_s2 = sharded(weight_term(patch_two, d_pre_five), m2)
+    cut = grad_s2.shape[1] // 32 * 16 or grad_s2.shape[1] // 2
+    low = batch_bits()
+    chain_rs = [
+        Chain(reduce_scattered(grad_s2[:, :cut], list(range(device_bits())))),
+        Chain(reduce_scattered(grad_s2[:, cut:], [0, low] + list(range(1, low)) + list(range(low + 1, device_bits())))),
+    ]
+    u4 = global_sum(u4, b=dict(start=chain_rs), c=dict(finish=chain_rs, start=chain_rs))
     d_pre_four, d_summed, u3 = call(
         functools.partial(k_back_four, full_count), micro,
         [(d_four, "m"), (pre_four, "m"), (t4, "w"), (u4, "w"), (g4, "w"), (mask, "m"), narrow_b,
-         (d_corner, "m"), (pre_three, "m"), (entry, "m"), (t3, "w"), (g3, "w"), (b3, "w")],
+         (d_corner, "m"), (pre_three, "m"), (slope_three, "m"), (t3, "w")],
         [per(m2, BF), per(channels, BF), full_table(channels)],
         [((channels // LANES, 4 * COLS, LANES), F32), ((1, cells, channels), F32)],
+        limit=24,
     )
     grad_n2 = [
         sharded(weight_term(block_out, d_pre_four[..., k : k + 256]), 256) for k in range(0, m2, 256)
@@ -1032,9 +1059,9 @@
     chain_r2 = Chain(reduce_first(jnp.concatenate(grad_n2, 1)))
     u3 = global_sum(
         u3,
-        b=dict(finish=[chain_rs], start=[chain_r2]),
-        c=dict(finish=[chain_r2], start=[chain_rs, chain_r2]),
-        d=dict(finish=[chain_r2], start=[chain_r2, chain_ds[0]]),
+        b=dict(start=[chain_r2]),
+        c=dict(finish=chain_rs + [chain_r2], start=chain_rs + [chain_r2]),
+        d=dict(start=[chain_ds[0]]),
     )
     d_pre_three, d_two, u2 = call(
         functools.partial(k_back_three, full_count), micro,
@@ -1046,9 +1073,9 @@
     chain_r3 = Chain(reduce_first(sharded(grad_e1, 256)))
     u2 = global_sum(
         u2,
-        b=dict(finish=[chain_rs, chain_r2, chain_ds[0]], start=[chain_r3]),
-        c=dict(finish=[chain_r3], start=[chain_r3]),
-        d=dict(finish=[chain_r3], start=[chain_rs, chain_r3] + chain_ds[1:2]),
+        b=dict(finish=[chain_r2], start=[chain_r3]),
+        c=dict(finish=chain_rs + [chain_ds[0], chain_r3], start=[chain_r3]),
+        d=dict(start=chain_rs + [chain_r2] + chain_ds[1:2]),
     )
     d_pre_two, d_one, u1 = call(
         functools.partial(k_back_two, full_count), micro,
@@ -1056,14 +1083,15 @@
          (spatial_a, "w"), (pre_one, "m"), (pre_spill, "m"), (t1, "w"), (g1, "w"), (b1, "w")],
         [per(m1, BF), per(m1), full_table(m1)],
         [((cells + 2 * COLS, m1), F32), ((cells + 2 * COLS, 3 * m1), BF), ((1, cells, m1), F32)],
+        limit=20,
     )
     grad_s1 = weight_term(patch_one, d_pre_two)
     chain_r1 = Chain(reduce_first(sharded(grad_s1, 256)))
     u1 = global_sum(
         u1,
-        b=dict(finish=[chain_r3] + chain_ds[1:2], start=[chain_r1]),
-        c=dict(finish=[chain_r1, chain_rs], start=[chain_r1]),
-        d=dict(finish=[chain_r1], start=[chain_r1, chain_rs]),
+        b=dict(finish=[chain_r3], start=[chain_r1]),
+        c=dict(finish=chain_rs + [chain_r2, chain_r1] + chain_ds[1:2], start=[chain_r1]),
+        d=dict(start=chain_rs + [chain_r3] + chain_ds[2:]),
     )
     (d_pre_one,) = call(
         functools.partial(k_back_one, full_count), micro,
@@ -1071,21 +1099,39 @@
         [per(m1, BF)], [((1, cells, m1), F32)],
     )
     chain_rn = Chain(reduce_first(sharded(weight_term(entry, d_pre_one), 256)))
+    chain_rb = Chain(spread_steps(part_b))
+    chain_rn.launch(chain_rn.ready[0])
+    landed = chain_rn.flying
+    chain_rn.land()
+    hook(landed, finish=[chain_r1], start=[chain_r1])
+    while not chain_rn.done:
+        chain_rn.launch(chain_rn.ready[0])
+        landed = chain_rn.flying
+        chain_rn.land()
     firsts = [c.value() for c in (chain_rn, chain_r1, chain_r2, chain_r3)]
     chain_last = Chain(reduce_last(jnp.concatenate(firsts, -2)))
-    d_more = lax.optimization_barrier((d_pre_one[:, mine : mine + more], firsts[0]))[0]
-    chain_dp = Chain(one_step(d_more, lambda x: from_behind(x, 1)))
+    chain_dp = Chain(one_step(d_pre_one[:, mine : mine + more], lambda x: from_behind(x, 1)))
+    chain_last.launch(chain_last.ready[0])
+    hook(landed, start=[chain_dp])
+    landed = chain_last.flying
+    chain_last.land()
+    chain_r4 = Chain(spread_steps(jnp.concatenate([c.value() for c in chain_rs], 0)))
+    hook(landed, start=[chain_rb, chain_r4])
+    chain_last.launch(chain_last.ready[0])
+    landed = chain_last.flying
+    chain_last.land()
     out_n1, out_s1, out_n2, out_e1 = unpack(
         chain_last.value(), [(channels, m1), (9 * m1, m1), (channels, m2), (m1, channels)]
     )
-    (out_s2,) = unpack(chain_rs.value(), [(9 * m2, m2)])
-    out_sc, out_e2 = unpack(Chain(spread_steps(part_b)).value(), [(channels, outward), (m2, outward)])
+    (out_s2,) = unpack(chain_r4.value(), [(9 * m2, m2)])
+    out_sc, out_e2 = unpack(chain_rb.value(), [(channels, outward), (m2, outward)])
     (grad_input,) = call(
         k_input, micro,
         [(d_pre_one, "m"), (chain_dp.value(), "m"), (d_summed, "m"), (narrow_a, "w")]
         + [(c.value(), "w") for c in chain_ds],
         [((micro, own * across * channels // LANES, LANES), F32, "m")],
         [((mine, m1), BF), ((mine, channels), F32)],
+        after=[landed],
     )
     grad_input = grad_input.reshape(features.shape)
     added = lambda k, us: jnp.concatenate([u[k] + u[k + 2] + u[k + 4] for u in us])

time: 545 us -> 524 us (0.961)
  starting transfers between devices: 208 us -> 168 us
  waiting for transfers between devices: 116 us -> 138 us
  Pallas kernels: 106 us -> 99.1 us
    ppermute x119 -> x124, starting transfers between devices: 186 us -> 146 us  [exchange(): return lax.ppermute(x, AXES, [(i, i ^ mask) for i in range(total)])]
    ppermute x8, waiting for transfers between devices: 19.4 us -> 54.6 us  [from_behind(): return lax.ppermute(x, 'rows', pairs)]
    ppermute x119 -> x124, waiting for transfers between devices: 96.1 us -> 82.9 us  [exchange(): return lax.ppermute(x, AXES, [(i, i ^ mask) for i in range(total)])]
    unnamed x188 -> x176, local copies, waits for them, and re-layouts: 41.5 us -> 37.4 us
  transfers between devices with their start and end apart: 130 -> 135, of which waited for: 67 -> 63; matrix products, arithmetic and copies ran while one was open for 9% -> 9% of each run, Pallas kernels for 13% -> 13%
where the time goes in v3:
time: 524 us; the launch traced here: 514 us
  starting transfers between devices  168 us (32%)
  waiting for transfers between devices  138 us (26%)
  Pallas kernels  99.1 us (19%)
  local copies, waits for them, and re-layouts  53.9 us (10%)
  other arithmetic  22.7 us (4%)
  matrix products  16.8 us (3%)
  between operations  16.1 us (3%)
    ppermute x124, starting transfers between devices, exchange(): return lax.ppermute(x, AXES, [(i, i ^ mask) for i in range(total)])  146 us
    pallas_call x16, Pallas kernels, call(): pl.pallas_call(run, grid=(micro,), in_specs=in_specs, out_specs=out_specs...  92.5 us
    ppermute x124, waiting for transfers between devices, exchange(): return lax.ppermute(x, AXES, [(i, i ^ mask) for i in range(total)])  82.9 us
    ppermute x8, waiting for transfers between devices, from_behind(): return lax.ppermute(x, 'rows', pairs)  54.6 us
    unnamed x176, local copies, waits for them, and re-layouts  37.4 us
    ppermute x8, starting transfers between devices, from_behind(): return lax.ppermute(x, 'rows', pairs)  21.9 us
    dot_general x8, matrix products, weight_term(): lax.dot_general(left.reshape(-1, k), right.reshape(-1, n), (((0,), (0,)),...  16.8 us
  transfers between devices with their start and end apart: 135, of which 63 were waited for; matrix products, arithmetic and copies ran while one was open for 9% of the time, Pallas kernels for 13%

profile of v3, /device:TPU:25, one launch (start us, length us, event | category | flops | bytes accessed | tf_op | source)
XLA Modules:
  0.0 514.4 jit_solution(3317879482507071012)
XLA Ops:
  12.2 3.4 k_masks.1
  26.9 5.4 %collective-permute-start.3 = (bf16[2,2,2,64,256]{4,3,2,1,0:T(8,128)(2,1)S(1)}, bf16[2,2,2,64,256]{4,3,2,1,0:T(8,128)(2,1)S(1)}, u32[]{:S(2)}, u32[]{:S(2)}) collective-permute-start(bf16[2,2,2,64,256]{4,3,2,1,0:T(8,128)(2,1)S(1)} %pad_maximum_fusion.11), channel_id=1, source_target_pairs={{0,1},{1,0},{2,3},{3,2},{4,5},{5,4},{6,7},{7,6},{8,9},{9,8},{10,11... | collective-permute-start | bytes 786440 | tf_op jit(solution)/shard_map/ppermute | solution.py:599
  47.9 2.6 collective-permute-start.11
  51.4 4.2 collective-permute-done.11.refs_1_.refs_9_.refs_2_
  55.6 4.1 collective-permute-start.16
  61.4 3.5 collective-permute-start.21
  66.8 3.9 collective-permute-start.23
  71.1 5.6 %k_second.1 = (f32[3,640,256]{2,1,0:T(8,128)S(1)}, bf16[3,640,2304]{2,1,0:T(8,128)(2,1)S(1)}, f32[8,256]{1,0:T(8,128)S(1)}) custom-call(f32[3,416,256]{2,1,0:T(8,128)S(1)} %copy-done.17, bf16[3,192,256]{2,1,0:T(8,128)(2,1)S(1)} %collective-permute-done.11.refs_1_.refs_9_.refs_2_, f32[8,256]{1,0:T(8,128)S(1)} %add_add_fusion.22.refs_2_.refs_10_.refs_3_, ...), custom_call_target="tpu_custom_call" | custom-call | tf_op jit(solution)/shard_map/k_second/pallas_call | solution.py:853
  76.7 3.5 copy-done.66
  84.5 8.2 %collective-permute-done.22.refs_3_ = bf16[12,14,1024]{2,1,0:T(8,128)(2,1)S(1)} collective-permute-done((bf16[12,14,1024]{2,1,0:T(8,128)(2,1)S(1)}, bf16[12,14,1024]{2,1,0:T(8,128)(2,1)S(1)}, u32[]{:S(2)}, u32[]{:S(2)}) %collective-permute-start.22) | collective-permute-done | bytes 344096 | tf_op jit(solution)/shard_map/ppermute | solution.py:605
  92.7 8.4 %collective-permute-done.23.refs_4_ = bf16[12,14,1024]{2,1,0:T(8,128)(2,1)S(1)} collective-permute-done((bf16[12,14,1024]{2,1,0:T(8,128)(2,1)S(1)}, bf16[12,14,1024]{2,1,0:T(8,128)(2,1)S(1)}, u32[]{:S(2)}, u32[]{:S(2)}) %collective-permute-start.23) | collective-permute-done | bytes 344096 | tf_op jit(solution)/shard_map/ppermute | solution.py:605
  110.5 6.0 %k_third.2 = (bf16[3,640,256]{2,1,0:T(8,128)(2,1)S(1)}, bf16[3,640,1024]{2,1,0:T(8,128)(2,1)S(1)}, f32[8,1024]{1,0:T(8,128)S(1)}) custom-call(f32[3,640,256]{2,1,0:T(8,128)S(1)} %get-tuple-element.126.refs_0_.refs_7_.refs_1_, f32[8,256]{1,0:T(8,128)S(1)} %add_add_fusion.20.refs_1_.refs_8_.refs_2_, f32[1,256]{1,0:T(1,128)S(1)} %bitcast.418, ...), custom_call_target="tpu_custom_call" | custom-call | tf_op jit(solution)/shard_map/k_third/pallas_call | solution.py:853
  119.6 3.8 collective-permute-start.30
  128.7 2.4 collective-permute-start.31
  132.7 3.1 collective-permute-done.32
  135.8 10.7 %k_fourth.1 = (bf16[3,640,1024]{2,1,0:T(8,128)(2,1)S(1)}, bf16[3,160,1024]{2,1,0:T(8,128)(2,1)S(1)}, bf16[3,640,1024]{2,1,0:T(8,128)(2,1)S(1)}, bf16[3,640,512]{2,1,0:T(8,128)(2,1)S(1)}, f32[8,512]{1,0:T(8,128)S(1)}) custom-call(bf16[3,640,1024]{2,1,0:T(8,128)(2,1)S(1)} %get-tuple-element.132.refs_0_.refs_8_.refs_1_, bf16[3,640,1024]{2,1,0:T(8,128)(2,1)S(1)} %copy-done.12, ...), custom_call_target="tpu_custom_call" | custom-call | tf_op jit(solution)/shard_map/k_fourth/pallas_call | solution.py:853
  146.5 2.0 copy-done.39
  150.4 2.0 collective-permute-start.34
  157.8 2.2 collective-permute-start.40
  164.8 6.6 %k_fifth.1 = (f32[3,160,512]{2,1,0:T(8,128)S(1)}, bf16[3,160,4608]{2,1,0:T(8,128)(2,1)S(1)}, f32[8,512]{1,0:T(8,128)S(1)}) custom-call(bf16[3,640,512]{2,1,0:T(8,128)(2,1)S(1)} %get-tuple-element.134.refs_0_.refs_8_.refs_1_, f32[8,512]{1,0:T(8,128)S(1)} %add_add_fusion.14.refs_1_.refs_9_.refs_2_, f32[1,512]{1,0:T(1,128)S(1)} %bitcast.403, ...), custom_call_target="tpu_custom_call" | custom-call | tf_op jit(solution)/shard_map/k_fifth/pallas_call | solution.py:853
  183.8 2.8 copy-done
  186.6 3.2 k_seventh.1
  189.9 4.1 k_third.3
  198.2 3.5 collective-permute-start.48
  207.6 2.2 collective-permute-done.50
  214.9 3.7 collective-permute-done.53
  224.6 8.2 %k_last.1 = (bf16[3,1,19,7,2048]{4,3,2,1,0:T(8,128)(2,1)}, bf16[3,160,2048]{2,1,0:T(8,128)(2,1)S(1)}, f32[8,4096]{1,0:T(8,128)S(1)}) custom-call(bf16[3,160,2048]{2,1,0:T(8,128)(2,1)S(1)} %copy-done.33, bf16[3,160,2048]{2,1,0:T(8,128)(2,1)S(1)} %copy-done.31, f32[8,2048]{1,0:T(8,128)S(1)} %get-tuple-element.314.refs_2_.refs_3_, ...), custom_call_target="tpu_custom_call" | custom-call | tf_op jit(solution)/shard_map/k_last/pallas_call | solution.py:853
  238.2 2.2 collective-permute-done.58
  242.0 2.1 collective-permute-start.60
  245.5 3.6 collective-permute-done.61
  250.7 7.4 %k_back_six.1 = (bf16[3,160,2048]{2,1,0:T(8,128)(2,1)S(1)}, bf16[3,160,2048]{2,1,0:T(8,128)(2,1)S(1)}, f32[3,160,512]{2,1,0:T(8,128)S(1)}, f32[8,512]{1,0:T(8,128)S(1)}) custom-call(bf16[3,160,2048]{2,1,0:T(8,128)(2,1)S(1)} %get-tuple-element.146.refs_0_, bf16[3,160,2048]{2,1,0:T(8,128)(2,1)S(1)} %copy-done.33, bf16[3,160,2048]{2,1,0:T(8,128)(2,1)S(1)} %copy-done.31, ...), custom_call_target="tpu_custom_call" | custom-call | tf_op jit(solution)/shard_map/k_back_six/pallas_call | solution.py:853
  258.6 2.4 bitcast_convert_fusion.1
  265.1 3.5 pad_maximum_fusion
  273.8 2.8 copy-done.6
  279.9 10.1 %k_back_five.1 = (bf16[3,160,512]{2,1,0:T(8,128)(2,1)S(1)}, f32[3,640,512]{2,1,0:T(8,128)S(1)}, f32[8,512]{1,0:T(8,128)S(1)}) custom-call(f32[3,160,512]{2,1,0:T(8,128)S(1)} %copy-done.53, f32[3,160,512]{2,1,0:T(8,128)S(1)} %copy-done.26, f32[8,512]{1,0:T(8,128)S(1)} %add_add_fusion.12.refs_1_.refs_9_.refs_2_, f32[8,512]{1,0:T(8,128)S(1)} %add_add_fusion.10.refs_3_, ...), custom_call_target="tpu_custom_call" | custom-call | tf_op jit(solution)/shard_map/k_back_five/pallas_call | solution.py:853
  291.9 5.3 %bitcast_convert_fusion = bf16[4608,512]{1,0:T(8,128)(2,1)S(1)} fusion(bf16[3,160,4608]{2,1,0:T(8,128)(2,1)} %copy-done.67, bf16[3,160,512]{2,1,0:T(8,128)(2,1)S(1)} %get-tuple-element.157), kind=kOutput, calls=%fused_computation | convolution fusion | flops 2267283456 | bytes 9633792 | tf_op jit(solution)/shard_map/dot_general | solution.py:869
  297.6 2.5 collective-permute-start.71
  305.6 2.8 copy-done.2
  310.0 4.9 k_corner.1.refs_7_
  324.0 8.4 %k_back_four.1 = (bf16[3,640,512]{2,1,0:T(8,128)(2,1)S(1)}, bf16[3,640,1024]{2,1,0:T(8,128)(2,1)S(1)}, f32[8,1024]{1,0:T(8,128)S(1)}) custom-call(f32[3,640,512]{2,1,0:T(8,128)S(1)} %copy-done.42, bf16[3,640,512]{2,1,0:T(8,128)(2,1)S(1)} %copy-done.10, f32[8,512]{1,0:T(8,128)S(1)} %add_add_fusion.14.refs_1_.refs_9_.refs_2_, ...), custom_call_target="tpu_custom_call" | custom-call | tf_op jit(solution)/shard_map/k_back_four/pallas_call | solution.py:853
  335.0 2.5 collective-permute-start.80
  351.4 7.7 %k_back_three.1 = (bf16[3,640,1024]{2,1,0:T(8,128)(2,1)S(1)}, f32[3,640,256]{2,1,0:T(8,128)S(1)}, f32[8,256]{1,0:T(8,128)S(1)}) custom-call(bf16[3,640,1024]{2,1,0:T(8,128)(2,1)S(1)} %get-tuple-element.163.refs_0_.refs_2_, bf16[3,640,1024]{2,1,0:T(8,128)(2,1)S(1)} %copy-done.5, f32[8,1024]{1,0:T(8,128)S(1)} %add_add_fusion.6.refs_2_.refs_10_, ...), custom_call_target="tpu_custom_call" | custom-call | tf_op jit(solution)/shard_map/k_back_three/pallas_call | solution.py:853
  359.1 4.4 collective-permute-start.90
  367.7 3.5 collective-permute-start.95
  371.2 3.6 collective-permute-start.98
  375.0 16.9 %collective-permute-done.98.refs_4_ = bf16[192,1024]{1,0:T(8,128)(2,1)S(1)} collective-permute-done((bf16[192,1024]{1,0:T(8,128)(2,1)S(1)}, bf16[192,1024]{1,0:T(8,128)(2,1)S(1)}, u32[]{:S(2)}, u32[]{:S(2)}) %collective-permute-start.98) | collective-permute-done | bytes 393248 | tf_op jit(solution)/shard_map/ppermute | solution.py:605
  391.8 2.7 collective-permute-start.100
  397.4 5.8 %k_back_two.1 = (bf16[3,640,256]{2,1,0:T(8,128)(2,1)S(1)}, f32[3,640,256]{2,1,0:T(8,128)S(1)}, f32[8,256]{1,0:T(8,128)S(1)}) custom-call(f32[3,640,256]{2,1,0:T(8,128)S(1)} %get-tuple-element.173.refs_0_, f32[3,640,256]{2,1,0:T(8,128)S(1)} %copy-done.8, f32[8,256]{1,0:T(8,128)S(1)} %add_add_fusion.20.refs_1_.refs_8_.refs_2_, ...), custom_call_target="tpu_custom_call" | custom-call | tf_op jit(solution)/shard_map/k_back_two/pallas_call | solution.py:853
  406.4 2.7 fusion
  411.9 5.4 %collective-permute-done.110 = bf16[2,2,64,256]{3,2,1,0:T(8,128)(2,1)S(1)} collective-permute-done((bf16[2,2,64,256]{3,2,1,0:T(8,128)(2,1)S(1)}, bf16[2,2,64,256]{3,2,1,0:T(8,128)(2,1)S(1)}, u32[]{:S(2)}, u32[]{:S(2)}) %collective-permute-start.110) | collective-permute-done | bytes 131104 | tf_op jit(solution)/shard_map/ppermute | solution.py:599
  421.0 4.1 collective-permute-done.109
  425.2 11.4 %collective-permute-done.111.refs_5_ = bf16[192,1024]{1,0:T(8,128)(2,1)S(1)} collective-permute-done((bf16[192,1024]{1,0:T(8,128)(2,1)S(1)}, bf16[192,1024]{1,0:T(8,128)(2,1)S(1)}, u32[]{:S(2)}, u32[]{:S(2)}) %collective-permute-start.111) | collective-permute-done | bytes 393248 | tf_op jit(solution)/shard_map/ppermute | solution.py:605
  437.9 2.2 collective-permute-start.112
  446.4 2.2 collective-permute-start.115
  450.1 4.5 collective-permute-done.116
  455.1 2.7 collective-permute-done.117
  461.1 2.2 collective-permute-start.119
  464.0 9.2 %collective-permute-done.123 = bf16[2,200,256]{2,1,0:T(8,128)(2,1)S(1)} collective-permute-done((bf16[2,200,256]{2,1,0:T(8,128)(2,1)S(1)}, bf16[2,200,256]{2,1,0:T(8,128)(2,1)S(1)}, u32[]{:S(2)}, u32[]{:S(2)}) %collective-permute-start.123) | collective-permute-done | bytes 204832 | tf_op jit(solution)/shard_map/ppermute | solution.py:599
  474.5 2.3 collective-permute-start.118
  476.8 2.4 collective-permute-done.124.refs_7_
  480.9 5.5 %collective-permute-done.118.refs_1_ = bf16[3,192,256]{2,1,0:T(8,128)(2,1)S(1)} collective-permute-done((bf16[3,192,256]{2,1,0:T(8,128)(2,1)S(1)}, bf16[3,192,256]{2,1,0:T(8,128)(2,1)S(1)}, u32[]{:S(2)}, u32[]{:S(2)}) %collective-permute-start.118) | collective-permute-done | bytes 294944 | tf_op jit(solution)/shard_map/ppermute | solution.py:605
  486.4 3.4 k_input.1
  494.9 4.7 collective-permute-start.129
  500.6 2.0 collective-permute-start.131
  (565 shorter events, 207.2 us)
Async XLA Ops:
  7.2 102.2 %all-gather.3.cloned.1.call-start = ((), (), s32[]{:S(2)}) async-start(), calls=%async_computation.1 | async-start | bytes 6488064 | tf_op jit(solution)/shard_map/all_gather | solution.py:722
  8.9 174.9 %all-gather.5.cloned.1.call-start = ((), (), s32[]{:S(2)}) async-start(), calls=%async_computation.2 | async-start | bytes 6488064 | tf_op jit(solution)/shard_map/all_gather | solution.py:722
  10.5 480.2 %reduce-scatter.2.cloned.1.call-start = ((), (), s32[]{:S(2)}) async-start(), calls=%async_computation.3 | async-start | bytes 6488064 | tf_op jit(solution)/shard_map/reduce_scatter | solution.py:1029
  25.7 6.6 %collective-permute-start.6 = (bf16[2,72,256]{2,1,0:T(8,128)(2,1)S(1)}, bf16[2,72,256]{2,1,0:T(8,128)(2,1)S(1)}, u32[]{:S(2)}, u32[]{:S(2)}) collective-permute-start(bf16[2,72,256]{2,1,0:T(8,128)(2,1)S(1)} %pad_maximum_fusion.15), channel_id=1, source_target_pairs={{0,8},{1,9},{2,10},{3,11},{4,12},{5,13},{6,14},{7,15},{8,0},{9,1},... | collective-permute-start | bytes 221192 | tf_op jit(solution)/shard_map/ppermute | solution.py:599
  26.9 6.7 %collective-permute-start.3 = (bf16[2,2,2,64,256]{4,3,2,1,0:T(8,128)(2,1)S(1)}, bf16[2,2,2,64,256]{4,3,2,1,0:T(8,128)(2,1)S(1)}, u32[]{:S(2)}, u32[]{:S(2)}) collective-permute-start(bf16[2,2,2,64,256]{4,3,2,1,0:T(8,128)(2,1)S(1)} %pad_maximum_fusion.11), channel_id=1, source_target_pairs={{0,1},{1,0},{2,3},{3,2},{4,5},{5,4},{6,7},{7,6},{8,9},{9,8},{10,11... | collective-permute-start | bytes 786440 | tf_op jit(solution)/shard_map/ppermute | solution.py:599
  32.3 5.5 %collective-permute-start.7 = (bf16[2,2,72,256]{3,2,1,0:T(8,128)(2,1)S(1)}, bf16[2,2,72,256]{3,2,1,0:T(8,128)(2,1)S(1)}, u32[]{:S(2)}, u32[]{:S(2)}) collective-permute-start(bf16[2,2,72,256]{3,2,1,0:T(8,128)(2,1)S(1)} %pad_maximum_fusion.12), channel_id=1, source_target_pairs={{0,4},{1,5},{2,6},{3,7},{4,0},{5,1},{6,2},{7,3},{8,12},{9,13},{10,... | collective-permute-start | bytes 442376 | tf_op jit(solution)/shard_map/ppermute | solution.py:599
  44.0 7.3 %collective-permute-start.15 = (bf16[2,2,2,72,256]{4,3,2,1,0:T(8,128)(2,1)S(1)}, bf16[2,2,2,72,256]{4,3,2,1,0:T(8,128)(2,1)S(1)}, u32[]{:S(2)}, u32[]{:S(2)}) collective-permute-start(bf16[2,2,2,72,256]{4,3,2,1,0:T(8,128)(2,1)S(1)} %pad_maximum_fusion.8), channel_id=1, source_target_pairs={{0,2},{1,3},{2,0},{3,1},{4,6},{5,7},{6,4},{7,5},{8,10},{9,11},{10,... | collective-permute-start | bytes 884744 | tf_op jit(solution)/shard_map/ppermute | solution.py:599
  44.4 6.1 %collective-permute-start.14 = (f32[8,256]{1,0:T(8,128)S(1)}, f32[8,256]{1,0:T(8,128)S(1)}, u32[]{:S(2)}, u32[]{:S(2)}) collective-permute-start(f32[8,256]{1,0:T(8,128)S(1)} %add_add_fusion.23), channel_id=1, source_target_pairs={{0,24},{1,25},{2,26},{3,27},{4,28},{5,29},{6,30},{7,31},{8,16},{9,... | collective-permute-start | bytes 24584 | tf_op jit(solution)/shard_map/ppermute | solution.py:599
  47.9 7.7 %collective-permute-start.11 = (bf16[3,192,256]{2,1,0:T(8,128)(2,1)}, bf16[3,192,256]{2,1,0:T(8,128)(2,1)S(1)}, u32[]{:S(2)}, u32[]{:S(2)}) collective-permute-start(bf16[3,192,256]{2,1,0:T(8,128)(2,1)} %copy-done.72), channel_id=1, source_target_pairs={{4,0},{8,4},{12,8},{16,12},{20,16},{24,20},{28,24},{5,1},{9,5},{13... | collective-permute-start | bytes 884744 | tf_op jit(solution)/shard_map/ppermute | solution.py:605
  55.6 15.2 %collective-permute-start.16 = (bf16[2,2,2,2,72,256]{5,4,3,2,1,0:T(8,128)(2,1)S(1)}, bf16[2,2,2,2,72,256]{5,4,3,2,1,0:T(8,128)(2,1)S(1)}, u32[]{:S(2)}, u32[]{:S(2)}) collective-permute-start(bf16[2,2,2,2,72,256]{5,4,3,2,1,0:T(8,128)(2,1)S(1)} %pad_maximum_fusion.3), channel_id=1, source_target_pairs={{0,1},{1,0},{2,3},{3,2},{4,5},{5,4},{6,7},{7,6},{8,9},{9,8},{10,11... | collective-permute-start | bytes 1769480 | tf_op jit(solution)/shard_map/ppermute | solution.py:599
  61.4 22.4 %collective-permute-start.21 = (bf16[12,14,1024]{2,1,0:T(8,128)(2,1)S(1)}, bf16[12,14,1024]{2,1,0:T(8,128)(2,1)S(1)}, u32[]{:S(2)}, u32[]{:S(2)}) collective-permute-start(bf16[12,14,1024]{2,1,0:T(8,128)(2,1)S(1)} %get-tuple-element.128), channel_id=1, source_target_pairs={{4,0},{8,4},{12,8},{16,12},{20,16},{24,20},{28,24},{5,1},{9,5},{13... | collective-permute-start | bytes 1032200 | tf_op jit(solution)/shard_map/ppermute | solution.py:605
  64.9 27.7 %collective-permute-start.22 = (bf16[12,14,1024]{2,1,0:T(8,128)(2,1)S(1)}, bf16[12,14,1024]{2,1,0:T(8,128)(2,1)S(1)}, u32[]{:S(2)}, u32[]{:S(2)}) collective-permute-start(bf16[12,14,1024]{2,1,0:T(8,128)(2,1)S(1)} %get-tuple-element.129), channel_id=1, source_target_pairs={{4,0},{8,4},{12,8},{16,12},{20,16},{24,20},{28,24},{5,1},{9,5},{13... | collective-permute-start | bytes 1032200 | tf_op jit(solution)/shard_map/ppermute | solution.py:605
  66.8 34.2 %collective-permute-start.23 = (bf16[12,14,1024]{2,1,0:T(8,128)(2,1)S(1)}, bf16[12,14,1024]{2,1,0:T(8,128)(2,1)S(1)}, u32[]{:S(2)}, u32[]{:S(2)}) collective-permute-start(bf16[12,14,1024]{2,1,0:T(8,128)(2,1)S(1)} %get-tuple-element.130), channel_id=1, source_target_pairs={{4,0},{8,4},{12,8},{16,12},{20,16},{24,20},{28,24},{5,1},{9,5},{13... | collective-permute-start | bytes 1032200 | tf_op jit(solution)/shard_map/ppermute | solution.py:605
  81.8 22.0 %collective-permute-start.20 = (f32[8,256]{1,0:T(8,128)S(1)}, f32[8,256]{1,0:T(8,128)S(1)}, u32[]{:S(2)}, u32[]{:S(2)}) collective-permute-start(f32[8,256]{1,0:T(8,128)S(1)} %add.849), channel_id=1, source_target_pairs={{0,6},{1,7},{2,4},{3,5},{4,2},{5,3},{6,0},{7,1},{8,14},{9,15},{10,... | collective-permute-start | bytes 24584 | tf_op jit(solution)/shard_map/ppermute | solution.py:599
  82.1 21.7 %collective-permute-start.19 = (f32[8,256]{1,0:T(8,128)S(1)}, f32[8,256]{1,0:T(8,128)S(1)}, u32[]{:S(2)}, u32[]{:S(2)}) collective-permute-start(f32[8,256]{1,0:T(8,128)S(1)} %add.849), channel_id=1, source_target_pairs={{0,4},{1,5},{2,6},{3,7},{4,0},{5,1},{6,2},{7,3},{8,12},{9,13},{10,... | collective-permute-start | bytes 24584 | tf_op jit(solution)/shard_map/ppermute | solution.py:599
  83.8 20.1 %collective-permute-start.18 = (f32[8,256]{1,0:T(8,128)S(1)}, f32[8,256]{1,0:T(8,128)S(1)}, u32[]{:S(2)}, u32[]{:S(2)}) collective-permute-start(f32[8,256]{1,0:T(8,128)S(1)} %add.849), channel_id=1, source_target_pairs={{0,2},{1,3},{2,0},{3,1},{4,6},{5,7},{6,4},{7,5},{8,10},{9,11},{10,... | collective-permute-start | bytes 24584 | tf_op jit(solution)/shard_map/ppermute | solution.py:599
  119.6 5.5 %collective-permute-start.30 = (f32[8,1024]{1,0:T(8,128)S(1)}, f32[8,1024]{1,0:T(8,128)S(1)}, u32[]{:S(2)}, u32[]{:S(2)}) collective-permute-start(f32[8,1024]{1,0:T(8,128)S(1)} %add.856), channel_id=1, source_target_pairs={{0,6},{1,7},{2,4},{3,5},{4,2},{5,3},{6,0},{7,1},{8,14},{9,15},{10,... | collective-permute-start | bytes 98312 | tf_op jit(solution)/shard_map/ppermute | solution.py:599
  128.5 7.2 %collective-permute-start.32 = (f32[8,1024]{1,0:T(8,128)S(1)}, f32[8,1024]{1,0:T(8,128)S(1)}, u32[]{:S(2)}, u32[]{:S(2)}) collective-permute-start(f32[8,1024]{1,0:T(8,128)S(1)} %add_add_fusion.7), channel_id=1, source_target_pairs={{0,16},{1,17},{2,18},{3,19},{4,20},{5,21},{6,22},{7,23},{8,24},{9,... | collective-permute-start | bytes 98312 | tf_op jit(solution)/shard_map/ppermute | solution.py:599
  128.7 7.1 %collective-permute-start.31 = (f32[8,1024]{1,0:T(8,128)S(1)}, f32[8,1024]{1,0:T(8,128)S(1)}, u32[]{:S(2)}, u32[]{:S(2)}) collective-permute-start(f32[8,1024]{1,0:T(8,128)S(1)} %add_add_fusion.7), channel_id=1, source_target_pairs={{0,8},{1,9},{2,10},{3,11},{4,12},{5,13},{6,14},{7,15},{8,0},{9,1},... | collective-permute-start | bytes 98312 | tf_op jit(solution)/shard_map/ppermute | solution.py:599
  180.2 9.7 %collective-permute-start.47 = (f32[8,512]{1,0:T(8,128)S(1)}, f32[8,512]{1,0:T(8,128)S(1)}, u32[]{:S(2)}, u32[]{:S(2)}) collective-permute-start(f32[8,512]{1,0:T(8,128)S(1)} %add_add_fusion.13), channel_id=1, source_target_pairs={{0,24},{1,25},{2,26},{3,27},{4,28},{5,29},{6,30},{7,31},{8,16},{9,... | collective-permute-start | bytes 49160 | tf_op jit(solution)/shard_map/ppermute | solution.py:599
  181.9 8.0 %collective-permute-start.46 = (f32[8,512]{1,0:T(8,128)S(1)}, f32[8,512]{1,0:T(8,128)S(1)}, u32[]{:S(2)}, u32[]{:S(2)}) collective-permute-start(f32[8,512]{1,0:T(8,128)S(1)} %add_add_fusion.13), channel_id=1, source_target_pairs={{0,16},{1,17},{2,18},{3,19},{4,20},{5,21},{6,22},{7,23},{8,24},{9,... | collective-permute-start | bytes 49160 | tf_op jit(solution)/shard_map/ppermute | solution.py:599
  182.5 7.3 %collective-permute-start.45 = (f32[8,512]{1,0:T(8,128)S(1)}, f32[8,512]{1,0:T(8,128)S(1)}, u32[]{:S(2)}, u32[]{:S(2)}) collective-permute-start(f32[8,512]{1,0:T(8,128)S(1)} %add_add_fusion.13), channel_id=1, source_target_pairs={{0,8},{1,9},{2,10},{3,11},{4,12},{5,13},{6,14},{7,15},{8,0},{9,1},... | collective-permute-start | bytes 49160 | tf_op jit(solution)/shard_map/ppermute | solution.py:599
  211.5 7.0 %collective-permute-start.53 = (f32[8,2048]{1,0:T(8,128)S(1)}, f32[8,2048]{1,0:T(8,128)S(1)}, u32[]{:S(2)}, u32[]{:S(2)}) collective-permute-start(f32[8,2048]{1,0:T(8,128)S(1)} %add_add_fusion.3), channel_id=1, source_target_pairs={{0,16},{1,17},{2,18},{3,19},{4,20},{5,21},{6,22},{7,23},{8,24},{9,... | collective-permute-start | bytes 196616 | tf_op jit(solution)/shard_map/ppermute | solution.py:599
  211.5 7.0 %collective-permute-start.52 = (f32[8,2048]{1,0:T(8,128)S(1)}, f32[8,2048]{1,0:T(8,128)S(1)}, u32[]{:S(2)}, u32[]{:S(2)}) collective-permute-start(f32[8,2048]{1,0:T(8,128)S(1)} %add_add_fusion.3), channel_id=1, source_target_pairs={{0,8},{1,9},{2,10},{3,11},{4,12},{5,13},{6,14},{7,15},{8,0},{9,1},... | collective-permute-start | bytes 196616 | tf_op jit(solution)/shard_map/ppermute | solution.py:599
  242.0 7.1 %collective-permute-start.61 = (f32[8,2048]{1,0:T(8,128)S(1)}, f32[8,2048]{1,0:T(8,128)S(1)}, u32[]{:S(2)}, u32[]{:S(2)}) collective-permute-start(f32[8,2048]{1,0:T(8,128)S(1)} %add_add_fusion.1), channel_id=1, source_target_pairs={{0,16},{1,17},{2,18},{3,19},{4,20},{5,21},{6,22},{7,23},{8,24},{9,... | collective-permute-start | bytes 196616 | tf_op jit(solution)/shard_map/ppermute | solution.py:599
  242.0 7.1 %collective-permute-start.60 = (f32[8,2048]{1,0:T(8,128)S(1)}, f32[8,2048]{1,0:T(8,128)S(1)}, u32[]{:S(2)}, u32[]{:S(2)}) collective-permute-start(f32[8,2048]{1,0:T(8,128)S(1)} %add_add_fusion.1), channel_id=1, source_target_pairs={{0,8},{1,9},{2,10},{3,11},{4,12},{5,13},{6,14},{7,15},{8,0},{9,1},... | collective-permute-start | bytes 196616 | tf_op jit(solution)/shard_map/ppermute | solution.py:599
  262.3 6.2 %collective-permute-start.67 = (f32[8,512]{1,0:T(8,128)S(1)}, f32[8,512]{1,0:T(8,128)S(1)}, u32[]{:S(2)}, u32[]{:S(2)}) collective-permute-start(f32[8,512]{1,0:T(8,128)S(1)} %add.893), channel_id=1, source_target_pairs={{0,6},{1,7},{2,4},{3,5},{4,2},{5,3},{6,0},{7,1},{8,14},{9,15},{10,... | collective-permute-start | bytes 49160 | tf_op jit(solution)/shard_map/ppermute | solution.py:599
  302.3 14.4 %collective-permute-start.76 = (bf16[2,2,2,2,80,512]{5,4,3,2,1,0:T(8,128)(2,1)}, bf16[2,2,2,2,80,512]{5,4,3,2,1,0:T(8,128)(2,1)}, u32[]{:S(2)}, u32[]{:S(2)}) collective-permute-start(bf16[2,2,2,2,80,512]{5,4,3,2,1,0:T(8,128)(2,1)} %dynamic-slice_bitcast_fusion), channel_id=1, source_target_pairs={{0,1},{1,0},{2,3},{3,2},{4,5},{5,4},{6,7},{7,6},{8,9},{9,8},{10,11... | collective-permute-start | bytes 3932168 | tf_op jit(solution)/shard_map/ppermute | solution.py:599
  302.8 12.1 %collective-permute-start.75 = (bf16[2,2,2,2,64,512]{5,4,3,2,1,0:T(8,128)(2,1)}, bf16[2,2,2,2,64,512]{5,4,3,2,1,0:T(8,128)(2,1)}, u32[]{:S(2)}, u32[]{:S(2)}) collective-permute-start(bf16[2,2,2,2,64,512]{5,4,3,2,1,0:T(8,128)(2,1)} %dynamic-slice_bitcast_fusion.1), channel_id=1, source_target_pairs={{0,1},{1,0},{2,3},{3,2},{4,5},{5,4},{6,7},{7,6},{8,9},{9,8},{10,11... | collective-permute-start | bytes 3145736 | tf_op jit(solution)/shard_map/ppermute | solution.py:599
  302.9 11.9 %collective-permute-start.74 = (f32[8,512]{1,0:T(8,128)S(1)}, f32[8,512]{1,0:T(8,128)S(1)}, u32[]{:S(2)}, u32[]{:S(2)}) collective-permute-start(f32[8,512]{1,0:T(8,128)S(1)} %add.900), channel_id=1, source_target_pairs={{0,6},{1,7},{2,4},{3,5},{4,2},{5,3},{6,0},{7,1},{8,14},{9,15},{10,... | collective-permute-start | bytes 49160 | tf_op jit(solution)/shard_map/ppermute | solution.py:599
  304.3 10.6 %collective-permute-start.73 = (f32[8,512]{1,0:T(8,128)S(1)}, f32[8,512]{1,0:T(8,128)S(1)}, u32[]{:S(2)}, u32[]{:S(2)}) collective-permute-start(f32[8,512]{1,0:T(8,128)S(1)} %add.900), channel_id=1, source_target_pairs={{0,4},{1,5},{2,6},{3,7},{4,0},{5,1},{6,2},{7,3},{8,12},{9,13},{10,... | collective-permute-start | bytes 49160 | tf_op jit(solution)/shard_map/ppermute | solution.py:599
  304.6 10.2 %collective-permute-start.72 = (f32[8,512]{1,0:T(8,128)S(1)}, f32[8,512]{1,0:T(8,128)S(1)}, u32[]{:S(2)}, u32[]{:S(2)}) collective-permute-start(f32[8,512]{1,0:T(8,128)S(1)} %add.900), channel_id=1, source_target_pairs={{0,2},{1,3},{2,0},{3,1},{4,6},{5,7},{6,4},{7,5},{8,10},{9,11},{10,... | collective-permute-start | bytes 49160 | tf_op jit(solution)/shard_map/ppermute | solution.py:599
  322.0 22.9 %collective-permute-start.84 = (bf16[2,2,2,64,512]{4,3,2,1,0:T(8,128)(2,1)S(1)}, bf16[2,2,2,64,512]{4,3,2,1,0:T(8,128)(2,1)S(1)}, u32[]{:S(2)}, u32[]{:S(2)}) collective-permute-start(bf16[2,2,2,64,512]{4,3,2,1,0:T(8,128)(2,1)S(1)} %get-tuple-element.168), channel_id=1, source_target_pairs={{0,2},{1,3},{2,0},{3,1},{4,6},{5,7},{6,4},{7,5},{8,10},{9,11},{10,... | collective-permute-start | bytes 1572872 | tf_op jit(solution)/shard_map/ppermute | solution.py:599
  322.6 22.5 %collective-permute-start.85 = (bf16[2,2,2,80,512]{4,3,2,1,0:T(8,128)(2,1)S(1)}, bf16[2,2,2,80,512]{4,3,2,1,0:T(8,128)(2,1)S(1)}, u32[]{:S(2)}, u32[]{:S(2)}) collective-permute-start(bf16[2,2,2,80,512]{4,3,2,1,0:T(8,128)(2,1)S(1)} %get-tuple-element.169), channel_id=1, source_target_pairs={{0,4},{1,5},{2,6},{3,7},{4,0},{5,1},{6,2},{7,3},{8,12},{9,13},{10,... | collective-permute-start | bytes 1966088 | tf_op jit(solution)/shard_map/ppermute | solution.py:599
  348.9 16.0 %collective-permute-start.91 = (bf16[2,2,2,64,256]{4,3,2,1,0:T(8,128)(2,1)S(1)}, bf16[2,2,2,64,256]{4,3,2,1,0:T(8,128)(2,1)S(1)}, u32[]{:S(2)}, u32[]{:S(2)}) collective-permute-start(bf16[2,2,2,64,256]{4,3,2,1,0:T(8,128)(2,1)S(1)} %fusion.13), channel_id=1, source_target_pairs={{0,4},{1,5},{2,6},{3,7},{4,0},{5,1},{6,2},{7,3},{8,12},{9,13},{10,... | collective-permute-start | bytes 786440 | tf_op jit(solution)/shard_map/ppermute | solution.py:599
  349.8 17.8 %collective-permute-start.96 = (bf16[2,2,64,512]{3,2,1,0:T(8,128)(2,1)S(1)}, bf16[2,2,64,512]{3,2,1,0:T(8,128)(2,1)S(1)}, u32[]{:S(2)}, u32[]{:S(2)}) collective-permute-start(bf16[2,2,64,512]{3,2,1,0:T(8,128)(2,1)S(1)} %get-tuple-element.180), channel_id=1, source_target_pairs={{0,4},{1,5},{2,6},{3,7},{4,0},{5,1},{6,2},{7,3},{8,12},{9,13},{10,... | collective-permute-start | bytes 786440 | tf_op jit(solution)/shard_map/ppermute | solution.py:599
  350.4 24.5 %collective-permute-start.97 = (bf16[2,2,80,512]{3,2,1,0:T(8,128)(2,1)S(1)}, bf16[2,2,80,512]{3,2,1,0:T(8,128)(2,1)S(1)}, u32[]{:S(2)}, u32[]{:S(2)}) collective-permute-start(bf16[2,2,80,512]{3,2,1,0:T(8,128)(2,1)S(1)} %get-tuple-element.181), channel_id=1, source_target_pairs={{0,2},{1,3},{2,0},{3,1},{4,6},{5,7},{6,4},{7,5},{8,10},{9,11},{10,... | collective-permute-start | bytes 983048 | tf_op jit(solution)/shard_map/ppermute | solution.py:599
  359.1 5.8 %collective-permute-start.90 = (f32[8,256]{1,0:T(8,128)S(1)}, f32[8,256]{1,0:T(8,128)S(1)}, u32[]{:S(2)}, u32[]{:S(2)}) collective-permute-start(f32[8,256]{1,0:T(8,128)S(1)} %get-tuple-element.174), channel_id=1, source_target_pairs={{0,1},{1,0},{2,3},{3,2},{4,5},{5,4},{6,7},{7,6},{8,9},{9,8},{10,11... | collective-permute-start | bytes 24584 | tf_op jit(solution)/shard_map/ppermute | solution.py:599
  364.9 6.3 %collective-permute-start.94 = (f32[8,256]{1,0:T(8,128)S(1)}, f32[8,256]{1,0:T(8,128)S(1)}, u32[]{:S(2)}, u32[]{:S(2)}) collective-permute-start(f32[8,256]{1,0:T(8,128)S(1)} %add.928), channel_id=1, source_target_pairs={{0,6},{1,7},{2,4},{3,5},{4,2},{5,3},{6,0},{7,1},{8,14},{9,15},{10,... | collective-permute-start | bytes 24584 | tf_op jit(solution)/shard_map/ppermute | solution.py:599
  366.3 8.6 %collective-permute-start.93 = (f32[8,256]{1,0:T(8,128)S(1)}, f32[8,256]{1,0:T(8,128)S(1)}, u32[]{:S(2)}, u32[]{:S(2)}) collective-permute-start(f32[8,256]{1,0:T(8,128)S(1)} %add.928), channel_id=1, source_target_pairs={{0,4},{1,5},{2,6},{3,7},{4,0},{5,1},{6,2},{7,3},{8,12},{9,13},{10,... | collective-permute-start | bytes 24584 | tf_op jit(solution)/shard_map/ppermute | solution.py:599
  366.8 8.0 %collective-permute-start.92 = (f32[8,256]{1,0:T(8,128)S(1)}, f32[8,256]{1,0:T(8,128)S(1)}, u32[]{:S(2)}, u32[]{:S(2)}) collective-permute-start(f32[8,256]{1,0:T(8,128)S(1)} %add.928), channel_id=1, source_target_pairs={{0,2},{1,3},{2,0},{3,1},{4,6},{5,7},{6,4},{7,5},{8,10},{9,11},{10,... | collective-permute-start | bytes 24584 | tf_op jit(solution)/shard_map/ppermute | solution.py:599
  367.7 7.2 %collective-permute-start.95 = (bf16[2,2,2,2,32,256]{5,4,3,0,1,2:T(8,128)(2,1)S(1)}, bf16[2,2,2,2,32,256]{5,4,3,0,1,2:T(8,128)(2,1)S(1)}, u32[]{:S(2)}, u32[]{:S(2)}) collective-permute-start(bf16[2,2,2,2,32,256]{5,4,3,0,1,2:T(8,128)(2,1)S(1)} %copy_bitcast_fusion), channel_id=1, source_target_pairs={{0,1},{1,0},{2,3},{3,2},{4,5},{5,4},{6,7},{7,6},{8,9},{9,8},{10,11... | collective-permute-start | bytes 786440 | tf_op jit(solution)/shard_map/ppermute | solution.py:599
  371.2 20.6 %collective-permute-start.98 = (bf16[192,1024]{1,0:T(8,128)(2,1)S(1)}, bf16[192,1024]{1,0:T(8,128)(2,1)S(1)}, u32[]{:S(2)}, u32[]{:S(2)}) collective-permute-start(bf16[192,1024]{1,0:T(8,128)(2,1)S(1)} %get-tuple-element.182), channel_id=1, source_target_pairs={{0,4},{4,8},{8,12},{12,16},{16,20},{20,24},{24,28},{1,5},{5,9},{9,... | collective-permute-start | bytes 1179656 | tf_op jit(solution)/shard_map/ppermute | solution.py:605
  395.4 13.7 %collective-permute-start.103 = (bf16[2,2,2,32,256]{4,3,2,0,1:T(8,128)(2,1)S(1)}, bf16[2,2,2,32,256]{4,3,2,0,1:T(8,128)(2,1)S(1)}, u32[]{:S(2)}, u32[]{:S(2)}) collective-permute-start(bf16[2,2,2,32,256]{4,3,2,0,1:T(8,128)(2,1)S(1)} %get-tuple-element.189), channel_id=1, source_target_pairs={{0,4},{1,5},{2,6},{3,7},{4,0},{5,1},{6,2},{7,3},{8,12},{9,13},{10,... | collective-permute-start | bytes 393224 | tf_op jit(solution)/shard_map/ppermute | solution.py:599
  403.1 6.0 %collective-permute-start.102 = (f32[8,256]{1,0:T(8,128)S(1)}, f32[8,256]{1,0:T(8,128)S(1)}, u32[]{:S(2)}, u32[]{:S(2)}) collective-permute-start(f32[8,256]{1,0:T(8,128)S(1)} %get-tuple-element.186), channel_id=1, source_target_pairs={{0,1},{1,0},{2,3},{3,2},{4,5},{5,4},{6,7},{7,6},{8,9},{9,8},{10,11... | collective-permute-start | bytes 24584 | tf_op jit(solution)/shard_map/ppermute | solution.py:599
  404.7 16.2 %collective-permute-start.108 = (bf16[2,64,512]{2,1,0:T(8,128)(2,1)S(1)}, bf16[2,64,512]{2,1,0:T(8,128)(2,1)S(1)}, u32[]{:S(2)}, u32[]{:S(2)}) collective-permute-start(bf16[2,64,512]{2,1,0:T(8,128)(2,1)S(1)} %get-tuple-element.192), channel_id=1, source_target_pairs={{0,8},{1,9},{2,10},{3,11},{4,12},{5,13},{6,14},{7,15},{8,0},{9,1},... | collective-permute-start | bytes 393224 | tf_op jit(solution)/shard_map/ppermute | solution.py:599
  406.3 10.9 %collective-permute-start.110 = (bf16[2,2,64,256]{3,2,1,0:T(8,128)(2,1)S(1)}, bf16[2,2,64,256]{3,2,1,0:T(8,128)(2,1)S(1)}, u32[]{:S(2)}, u32[]{:S(2)}) collective-permute-start(bf16[2,2,64,256]{3,2,1,0:T(8,128)(2,1)S(1)} %fusion.21), channel_id=1, source_target_pairs={{0,8},{1,9},{2,10},{3,11},{4,12},{5,13},{6,14},{7,15},{8,0},{9,1},... | collective-permute-start | bytes 393224 | tf_op jit(solution)/shard_map/ppermute | solution.py:599
  409.1 8.7 %collective-permute-start.106 = (f32[8,256]{1,0:T(8,128)S(1)}, f32[8,256]{1,0:T(8,128)S(1)}, u32[]{:S(2)}, u32[]{:S(2)}) collective-permute-start(f32[8,256]{1,0:T(8,128)S(1)} %add.946), channel_id=1, source_target_pairs={{0,6},{1,7},{2,4},{3,5},{4,2},{5,3},{6,0},{7,1},{8,14},{9,15},{10,... | collective-permute-start | bytes 24584 | tf_op jit(solution)/shard_map/ppermute | solution.py:599
  409.5 9.5 %collective-permute-start.105 = (f32[8,256]{1,0:T(8,128)S(1)}, f32[8,256]{1,0:T(8,128)S(1)}, u32[]{:S(2)}, u32[]{:S(2)}) collective-permute-start(f32[8,256]{1,0:T(8,128)S(1)} %add.946), channel_id=1, source_target_pairs={{0,4},{1,5},{2,6},{3,7},{4,0},{5,1},{6,2},{7,3},{8,12},{9,13},{10,... | collective-permute-start | bytes 24584 | tf_op jit(solution)/shard_map/ppermute | solution.py:599
  410.8 10.1 %collective-permute-start.104 = (f32[8,256]{1,0:T(8,128)S(1)}, f32[8,256]{1,0:T(8,128)S(1)}, u32[]{:S(2)}, u32[]{:S(2)}) collective-permute-start(f32[8,256]{1,0:T(8,128)S(1)} %add.946), channel_id=1, source_target_pairs={{0,2},{1,3},{2,0},{3,1},{4,6},{5,7},{6,4},{7,5},{8,10},{9,11},{10,... | collective-permute-start | bytes 24584 | tf_op jit(solution)/shard_map/ppermute | solution.py:599
  417.3 7.9 %collective-permute-start.107 = (bf16[2,2,2,2,72,256]{5,4,3,2,1,0:T(8,128)(2,1)S(1)}, bf16[2,2,2,2,72,256]{5,4,3,2,1,0:T(8,128)(2,1)S(1)}, u32[]{:S(2)}, u32[]{:S(2)}) collective-permute-start(bf16[2,2,2,2,72,256]{5,4,3,2,1,0:T(8,128)(2,1)S(1)} %dynamic-slice_bitcast_fusion.2), channel_id=1, source_target_pairs={{0,1},{1,0},{2,3},{3,2},{4,5},{5,4},{6,7},{7,6},{8,9},{9,8},{10,11... | collective-permute-start | bytes 1769480 | tf_op jit(solution)/shard_map/ppermute | solution.py:599
  417.9 7.2 %collective-permute-start.109 = (bf16[2,80,512]{2,1,0:T(8,128)(2,1)S(1)}, bf16[2,80,512]{2,1,0:T(8,128)(2,1)S(1)}, u32[]{:S(2)}, u32[]{:S(2)}) collective-permute-start(bf16[2,80,512]{2,1,0:T(8,128)(2,1)S(1)} %get-tuple-element.193), channel_id=1, source_target_pairs={{0,8},{1,9},{2,10},{3,11},{4,12},{5,13},{6,14},{7,15},{8,0},{9,1},... | collective-permute-start | bytes 491528 | tf_op jit(solution)/shard_map/ppermute | solution.py:599
  419.0 17.6 %collective-permute-start.111 = (bf16[192,1024]{1,0:T(8,128)(2,1)S(1)}, bf16[192,1024]{1,0:T(8,128)(2,1)S(1)}, u32[]{:S(2)}, u32[]{:S(2)}) collective-permute-start(bf16[192,1024]{1,0:T(8,128)(2,1)S(1)} %get-tuple-element.195), channel_id=1, source_target_pairs={{0,4},{4,8},{8,12},{12,16},{16,20},{20,24},{24,28},{1,5},{5,9},{9,... | collective-permute-start | bytes 1179656 | tf_op jit(solution)/shard_map/ppermute | solution.py:605
  440.2 9.8 %collective-permute-start.120 = (bf16[2,2,2,72,256]{4,3,2,1,0:T(8,128)(2,1)S(1)}, bf16[2,2,2,72,256]{4,3,2,1,0:T(8,128)(2,1)S(1)}, u32[]{:S(2)}, u32[]{:S(2)}) collective-permute-start(bf16[2,2,2,72,256]{4,3,2,1,0:T(8,128)(2,1)S(1)} %bitcast_add_fusion.5), channel_id=1, source_target_pairs={{0,4},{1,5},{2,6},{3,7},{4,0},{5,1},{6,2},{7,3},{8,12},{9,13},{10,... | collective-permute-start | bytes 884744 | tf_op jit(solution)/shard_map/ppermute | solution.py:599
  441.5 7.2 %collective-permute-start.122 = (bf16[2,2,32,256]{3,2,1,0:T(8,128)(2,1)S(1)}, bf16[2,2,32,256]{3,2,1,0:T(8,128)(2,1)S(1)}, u32[]{:S(2)}, u32[]{:S(2)}) collective-permute-start(bf16[2,2,32,256]{3,2,1,0:T(8,128)(2,1)S(1)} %add_bitcast_fusion.3), channel_id=1, source_target_pairs={{0,8},{1,9},{2,10},{3,11},{4,12},{5,13},{6,14},{7,15},{8,0},{9,1},... | collective-permute-start | bytes 196616 | tf_op jit(solution)/shard_map/ppermute | solution.py:599
  457.9 15.2 %collective-permute-start.123 = (bf16[2,200,256]{2,1,0:T(8,128)(2,1)S(1)}, bf16[2,200,256]{2,1,0:T(8,128)(2,1)S(1)}, u32[]{:S(2)}, u32[]{:S(2)}) collective-permute-start(bf16[2,200,256]{2,1,0:T(8,128)(2,1)S(1)} %dynamic-slice_bitcast_fusion.6), channel_id=1, source_target_pairs={{0,16},{1,17},{2,18},{3,19},{4,20},{5,21},{6,22},{7,23},{8,24},{9,... | collective-permute-start | bytes 614408 | tf_op jit(solution)/shard_map/ppermute | solution.py:599
  458.7 15.9 %collective-permute-start.126 = (bf16[64,512]{1,0:T(8,128)(2,1)S(1)}, bf16[64,512]{1,0:T(8,128)(2,1)S(1)}, u32[]{:S(2)}, u32[]{:S(2)}) collective-permute-start(bf16[64,512]{1,0:T(8,128)(2,1)S(1)} %fusion.27), channel_id=1, source_target_pairs={{0,16},{1,17},{2,18},{3,19},{4,20},{5,21},{6,22},{7,23},{8,24},{9,... | collective-permute-start | bytes 196616 | tf_op jit(solution)/shard_map/ppermute | solution.py:599
  460.4 20.4 %collective-permute-start.127 = (bf16[80,512]{1,0:T(8,128)(2,1)S(1)}, bf16[80,512]{1,0:T(8,128)(2,1)S(1)}, u32[]{:S(2)}, u32[]{:S(2)}) collective-permute-start(bf16[80,512]{1,0:T(8,128)(2,1)S(1)} %fusion.25), channel_id=1, source_target_pairs={{0,16},{1,17},{2,18},{3,19},{4,20},{5,21},{6,22},{7,23},{8,24},{9,... | collective-permute-start | bytes 245768 | tf_op jit(solution)/shard_map/ppermute | solution.py:599
  461.1 19.8 %collective-permute-start.119 = (bf16[192,1024]{1,0:T(8,128)(2,1)S(1)}, bf16[192,1024]{1,0:T(8,128)(2,1)S(1)}, u32[]{:S(2)}, u32[]{:S(2)}) collective-permute-start(bf16[192,1024]{1,0:T(8,128)(2,1)S(1)} %get-tuple-element.199), channel_id=1, source_target_pairs={{0,4},{4,8},{8,12},{12,16},{16,20},{20,24},{24,28},{1,5},{5,9},{9,... | collective-permute-start | bytes 1179656 | tf_op jit(solution)/shard_map/ppermute | solution.py:605
  473.2 6.1 %collective-permute-start.124 = (bf16[2,200,256]{2,1,0:T(8,128)(2,1)S(1)}, bf16[2,200,256]{2,1,0:T(8,128)(2,1)S(1)}, u32[]{:S(2)}, u32[]{:S(2)}) collective-permute-start(bf16[2,200,256]{2,1,0:T(8,128)(2,1)S(1)} %bitcast_add_fusion.6), channel_id=1, source_target_pairs={{0,2},{1,3},{2,0},{3,1},{4,6},{5,7},{6,4},{7,5},{8,10},{9,11},{10,... | collective-permute-start | bytes 614408 | tf_op jit(solution)/shard_map/ppermute | solution.py:599
  474.5 11.9 %collective-permute-start.118 = (bf16[3,192,256]{2,1,0:T(8,128)(2,1)S(1)}, bf16[3,192,256]{2,1,0:T(8,128)(2,1)S(1)}, u32[]{:S(2)}, u32[]{:S(2)}) collective-permute-start(bf16[3,192,256]{2,1,0:T(8,128)(2,1)S(1)} %slice.228), channel_id=1, source_target_pairs={{0,4},{4,8},{8,12},{12,16},{16,20},{20,24},{24,28},{1,5},{5,9},{9,... | collective-permute-start | bytes 884744 | tf_op jit(solution)/shard_map/ppermute | solution.py:605
  479.3 10.5 %collective-permute-start.125 = (bf16[2,200,256]{2,1,0:T(8,128)(2,1)S(1)}, bf16[2,200,256]{2,1,0:T(8,128)(2,1)S(1)}, u32[]{:S(2)}, u32[]{:S(2)}) collective-permute-start(bf16[2,200,256]{2,1,0:T(8,128)(2,1)S(1)} %add.986), channel_id=1, source_target_pairs={{0,1},{1,0},{2,3},{3,2},{4,5},{5,4},{6,7},{7,6},{8,9},{9,8},{10,11... | collective-permute-start | bytes 614408 | tf_op jit(solution)/shard_map/ppermute | solution.py:599
  492.4 7.2 %collective-permute-start.130 = (bf16[48,2048]{1,0:T(8,128)(2,1)}, bf16[48,2048]{1,0:T(8,128)(2,1)S(1)}, u32[]{:S(2)}, u32[]{:S(2)}) collective-permute-start(bf16[48,2048]{1,0:T(8,128)(2,1)} %reduce-scatter.2.cloned.1.call-done), channel_id=1, source_target_pairs={{0,2},{1,3},{2,0},{3,1},{4,6},{5,7},{6,4},{7,5},{8,10},{9,11},{10,... | collective-permute-start | bytes 589832 | tf_op jit(solution)/shard_map/ppermute | solution.py:599
  494.9 9.4 %collective-permute-start.129 = (bf16[2,144,512]{2,1,0:T(8,128)(2,1)S(1)}, bf16[2,144,512]{2,1,0:T(8,128)(2,1)S(1)}, u32[]{:S(2)}, u32[]{:S(2)}) collective-permute-start(bf16[2,144,512]{2,1,0:T(8,128)(2,1)S(1)} %pad_maximum_fusion.9), channel_id=1, source_target_pairs={{0,1},{1,0},{2,3},{3,2},{4,5},{5,4},{6,7},{7,6},{8,9},{9,8},{10,11... | collective-permute-start | bytes 884744 | tf_op jit(solution)/shard_map/ppermute | solution.py:599
  (158 other events, 1624.7 us)
Sparse Core Ops, SparseCore 0:
  11.5 78.4 all-gather.2
  93.4 74.3 all-gather.4
  305.8 127.2 reduce-scatter.1

commit v4 on v3

--- a/solution.py
+++ b/solution.py
@@ -1061,7 +1061,6 @@
         u3,
         b=dict(start=[chain_r2]),
         c=dict(finish=chain_rs + [chain_r2], start=chain_rs + [chain_r2]),
-        d=dict(start=[chain_ds[0]]),
     )
     d_pre_three, d_two, u2 = call(
         functools.partial(k_back_three, full_count), micro,
@@ -1074,8 +1073,8 @@
     u2 = global_sum(
         u2,
         b=dict(finish=[chain_r2], start=[chain_r3]),
-        c=dict(finish=chain_rs + [chain_ds[0], chain_r3], start=[chain_r3]),
-        d=dict(start=chain_rs + [chain_r2] + chain_ds[1:2]),
+        c=dict(finish=chain_rs + [chain_r3], start=[chain_r3]),
+        d=dict(start=chain_rs + [chain_r2]),
     )
     d_pre_two, d_one, u1 = call(
         functools.partial(k_back_two, full_count), micro,
@@ -1090,8 +1089,8 @@
     u1 = global_sum(
         u1,
         b=dict(finish=[chain_r3], start=[chain_r1]),
-        c=dict(finish=chain_rs + [chain_r2, chain_r1] + chain_ds[1:2], start=[chain_r1]),
-        d=dict(start=chain_rs + [chain_r3] + chain_ds[2:]),
+        c=dict(finish=chain_rs + [chain_r2, chain_r1], start=[chain_r1]),
+        d=dict(start=chain_rs + [chain_r3] + chain_ds[:1]),
     )
     (d_pre_one,) = call(
         functools.partial(k_back_one, full_count), micro,
@@ -1112,9 +1111,9 @@
     chain_last = Chain(reduce_last(jnp.concatenate(firsts, -2)))
     chain_dp = Chain(one_step(d_pre_one[:, mine : mine + more], lambda x: from_behind(x, 1)))
     chain_last.launch(chain_last.ready[0])
-    hook(landed, start=[chain_dp])
     landed = chain_last.flying
     chain_last.land()
+    hook(landed, start=[chain_dp] + chain_ds[1:])
     chain_r4 = Chain(spread_steps(jnp.concatenate([c.value() for c in chain_rs], 0)))
     hook(landed, start=[chain_rb, chain_r4])
     chain_last.launch(chain_last.ready[0])
@@ -1131,7 +1130,7 @@
         + [(c.value(), "w") for c in chain_ds],
         [((micro, own * across * channels // LANES, LANES), F32, "m")],
         [((mine, m1), BF), ((mine, channels), F32)],
-        after=[landed],
+        after=[landed, chain_last.value(), chain_r4.value(), chain_rb.value()],
     )
     grad_input = grad_input.reshape(features.shape)
     added = lambda k, us: jnp.concatenate([u[k] + u[k + 2] + u[k + 4] for u in us])

time: 524 us -> 514 us (0.981)
  waiting for transfers between devices: 138 us -> 115 us
  starting transfers between devices: 168 us -> 179 us
    ppermute x8, waiting for transfers between devices: 54.6 us -> 13.4 us  [from_behind(): return lax.ppermute(x, 'rows', pairs)]
    ppermute x124, waiting for transfers between devices: 82.9 us -> 102 us  [exchange(): return lax.ppermute(x, AXES, [(i, i ^ mask) for i in range(total)])]
    ppermute x8, starting transfers between devices: 21.9 us -> 29.1 us  [from_behind(): return lax.ppermute(x, 'rows', pairs)]
    unnamed x176 -> x180, local copies, waits for them, and re-layouts: 37.4 us -> 37.3 us
  transfers between devices with their start and end apart: 135 -> 135, of which waited for: 63 -> 61; matrix products, arithmetic and copies ran while one was open for 9% -> 10% of each run, Pallas kernels for 13% -> 13%
where the time goes in v4:
time: 514 us; the launch traced here: 507 us
  starting transfers between devices  179 us (35%)
  waiting for transfers between devices  115 us (22%)
  Pallas kernels  100 us (19%)
  local copies, waits for them, and re-layouts  54.6 us (11%)
  other arithmetic  25.5 us (5%)
  matrix products  16.9 us (3%)
  between operations  16 us (3%)
    ppermute x124, starting transfers between devices, exchange(): return lax.ppermute(x, AXES, [(i, i ^ mask) for i in range(total)])  150 us
    ppermute x124, waiting for transfers between devices, exchange(): return lax.ppermute(x, AXES, [(i, i ^ mask) for i in range(total)])  102 us
    pallas_call x16, Pallas kernels, call(): pl.pallas_call(run, grid=(micro,), in_specs=in_specs, out_specs=out_specs...  93.4 us
    unnamed x180, local copies, waits for them, and re-layouts  37.3 us
    ppermute x8, starting transfers between devices, from_behind(): return lax.ppermute(x, 'rows', pairs)  29.1 us
    dot_general x8, matrix products, weight_term(): lax.dot_general(left.reshape(-1, k), right.reshape(-1, n), (((0,), (0,)),...  16.9 us
    ppermute x8, waiting for transfers between devices, from_behind(): return lax.ppermute(x, 'rows', pairs)  13.4 us
  transfers between devices with their start and end apart: 135, of which 61 were waited for; matrix products, arithmetic and copies ran while one was open for 10% of the time, Pallas kernels for 13%

profile of v4, /device:TPU:25, one launch (start us, length us, event | category | flops | bytes accessed | tf_op | source)
XLA Modules:
  0.0 507.4 jit_solution(41922775789602261)
XLA Ops:
  12.2 3.4 k_masks.1
  29.9 2.7 collective-permute-start.3
  45.3 2.7 collective-permute-start.14
  48.9 2.7 collective-permute-start.11
  52.1 4.5 collective-permute-done.11.refs_1_.refs_9_.refs_2_
  56.6 10.4 %collective-permute-start.16 = (bf16[2,2,2,2,72,256]{5,4,3,2,1,0:T(8,128)(2,1)S(1)}, bf16[2,2,2,2,72,256]{5,4,3,2,1,0:T(8,128)(2,1)S(1)}, u32[]{:S(2)}, u32[]{:S(2)}) collective-permute-start(bf16[2,2,2,2,72,256]{5,4,3,2,1,0:T(8,128)(2,1)S(1)} %pad_maximum_fusion.3), channel_id=1, source_target_pairs={{0,1},{1,0},{2,3},{3,2},{4,5},{5,4},{6,7},{7,6},{8,9},{9,8},{10,11... | collective-permute-start | bytes 1769480 | tf_op jit(solution)/shard_map/ppermute | solution.py:599
  68.6 5.2 %collective-permute-start.21 = (bf16[12,14,1024]{2,1,0:T(8,128)(2,1)S(1)}, bf16[12,14,1024]{2,1,0:T(8,128)(2,1)S(1)}, u32[]{:S(2)}, u32[]{:S(2)}) collective-permute-start(bf16[12,14,1024]{2,1,0:T(8,128)(2,1)S(1)} %get-tuple-element.127), channel_id=1, source_target_pairs={{4,0},{8,4},{12,8},{16,12},{20,16},{24,20},{28,24},{5,1},{9,5},{13... | collective-permute-start | bytes 1032200 | tf_op jit(solution)/shard_map/ppermute | solution.py:605
  73.8 7.4 %collective-permute-start.22 = (bf16[12,14,1024]{2,1,0:T(8,128)(2,1)S(1)}, bf16[12,14,1024]{2,1,0:T(8,128)(2,1)S(1)}, u32[]{:S(2)}, u32[]{:S(2)}) collective-permute-start(bf16[12,14,1024]{2,1,0:T(8,128)(2,1)S(1)} %get-tuple-element.128), channel_id=1, source_target_pairs={{4,0},{8,4},{12,8},{16,12},{20,16},{24,20},{28,24},{5,1},{9,5},{13... | collective-permute-start | bytes 1032200 | tf_op jit(solution)/shard_map/ppermute | solution.py:605
  81.2 5.3 %collective-permute-start.23 = (bf16[12,14,1024]{2,1,0:T(8,128)(2,1)S(1)}, bf16[12,14,1024]{2,1,0:T(8,128)(2,1)S(1)}, u32[]{:S(2)}, u32[]{:S(2)}) collective-permute-start(bf16[12,14,1024]{2,1,0:T(8,128)(2,1)S(1)} %get-tuple-element.129), channel_id=1, source_target_pairs={{4,0},{8,4},{12,8},{16,12},{20,16},{24,20},{28,24},{5,1},{9,5},{13... | collective-permute-start | bytes 1032200 | tf_op jit(solution)/shard_map/ppermute | solution.py:605
  86.8 5.6 %k_second.1 = (f32[3,640,256]{2,1,0:T(8,128)S(1)}, bf16[3,640,2304]{2,1,0:T(8,128)(2,1)S(1)}, f32[8,256]{1,0:T(8,128)S(1)}) custom-call(f32[3,416,256]{2,1,0:T(8,128)S(1)} %copy-done.19, bf16[3,192,256]{2,1,0:T(8,128)(2,1)S(1)} %collective-permute-done.11.refs_1_.refs_9_.refs_2_, f32[8,256]{1,0:T(8,128)S(1)} %add_add_fusion.22.refs_2_.refs_10_.refs_3_, ...), custom_call_target="tpu_custom_call" | custom-call | tf_op jit(solution)/shard_map/k_second/pallas_call | solution.py:853
  92.4 3.4 copy-done.68
  97.5 2.1 collective-permute-start.19
  100.2 7.1 %collective-permute-done.23.refs_4_ = bf16[12,14,1024]{2,1,0:T(8,128)(2,1)S(1)} collective-permute-done((bf16[12,14,1024]{2,1,0:T(8,128)(2,1)S(1)}, bf16[12,14,1024]{2,1,0:T(8,128)(2,1)S(1)}, u32[]{:S(2)}, u32[]{:S(2)}) %collective-permute-start.23) | collective-permute-done | bytes 344096 | tf_op jit(solution)/shard_map/ppermute | solution.py:605
  110.7 4.9 collective-permute-start.25
  119.5 6.0 %k_third.2 = (bf16[3,640,256]{2,1,0:T(8,128)(2,1)S(1)}, bf16[3,640,1024]{2,1,0:T(8,128)(2,1)S(1)}, f32[8,1024]{1,0:T(8,128)S(1)}) custom-call(f32[3,640,256]{2,1,0:T(8,128)S(1)} %get-tuple-element.125.refs_0_.refs_7_.refs_1_, f32[8,256]{1,0:T(8,128)S(1)} %add_add_fusion.20.refs_1_.refs_8_.refs_2_, f32[1,256]{1,0:T(1,128)S(1)} %bitcast.441, ...), custom_call_target="tpu_custom_call" | custom-call | tf_op jit(solution)/shard_map/k_third/pallas_call | solution.py:853
  126.5 2.3 collective-permute-start.27
  129.7 2.9 collective-permute-start.30
  135.4 2.8 collective-permute-start.33
  140.7 4.4 collective-permute-done.32
  145.1 10.7 %k_fourth.1 = (bf16[3,640,1024]{2,1,0:T(8,128)(2,1)S(1)}, bf16[3,160,1024]{2,1,0:T(8,128)(2,1)S(1)}, bf16[3,640,1024]{2,1,0:T(8,128)(2,1)S(1)}, bf16[3,640,512]{2,1,0:T(8,128)(2,1)S(1)}, f32[8,512]{1,0:T(8,128)S(1)}) custom-call(bf16[3,640,1024]{2,1,0:T(8,128)(2,1)S(1)} %get-tuple-element.131.refs_0_.refs_8_.refs_1_, bf16[3,640,1024]{2,1,0:T(8,128)(2,1)S(1)} %copy-done.14, ...), custom_call_target="tpu_custom_call" | custom-call | tf_op jit(solution)/shard_map/k_fourth/pallas_call | solution.py:853
  168.1 2.3 collective-permute-start.38
  171.8 6.6 %k_fifth.1 = (f32[3,160,512]{2,1,0:T(8,128)S(1)}, bf16[3,160,4608]{2,1,0:T(8,128)(2,1)S(1)}, f32[8,512]{1,0:T(8,128)S(1)}) custom-call(bf16[3,640,512]{2,1,0:T(8,128)(2,1)S(1)} %get-tuple-element.133.refs_0_.refs_8_.refs_1_, f32[8,512]{1,0:T(8,128)S(1)} %add_add_fusion.14.refs_1_.refs_9_.refs_2_, f32[1,512]{1,0:T(1,128)S(1)} %bitcast.426, ...), custom_call_target="tpu_custom_call" | custom-call | tf_op jit(solution)/shard_map/k_fifth/pallas_call | solution.py:853
  179.4 3.0 collective-permute-start.41
  183.2 2.6 collective-permute-start.44
  192.4 2.8 copy-done
  195.1 3.3 k_seventh.1
  198.5 4.1 k_third.3
  206.8 3.3 collective-permute-start.48
  216.0 2.1 collective-permute-done.50
  223.1 3.8 collective-permute-done.53
  233.6 8.2 %k_last.1 = (bf16[3,1,19,7,2048]{4,3,2,1,0:T(8,128)(2,1)}, bf16[3,160,2048]{2,1,0:T(8,128)(2,1)S(1)}, f32[8,4096]{1,0:T(8,128)S(1)}) custom-call(bf16[3,160,2048]{2,1,0:T(8,128)(2,1)S(1)} %copy-done.35, bf16[3,160,2048]{2,1,0:T(8,128)(2,1)S(1)} %copy-done.33, f32[8,2048]{1,0:T(8,128)S(1)} %get-tuple-element.316.refs_2_.refs_3_, ...), custom_call_target="tpu_custom_call" | custom-call | tf_op jit(solution)/shard_map/k_last/pallas_call | solution.py:853
  250.6 2.2 collective-permute-start.60
  254.3 3.5 collective-permute-done.61
  259.5 7.4 %k_back_six.1 = (bf16[3,160,2048]{2,1,0:T(8,128)(2,1)S(1)}, bf16[3,160,2048]{2,1,0:T(8,128)(2,1)S(1)}, f32[3,160,512]{2,1,0:T(8,128)S(1)}, f32[8,512]{1,0:T(8,128)S(1)}) custom-call(bf16[3,160,2048]{2,1,0:T(8,128)(2,1)S(1)} %get-tuple-element.145.refs_0_, bf16[3,160,2048]{2,1,0:T(8,128)(2,1)S(1)} %copy-done.35, bf16[3,160,2048]{2,1,0:T(8,128)(2,1)S(1)} %copy-done.33, ...), custom_call_target="tpu_custom_call" | custom-call | tf_op jit(solution)/shard_map/k_back_six/pallas_call | solution.py:853
  267.3 2.4 bitcast_convert_fusion.1
  273.8 3.5 pad_maximum_fusion
  282.5 2.8 copy-done.6
  288.6 10.1 %k_back_five.1 = (bf16[3,160,512]{2,1,0:T(8,128)(2,1)S(1)}, f32[3,640,512]{2,1,0:T(8,128)S(1)}, f32[8,512]{1,0:T(8,128)S(1)}) custom-call(f32[3,160,512]{2,1,0:T(8,128)S(1)} %copy-done.55, f32[3,160,512]{2,1,0:T(8,128)S(1)} %copy-done.28, f32[8,512]{1,0:T(8,128)S(1)} %add_add_fusion.12.refs_1_.refs_9_.refs_2_, f32[8,512]{1,0:T(8,128)S(1)} %add_add_fusion.10.refs_3_, ...), custom_call_target="tpu_custom_call" | custom-call | tf_op jit(solution)/shard_map/k_back_five/pallas_call | solution.py:853
  300.7 5.3 %bitcast_convert_fusion = bf16[4608,512]{1,0:T(8,128)(2,1)S(1)} fusion(bf16[3,160,4608]{2,1,0:T(8,128)(2,1)} %copy-done.69, bf16[3,160,512]{2,1,0:T(8,128)(2,1)S(1)} %get-tuple-element.156), kind=kOutput, calls=%fused_computation | convolution fusion | flops 2267283456 | bytes 9633792 | tf_op jit(solution)/shard_map/dot_general | solution.py:869
  306.4 2.5 collective-permute-start.71
  311.7 2.8 copy-done.2
  316.0 4.8 k_corner.1.refs_7_
  334.8 8.4 %k_back_four.1 = (bf16[3,640,512]{2,1,0:T(8,128)(2,1)S(1)}, bf16[3,640,1024]{2,1,0:T(8,128)(2,1)S(1)}, f32[8,1024]{1,0:T(8,128)S(1)}) custom-call(f32[3,640,512]{2,1,0:T(8,128)S(1)} %copy-done.44, bf16[3,640,512]{2,1,0:T(8,128)(2,1)S(1)} %copy-done.12, f32[8,512]{1,0:T(8,128)S(1)} %add_add_fusion.14.refs_1_.refs_9_.refs_2_, ...), custom_call_target="tpu_custom_call" | custom-call | tf_op jit(solution)/shard_map/k_back_four/pallas_call | solution.py:853
  345.8 3.6 collective-permute-start.80
  363.1 7.7 %k_back_three.1 = (bf16[3,640,1024]{2,1,0:T(8,128)(2,1)S(1)}, f32[3,640,256]{2,1,0:T(8,128)S(1)}, f32[8,256]{1,0:T(8,128)S(1)}) custom-call(bf16[3,640,1024]{2,1,0:T(8,128)(2,1)S(1)} %get-tuple-element.162.refs_0_.refs_2_, bf16[3,640,1024]{2,1,0:T(8,128)(2,1)S(1)} %copy-done.5, f32[8,1024]{1,0:T(8,128)S(1)} %add_add_fusion.6.refs_2_.refs_10_, ...), custom_call_target="tpu_custom_call" | custom-call | tf_op jit(solution)/shard_map/k_back_three/pallas_call | solution.py:853
  370.8 5.5 %collective-permute-start.90 = (f32[8,256]{1,0:T(8,128)S(1)}, f32[8,256]{1,0:T(8,128)S(1)}, u32[]{:S(2)}, u32[]{:S(2)}) collective-permute-start(f32[8,256]{1,0:T(8,128)S(1)} %get-tuple-element.172), channel_id=1, source_target_pairs={{0,1},{1,0},{2,3},{3,2},{4,5},{5,4},{6,7},{7,6},{8,9},{9,8},{10,11... | collective-permute-start | bytes 24584 | tf_op jit(solution)/shard_map/ppermute | solution.py:599
  380.5 3.5 collective-permute-done.96
  384.0 3.0 collective-permute-start.95
  389.4 2.4 collective-permute-start.98
  394.8 5.8 %k_back_two.1 = (bf16[3,640,256]{2,1,0:T(8,128)(2,1)S(1)}, f32[3,640,256]{2,1,0:T(8,128)S(1)}, f32[8,256]{1,0:T(8,128)S(1)}) custom-call(f32[3,640,256]{2,1,0:T(8,128)S(1)} %get-tuple-element.171.refs_0_, f32[3,640,256]{2,1,0:T(8,128)S(1)} %copy-done.10, f32[8,256]{1,0:T(8,128)S(1)} %add_add_fusion.20.refs_1_.refs_8_.refs_2_, ...), custom_call_target="tpu_custom_call" | custom-call | tf_op jit(solution)/shard_map/k_back_two/pallas_call | solution.py:853
  402.6 2.8 fusion
  408.2 7.3 %collective-permute-done.109 = bf16[2,2,64,256]{3,2,1,0:T(8,128)(2,1)S(1)} collective-permute-done((bf16[2,2,64,256]{3,2,1,0:T(8,128)(2,1)S(1)}, bf16[2,2,64,256]{3,2,1,0:T(8,128)(2,1)S(1)}, u32[]{:S(2)}, u32[]{:S(2)}) %collective-permute-start.109) | collective-permute-done | bytes 131104 | tf_op jit(solution)/shard_map/ppermute | solution.py:599
  416.9 5.7 %collective-permute-done.108 = bf16[2,80,512]{2,1,0:T(8,128)(2,1)S(1)} collective-permute-done((bf16[2,80,512]{2,1,0:T(8,128)(2,1)S(1)}, bf16[2,80,512]{2,1,0:T(8,128)(2,1)S(1)}, u32[]{:S(2)}, u32[]{:S(2)}) %collective-permute-start.108) | collective-permute-done | bytes 163872 | tf_op jit(solution)/shard_map/ppermute | solution.py:599
  432.7 2.4 collective-permute-start.113
  437.7 3.4 collective-permute-done.114
  441.4 2.9 collective-permute-done.115
  448.3 2.6 collective-permute-start.121
  451.5 8.1 %collective-permute-done.119 = bf16[2,200,256]{2,1,0:T(8,128)(2,1)S(1)} collective-permute-done((bf16[2,200,256]{2,1,0:T(8,128)(2,1)S(1)}, bf16[2,200,256]{2,1,0:T(8,128)(2,1)S(1)}, u32[]{:S(2)}, u32[]{:S(2)}) %collective-permute-start.119) | collective-permute-done | bytes 204832 | tf_op jit(solution)/shard_map/ppermute | solution.py:599
  461.0 4.4 collective-permute-done.124.refs_7_
  468.0 2.1 collective-permute-start.120
  478.3 3.6 collective-permute-done.128
  483.0 4.3 collective-permute-done.130
  487.4 2.1 collective-permute-start.129
  496.5 4.3 k_input.1
  (570 shorter events, 209.9 us)
Async XLA Ops:
  7.2 111.2 %all-gather.3.cloned.1.call-start = ((), (), s32[]{:S(2)}) async-start(), calls=%async_computation.1 | async-start | bytes 6488064 | tf_op jit(solution)/shard_map/all_gather | solution.py:722
  8.9 183.5 %all-gather.5.cloned.1.call-start = ((), (), s32[]{:S(2)}) async-start(), calls=%async_computation.2 | async-start | bytes 6488064 | tf_op jit(solution)/shard_map/all_gather | solution.py:722
  10.6 466.0 %reduce-scatter.2.cloned.1.call-start = ((), (), s32[]{:S(2)}) async-start(), calls=%async_computation.3 | async-start | bytes 6488064 | tf_op jit(solution)/shard_map/reduce_scatter | solution.py:1029
  21.2 5.9 %collective-permute-start.5 = (bf16[72,256]{1,0:T(8,128)(2,1)}, bf16[72,256]{1,0:T(8,128)(2,1)}, u32[]{:S(2)}, u32[]{:S(2)}) collective-permute-start(bf16[72,256]{1,0:T(8,128)(2,1)} %dynamic-slice_bitcast_fusion.7), channel_id=1, source_target_pairs={{0,16},{1,17},{2,18},{3,19},{4,20},{5,21},{6,22},{7,23},{8,24},{9,... | collective-permute-start | bytes 110600 | tf_op jit(solution)/shard_map/ppermute | solution.py:599
  32.7 6.1 %collective-permute-start.7 = (bf16[2,2,72,256]{3,2,1,0:T(8,128)(2,1)S(1)}, bf16[2,2,72,256]{3,2,1,0:T(8,128)(2,1)S(1)}, u32[]{:S(2)}, u32[]{:S(2)}) collective-permute-start(bf16[2,2,72,256]{3,2,1,0:T(8,128)(2,1)S(1)} %pad_maximum_fusion.13), channel_id=1, source_target_pairs={{0,4},{1,5},{2,6},{3,7},{4,0},{5,1},{6,2},{7,3},{8,12},{9,13},{10,... | collective-permute-start | bytes 442376 | tf_op jit(solution)/shard_map/ppermute | solution.py:599
  45.0 7.0 %collective-permute-start.15 = (bf16[2,2,2,72,256]{4,3,2,1,0:T(8,128)(2,1)S(1)}, bf16[2,2,2,72,256]{4,3,2,1,0:T(8,128)(2,1)S(1)}, u32[]{:S(2)}, u32[]{:S(2)}) collective-permute-start(bf16[2,2,2,72,256]{4,3,2,1,0:T(8,128)(2,1)S(1)} %pad_maximum_fusion.9), channel_id=1, source_target_pairs={{0,2},{1,3},{2,0},{3,1},{4,6},{5,7},{6,4},{7,5},{8,10},{9,11},{10,... | collective-permute-start | bytes 884744 | tf_op jit(solution)/shard_map/ppermute | solution.py:599
  45.3 6.2 %collective-permute-start.14 = (f32[8,256]{1,0:T(8,128)S(1)}, f32[8,256]{1,0:T(8,128)S(1)}, u32[]{:S(2)}, u32[]{:S(2)}) collective-permute-start(f32[8,256]{1,0:T(8,128)S(1)} %add_add_fusion.23), channel_id=1, source_target_pairs={{0,24},{1,25},{2,26},{3,27},{4,28},{5,29},{6,30},{7,31},{8,16},{9,... | collective-permute-start | bytes 24584 | tf_op jit(solution)/shard_map/ppermute | solution.py:599
  48.9 7.7 %collective-permute-start.11 = (bf16[3,192,256]{2,1,0:T(8,128)(2,1)}, bf16[3,192,256]{2,1,0:T(8,128)(2,1)S(1)}, u32[]{:S(2)}, u32[]{:S(2)}) collective-permute-start(bf16[3,192,256]{2,1,0:T(8,128)(2,1)} %copy-done.74), channel_id=1, source_target_pairs={{4,0},{8,4},{12,8},{16,12},{20,16},{24,20},{28,24},{5,1},{9,5},{13... | collective-permute-start | bytes 884744 | tf_op jit(solution)/shard_map/ppermute | solution.py:605
  56.6 29.9 %collective-permute-start.16 = (bf16[2,2,2,2,72,256]{5,4,3,2,1,0:T(8,128)(2,1)S(1)}, bf16[2,2,2,2,72,256]{5,4,3,2,1,0:T(8,128)(2,1)S(1)}, u32[]{:S(2)}, u32[]{:S(2)}) collective-permute-start(bf16[2,2,2,2,72,256]{5,4,3,2,1,0:T(8,128)(2,1)S(1)} %pad_maximum_fusion.3), channel_id=1, source_target_pairs={{0,1},{1,0},{2,3},{3,2},{4,5},{5,4},{6,7},{7,6},{8,9},{9,8},{10,11... | collective-permute-start | bytes 1769480 | tf_op jit(solution)/shard_map/ppermute | solution.py:599
  68.6 31.1 %collective-permute-start.21 = (bf16[12,14,1024]{2,1,0:T(8,128)(2,1)S(1)}, bf16[12,14,1024]{2,1,0:T(8,128)(2,1)S(1)}, u32[]{:S(2)}, u32[]{:S(2)}) collective-permute-start(bf16[12,14,1024]{2,1,0:T(8,128)(2,1)S(1)} %get-tuple-element.127), channel_id=1, source_target_pairs={{4,0},{8,4},{12,8},{16,12},{20,16},{24,20},{28,24},{5,1},{9,5},{13... | collective-permute-start | bytes 1032200 | tf_op jit(solution)/shard_map/ppermute | solution.py:605
  73.8 26.4 %collective-permute-start.22 = (bf16[12,14,1024]{2,1,0:T(8,128)(2,1)S(1)}, bf16[12,14,1024]{2,1,0:T(8,128)(2,1)S(1)}, u32[]{:S(2)}, u32[]{:S(2)}) collective-permute-start(bf16[12,14,1024]{2,1,0:T(8,128)(2,1)S(1)} %get-tuple-element.128), channel_id=1, source_target_pairs={{4,0},{8,4},{12,8},{16,12},{20,16},{24,20},{28,24},{5,1},{9,5},{13... | collective-permute-start | bytes 1032200 | tf_op jit(solution)/shard_map/ppermute | solution.py:605
  81.2 26.0 %collective-permute-start.23 = (bf16[12,14,1024]{2,1,0:T(8,128)(2,1)S(1)}, bf16[12,14,1024]{2,1,0:T(8,128)(2,1)S(1)}, u32[]{:S(2)}, u32[]{:S(2)}) collective-permute-start(bf16[12,14,1024]{2,1,0:T(8,128)(2,1)S(1)} %get-tuple-element.129), channel_id=1, source_target_pairs={{4,0},{8,4},{12,8},{16,12},{20,16},{24,20},{28,24},{5,1},{9,5},{13... | collective-permute-start | bytes 1032200 | tf_op jit(solution)/shard_map/ppermute | solution.py:605
  97.5 12.5 %collective-permute-start.20 = (f32[8,256]{1,0:T(8,128)S(1)}, f32[8,256]{1,0:T(8,128)S(1)}, u32[]{:S(2)}, u32[]{:S(2)}) collective-permute-start(f32[8,256]{1,0:T(8,128)S(1)} %add.849), channel_id=1, source_target_pairs={{0,6},{1,7},{2,4},{3,5},{4,2},{5,3},{6,0},{7,1},{8,14},{9,15},{10,... | collective-permute-start | bytes 24584 | tf_op jit(solution)/shard_map/ppermute | solution.py:599
  97.5 12.5 %collective-permute-start.19 = (f32[8,256]{1,0:T(8,128)S(1)}, f32[8,256]{1,0:T(8,128)S(1)}, u32[]{:S(2)}, u32[]{:S(2)}) collective-permute-start(f32[8,256]{1,0:T(8,128)S(1)} %add.849), channel_id=1, source_target_pairs={{0,4},{1,5},{2,6},{3,7},{4,0},{5,1},{6,2},{7,3},{8,12},{9,13},{10,... | collective-permute-start | bytes 24584 | tf_op jit(solution)/shard_map/ppermute | solution.py:599
  99.6 10.4 %collective-permute-start.18 = (f32[8,256]{1,0:T(8,128)S(1)}, f32[8,256]{1,0:T(8,128)S(1)}, u32[]{:S(2)}, u32[]{:S(2)}) collective-permute-start(f32[8,256]{1,0:T(8,128)S(1)} %add.849), channel_id=1, source_target_pairs={{0,2},{1,3},{2,0},{3,1},{4,6},{5,7},{6,4},{7,5},{8,10},{9,11},{10,... | collective-permute-start | bytes 24584 | tf_op jit(solution)/shard_map/ppermute | solution.py:599
  110.1 5.5 %collective-permute-start.26 = (f32[8,256]{1,0:T(8,128)S(1)}, f32[8,256]{1,0:T(8,128)S(1)}, u32[]{:S(2)}, u32[]{:S(2)}) collective-permute-start(f32[8,256]{1,0:T(8,128)S(1)} %add_add_fusion.21), channel_id=1, source_target_pairs={{0,24},{1,25},{2,26},{3,27},{4,28},{5,29},{6,30},{7,31},{8,16},{9,... | collective-permute-start | bytes 24584 | tf_op jit(solution)/shard_map/ppermute | solution.py:599
  110.7 6.0 %collective-permute-start.25 = (f32[8,256]{1,0:T(8,128)S(1)}, f32[8,256]{1,0:T(8,128)S(1)}, u32[]{:S(2)}, u32[]{:S(2)}) collective-permute-start(f32[8,256]{1,0:T(8,128)S(1)} %add_add_fusion.21), channel_id=1, source_target_pairs={{0,16},{1,17},{2,18},{3,19},{4,20},{5,21},{6,22},{7,23},{8,24},{9,... | collective-permute-start | bytes 24584 | tf_op jit(solution)/shard_map/ppermute | solution.py:599
  135.4 5.3 %collective-permute-start.33 = (f32[8,1024]{1,0:T(8,128)S(1)}, f32[8,1024]{1,0:T(8,128)S(1)}, u32[]{:S(2)}, u32[]{:S(2)}) collective-permute-start(f32[8,1024]{1,0:T(8,128)S(1)} %add_add_fusion.7), channel_id=1, source_target_pairs={{0,24},{1,25},{2,26},{3,27},{4,28},{5,29},{6,30},{7,31},{8,16},{9,... | collective-permute-start | bytes 98312 | tf_op jit(solution)/shard_map/ppermute | solution.py:599
  138.2 6.9 %collective-permute-start.32 = (f32[8,1024]{1,0:T(8,128)S(1)}, f32[8,1024]{1,0:T(8,128)S(1)}, u32[]{:S(2)}, u32[]{:S(2)}) collective-permute-start(f32[8,1024]{1,0:T(8,128)S(1)} %add_add_fusion.7), channel_id=1, source_target_pairs={{0,16},{1,17},{2,18},{3,19},{4,20},{5,21},{6,22},{7,23},{8,24},{9,... | collective-permute-start | bytes 98312 | tf_op jit(solution)/shard_map/ppermute | solution.py:599
  138.2 6.9 %collective-permute-start.31 = (f32[8,1024]{1,0:T(8,128)S(1)}, f32[8,1024]{1,0:T(8,128)S(1)}, u32[]{:S(2)}, u32[]{:S(2)}) collective-permute-start(f32[8,1024]{1,0:T(8,128)S(1)} %add_add_fusion.7), channel_id=1, source_target_pairs={{0,8},{1,9},{2,10},{3,11},{4,12},{5,13},{6,14},{7,15},{8,0},{9,1},... | collective-permute-start | bytes 98312 | tf_op jit(solution)/shard_map/ppermute | solution.py:599
  188.7 9.7 %collective-permute-start.47 = (f32[8,512]{1,0:T(8,128)S(1)}, f32[8,512]{1,0:T(8,128)S(1)}, u32[]{:S(2)}, u32[]{:S(2)}) collective-permute-start(f32[8,512]{1,0:T(8,128)S(1)} %add_add_fusion.13), channel_id=1, source_target_pairs={{0,24},{1,25},{2,26},{3,27},{4,28},{5,29},{6,30},{7,31},{8,16},{9,... | collective-permute-start | bytes 49160 | tf_op jit(solution)/shard_map/ppermute | solution.py:599
  190.6 7.8 %collective-permute-start.46 = (f32[8,512]{1,0:T(8,128)S(1)}, f32[8,512]{1,0:T(8,128)S(1)}, u32[]{:S(2)}, u32[]{:S(2)}) collective-permute-start(f32[8,512]{1,0:T(8,128)S(1)} %add_add_fusion.13), channel_id=1, source_target_pairs={{0,16},{1,17},{2,18},{3,19},{4,20},{5,21},{6,22},{7,23},{8,24},{9,... | collective-permute-start | bytes 49160 | tf_op jit(solution)/shard_map/ppermute | solution.py:599
  191.5 7.0 %collective-permute-start.45 = (f32[8,512]{1,0:T(8,128)S(1)}, f32[8,512]{1,0:T(8,128)S(1)}, u32[]{:S(2)}, u32[]{:S(2)}) collective-permute-start(f32[8,512]{1,0:T(8,128)S(1)} %add_add_fusion.13), channel_id=1, source_target_pairs={{0,8},{1,9},{2,10},{3,11},{4,12},{5,13},{6,14},{7,15},{8,0},{9,1},... | collective-permute-start | bytes 49160 | tf_op jit(solution)/shard_map/ppermute | solution.py:599
  220.1 6.9 %collective-permute-start.53 = (f32[8,2048]{1,0:T(8,128)S(1)}, f32[8,2048]{1,0:T(8,128)S(1)}, u32[]{:S(2)}, u32[]{:S(2)}) collective-permute-start(f32[8,2048]{1,0:T(8,128)S(1)} %add_add_fusion.3), channel_id=1, source_target_pairs={{0,16},{1,17},{2,18},{3,19},{4,20},{5,21},{6,22},{7,23},{8,24},{9,... | collective-permute-start | bytes 196616 | tf_op jit(solution)/shard_map/ppermute | solution.py:599
  220.1 6.9 %collective-permute-start.52 = (f32[8,2048]{1,0:T(8,128)S(1)}, f32[8,2048]{1,0:T(8,128)S(1)}, u32[]{:S(2)}, u32[]{:S(2)}) collective-permute-start(f32[8,2048]{1,0:T(8,128)S(1)} %add_add_fusion.3), channel_id=1, source_target_pairs={{0,8},{1,9},{2,10},{3,11},{4,12},{5,13},{6,14},{7,15},{8,0},{9,1},... | collective-permute-start | bytes 196616 | tf_op jit(solution)/shard_map/ppermute | solution.py:599
  250.6 7.1 %collective-permute-start.61 = (f32[8,2048]{1,0:T(8,128)S(1)}, f32[8,2048]{1,0:T(8,128)S(1)}, u32[]{:S(2)}, u32[]{:S(2)}) collective-permute-start(f32[8,2048]{1,0:T(8,128)S(1)} %add_add_fusion.1), channel_id=1, source_target_pairs={{0,16},{1,17},{2,18},{3,19},{4,20},{5,21},{6,22},{7,23},{8,24},{9,... | collective-permute-start | bytes 196616 | tf_op jit(solution)/shard_map/ppermute | solution.py:599
  250.6 7.1 %collective-permute-start.60 = (f32[8,2048]{1,0:T(8,128)S(1)}, f32[8,2048]{1,0:T(8,128)S(1)}, u32[]{:S(2)}, u32[]{:S(2)}) collective-permute-start(f32[8,2048]{1,0:T(8,128)S(1)} %add_add_fusion.1), channel_id=1, source_target_pairs={{0,8},{1,9},{2,10},{3,11},{4,12},{5,13},{6,14},{7,15},{8,0},{9,1},... | collective-permute-start | bytes 196616 | tf_op jit(solution)/shard_map/ppermute | solution.py:599
  271.1 6.2 %collective-permute-start.67 = (f32[8,512]{1,0:T(8,128)S(1)}, f32[8,512]{1,0:T(8,128)S(1)}, u32[]{:S(2)}, u32[]{:S(2)}) collective-permute-start(f32[8,512]{1,0:T(8,128)S(1)} %add.893), channel_id=1, source_target_pairs={{0,6},{1,7},{2,4},{3,5},{4,2},{5,3},{6,0},{7,1},{8,14},{9,15},{10,... | collective-permute-start | bytes 49160 | tf_op jit(solution)/shard_map/ppermute | solution.py:599
  311.1 14.8 %collective-permute-start.75 = (bf16[2,2,2,2,64,512]{5,4,0,1,2,3:T(8,128)(2,1)}, bf16[2,2,2,2,64,512]{5,4,0,1,2,3:T(8,128)(2,1)}, u32[]{:S(2)}, u32[]{:S(2)}) collective-permute-start(bf16[2,2,2,2,64,512]{5,4,0,1,2,3:T(8,128)(2,1)} %copy_bitcast_fusion.1), channel_id=1, source_target_pairs={{0,1},{1,0},{2,3},{3,2},{4,5},{5,4},{6,7},{7,6},{8,9},{9,8},{10,11... | collective-permute-start | bytes 3145736 | tf_op jit(solution)/shard_map/ppermute | solution.py:599
  311.6 15.7 %collective-permute-start.76 = (bf16[2,2,2,2,80,512]{5,4,0,1,3,2:T(8,128)(2,1)}, bf16[2,2,2,2,80,512]{5,4,0,1,3,2:T(8,128)(2,1)}, u32[]{:S(2)}, u32[]{:S(2)}) collective-permute-start(bf16[2,2,2,2,80,512]{5,4,0,1,3,2:T(8,128)(2,1)} %copy_bitcast_fusion), channel_id=1, source_target_pairs={{0,1},{1,0},{2,3},{3,2},{4,5},{5,4},{6,7},{7,6},{8,9},{9,8},{10,11... | collective-permute-start | bytes 3932168 | tf_op jit(solution)/shard_map/ppermute | solution.py:599
  329.0 5.7 %collective-permute-start.79 = (f32[8,512]{1,0:T(8,128)S(1)}, f32[8,512]{1,0:T(8,128)S(1)}, u32[]{:S(2)}, u32[]{:S(2)}) collective-permute-start(f32[8,512]{1,0:T(8,128)S(1)} %add_add_fusion.9), channel_id=1, source_target_pairs={{0,24},{1,25},{2,26},{3,27},{4,28},{5,29},{6,30},{7,31},{8,16},{9,... | collective-permute-start | bytes 49160 | tf_op jit(solution)/shard_map/ppermute | solution.py:599
  332.6 24.4 %collective-permute-start.84 = (bf16[2,2,2,64,512]{4,3,0,1,2:T(8,128)(2,1)S(1)}, bf16[2,2,2,64,512]{4,3,0,1,2:T(8,128)(2,1)S(1)}, u32[]{:S(2)}, u32[]{:S(2)}) collective-permute-start(bf16[2,2,2,64,512]{4,3,0,1,2:T(8,128)(2,1)S(1)} %get-tuple-element.167), channel_id=1, source_target_pairs={{0,2},{1,3},{2,0},{3,1},{4,6},{5,7},{6,4},{7,5},{8,10},{9,11},{10,... | collective-permute-start | bytes 1572872 | tf_op jit(solution)/shard_map/ppermute | solution.py:599
  333.5 23.8 %collective-permute-start.85 = (bf16[2,2,2,80,512]{4,3,0,1,2:T(8,128)(2,1)S(1)}, bf16[2,2,2,80,512]{4,3,0,1,2:T(8,128)(2,1)S(1)}, u32[]{:S(2)}, u32[]{:S(2)}) collective-permute-start(bf16[2,2,2,80,512]{4,3,0,1,2:T(8,128)(2,1)S(1)} %get-tuple-element.168), channel_id=1, source_target_pairs={{0,4},{1,5},{2,6},{3,7},{4,0},{5,1},{6,2},{7,3},{8,12},{9,13},{10,... | collective-permute-start | bytes 1966088 | tf_op jit(solution)/shard_map/ppermute | solution.py:599
  351.8 5.4 %collective-permute-start.86 = (bf16[2,2,2,2,64,256]{5,4,3,2,1,0:T(8,128)(2,1)S(1)}, bf16[2,2,2,2,64,256]{5,4,3,2,1,0:T(8,128)(2,1)S(1)}, u32[]{:S(2)}, u32[]{:S(2)}) collective-permute-start(bf16[2,2,2,2,64,256]{5,4,3,2,1,0:T(8,128)(2,1)S(1)} %fusion.10), channel_id=1, source_target_pairs={{0,1},{1,0},{2,3},{3,2},{4,5},{5,4},{6,7},{7,6},{8,9},{9,8},{10,11... | collective-permute-start | bytes 1572872 | tf_op jit(solution)/shard_map/ppermute | solution.py:599
  357.4 5.2 %collective-permute-start.89 = (f32[8,1024]{1,0:T(8,128)S(1)}, f32[8,1024]{1,0:T(8,128)S(1)}, u32[]{:S(2)}, u32[]{:S(2)}) collective-permute-start(f32[8,1024]{1,0:T(8,128)S(1)} %add_add_fusion.5), channel_id=1, source_target_pairs={{0,24},{1,25},{2,26},{3,27},{4,28},{5,29},{6,30},{7,31},{8,16},{9,... | collective-permute-start | bytes 98312 | tf_op jit(solution)/shard_map/ppermute | solution.py:599
  361.1 16.7 %collective-permute-start.91 = (bf16[2,2,2,64,256]{4,3,2,1,0:T(8,128)(2,1)S(1)}, bf16[2,2,2,64,256]{4,3,2,1,0:T(8,128)(2,1)S(1)}, u32[]{:S(2)}, u32[]{:S(2)}) collective-permute-start(bf16[2,2,2,64,256]{4,3,2,1,0:T(8,128)(2,1)S(1)} %fusion.17), channel_id=1, source_target_pairs={{0,4},{1,5},{2,6},{3,7},{4,0},{5,1},{6,2},{7,3},{8,12},{9,13},{10,... | collective-permute-start | bytes 786440 | tf_op jit(solution)/shard_map/ppermute | solution.py:599
  361.6 22.4 %collective-permute-start.96 = (bf16[2,2,64,512]{3,2,0,1:T(8,128)(2,1)S(1)}, bf16[2,2,64,512]{3,2,0,1:T(8,128)(2,1)S(1)}, u32[]{:S(2)}, u32[]{:S(2)}) collective-permute-start(bf16[2,2,64,512]{3,2,0,1:T(8,128)(2,1)S(1)} %get-tuple-element.178), channel_id=1, source_target_pairs={{0,4},{1,5},{2,6},{3,7},{4,0},{5,1},{6,2},{7,3},{8,12},{9,13},{10,... | collective-permute-start | bytes 786440 | tf_op jit(solution)/shard_map/ppermute | solution.py:599
  362.6 25.6 %collective-permute-start.97 = (bf16[2,2,80,512]{3,2,0,1:T(8,128)(2,1)S(1)}, bf16[2,2,80,512]{3,2,0,1:T(8,128)(2,1)S(1)}, u32[]{:S(2)}, u32[]{:S(2)}) collective-permute-start(bf16[2,2,80,512]{3,2,0,1:T(8,128)(2,1)S(1)} %get-tuple-element.179), channel_id=1, source_target_pairs={{0,2},{1,3},{2,0},{3,1},{4,6},{5,7},{6,4},{7,5},{8,10},{9,11},{10,... | collective-permute-start | bytes 983048 | tf_op jit(solution)/shard_map/ppermute | solution.py:599
  370.8 6.9 %collective-permute-start.90 = (f32[8,256]{1,0:T(8,128)S(1)}, f32[8,256]{1,0:T(8,128)S(1)}, u32[]{:S(2)}, u32[]{:S(2)}) collective-permute-start(f32[8,256]{1,0:T(8,128)S(1)} %get-tuple-element.172), channel_id=1, source_target_pairs={{0,1},{1,0},{2,3},{3,2},{4,5},{5,4},{6,7},{7,6},{8,9},{9,8},{10,11... | collective-permute-start | bytes 24584 | tf_op jit(solution)/shard_map/ppermute | solution.py:599
  377.7 9.3 %collective-permute-start.94 = (f32[8,256]{1,0:T(8,128)S(1)}, f32[8,256]{1,0:T(8,128)S(1)}, u32[]{:S(2)}, u32[]{:S(2)}) collective-permute-start(f32[8,256]{1,0:T(8,128)S(1)} %add.928), channel_id=1, source_target_pairs={{0,6},{1,7},{2,4},{3,5},{4,2},{5,3},{6,0},{7,1},{8,14},{9,15},{10,... | collective-permute-start | bytes 24584 | tf_op jit(solution)/shard_map/ppermute | solution.py:599
  379.0 8.0 %collective-permute-start.93 = (f32[8,256]{1,0:T(8,128)S(1)}, f32[8,256]{1,0:T(8,128)S(1)}, u32[]{:S(2)}, u32[]{:S(2)}) collective-permute-start(f32[8,256]{1,0:T(8,128)S(1)} %add.928), channel_id=1, source_target_pairs={{0,4},{1,5},{2,6},{3,7},{4,0},{5,1},{6,2},{7,3},{8,12},{9,13},{10,... | collective-permute-start | bytes 24584 | tf_op jit(solution)/shard_map/ppermute | solution.py:599
  379.0 8.0 %collective-permute-start.92 = (f32[8,256]{1,0:T(8,128)S(1)}, f32[8,256]{1,0:T(8,128)S(1)}, u32[]{:S(2)}, u32[]{:S(2)}) collective-permute-start(f32[8,256]{1,0:T(8,128)S(1)} %add.928), channel_id=1, source_target_pairs={{0,2},{1,3},{2,0},{3,1},{4,6},{5,7},{6,4},{7,5},{8,10},{9,11},{10,... | collective-permute-start | bytes 24584 | tf_op jit(solution)/shard_map/ppermute | solution.py:599
  389.4 5.3 %collective-permute-start.98 = (f32[8,256]{1,0:T(8,128)S(1)}, f32[8,256]{1,0:T(8,128)S(1)}, u32[]{:S(2)}, u32[]{:S(2)}) collective-permute-start(f32[8,256]{1,0:T(8,128)S(1)} %add_add_fusion.19), channel_id=1, source_target_pairs={{0,8},{1,9},{2,10},{3,11},{4,12},{5,13},{6,14},{7,15},{8,0},{9,1},... | collective-permute-start | bytes 24584 | tf_op jit(solution)/shard_map/ppermute | solution.py:599
  391.8 13.6 %collective-permute-start.102 = (bf16[2,2,2,32,256]{4,3,2,0,1:T(8,128)(2,1)S(1)}, bf16[2,2,2,32,256]{4,3,2,0,1:T(8,128)(2,1)S(1)}, u32[]{:S(2)}, u32[]{:S(2)}) collective-permute-start(bf16[2,2,2,32,256]{4,3,2,0,1:T(8,128)(2,1)S(1)} %get-tuple-element.186), channel_id=1, source_target_pairs={{0,4},{1,5},{2,6},{3,7},{4,0},{5,1},{6,2},{7,3},{8,12},{9,13},{10,... | collective-permute-start | bytes 393224 | tf_op jit(solution)/shard_map/ppermute | solution.py:599
  401.1 15.8 %collective-permute-start.107 = (bf16[2,64,512]{2,1,0:T(8,128)(2,1)S(1)}, bf16[2,64,512]{2,1,0:T(8,128)(2,1)S(1)}, u32[]{:S(2)}, u32[]{:S(2)}) collective-permute-start(bf16[2,64,512]{2,1,0:T(8,128)(2,1)S(1)} %get-tuple-element.189), channel_id=1, source_target_pairs={{0,8},{1,9},{2,10},{3,11},{4,12},{5,13},{6,14},{7,15},{8,0},{9,1},... | collective-permute-start | bytes 393224 | tf_op jit(solution)/shard_map/ppermute | solution.py:599
  402.4 13.0 %collective-permute-start.109 = (bf16[2,2,64,256]{3,2,1,0:T(8,128)(2,1)S(1)}, bf16[2,2,64,256]{3,2,1,0:T(8,128)(2,1)S(1)}, u32[]{:S(2)}, u32[]{:S(2)}) collective-permute-start(bf16[2,2,64,256]{3,2,1,0:T(8,128)(2,1)S(1)} %fusion.25), channel_id=1, source_target_pairs={{0,8},{1,9},{2,10},{3,11},{4,12},{5,13},{6,14},{7,15},{8,0},{9,1},... | collective-permute-start | bytes 393224 | tf_op jit(solution)/shard_map/ppermute | solution.py:599
  405.4 11.3 %collective-permute-start.105 = (f32[8,256]{1,0:T(8,128)S(1)}, f32[8,256]{1,0:T(8,128)S(1)}, u32[]{:S(2)}, u32[]{:S(2)}) collective-permute-start(f32[8,256]{1,0:T(8,128)S(1)} %add.946), channel_id=1, source_target_pairs={{0,6},{1,7},{2,4},{3,5},{4,2},{5,3},{6,0},{7,1},{8,14},{9,15},{10,... | collective-permute-start | bytes 24584 | tf_op jit(solution)/shard_map/ppermute | solution.py:599
  406.9 9.9 %collective-permute-start.104 = (f32[8,256]{1,0:T(8,128)S(1)}, f32[8,256]{1,0:T(8,128)S(1)}, u32[]{:S(2)}, u32[]{:S(2)}) collective-permute-start(f32[8,256]{1,0:T(8,128)S(1)} %add.946), channel_id=1, source_target_pairs={{0,4},{1,5},{2,6},{3,7},{4,0},{5,1},{6,2},{7,3},{8,12},{9,13},{10,... | collective-permute-start | bytes 24584 | tf_op jit(solution)/shard_map/ppermute | solution.py:599
  407.5 9.4 %collective-permute-start.103 = (f32[8,256]{1,0:T(8,128)S(1)}, f32[8,256]{1,0:T(8,128)S(1)}, u32[]{:S(2)}, u32[]{:S(2)}) collective-permute-start(f32[8,256]{1,0:T(8,128)S(1)} %add.946), channel_id=1, source_target_pairs={{0,2},{1,3},{2,0},{3,1},{4,6},{5,7},{6,4},{7,5},{8,10},{9,11},{10,... | collective-permute-start | bytes 24584 | tf_op jit(solution)/shard_map/ppermute | solution.py:599
  415.4 7.2 %collective-permute-start.106 = (bf16[2,2,2,2,72,256]{5,4,3,2,1,0:T(8,128)(2,1)S(1)}, bf16[2,2,2,2,72,256]{5,4,3,2,1,0:T(8,128)(2,1)S(1)}, u32[]{:S(2)}, u32[]{:S(2)}) collective-permute-start(bf16[2,2,2,2,72,256]{5,4,3,2,1,0:T(8,128)(2,1)S(1)} %dynamic-slice_bitcast_fusion), channel_id=1, source_target_pairs={{0,1},{1,0},{2,3},{3,2},{4,5},{5,4},{6,7},{7,6},{8,9},{9,8},{10,11... | collective-permute-start | bytes 1769480 | tf_op jit(solution)/shard_map/ppermute | solution.py:599
  416.7 5.9 %collective-permute-start.108 = (bf16[2,80,512]{2,1,0:T(8,128)(2,1)S(1)}, bf16[2,80,512]{2,1,0:T(8,128)(2,1)S(1)}, u32[]{:S(2)}, u32[]{:S(2)}) collective-permute-start(bf16[2,80,512]{2,1,0:T(8,128)(2,1)S(1)} %get-tuple-element.190), channel_id=1, source_target_pairs={{0,8},{1,9},{2,10},{3,11},{4,12},{5,13},{6,14},{7,15},{8,0},{9,1},... | collective-permute-start | bytes 491528 | tf_op jit(solution)/shard_map/ppermute | solution.py:599
  426.3 10.2 %collective-permute-start.116 = (bf16[2,2,2,72,256]{4,3,2,1,0:T(8,128)(2,1)S(1)}, bf16[2,2,2,72,256]{4,3,2,1,0:T(8,128)(2,1)S(1)}, u32[]{:S(2)}, u32[]{:S(2)}) collective-permute-start(bf16[2,2,2,72,256]{4,3,2,1,0:T(8,128)(2,1)S(1)} %bitcast_add_fusion.1), channel_id=1, source_target_pairs={{0,4},{1,5},{2,6},{3,7},{4,0},{5,1},{6,2},{7,3},{8,12},{9,13},{10,... | collective-permute-start | bytes 884744 | tf_op jit(solution)/shard_map/ppermute | solution.py:599
  428.2 6.9 %collective-permute-start.118 = (bf16[2,2,32,256]{3,2,1,0:T(8,128)(2,1)S(1)}, bf16[2,2,32,256]{3,2,1,0:T(8,128)(2,1)S(1)}, u32[]{:S(2)}, u32[]{:S(2)}) collective-permute-start(bf16[2,2,32,256]{3,2,1,0:T(8,128)(2,1)S(1)} %add_bitcast_fusion.3), channel_id=1, source_target_pairs={{0,8},{1,9},{2,10},{3,11},{4,12},{5,13},{6,14},{7,15},{8,0},{9,1},... | collective-permute-start | bytes 196616 | tf_op jit(solution)/shard_map/ppermute | solution.py:599
  444.4 15.2 %collective-permute-start.119 = (bf16[2,200,256]{2,1,0:T(8,128)(2,1)S(1)}, bf16[2,200,256]{2,1,0:T(8,128)(2,1)S(1)}, u32[]{:S(2)}, u32[]{:S(2)}) collective-permute-start(bf16[2,200,256]{2,1,0:T(8,128)(2,1)S(1)} %dynamic-slice_bitcast_fusion.4), channel_id=1, source_target_pairs={{0,16},{1,17},{2,18},{3,19},{4,20},{5,21},{6,22},{7,23},{8,24},{9,... | collective-permute-start | bytes 614408 | tf_op jit(solution)/shard_map/ppermute | solution.py:599
  445.9 15.1 %collective-permute-start.126 = (bf16[64,512]{1,0:T(8,128)(2,1)S(1)}, bf16[64,512]{1,0:T(8,128)(2,1)S(1)}, u32[]{:S(2)}, u32[]{:S(2)}) collective-permute-start(bf16[64,512]{1,0:T(8,128)(2,1)S(1)} %fusion.31), channel_id=1, source_target_pairs={{0,16},{1,17},{2,18},{3,19},{4,20},{5,21},{6,22},{7,23},{8,24},{9,... | collective-permute-start | bytes 196616 | tf_op jit(solution)/shard_map/ppermute | solution.py:599
  447.6 19.8 %collective-permute-start.127 = (bf16[80,512]{1,0:T(8,128)(2,1)S(1)}, bf16[80,512]{1,0:T(8,128)(2,1)S(1)}, u32[]{:S(2)}, u32[]{:S(2)}) collective-permute-start(bf16[80,512]{1,0:T(8,128)(2,1)S(1)} %fusion.29), channel_id=1, source_target_pairs={{0,16},{1,17},{2,18},{3,19},{4,20},{5,21},{6,22},{7,23},{8,24},{9,... | collective-permute-start | bytes 245768 | tf_op jit(solution)/shard_map/ppermute | solution.py:599
  448.3 46.3 %collective-permute-start.121 = (bf16[192,1024]{1,0:T(8,128)(2,1)}, bf16[192,1024]{1,0:T(8,128)(2,1)S(1)}, u32[]{:S(2)}, u32[]{:S(2)}) collective-permute-start(bf16[192,1024]{1,0:T(8,128)(2,1)} %get-tuple-element.198), channel_id=1, source_target_pairs={{0,4},{4,8},{8,12},{12,16},{16,20},{20,24},{24,28},{1,5},{5,9},{9,... | collective-permute-start | bytes 1179656 | tf_op jit(solution)/shard_map/ppermute | solution.py:605
  459.6 5.8 %collective-permute-start.124 = (bf16[2,200,256]{2,1,0:T(8,128)(2,1)S(1)}, bf16[2,200,256]{2,1,0:T(8,128)(2,1)S(1)}, u32[]{:S(2)}, u32[]{:S(2)}) collective-permute-start(bf16[2,200,256]{2,1,0:T(8,128)(2,1)S(1)} %bitcast_add_fusion.2), channel_id=1, source_target_pairs={{0,2},{1,3},{2,0},{3,1},{4,6},{5,7},{6,4},{7,5},{8,10},{9,11},{10,... | collective-permute-start | bytes 614408 | tf_op jit(solution)/shard_map/ppermute | solution.py:599
  465.5 8.5 %collective-permute-start.125 = (bf16[2,200,256]{2,1,0:T(8,128)(2,1)S(1)}, bf16[2,200,256]{2,1,0:T(8,128)(2,1)S(1)}, u32[]{:S(2)}, u32[]{:S(2)}) collective-permute-start(bf16[2,200,256]{2,1,0:T(8,128)(2,1)S(1)} %add.986), channel_id=1, source_target_pairs={{0,1},{1,0},{2,3},{3,2},{4,5},{5,4},{6,7},{7,6},{8,9},{9,8},{10,11... | collective-permute-start | bytes 614408 | tf_op jit(solution)/shard_map/ppermute | solution.py:599
  468.0 26.6 %collective-permute-start.120 = (bf16[3,192,256]{2,1,0:T(8,128)(2,1)}, bf16[3,192,256]{2,1,0:T(8,128)(2,1)}, u32[]{:S(2)}, u32[]{:S(2)}) collective-permute-start(bf16[3,192,256]{2,1,0:T(8,128)(2,1)} %slice.228), channel_id=1, source_target_pairs={{0,4},{4,8},{8,12},{12,16},{16,20},{20,24},{24,28},{1,5},{5,9},{9,... | collective-permute-start | bytes 884744 | tf_op jit(solution)/shard_map/ppermute | solution.py:605
  470.2 24.4 %collective-permute-start.122 = (bf16[192,1024]{1,0:T(8,128)(2,1)}, bf16[192,1024]{1,0:T(8,128)(2,1)S(1)}, u32[]{:S(2)}, u32[]{:S(2)}) collective-permute-start(bf16[192,1024]{1,0:T(8,128)(2,1)} %get-tuple-element.199), channel_id=1, source_target_pairs={{0,4},{4,8},{8,12},{12,16},{16,20},{20,24},{24,28},{1,5},{5,9},{9,... | collective-permute-start | bytes 1179656 | tf_op jit(solution)/shard_map/ppermute | solution.py:605
  472.1 24.4 %collective-permute-start.123 = (bf16[192,1024]{1,0:T(8,128)(2,1)}, bf16[192,1024]{1,0:T(8,128)(2,1)S(1)}, u32[]{:S(2)}, u32[]{:S(2)}) collective-permute-start(bf16[192,1024]{1,0:T(8,128)(2,1)} %get-tuple-element.200), channel_id=1, source_target_pairs={{0,4},{4,8},{8,12},{12,16},{16,20},{20,24},{24,28},{1,5},{5,9},{9,... | collective-permute-start | bytes 1179656 | tf_op jit(solution)/shard_map/ppermute | solution.py:605
  476.6 5.3 %collective-permute-start.128 = (bf16[144,512]{1,0:T(8,128)(2,1)}, bf16[144,512]{1,0:T(8,128)(2,1)S(1)}, u32[]{:S(2)}, u32[]{:S(2)}) collective-permute-start(bf16[144,512]{1,0:T(8,128)(2,1)} %pad_maximum_fusion.14), channel_id=1, source_target_pairs={{0,2},{1,3},{2,0},{3,1},{4,6},{5,7},{6,4},{7,5},{8,10},{9,11},{10,... | collective-permute-start | bytes 442376 | tf_op jit(solution)/shard_map/ppermute | solution.py:599
  481.9 5.5 %collective-permute-start.130 = (bf16[48,2048]{1,0:T(8,128)(2,1)}, bf16[48,2048]{1,0:T(8,128)(2,1)S(1)}, u32[]{:S(2)}, u32[]{:S(2)}) collective-permute-start(bf16[48,2048]{1,0:T(8,128)(2,1)} %reduce-scatter.2.cloned.1.call-done), channel_id=1, source_target_pairs={{0,2},{1,3},{2,0},{3,1},{4,6},{5,7},{6,4},{7,5},{8,10},{9,11},{10,... | collective-permute-start | bytes 589832 | tf_op jit(solution)/shard_map/ppermute | solution.py:599
  (160 other events, 1494.1 us)
Sparse Core Ops, SparseCore 0:
  11.5 71.5 all-gather.2
  86.5 75.0 all-gather.4
  311.8 124.6 reduce-scatter.1

commit v5 on v4

--- a/solution.py
+++ b/solution.py
@@ -1102,7 +1102,8 @@
     chain_rn.launch(chain_rn.ready[0])
     landed = chain_rn.flying
     chain_rn.land()
-    hook(landed, finish=[chain_r1], start=[chain_r1])
+    chain_r4 = Chain(spread_steps(jnp.concatenate([c.value() for c in chain_rs], 0)))
+    hook(landed, finish=[chain_r1], start=[chain_r1, chain_rb, chain_r4])
     while not chain_rn.done:
         chain_rn.launch(chain_rn.ready[0])
         landed = chain_rn.flying
@@ -1114,8 +1115,7 @@
     landed = chain_last.flying
     chain_last.land()
     hook(landed, start=[chain_dp] + chain_ds[1:])
-    chain_r4 = Chain(spread_steps(jnp.concatenate([c.value() for c in chain_rs], 0)))
-    hook(landed, start=[chain_rb, chain_r4])
+    hook(landed, finish=[chain_rb, chain_r4], start=[chain_rb, chain_r4])
     chain_last.launch(chain_last.ready[0])
     landed = chain_last.flying
     chain_last.land()

time: 514 us -> 508 us (0.988)
  starting transfers between devices: 179 us -> 166 us
  waiting for transfers between devices: 115 us -> 127 us
    ppermute x8, waiting for transfers between devices: 13.4 us -> 41.1 us  [from_behind(): return lax.ppermute(x, 'rows', pairs)]
    ppermute x124, waiting for transfers between devices: 102 us -> 85.8 us  [exchange(): return lax.ppermute(x, AXES, [(i, i ^ mask) for i in range(total)])]
    ppermute x8, starting transfers between devices: 29.1 us -> 20.3 us  [from_behind(): return lax.ppermute(x, 'rows', pairs)]
    unnamed x180 -> x190, local copies, waits for them, and re-layouts: 37.3 us -> 37.2 us
  transfers between devices with their start and end apart: 135 -> 135, of which waited for: 61 -> 65; matrix products, arithmetic and copies ran while one was open for 10% -> 10% of each run, Pallas kernels for 13% -> 13%
where the time goes in v5:
time: 508 us; the launch traced here: 503 us
  starting transfers between devices  166 us (33%)
  waiting for transfers between devices  127 us (25%)
  Pallas kernels  99.1 us (20%)
  local copies, waits for them, and re-layouts  53.7 us (11%)
  other arithmetic  24.3 us (5%)
  matrix products  16.9 us (3%)
  between operations  16.1 us (3%)
    ppermute x124, starting transfers between devices, exchange(): return lax.ppermute(x, AXES, [(i, i ^ mask) for i in range(total)])  146 us
    pallas_call x16, Pallas kernels, call(): pl.pallas_call(run, grid=(micro,), in_specs=in_specs, out_specs=out_specs...  92.4 us
    ppermute x124, waiting for transfers between devices, exchange(): return lax.ppermute(x, AXES, [(i, i ^ mask) for i in range(total)])  85.8 us
    ppermute x8, waiting for transfers between devices, from_behind(): return lax.ppermute(x, 'rows', pairs)  41.1 us
    unnamed x190, local copies, waits for them, and re-layouts  37.2 us
    ppermute x8, starting transfers between devices, from_behind(): return lax.ppermute(x, 'rows', pairs)  20.3 us
    dot_general x8, matrix products, weight_term(): lax.dot_general(left.reshape(-1, k), right.reshape(-1, n), (((0,), (0,)),...  16.9 us
  transfers between devices with their start and end apart: 135, of which 65 were waited for; matrix products, arithmetic and copies ran while one was open for 10% of the time, Pallas kernels for 13%

profile of v5, /device:TPU:25, one launch (start us, length us, event | category | flops | bytes accessed | tf_op | source)
XLA Modules:
  0.0 503.3 jit_solution(3215668009330119509)
XLA Ops:
  12.2 3.4 k_masks.1
  26.9 5.4 %collective-permute-start.3 = (bf16[2,2,2,64,256]{4,3,2,1,0:T(8,128)(2,1)S(1)}, bf16[2,2,2,64,256]{4,3,2,1,0:T(8,128)(2,1)S(1)}, u32[]{:S(2)}, u32[]{:S(2)}) collective-permute-start(bf16[2,2,2,64,256]{4,3,2,1,0:T(8,128)(2,1)S(1)} %pad_maximum_fusion.12), channel_id=1, source_target_pairs={{0,1},{1,0},{2,3},{3,2},{4,5},{5,4},{6,7},{7,6},{8,9},{9,8},{10,11... | collective-permute-start | bytes 786440 | tf_op jit(solution)/shard_map/ppermute | solution.py:599
  38.6 1.9 collective-permute-start.10
  47.9 2.6 collective-permute-start.11
  51.4 4.2 collective-permute-done.11.refs_1_.refs_9_.refs_2_
  55.6 4.1 collective-permute-start.16
  61.4 3.5 collective-permute-start.21
  64.9 1.9 collective-permute-start.22
  66.8 3.9 collective-permute-start.23
  71.0 5.6 %k_second.1 = (f32[3,640,256]{2,1,0:T(8,128)S(1)}, bf16[3,640,2304]{2,1,0:T(8,128)(2,1)S(1)}, f32[8,256]{1,0:T(8,128)S(1)}) custom-call(f32[3,416,256]{2,1,0:T(8,128)S(1)} %copy-done.19, bf16[3,192,256]{2,1,0:T(8,128)(2,1)S(1)} %collective-permute-done.11.refs_1_.refs_9_.refs_2_, f32[8,256]{1,0:T(8,128)S(1)} %add_add_fusion.22.refs_2_.refs_10_.refs_3_, ...), custom_call_target="tpu_custom_call" | custom-call | tf_op jit(solution)/shard_map/k_second/pallas_call | solution.py:853
  76.7 3.4 copy-done.68
  84.4 8.2 %collective-permute-done.22.refs_3_ = bf16[12,14,1024]{2,1,0:T(8,128)(2,1)S(1)} collective-permute-done((bf16[12,14,1024]{2,1,0:T(8,128)(2,1)S(1)}, bf16[12,14,1024]{2,1,0:T(8,128)(2,1)S(1)}, u32[]{:S(2)}, u32[]{:S(2)}) %collective-permute-start.22) | collective-permute-done | bytes 344096 | tf_op jit(solution)/shard_map/ppermute | solution.py:605
  92.7 8.4 %collective-permute-done.23.refs_4_ = bf16[12,14,1024]{2,1,0:T(8,128)(2,1)S(1)} collective-permute-done((bf16[12,14,1024]{2,1,0:T(8,128)(2,1)S(1)}, bf16[12,14,1024]{2,1,0:T(8,128)(2,1)S(1)}, u32[]{:S(2)}, u32[]{:S(2)}) %collective-permute-start.23) | collective-permute-done | bytes 344096 | tf_op jit(solution)/shard_map/ppermute | solution.py:605
  105.5 2.0 collective-permute-start.24
  110.5 6.0 %k_third.2 = (bf16[3,640,256]{2,1,0:T(8,128)(2,1)S(1)}, bf16[3,640,1024]{2,1,0:T(8,128)(2,1)S(1)}, f32[8,1024]{1,0:T(8,128)S(1)}) custom-call(f32[3,640,256]{2,1,0:T(8,128)S(1)} %get-tuple-element.127.refs_0_.refs_7_.refs_1_, f32[8,256]{1,0:T(8,128)S(1)} %add_add_fusion.20.refs_1_.refs_8_.refs_2_, f32[1,256]{1,0:T(1,128)S(1)} %bitcast.441, ...), custom_call_target="tpu_custom_call" | custom-call | tf_op jit(solution)/shard_map/k_third/pallas_call | solution.py:853
  119.5 3.8 collective-permute-start.30
  128.6 2.5 collective-permute-start.31
  132.7 3.0 collective-permute-done.32
  135.8 10.7 %k_fourth.1 = (bf16[3,640,1024]{2,1,0:T(8,128)(2,1)S(1)}, bf16[3,160,1024]{2,1,0:T(8,128)(2,1)S(1)}, bf16[3,640,1024]{2,1,0:T(8,128)(2,1)S(1)}, bf16[3,640,512]{2,1,0:T(8,128)(2,1)S(1)}, f32[8,512]{1,0:T(8,128)S(1)}) custom-call(bf16[3,640,1024]{2,1,0:T(8,128)(2,1)S(1)} %get-tuple-element.133.refs_0_.refs_8_.refs_1_, bf16[3,640,1024]{2,1,0:T(8,128)(2,1)S(1)} %copy-done.14, ...), custom_call_target="tpu_custom_call" | custom-call | tf_op jit(solution)/shard_map/k_fourth/pallas_call | solution.py:853
  148.4 1.9 copy-done.70
  150.3 2.0 collective-permute-start.34
  157.6 2.3 collective-permute-start.40
  162.6 2.2 collective-permute-done.39
  164.8 6.5 %k_fifth.1 = (f32[3,160,512]{2,1,0:T(8,128)S(1)}, bf16[3,160,4608]{2,1,0:T(8,128)(2,1)S(1)}, f32[8,512]{1,0:T(8,128)S(1)}) custom-call(bf16[3,640,512]{2,1,0:T(8,128)(2,1)S(1)} %get-tuple-element.135.refs_0_.refs_8_.refs_1_, f32[8,512]{1,0:T(8,128)S(1)} %add_add_fusion.14.refs_1_.refs_9_.refs_2_, f32[1,512]{1,0:T(1,128)S(1)} %bitcast.426, ...), custom_call_target="tpu_custom_call" | custom-call | tf_op jit(solution)/shard_map/k_fifth/pallas_call | solution.py:853
  183.8 2.8 copy-done
  186.6 3.3 k_seventh.1
  190.0 4.1 k_third.3
  198.2 3.5 collective-permute-start.48
  207.6 2.2 collective-permute-done.50
  214.8 3.7 collective-permute-done.53
  224.6 8.2 %k_last.1 = (bf16[3,1,19,7,2048]{4,3,2,1,0:T(8,128)(2,1)}, bf16[3,160,2048]{2,1,0:T(8,128)(2,1)S(1)}, f32[8,4096]{1,0:T(8,128)S(1)}) custom-call(bf16[3,160,2048]{2,1,0:T(8,128)(2,1)S(1)} %copy-done.35, bf16[3,160,2048]{2,1,0:T(8,128)(2,1)S(1)} %copy-done.33, f32[8,2048]{1,0:T(8,128)S(1)} %get-tuple-element.320.refs_2_.refs_3_, ...), custom_call_target="tpu_custom_call" | custom-call | tf_op jit(solution)/shard_map/k_last/pallas_call | solution.py:853
  238.2 2.2 collective-permute-done.58
  242.0 2.0 collective-permute-start.60
  245.4 3.6 collective-permute-done.61
  250.7 7.4 %k_back_six.1 = (bf16[3,160,2048]{2,1,0:T(8,128)(2,1)S(1)}, bf16[3,160,2048]{2,1,0:T(8,128)(2,1)S(1)}, f32[3,160,512]{2,1,0:T(8,128)S(1)}, f32[8,512]{1,0:T(8,128)S(1)}) custom-call(bf16[3,160,2048]{2,1,0:T(8,128)(2,1)S(1)} %get-tuple-element.147.refs_0_, bf16[3,160,2048]{2,1,0:T(8,128)(2,1)S(1)} %copy-done.35, bf16[3,160,2048]{2,1,0:T(8,128)(2,1)S(1)} %copy-done.33, ...), custom_call_target="tpu_custom_call" | custom-call | tf_op jit(solution)/shard_map/k_back_six/pallas_call | solution.py:853
  258.5 2.4 bitcast_convert_fusion.1
  265.0 3.4 pad_maximum_fusion
  273.7 2.8 copy-done.6
  279.8 10.1 %k_back_five.1 = (bf16[3,160,512]{2,1,0:T(8,128)(2,1)S(1)}, f32[3,640,512]{2,1,0:T(8,128)S(1)}, f32[8,512]{1,0:T(8,128)S(1)}) custom-call(f32[3,160,512]{2,1,0:T(8,128)S(1)} %copy-done.55, f32[3,160,512]{2,1,0:T(8,128)S(1)} %copy-done.28, f32[8,512]{1,0:T(8,128)S(1)} %add_add_fusion.12.refs_1_.refs_9_.refs_2_, f32[8,512]{1,0:T(8,128)S(1)} %add_add_fusion.10.refs_3_, ...), custom_call_target="tpu_custom_call" | custom-call | tf_op jit(solution)/shard_map/k_back_five/pallas_call | solution.py:853
  291.7 5.3 %bitcast_convert_fusion = bf16[4608,512]{1,0:T(8,128)(2,1)S(1)} fusion(bf16[3,160,4608]{2,1,0:T(8,128)(2,1)} %copy-done.69, bf16[3,160,512]{2,1,0:T(8,128)(2,1)S(1)} %get-tuple-element.158), kind=kOutput, calls=%fused_computation | convolution fusion | flops 2267283456 | bytes 9633792 | tf_op jit(solution)/shard_map/dot_general | solution.py:869
  297.4 2.5 collective-permute-start.71
  302.8 2.8 copy-done.2
  307.1 4.9 k_corner.1.refs_7_
  325.4 8.4 %k_back_four.1 = (bf16[3,640,512]{2,1,0:T(8,128)(2,1)S(1)}, bf16[3,640,1024]{2,1,0:T(8,128)(2,1)S(1)}, f32[8,1024]{1,0:T(8,128)S(1)}) custom-call(f32[3,640,512]{2,1,0:T(8,128)S(1)} %copy-done.44, bf16[3,640,512]{2,1,0:T(8,128)(2,1)S(1)} %copy-done.12, f32[8,512]{1,0:T(8,128)S(1)} %add_add_fusion.14.refs_1_.refs_9_.refs_2_, ...), custom_call_target="tpu_custom_call" | custom-call | tf_op jit(solution)/shard_map/k_back_four/pallas_call | solution.py:853
  336.4 3.6 collective-permute-start.80
  354.0 7.7 %k_back_three.1 = (bf16[3,640,1024]{2,1,0:T(8,128)(2,1)S(1)}, f32[3,640,256]{2,1,0:T(8,128)S(1)}, f32[8,256]{1,0:T(8,128)S(1)}) custom-call(bf16[3,640,1024]{2,1,0:T(8,128)(2,1)S(1)} %get-tuple-element.164.refs_0_.refs_2_, bf16[3,640,1024]{2,1,0:T(8,128)(2,1)S(1)} %copy-done.5, f32[8,1024]{1,0:T(8,128)S(1)} %add_add_fusion.6.refs_2_.refs_10_, ...), custom_call_target="tpu_custom_call" | custom-call | tf_op jit(solution)/shard_map/k_back_three/pallas_call | solution.py:853
  361.7 4.7 collective-permute-start.90
  370.8 2.3 collective-permute-done.96
  373.1 4.4 collective-permute-start.95
  380.0 2.3 collective-permute-start.98
  385.3 5.8 %k_back_two.1 = (bf16[3,640,256]{2,1,0:T(8,128)(2,1)S(1)}, f32[3,640,256]{2,1,0:T(8,128)S(1)}, f32[8,256]{1,0:T(8,128)S(1)}) custom-call(f32[3,640,256]{2,1,0:T(8,128)S(1)} %get-tuple-element.173.refs_0_, f32[3,640,256]{2,1,0:T(8,128)S(1)} %copy-done.10, f32[8,256]{1,0:T(8,128)S(1)} %add_add_fusion.20.refs_1_.refs_8_.refs_2_, ...), custom_call_target="tpu_custom_call" | custom-call | tf_op jit(solution)/shard_map/k_back_two/pallas_call | solution.py:853
  393.1 2.8 fusion
  398.7 7.0 %collective-permute-done.109 = bf16[2,2,64,256]{3,2,1,0:T(8,128)(2,1)S(1)} collective-permute-done((bf16[2,2,64,256]{3,2,1,0:T(8,128)(2,1)S(1)}, bf16[2,2,64,256]{3,2,1,0:T(8,128)(2,1)S(1)}, u32[]{:S(2)}, u32[]{:S(2)}) %collective-permute-start.109) | collective-permute-done | bytes 131104 | tf_op jit(solution)/shard_map/ppermute | solution.py:599
  407.5 5.5 %collective-permute-done.108 = bf16[2,80,512]{2,1,0:T(8,128)(2,1)S(1)} collective-permute-done((bf16[2,80,512]{2,1,0:T(8,128)(2,1)S(1)}, bf16[2,80,512]{2,1,0:T(8,128)(2,1)S(1)}, u32[]{:S(2)}, u32[]{:S(2)}) %collective-permute-start.108) | collective-permute-done | bytes 163872 | tf_op jit(solution)/shard_map/ppermute | solution.py:599
  425.4 3.0 collective-permute-start.113
  428.5 2.2 collective-permute-done.118
  431.9 3.1 collective-permute-done.114
  444.5 8.8 %collective-permute-done.121 = bf16[2,200,256]{2,1,0:T(8,128)(2,1)S(1)} collective-permute-done((bf16[2,200,256]{2,1,0:T(8,128)(2,1)S(1)}, bf16[2,200,256]{2,1,0:T(8,128)(2,1)S(1)}, u32[]{:S(2)}, u32[]{:S(2)}) %collective-permute-start.121) | collective-permute-done | bytes 204832 | tf_op jit(solution)/shard_map/ppermute | solution.py:599
  456.5 2.7 collective-permute-start.123
  464.1 1.9 collective-permute-start.125
  473.0 3.4 collective-permute-done.122.refs_1_
  476.4 8.4 %collective-permute-done.124.refs_5_ = bf16[192,1024]{1,0:T(8,128)(2,1)S(1)} collective-permute-done((bf16[192,1024]{1,0:T(8,128)(2,1)S(1)}, bf16[192,1024]{1,0:T(8,128)(2,1)S(1)}, u32[]{:S(2)}, u32[]{:S(2)}) %collective-permute-start.124) | collective-permute-done | bytes 393248 | tf_op jit(solution)/shard_map/ppermute | solution.py:605
  484.8 8.4 %collective-permute-done.125.refs_6_ = bf16[192,1024]{1,0:T(8,128)(2,1)S(1)} collective-permute-done((bf16[192,1024]{1,0:T(8,128)(2,1)S(1)}, bf16[192,1024]{1,0:T(8,128)(2,1)S(1)}, u32[]{:S(2)}, u32[]{:S(2)}) %collective-permute-start.125) | collective-permute-done | bytes 393248 | tf_op jit(solution)/shard_map/ppermute | solution.py:605
  493.3 3.4 k_input.1
  (580 shorter events, 211.2 us)
Async XLA Ops:
  7.2 102.1 %all-gather.3.cloned.1.call-start = ((), (), s32[]{:S(2)}) async-start(), calls=%async_computation.1 | async-start | bytes 6488064 | tf_op jit(solution)/shard_map/all_gather | solution.py:722
  8.9 174.9 %all-gather.5.cloned.1.call-start = ((), (), s32[]{:S(2)}) async-start(), calls=%async_computation.2 | async-start | bytes 6488064 | tf_op jit(solution)/shard_map/all_gather | solution.py:722
  10.6 425.5 %reduce-scatter.2.cloned.1.call-start = ((), (), s32[]{:S(2)}) async-start(), calls=%async_computation.3 | async-start | bytes 6488064 | tf_op jit(solution)/shard_map/reduce_scatter | solution.py:1029
  25.7 6.6 %collective-permute-start.6 = (bf16[2,72,256]{2,1,0:T(8,128)(2,1)S(1)}, bf16[2,72,256]{2,1,0:T(8,128)(2,1)S(1)}, u32[]{:S(2)}, u32[]{:S(2)}) collective-permute-start(bf16[2,72,256]{2,1,0:T(8,128)(2,1)S(1)} %pad_maximum_fusion.16), channel_id=1, source_target_pairs={{0,8},{1,9},{2,10},{3,11},{4,12},{5,13},{6,14},{7,15},{8,0},{9,1},... | collective-permute-start | bytes 221192 | tf_op jit(solution)/shard_map/ppermute | solution.py:599
  26.9 6.7 %collective-permute-start.3 = (bf16[2,2,2,64,256]{4,3,2,1,0:T(8,128)(2,1)S(1)}, bf16[2,2,2,64,256]{4,3,2,1,0:T(8,128)(2,1)S(1)}, u32[]{:S(2)}, u32[]{:S(2)}) collective-permute-start(bf16[2,2,2,64,256]{4,3,2,1,0:T(8,128)(2,1)S(1)} %pad_maximum_fusion.12), channel_id=1, source_target_pairs={{0,1},{1,0},{2,3},{3,2},{4,5},{5,4},{6,7},{7,6},{8,9},{9,8},{10,11... | collective-permute-start | bytes 786440 | tf_op jit(solution)/shard_map/ppermute | solution.py:599
  32.3 5.5 %collective-permute-start.7 = (bf16[2,2,72,256]{3,2,1,0:T(8,128)(2,1)S(1)}, bf16[2,2,72,256]{3,2,1,0:T(8,128)(2,1)S(1)}, u32[]{:S(2)}, u32[]{:S(2)}) collective-permute-start(bf16[2,2,72,256]{3,2,1,0:T(8,128)(2,1)S(1)} %pad_maximum_fusion.13), channel_id=1, source_target_pairs={{0,4},{1,5},{2,6},{3,7},{4,0},{5,1},{6,2},{7,3},{8,12},{9,13},{10,... | collective-permute-start | bytes 442376 | tf_op jit(solution)/shard_map/ppermute | solution.py:599
  44.0 7.3 %collective-permute-start.15 = (bf16[2,2,2,72,256]{4,3,2,1,0:T(8,128)(2,1)S(1)}, bf16[2,2,2,72,256]{4,3,2,1,0:T(8,128)(2,1)S(1)}, u32[]{:S(2)}, u32[]{:S(2)}) collective-permute-start(bf16[2,2,2,72,256]{4,3,2,1,0:T(8,128)(2,1)S(1)} %pad_maximum_fusion.9), channel_id=1, source_target_pairs={{0,2},{1,3},{2,0},{3,1},{4,6},{5,7},{6,4},{7,5},{8,10},{9,11},{10,... | collective-permute-start | bytes 884744 | tf_op jit(solution)/shard_map/ppermute | solution.py:599
  44.4 6.1 %collective-permute-start.14 = (f32[8,256]{1,0:T(8,128)S(1)}, f32[8,256]{1,0:T(8,128)S(1)}, u32[]{:S(2)}, u32[]{:S(2)}) collective-permute-start(f32[8,256]{1,0:T(8,128)S(1)} %add_add_fusion.23), channel_id=1, source_target_pairs={{0,24},{1,25},{2,26},{3,27},{4,28},{5,29},{6,30},{7,31},{8,16},{9,... | collective-permute-start | bytes 24584 | tf_op jit(solution)/shard_map/ppermute | solution.py:599
  47.9 7.7 %collective-permute-start.11 = (bf16[3,192,256]{2,1,0:T(8,128)(2,1)}, bf16[3,192,256]{2,1,0:T(8,128)(2,1)S(1)}, u32[]{:S(2)}, u32[]{:S(2)}) collective-permute-start(bf16[3,192,256]{2,1,0:T(8,128)(2,1)} %copy-done.74), channel_id=1, source_target_pairs={{4,0},{8,4},{12,8},{16,12},{20,16},{24,20},{28,24},{5,1},{9,5},{13... | collective-permute-start | bytes 884744 | tf_op jit(solution)/shard_map/ppermute | solution.py:605
  55.6 15.2 %collective-permute-start.16 = (bf16[2,2,2,2,72,256]{5,4,3,2,1,0:T(8,128)(2,1)S(1)}, bf16[2,2,2,2,72,256]{5,4,3,2,1,0:T(8,128)(2,1)S(1)}, u32[]{:S(2)}, u32[]{:S(2)}) collective-permute-start(bf16[2,2,2,2,72,256]{5,4,3,2,1,0:T(8,128)(2,1)S(1)} %pad_maximum_fusion.3), channel_id=1, source_target_pairs={{0,1},{1,0},{2,3},{3,2},{4,5},{5,4},{6,7},{7,6},{8,9},{9,8},{10,11... | collective-permute-start | bytes 1769480 | tf_op jit(solution)/shard_map/ppermute | solution.py:599
  61.4 22.4 %collective-permute-start.21 = (bf16[12,14,1024]{2,1,0:T(8,128)(2,1)S(1)}, bf16[12,14,1024]{2,1,0:T(8,128)(2,1)S(1)}, u32[]{:S(2)}, u32[]{:S(2)}) collective-permute-start(bf16[12,14,1024]{2,1,0:T(8,128)(2,1)S(1)} %get-tuple-element.129), channel_id=1, source_target_pairs={{4,0},{8,4},{12,8},{16,12},{20,16},{24,20},{28,24},{5,1},{9,5},{13... | collective-permute-start | bytes 1032200 | tf_op jit(solution)/shard_map/ppermute | solution.py:605
  64.9 27.7 %collective-permute-start.22 = (bf16[12,14,1024]{2,1,0:T(8,128)(2,1)S(1)}, bf16[12,14,1024]{2,1,0:T(8,128)(2,1)S(1)}, u32[]{:S(2)}, u32[]{:S(2)}) collective-permute-start(bf16[12,14,1024]{2,1,0:T(8,128)(2,1)S(1)} %get-tuple-element.130), channel_id=1, source_target_pairs={{4,0},{8,4},{12,8},{16,12},{20,16},{24,20},{28,24},{5,1},{9,5},{13... | collective-permute-start | bytes 1032200 | tf_op jit(solution)/shard_map/ppermute | solution.py:605
  66.8 34.2 %collective-permute-start.23 = (bf16[12,14,1024]{2,1,0:T(8,128)(2,1)S(1)}, bf16[12,14,1024]{2,1,0:T(8,128)(2,1)S(1)}, u32[]{:S(2)}, u32[]{:S(2)}) collective-permute-start(bf16[12,14,1024]{2,1,0:T(8,128)(2,1)S(1)} %get-tuple-element.131), channel_id=1, source_target_pairs={{4,0},{8,4},{12,8},{16,12},{20,16},{24,20},{28,24},{5,1},{9,5},{13... | collective-permute-start | bytes 1032200 | tf_op jit(solution)/shard_map/ppermute | solution.py:605
  81.8 22.1 %collective-permute-start.20 = (f32[8,256]{1,0:T(8,128)S(1)}, f32[8,256]{1,0:T(8,128)S(1)}, u32[]{:S(2)}, u32[]{:S(2)}) collective-permute-start(f32[8,256]{1,0:T(8,128)S(1)} %add.849), channel_id=1, source_target_pairs={{0,6},{1,7},{2,4},{3,5},{4,2},{5,3},{6,0},{7,1},{8,14},{9,15},{10,... | collective-permute-start | bytes 24584 | tf_op jit(solution)/shard_map/ppermute | solution.py:599
  82.1 21.7 %collective-permute-start.19 = (f32[8,256]{1,0:T(8,128)S(1)}, f32[8,256]{1,0:T(8,128)S(1)}, u32[]{:S(2)}, u32[]{:S(2)}) collective-permute-start(f32[8,256]{1,0:T(8,128)S(1)} %add.849), channel_id=1, source_target_pairs={{0,4},{1,5},{2,6},{3,7},{4,0},{5,1},{6,2},{7,3},{8,12},{9,13},{10,... | collective-permute-start | bytes 24584 | tf_op jit(solution)/shard_map/ppermute | solution.py:599
  83.8 20.1 %collective-permute-start.18 = (f32[8,256]{1,0:T(8,128)S(1)}, f32[8,256]{1,0:T(8,128)S(1)}, u32[]{:S(2)}, u32[]{:S(2)}) collective-permute-start(f32[8,256]{1,0:T(8,128)S(1)} %add.849), channel_id=1, source_target_pairs={{0,2},{1,3},{2,0},{3,1},{4,6},{5,7},{6,4},{7,5},{8,10},{9,11},{10,... | collective-permute-start | bytes 24584 | tf_op jit(solution)/shard_map/ppermute | solution.py:599
  119.5 5.5 %collective-permute-start.30 = (f32[8,1024]{1,0:T(8,128)S(1)}, f32[8,1024]{1,0:T(8,128)S(1)}, u32[]{:S(2)}, u32[]{:S(2)}) collective-permute-start(f32[8,1024]{1,0:T(8,128)S(1)} %add.856), channel_id=1, source_target_pairs={{0,6},{1,7},{2,4},{3,5},{4,2},{5,3},{6,0},{7,1},{8,14},{9,15},{10,... | collective-permute-start | bytes 98312 | tf_op jit(solution)/shard_map/ppermute | solution.py:599
  128.5 7.2 %collective-permute-start.32 = (f32[8,1024]{1,0:T(8,128)S(1)}, f32[8,1024]{1,0:T(8,128)S(1)}, u32[]{:S(2)}, u32[]{:S(2)}) collective-permute-start(f32[8,1024]{1,0:T(8,128)S(1)} %add_add_fusion.7), channel_id=1, source_target_pairs={{0,16},{1,17},{2,18},{3,19},{4,20},{5,21},{6,22},{7,23},{8,24},{9,... | collective-permute-start | bytes 98312 | tf_op jit(solution)/shard_map/ppermute | solution.py:599
  128.6 7.1 %collective-permute-start.31 = (f32[8,1024]{1,0:T(8,128)S(1)}, f32[8,1024]{1,0:T(8,128)S(1)}, u32[]{:S(2)}, u32[]{:S(2)}) collective-permute-start(f32[8,1024]{1,0:T(8,128)S(1)} %add_add_fusion.7), channel_id=1, source_target_pairs={{0,8},{1,9},{2,10},{3,11},{4,12},{5,13},{6,14},{7,15},{8,0},{9,1},... | collective-permute-start | bytes 98312 | tf_op jit(solution)/shard_map/ppermute | solution.py:599
  180.2 9.7 %collective-permute-start.47 = (f32[8,512]{1,0:T(8,128)S(1)}, f32[8,512]{1,0:T(8,128)S(1)}, u32[]{:S(2)}, u32[]{:S(2)}) collective-permute-start(f32[8,512]{1,0:T(8,128)S(1)} %add_add_fusion.13), channel_id=1, source_target_pairs={{0,24},{1,25},{2,26},{3,27},{4,28},{5,29},{6,30},{7,31},{8,16},{9,... | collective-permute-start | bytes 49160 | tf_op jit(solution)/shard_map/ppermute | solution.py:599
  181.9 8.0 %collective-permute-start.46 = (f32[8,512]{1,0:T(8,128)S(1)}, f32[8,512]{1,0:T(8,128)S(1)}, u32[]{:S(2)}, u32[]{:S(2)}) collective-permute-start(f32[8,512]{1,0:T(8,128)S(1)} %add_add_fusion.13), channel_id=1, source_target_pairs={{0,16},{1,17},{2,18},{3,19},{4,20},{5,21},{6,22},{7,23},{8,24},{9,... | collective-permute-start | bytes 49160 | tf_op jit(solution)/shard_map/ppermute | solution.py:599
  182.4 7.5 %collective-permute-start.45 = (f32[8,512]{1,0:T(8,128)S(1)}, f32[8,512]{1,0:T(8,128)S(1)}, u32[]{:S(2)}, u32[]{:S(2)}) collective-permute-start(f32[8,512]{1,0:T(8,128)S(1)} %add_add_fusion.13), channel_id=1, source_target_pairs={{0,8},{1,9},{2,10},{3,11},{4,12},{5,13},{6,14},{7,15},{8,0},{9,1},... | collective-permute-start | bytes 49160 | tf_op jit(solution)/shard_map/ppermute | solution.py:599
  211.5 7.0 %collective-permute-start.53 = (f32[8,2048]{1,0:T(8,128)S(1)}, f32[8,2048]{1,0:T(8,128)S(1)}, u32[]{:S(2)}, u32[]{:S(2)}) collective-permute-start(f32[8,2048]{1,0:T(8,128)S(1)} %add_add_fusion.3), channel_id=1, source_target_pairs={{0,16},{1,17},{2,18},{3,19},{4,20},{5,21},{6,22},{7,23},{8,24},{9,... | collective-permute-start | bytes 196616 | tf_op jit(solution)/shard_map/ppermute | solution.py:599
  211.5 7.0 %collective-permute-start.52 = (f32[8,2048]{1,0:T(8,128)S(1)}, f32[8,2048]{1,0:T(8,128)S(1)}, u32[]{:S(2)}, u32[]{:S(2)}) collective-permute-start(f32[8,2048]{1,0:T(8,128)S(1)} %add_add_fusion.3), channel_id=1, source_target_pairs={{0,8},{1,9},{2,10},{3,11},{4,12},{5,13},{6,14},{7,15},{8,0},{9,1},... | collective-permute-start | bytes 196616 | tf_op jit(solution)/shard_map/ppermute | solution.py:599
  242.0 7.0 %collective-permute-start.61 = (f32[8,2048]{1,0:T(8,128)S(1)}, f32[8,2048]{1,0:T(8,128)S(1)}, u32[]{:S(2)}, u32[]{:S(2)}) collective-permute-start(f32[8,2048]{1,0:T(8,128)S(1)} %add_add_fusion.1), channel_id=1, source_target_pairs={{0,16},{1,17},{2,18},{3,19},{4,20},{5,21},{6,22},{7,23},{8,24},{9,... | collective-permute-start | bytes 196616 | tf_op jit(solution)/shard_map/ppermute | solution.py:599
  242.0 7.0 %collective-permute-start.60 = (f32[8,2048]{1,0:T(8,128)S(1)}, f32[8,2048]{1,0:T(8,128)S(1)}, u32[]{:S(2)}, u32[]{:S(2)}) collective-permute-start(f32[8,2048]{1,0:T(8,128)S(1)} %add_add_fusion.1), channel_id=1, source_target_pairs={{0,8},{1,9},{2,10},{3,11},{4,12},{5,13},{6,14},{7,15},{8,0},{9,1},... | collective-permute-start | bytes 196616 | tf_op jit(solution)/shard_map/ppermute | solution.py:599
  262.3 6.1 %collective-permute-start.67 = (f32[8,512]{1,0:T(8,128)S(1)}, f32[8,512]{1,0:T(8,128)S(1)}, u32[]{:S(2)}, u32[]{:S(2)}) collective-permute-start(f32[8,512]{1,0:T(8,128)S(1)} %add.893), channel_id=1, source_target_pairs={{0,6},{1,7},{2,4},{3,5},{4,2},{5,3},{6,0},{7,1},{8,14},{9,15},{10,... | collective-permute-start | bytes 49160 | tf_op jit(solution)/shard_map/ppermute | solution.py:599
  302.2 14.6 %collective-permute-start.75 = (bf16[2,2,2,2,64,512]{5,4,0,1,2,3:T(8,128)(2,1)}, bf16[2,2,2,2,64,512]{5,4,0,1,2,3:T(8,128)(2,1)}, u32[]{:S(2)}, u32[]{:S(2)}) collective-permute-start(bf16[2,2,2,2,64,512]{5,4,0,1,2,3:T(8,128)(2,1)} %copy_bitcast_fusion.1), channel_id=1, source_target_pairs={{0,1},{1,0},{2,3},{3,2},{4,5},{5,4},{6,7},{7,6},{8,9},{9,8},{10,11... | collective-permute-start | bytes 3145736 | tf_op jit(solution)/shard_map/ppermute | solution.py:599
  302.7 15.6 %collective-permute-start.76 = (bf16[2,2,2,2,80,512]{5,4,0,1,3,2:T(8,128)(2,1)}, bf16[2,2,2,2,80,512]{5,4,0,1,3,2:T(8,128)(2,1)}, u32[]{:S(2)}, u32[]{:S(2)}) collective-permute-start(bf16[2,2,2,2,80,512]{5,4,0,1,3,2:T(8,128)(2,1)} %copy_bitcast_fusion), channel_id=1, source_target_pairs={{0,1},{1,0},{2,3},{3,2},{4,5},{5,4},{6,7},{7,6},{8,9},{9,8},{10,11... | collective-permute-start | bytes 3932168 | tf_op jit(solution)/shard_map/ppermute | solution.py:599
  319.9 5.3 %collective-permute-start.79 = (f32[8,512]{1,0:T(8,128)S(1)}, f32[8,512]{1,0:T(8,128)S(1)}, u32[]{:S(2)}, u32[]{:S(2)}) collective-permute-start(f32[8,512]{1,0:T(8,128)S(1)} %add_add_fusion.9), channel_id=1, source_target_pairs={{0,24},{1,25},{2,26},{3,27},{4,28},{5,29},{6,30},{7,31},{8,16},{9,... | collective-permute-start | bytes 49160 | tf_op jit(solution)/shard_map/ppermute | solution.py:599
  323.5 24.1 %collective-permute-start.84 = (bf16[2,2,2,64,512]{4,3,0,1,2:T(8,128)(2,1)S(1)}, bf16[2,2,2,64,512]{4,3,0,1,2:T(8,128)(2,1)S(1)}, u32[]{:S(2)}, u32[]{:S(2)}) collective-permute-start(bf16[2,2,2,64,512]{4,3,0,1,2:T(8,128)(2,1)S(1)} %get-tuple-element.169), channel_id=1, source_target_pairs={{0,2},{1,3},{2,0},{3,1},{4,6},{5,7},{6,4},{7,5},{8,10},{9,11},{10,... | collective-permute-start | bytes 1572872 | tf_op jit(solution)/shard_map/ppermute | solution.py:599
  324.3 23.5 %collective-permute-start.85 = (bf16[2,2,2,80,512]{4,3,0,1,2:T(8,128)(2,1)S(1)}, bf16[2,2,2,80,512]{4,3,0,1,2:T(8,128)(2,1)S(1)}, u32[]{:S(2)}, u32[]{:S(2)}) collective-permute-start(bf16[2,2,2,80,512]{4,3,0,1,2:T(8,128)(2,1)S(1)} %get-tuple-element.170), channel_id=1, source_target_pairs={{0,4},{1,5},{2,6},{3,7},{4,0},{5,1},{6,2},{7,3},{8,12},{9,13},{10,... | collective-permute-start | bytes 1966088 | tf_op jit(solution)/shard_map/ppermute | solution.py:599
  342.4 5.3 %collective-permute-start.86 = (bf16[2,2,2,2,64,256]{5,4,3,2,1,0:T(8,128)(2,1)S(1)}, bf16[2,2,2,2,64,256]{5,4,3,2,1,0:T(8,128)(2,1)S(1)}, u32[]{:S(2)}, u32[]{:S(2)}) collective-permute-start(bf16[2,2,2,2,64,256]{5,4,3,2,1,0:T(8,128)(2,1)S(1)} %fusion.10), channel_id=1, source_target_pairs={{0,1},{1,0},{2,3},{3,2},{4,5},{5,4},{6,7},{7,6},{8,9},{9,8},{10,11... | collective-permute-start | bytes 1572872 | tf_op jit(solution)/shard_map/ppermute | solution.py:599
  347.9 5.2 %collective-permute-start.89 = (f32[8,1024]{1,0:T(8,128)S(1)}, f32[8,1024]{1,0:T(8,128)S(1)}, u32[]{:S(2)}, u32[]{:S(2)}) collective-permute-start(f32[8,1024]{1,0:T(8,128)S(1)} %add_add_fusion.5), channel_id=1, source_target_pairs={{0,24},{1,25},{2,26},{3,27},{4,28},{5,29},{6,30},{7,31},{8,16},{9,... | collective-permute-start | bytes 98312 | tf_op jit(solution)/shard_map/ppermute | solution.py:599
  351.6 16.3 %collective-permute-start.91 = (bf16[2,2,2,64,256]{4,3,2,1,0:T(8,128)(2,1)S(1)}, bf16[2,2,2,64,256]{4,3,2,1,0:T(8,128)(2,1)S(1)}, u32[]{:S(2)}, u32[]{:S(2)}) collective-permute-start(bf16[2,2,2,64,256]{4,3,2,1,0:T(8,128)(2,1)S(1)} %fusion.17), channel_id=1, source_target_pairs={{0,4},{1,5},{2,6},{3,7},{4,0},{5,1},{6,2},{7,3},{8,12},{9,13},{10,... | collective-permute-start | bytes 786440 | tf_op jit(solution)/shard_map/ppermute | solution.py:599
  352.4 20.7 %collective-permute-start.96 = (bf16[2,2,64,512]{3,2,0,1:T(8,128)(2,1)S(1)}, bf16[2,2,64,512]{3,2,0,1:T(8,128)(2,1)S(1)}, u32[]{:S(2)}, u32[]{:S(2)}) collective-permute-start(bf16[2,2,64,512]{3,2,0,1:T(8,128)(2,1)S(1)} %get-tuple-element.180), channel_id=1, source_target_pairs={{0,4},{1,5},{2,6},{3,7},{4,0},{5,1},{6,2},{7,3},{8,12},{9,13},{10,... | collective-permute-start | bytes 786440 | tf_op jit(solution)/shard_map/ppermute | solution.py:599
  353.1 25.6 %collective-permute-start.97 = (bf16[2,2,80,512]{3,2,0,1:T(8,128)(2,1)S(1)}, bf16[2,2,80,512]{3,2,0,1:T(8,128)(2,1)S(1)}, u32[]{:S(2)}, u32[]{:S(2)}) collective-permute-start(bf16[2,2,80,512]{3,2,0,1:T(8,128)(2,1)S(1)} %get-tuple-element.181), channel_id=1, source_target_pairs={{0,2},{1,3},{2,0},{3,1},{4,6},{5,7},{6,4},{7,5},{8,10},{9,11},{10,... | collective-permute-start | bytes 983048 | tf_op jit(solution)/shard_map/ppermute | solution.py:599
  361.7 6.1 %collective-permute-start.90 = (f32[8,256]{1,0:T(8,128)S(1)}, f32[8,256]{1,0:T(8,128)S(1)}, u32[]{:S(2)}, u32[]{:S(2)}) collective-permute-start(f32[8,256]{1,0:T(8,128)S(1)} %get-tuple-element.174), channel_id=1, source_target_pairs={{0,1},{1,0},{2,3},{3,2},{4,5},{5,4},{6,7},{7,6},{8,9},{9,8},{10,11... | collective-permute-start | bytes 24584 | tf_op jit(solution)/shard_map/ppermute | solution.py:599
  367.9 9.7 %collective-permute-start.94 = (f32[8,256]{1,0:T(8,128)S(1)}, f32[8,256]{1,0:T(8,128)S(1)}, u32[]{:S(2)}, u32[]{:S(2)}) collective-permute-start(f32[8,256]{1,0:T(8,128)S(1)} %add.928), channel_id=1, source_target_pairs={{0,6},{1,7},{2,4},{3,5},{4,2},{5,3},{6,0},{7,1},{8,14},{9,15},{10,... | collective-permute-start | bytes 24584 | tf_op jit(solution)/shard_map/ppermute | solution.py:599
  369.5 8.1 %collective-permute-start.93 = (f32[8,256]{1,0:T(8,128)S(1)}, f32[8,256]{1,0:T(8,128)S(1)}, u32[]{:S(2)}, u32[]{:S(2)}) collective-permute-start(f32[8,256]{1,0:T(8,128)S(1)} %add.928), channel_id=1, source_target_pairs={{0,4},{1,5},{2,6},{3,7},{4,0},{5,1},{6,2},{7,3},{8,12},{9,13},{10,... | collective-permute-start | bytes 24584 | tf_op jit(solution)/shard_map/ppermute | solution.py:599
  369.8 7.7 %collective-permute-start.92 = (f32[8,256]{1,0:T(8,128)S(1)}, f32[8,256]{1,0:T(8,128)S(1)}, u32[]{:S(2)}, u32[]{:S(2)}) collective-permute-start(f32[8,256]{1,0:T(8,128)S(1)} %add.928), channel_id=1, source_target_pairs={{0,2},{1,3},{2,0},{3,1},{4,6},{5,7},{6,4},{7,5},{8,10},{9,11},{10,... | collective-permute-start | bytes 24584 | tf_op jit(solution)/shard_map/ppermute | solution.py:599
  373.1 5.6 %collective-permute-start.95 = (bf16[2,2,2,2,32,256]{5,4,3,0,1,2:T(8,128)(2,1)S(1)}, bf16[2,2,2,2,32,256]{5,4,3,0,1,2:T(8,128)(2,1)S(1)}, u32[]{:S(2)}, u32[]{:S(2)}) collective-permute-start(bf16[2,2,2,2,32,256]{5,4,3,0,1,2:T(8,128)(2,1)S(1)} %copy_bitcast_fusion.6), channel_id=1, source_target_pairs={{0,1},{1,0},{2,3},{3,2},{4,5},{5,4},{6,7},{7,6},{8,9},{9,8},{10,11... | collective-permute-start | bytes 786440 | tf_op jit(solution)/shard_map/ppermute | solution.py:599
  380.0 5.2 %collective-permute-start.99 = (f32[8,256]{1,0:T(8,128)S(1)}, f32[8,256]{1,0:T(8,128)S(1)}, u32[]{:S(2)}, u32[]{:S(2)}) collective-permute-start(f32[8,256]{1,0:T(8,128)S(1)} %add_add_fusion.19), channel_id=1, source_target_pairs={{0,16},{1,17},{2,18},{3,19},{4,20},{5,21},{6,22},{7,23},{8,24},{9,... | collective-permute-start | bytes 24584 | tf_op jit(solution)/shard_map/ppermute | solution.py:599
  382.4 13.6 %collective-permute-start.102 = (bf16[2,2,2,32,256]{4,3,2,0,1:T(8,128)(2,1)S(1)}, bf16[2,2,2,32,256]{4,3,2,0,1:T(8,128)(2,1)S(1)}, u32[]{:S(2)}, u32[]{:S(2)}) collective-permute-start(bf16[2,2,2,32,256]{4,3,2,0,1:T(8,128)(2,1)S(1)} %get-tuple-element.188), channel_id=1, source_target_pairs={{0,4},{1,5},{2,6},{3,7},{4,0},{5,1},{6,2},{7,3},{8,12},{9,13},{10,... | collective-permute-start | bytes 393224 | tf_op jit(solution)/shard_map/ppermute | solution.py:599
  391.5 16.0 %collective-permute-start.107 = (bf16[2,64,512]{2,1,0:T(8,128)(2,1)S(1)}, bf16[2,64,512]{2,1,0:T(8,128)(2,1)S(1)}, u32[]{:S(2)}, u32[]{:S(2)}) collective-permute-start(bf16[2,64,512]{2,1,0:T(8,128)(2,1)S(1)} %get-tuple-element.191), channel_id=1, source_target_pairs={{0,8},{1,9},{2,10},{3,11},{4,12},{5,13},{6,14},{7,15},{8,0},{9,1},... | collective-permute-start | bytes 393224 | tf_op jit(solution)/shard_map/ppermute | solution.py:599
  393.0 12.7 %collective-permute-start.109 = (bf16[2,2,64,256]{3,2,1,0:T(8,128)(2,1)S(1)}, bf16[2,2,64,256]{3,2,1,0:T(8,128)(2,1)S(1)}, u32[]{:S(2)}, u32[]{:S(2)}) collective-permute-start(bf16[2,2,64,256]{3,2,1,0:T(8,128)(2,1)S(1)} %fusion.25), channel_id=1, source_target_pairs={{0,8},{1,9},{2,10},{3,11},{4,12},{5,13},{6,14},{7,15},{8,0},{9,1},... | collective-permute-start | bytes 393224 | tf_op jit(solution)/shard_map/ppermute | solution.py:599
  395.9 11.1 %collective-permute-start.105 = (f32[8,256]{1,0:T(8,128)S(1)}, f32[8,256]{1,0:T(8,128)S(1)}, u32[]{:S(2)}, u32[]{:S(2)}) collective-permute-start(f32[8,256]{1,0:T(8,128)S(1)} %add.946), channel_id=1, source_target_pairs={{0,6},{1,7},{2,4},{3,5},{4,2},{5,3},{6,0},{7,1},{8,14},{9,15},{10,... | collective-permute-start | bytes 24584 | tf_op jit(solution)/shard_map/ppermute | solution.py:599
  397.3 10.2 %collective-permute-start.104 = (f32[8,256]{1,0:T(8,128)S(1)}, f32[8,256]{1,0:T(8,128)S(1)}, u32[]{:S(2)}, u32[]{:S(2)}) collective-permute-start(f32[8,256]{1,0:T(8,128)S(1)} %add.946), channel_id=1, source_target_pairs={{0,4},{1,5},{2,6},{3,7},{4,0},{5,1},{6,2},{7,3},{8,12},{9,13},{10,... | collective-permute-start | bytes 24584 | tf_op jit(solution)/shard_map/ppermute | solution.py:599
  398.5 8.9 %collective-permute-start.103 = (f32[8,256]{1,0:T(8,128)S(1)}, f32[8,256]{1,0:T(8,128)S(1)}, u32[]{:S(2)}, u32[]{:S(2)}) collective-permute-start(f32[8,256]{1,0:T(8,128)S(1)} %add.946), channel_id=1, source_target_pairs={{0,2},{1,3},{2,0},{3,1},{4,6},{5,7},{6,4},{7,5},{8,10},{9,11},{10,... | collective-permute-start | bytes 24584 | tf_op jit(solution)/shard_map/ppermute | solution.py:599
  405.7 7.3 %collective-permute-start.106 = (bf16[2,2,2,2,72,256]{5,4,3,2,1,0:T(8,128)(2,1)S(1)}, bf16[2,2,2,2,72,256]{5,4,3,2,1,0:T(8,128)(2,1)S(1)}, u32[]{:S(2)}, u32[]{:S(2)}) collective-permute-start(bf16[2,2,2,2,72,256]{5,4,3,2,1,0:T(8,128)(2,1)S(1)} %dynamic-slice_bitcast_fusion), channel_id=1, source_target_pairs={{0,1},{1,0},{2,3},{3,2},{4,5},{5,4},{6,7},{7,6},{8,9},{9,8},{10,11... | collective-permute-start | bytes 1769480 | tf_op jit(solution)/shard_map/ppermute | solution.py:599
  407.1 5.9 %collective-permute-start.108 = (bf16[2,80,512]{2,1,0:T(8,128)(2,1)S(1)}, bf16[2,80,512]{2,1,0:T(8,128)(2,1)S(1)}, u32[]{:S(2)}, u32[]{:S(2)}) collective-permute-start(bf16[2,80,512]{2,1,0:T(8,128)(2,1)S(1)} %get-tuple-element.192), channel_id=1, source_target_pairs={{0,8},{1,9},{2,10},{3,11},{4,12},{5,13},{6,14},{7,15},{8,0},{9,1},... | collective-permute-start | bytes 491528 | tf_op jit(solution)/shard_map/ppermute | solution.py:599
  416.7 18.5 %collective-permute-start.116 = (bf16[2,2,2,72,256]{4,3,2,1,0:T(8,128)(2,1)S(1)}, bf16[2,2,2,72,256]{4,3,2,1,0:T(8,128)(2,1)}, u32[]{:S(2)}, u32[]{:S(2)}) collective-permute-start(bf16[2,2,2,72,256]{4,3,2,1,0:T(8,128)(2,1)S(1)} %bitcast_add_fusion.1), channel_id=1, source_target_pairs={{0,4},{1,5},{2,6},{3,7},{4,0},{5,1},{6,2},{7,3},{8,12},{9,13},{10,... | collective-permute-start | bytes 884744 | tf_op jit(solution)/shard_map/ppermute | solution.py:599
  418.7 9.8 %collective-permute-start.117 = (bf16[64,512]{1,0:T(8,128)(2,1)S(1)}, bf16[64,512]{1,0:T(8,128)(2,1)S(1)}, u32[]{:S(2)}, u32[]{:S(2)}) collective-permute-start(bf16[64,512]{1,0:T(8,128)(2,1)S(1)} %fusion.31), channel_id=1, source_target_pairs={{0,16},{1,17},{2,18},{3,19},{4,20},{5,21},{6,22},{7,23},{8,24},{9,... | collective-permute-start | bytes 196616 | tf_op jit(solution)/shard_map/ppermute | solution.py:599
  420.1 8.3 %collective-permute-start.120 = (bf16[2,2,32,256]{3,2,1,0:T(8,128)(2,1)S(1)}, bf16[2,2,32,256]{3,2,1,0:T(8,128)(2,1)S(1)}, u32[]{:S(2)}, u32[]{:S(2)}) collective-permute-start(bf16[2,2,32,256]{3,2,1,0:T(8,128)(2,1)S(1)} %add_bitcast_fusion.3), channel_id=1, source_target_pairs={{0,8},{1,9},{2,10},{3,11},{4,12},{5,13},{6,14},{7,15},{8,0},{9,1},... | collective-permute-start | bytes 196616 | tf_op jit(solution)/shard_map/ppermute | solution.py:599
  420.2 10.5 %collective-permute-start.118 = (bf16[80,512]{1,0:T(8,128)(2,1)S(1)}, bf16[80,512]{1,0:T(8,128)(2,1)S(1)}, u32[]{:S(2)}, u32[]{:S(2)}) collective-permute-start(bf16[80,512]{1,0:T(8,128)(2,1)S(1)} %fusion.29), channel_id=1, source_target_pairs={{0,16},{1,17},{2,18},{3,19},{4,20},{5,21},{6,22},{7,23},{8,24},{9,... | collective-permute-start | bytes 245768 | tf_op jit(solution)/shard_map/ppermute | solution.py:599
  425.4 5.3 %collective-permute-start.113 = (bf16[2,2,2,2,32,256]{5,4,3,2,1,0:T(8,128)(2,1)S(1)}, bf16[2,2,2,2,32,256]{5,4,3,2,1,0:T(8,128)(2,1)S(1)}, u32[]{:S(2)}, u32[]{:S(2)}) collective-permute-start(bf16[2,2,2,2,32,256]{5,4,3,2,1,0:T(8,128)(2,1)S(1)} %dynamic-slice_bitcast_fusion.2), channel_id=1, source_target_pairs={{0,1},{1,0},{2,3},{3,2},{4,5},{5,4},{6,7},{7,6},{8,9},{9,8},{10,11... | collective-permute-start | bytes 786440 | tf_op jit(solution)/shard_map/ppermute | solution.py:599
  441.9 11.3 %collective-permute-start.121 = (bf16[2,200,256]{2,1,0:T(8,128)(2,1)S(1)}, bf16[2,200,256]{2,1,0:T(8,128)(2,1)S(1)}, u32[]{:S(2)}, u32[]{:S(2)}) collective-permute-start(bf16[2,200,256]{2,1,0:T(8,128)(2,1)S(1)} %dynamic-slice_bitcast_fusion.4), channel_id=1, source_target_pairs={{0,16},{1,17},{2,18},{3,19},{4,20},{5,21},{6,22},{7,23},{8,24},{9,... | collective-permute-start | bytes 614408 | tf_op jit(solution)/shard_map/ppermute | solution.py:599
  453.3 8.8 %collective-permute-start.126 = (bf16[2,200,256]{2,1,0:T(8,128)(2,1)S(1)}, bf16[2,200,256]{2,1,0:T(8,128)(2,1)S(1)}, u32[]{:S(2)}, u32[]{:S(2)}) collective-permute-start(bf16[2,200,256]{2,1,0:T(8,128)(2,1)S(1)} %bitcast_add_fusion.2), channel_id=1, source_target_pairs={{0,2},{1,3},{2,0},{3,1},{4,6},{5,7},{6,4},{7,5},{8,10},{9,11},{10,... | collective-permute-start | bytes 614408 | tf_op jit(solution)/shard_map/ppermute | solution.py:599
  454.8 9.3 %collective-permute-start.130 = (bf16[2,144,512]{2,1,0:T(8,128)(2,1)S(1)}, bf16[2,144,512]{2,1,0:T(8,128)(2,1)S(1)}, u32[]{:S(2)}, u32[]{:S(2)}) collective-permute-start(bf16[2,144,512]{2,1,0:T(8,128)(2,1)S(1)} %pad_maximum_fusion.10), channel_id=1, source_target_pairs={{0,1},{1,0},{2,3},{3,2},{4,5},{5,4},{6,7},{7,6},{8,9},{9,8},{10,11... | collective-permute-start | bytes 884744 | tf_op jit(solution)/shard_map/ppermute | solution.py:599
  456.5 16.4 %collective-permute-start.123 = (bf16[192,1024]{1,0:T(8,128)(2,1)S(1)}, bf16[192,1024]{1,0:T(8,128)(2,1)S(1)}, u32[]{:S(2)}, u32[]{:S(2)}) collective-permute-start(bf16[192,1024]{1,0:T(8,128)(2,1)S(1)} %copy-done.81), channel_id=1, source_target_pairs={{0,4},{4,8},{8,12},{12,16},{16,20},{20,24},{24,28},{1,5},{5,9},{9,... | collective-permute-start | bytes 1179656 | tf_op jit(solution)/shard_map/ppermute | solution.py:605
  459.8 16.6 %collective-permute-start.122 = (bf16[3,192,256]{2,1,0:T(8,128)(2,1)S(1)}, bf16[3,192,256]{2,1,0:T(8,128)(2,1)S(1)}, u32[]{:S(2)}, u32[]{:S(2)}) collective-permute-start(bf16[3,192,256]{2,1,0:T(8,128)(2,1)S(1)} %slice.228), channel_id=1, source_target_pairs={{0,4},{4,8},{8,12},{12,16},{16,20},{20,24},{24,28},{1,5},{5,9},{9,... | collective-permute-start | bytes 884744 | tf_op jit(solution)/shard_map/ppermute | solution.py:605
  461.7 5.6 %collective-permute-start.131 = (bf16[2,48,2048]{2,1,0:T(8,128)(2,1)S(1)}, bf16[2,48,2048]{2,1,0:T(8,128)(2,1)S(1)}, u32[]{:S(2)}, u32[]{:S(2)}) collective-permute-start(bf16[2,48,2048]{2,1,0:T(8,128)(2,1)S(1)} %pad_maximum_fusion.8), channel_id=1, source_target_pairs={{0,1},{1,0},{2,3},{3,2},{4,5},{5,4},{6,7},{7,6},{8,9},{9,8},{10,11... | collective-permute-start | bytes 1179656 | tf_op jit(solution)/shard_map/ppermute | solution.py:599
  462.1 22.7 %collective-permute-start.124 = (bf16[192,1024]{1,0:T(8,128)(2,1)S(1)}, bf16[192,1024]{1,0:T(8,128)(2,1)S(1)}, u32[]{:S(2)}, u32[]{:S(2)}) collective-permute-start(bf16[192,1024]{1,0:T(8,128)(2,1)S(1)} %copy-done.80), channel_id=1, source_target_pairs={{0,4},{4,8},{8,12},{12,16},{16,20},{20,24},{24,28},{1,5},{5,9},{9,... | collective-permute-start | bytes 1179656 | tf_op jit(solution)/shard_map/ppermute | solution.py:605
  464.1 29.2 %collective-permute-start.125 = (bf16[192,1024]{1,0:T(8,128)(2,1)S(1)}, bf16[192,1024]{1,0:T(8,128)(2,1)S(1)}, u32[]{:S(2)}, u32[]{:S(2)}) collective-permute-start(bf16[192,1024]{1,0:T(8,128)(2,1)S(1)} %copy-done.79), channel_id=1, source_target_pairs={{0,4},{4,8},{8,12},{12,16},{16,20},{20,24},{24,28},{1,5},{5,9},{9,... | collective-permute-start | bytes 1179656 | tf_op jit(solution)/shard_map/ppermute | solution.py:605
  (165 other events, 1579.1 us)
Sparse Core Ops, SparseCore 0:
  11.5 78.4 all-gather.2
  93.4 74.2 all-gather.4
  302.9 126.1 reduce-scatter.1
